TPU v7x, 32 devices: a whole 2x2x4 slice. The times are simulated.
32 devices in a mesh: seq: 8 (over z, x), head: 4 (over y, core).
Axes of the slice: x: 2, y: 2, z: 4, core: 2. Of those that a mesh axis runs over, the one named last changes fastest.
Arguments:
- queries: bfloat16 [8192, 2048], P('seq', 'head'), may hold values from -1.796875 to 1.796875
- keys: bfloat16 [8192, 2048], P('seq', 'head'), may hold values from -1.796875 to 1.796875
- values: bfloat16 [8192, 2048], P('seq', 'head'), may hold values from -16 to 16
- grad_out: bfloat16 [8192, 2048], P('seq', 'head'), may hold values from -1.1953125 to 1.1953125
Outputs:
- output: bfloat16 [8192, 2048], P('seq', 'head')
- grad_query: bfloat16 [8192, 2048], P('seq', 'head')
- grad_key: bfloat16 [8192, 2048], P('seq', 'head')
- grad_value: bfloat16 [8192, 2048], P('seq', 'head')
All inputs are finite; a program needn't handle non-finite values.
Results may differ from a plain program's by a relative error of at most 0.0065.
Values sent between devices are 32-bit elements; how exact they have to be, the bound alone decides.
No kernel may reach another device: no remote copies, remote signals or barrier semaphores. Data moves between devices by JAX's collectives and lax.ppermute only.
A program may use at most 128 MiB of HBM per device.

v0:
```python
import jax
import jax.numpy as jnp
from jax import lax
from jax.sharding import PartitionSpec as P

HEADS = 16
HEAD_DIM = 128


EPSILON = 1e-06


def entering(shard, axis, combine, identity, reverse):
    size, here = (lax.axis_size(axis), lax.axis_index(axis))
    everything = lax.all_gather(shard, axis)
    start = jnp.broadcast_to(jnp.asarray(identity, shard.dtype), shard.shape)

    def step(k, before):
        at = size - 1 - k if reverse else k
        reached = at > here if reverse else at < here
        new = combine(before, everything[at])
        return jnp.where(reached, new, before)

    return lax.fori_loop(0, size, step, start)


def add_states(earlier, later):
    return earlier + later


def masked_scores(query_side, key_side):
    raw_scores = jnp.einsum(
        "thd,shd->hts", query_side, key_side, preferred_element_type=jnp.float32
    )
    count = query_side.shape[0]
    row_index = lax.broadcasted_iota(jnp.int32, (count, count), 0)
    col_index = lax.broadcasted_iota(jnp.int32, (count, count), 1)
    keep = (row_index >= col_index)[None]
    return jnp.where(keep, raw_scores, jnp.zeros_like(raw_scores)).astype(jnp.bfloat16)


def shards(queries, keys, values, grad_out):
    tok_rows = queries.shape[0]
    local_heads = queries.shape[1] // HEAD_DIM
    shaped = (tok_rows, local_heads, HEAD_DIM)
    full_width = HEADS * HEAD_DIM
    query_rows = queries.reshape(shaped)
    key_rows = keys.reshape(shaped)
    value_rows = values.reshape(shaped)
    local_state = jnp.einsum(
        "thd,the->hde", key_rows, value_rows, preferred_element_type=jnp.float32
    )
    zero_state = jnp.zeros_like(local_state)
    prefix = entering(local_state, "seq", add_states, zero_state, False)
    scores = masked_scores(query_rows, key_rows)
    prefix_round = prefix.astype(jnp.bfloat16)
    mixed = jnp.einsum("hts,she->the", scores, value_rows, preferred_element_type=jnp.float32)
    mixed = mixed + jnp.einsum(
        "thd,hde->the", query_rows, prefix_round, preferred_element_type=jnp.float32
    )
    mixed_rows = mixed.reshape(tok_rows, -1)
    grad_float = grad_out.astype(jnp.float32)
    squares = lax.psum(jnp.sum(mixed_rows * mixed_rows, axis=1), "head")
    inverse_rms = lax.rsqrt(squares / full_width + EPSILON)
    normed = mixed_rows * inverse_rms[:, None]
    crossed = lax.psum(jnp.sum(grad_float * normed, axis=1), "head")
    cross_mean = (crossed / full_width)[:, None]
    output = normed.astype(jnp.bfloat16)
    grad_mixed = (
        (inverse_rms[:, None] * (grad_float - normed * cross_mean))
        .astype(jnp.bfloat16)
        .reshape(shaped)
    )
    grad_state = jnp.einsum(
        "thd,the->hde", query_rows, grad_mixed, preferred_element_type=jnp.float32
    )
    suffix = entering(grad_state, "seq", add_states, zero_state, True)
    suffix_round = suffix.astype(jnp.bfloat16)
    grad_scores = masked_scores(grad_mixed, value_rows)
    grad_q = jnp.einsum("hts,shd->thd", grad_scores, key_rows, preferred_element_type=jnp.float32)
    grad_q = grad_q + jnp.einsum(
        "the,hde->thd", grad_mixed, prefix_round, preferred_element_type=jnp.float32
    )
    grad_k = jnp.einsum("hts,thd->shd", grad_scores, query_rows, preferred_element_type=jnp.float32)
    grad_k = grad_k + jnp.einsum(
        "she,hde->shd", value_rows, suffix_round, preferred_element_type=jnp.float32
    )
    grad_v = jnp.einsum("hts,the->she", scores, grad_mixed, preferred_element_type=jnp.float32)
    grad_v = grad_v + jnp.einsum(
        "shd,hde->she", key_rows, suffix_round, preferred_element_type=jnp.float32
    )
    flat_shape = (tok_rows, local_heads * HEAD_DIM)
    return (
        output,
        grad_q.astype(jnp.bfloat16).reshape(flat_shape),
        grad_k.astype(jnp.bfloat16).reshape(flat_shape),
        grad_v.astype(jnp.bfloat16).reshape(flat_shape),
    )


def solution(mesh):
    return jax.shard_map(
        shards,
        mesh=mesh,
        in_specs=(P("seq", "head"), P("seq", "head"), P("seq", "head"), P("seq", "head")),
        out_specs=(P("seq", "head"), P("seq", "head"), P("seq", "head"), P("seq", "head")),
        check_vma=False,
    )
```

profile of v0, /device:TPU:0, one launch (start us, length us, event | category | flops | bytes accessed | tf_op | source)
XLA Modules:
  0.0 174.3 jit_solution(6285183285674821113)
XLA Ops:
  7.2 0.0 copy-start
  7.2 0.0 copy-start.7
  7.2 0.0 all-gather.5.cloned.1.call-start
  7.2 2.4 %copy.100 = bf16[1024,512]{0,1:T(8,128)(2,1)} copy(bf16[1024,512]{1,0:T(8,128)(2,1)} %param.9) | data formatting | bytes 2097152 | tf_op jit(solution)/shard_map/reshape | solution.py:48
  9.6 0.0 copy-done.7
  9.6 2.4 %fusion.10 = f32[4,128,128]{2,1,0:T(8,128)} fusion(bf16[1024,4,128]{0,2,1:T(8,128)(2,1)} %bitcast.112, bf16[1024,512]{1,0:T(8,128)(2,1)S(1)} %copy-done.7), kind=kOutput, calls=%fused_computation.24 | convolution fusion | flops 134217728 | bytes 2359296 | tf_op jit(solution)/shard_map/thd,the->hde/dot_general | solution.py:50
  12.1 0.0 all-gather.5.cloned.1.call-update
  12.1 0.0 all-gather.7.cloned.1.call-start
  12.2 0.3 iota_compare_fusion
  12.5 0.0 copy-start.10
  12.5 1.0 copy-done.10
  13.5 0.0 copy-done
  13.5 0.0 copy-done.5
  13.5 2.5 %select_convert_fusion.1 = bf16[4,1024,1024]{2,1,0:T(8,128)(2,1)S(1)} fusion(pred[1024,1024]{1,0:T(8,128)(4,1)S(1)} %iota_compare_fusion, bf16[1024,512]{1,0:T(8,128)(2,1)S(1)} %copy-done.5, bf16[1024,512]{1,0:T(8,128)(2,1)S(1)} %copy-done), kind=kOutput, calls=%fused_computation.3 | convolution fusion | flops 1082130432 | bytes 11534336 | tf_op jit(solution)/shard_map/thd,shd->hts/dot_general | solution.py:32
  16.0 0.0 copy-start.1
  16.0 3.2 %copy-done.1 = bf16[4,1024,1024]{2,1,0:T(8,128)(2,1)} copy-done((bf16[4,1024,1024]{2,1,0:T(8,128)(2,1)}, bf16[4,1024,1024]{2,1,0:T(8,128)(2,1)S(1)}, u32[]{:S(2)}) %copy-start.1) | copy-done | bytes 8388632
  19.3 0.0 copy-done.8
  19.3 2.9 %fusion.5 = f32[4,1024,128]{1,2,0:T(8,128)S(1)} fusion(bf16[4,1024,1024]{2,1,0:T(8,128)(2,1)S(1)} %select_convert_fusion.1, bf16[1024,512]{1,0:T(8,128)(2,1)S(1)} %copy-done.8), kind=kOutput, calls=%fused_computation.19 | convolution fusion | flops 1073741824 | bytes 11534336 | tf_op jit(solution)/shard_map/hts,she->the/dot_general | solution.py:57
  22.2 42.3 %all-gather.5.cloned.1.call-done = f32[32,128,128]{2,1,0:T(8,128)} async-done(((f32[4,128,128]{2,1,0:T(8,128)}), f32[32,128,128]{2,1,0:T(8,128)}) %all-gather.5.cloned.1.call-update) | async-done | bytes 2097168 | tf_op jit(solution)/shard_map/all_gather | solution.py:15
  64.4 8.5 %while.30 = (s32[]{:T(128)}, f32[4,128,128]{2,1,0:T(8,128)S(1)}, s32[]{:T(128)}, f32[8,4,128,128]{3,2,1,0:T(8,128)}, s32[]{:T(128)}, /*index=5*/s32[]{:T(128)}) while((s32[]{:T(128)}, f32[4,128,128]{2,1,0:T(8,128)S(1)}, s32[]{:T(128)}, f32[8,4,128,128]{3,2,1,0:T(8,128)}, s32[]{:T(128)}, /*index=5*/s32[]{:T(128)}) %tuple.87), condition=%wide.region_1.2_spmd.clone, body=%wide.region_0.1_spmd.clone.sunk | while | flops 196612 | bytes 786533 | solution.py:24
  64.4 1.0 add_select_fusion.4
  65.5 1.0 add_select_fusion.4
  66.5 1.0 add_select_fusion.4
  67.6 1.0 add_select_fusion.4
  68.7 1.0 add_select_fusion.4
  69.7 1.0 add_select_fusion.4
  70.8 1.0 add_select_fusion.4
  71.9 1.0 add_select_fusion.4
  72.9 1.8 %multiply_reduce_fusion = (f32[1024]{0:T(1024)S(1)}, f32[1024,4,128]{0,2,1:T(8,128)}) fusion(f32[4,128,128]{2,1,0:T(8,128)S(1)} %get-tuple-element.193, f32[4,1024,128]{1,2,0:T(8,128)S(1)} %fusion.5, bf16[1024,512]{1,0:T(8,128)(2,1)S(1)} %copy-done), kind=kOutput, calls=%fused_computation.16 | convolution fusion | flops 135855104 | bytes 5509120 | tf_op jit(solution)/shard_map/thd,hde->the/dot_general | solution.py:58
  74.8 5.6 %psum.14 = f32[1024]{0:T(1024)S(1)} all-reduce(f32[1024]{0:T(1024)S(1)} %get-tuple-element.255), channel_id=1, replica_groups=mesh['seq'=8,'head'=4] {'head'}, use_global_device_ids=true, to_apply=%region_3.4 | all-reduce | flops 1024 | bytes 8192 | tf_op jit(solution)/shard_map/psum | solution.py:63
  80.4 1.9 %copy.38 = f32[1024,512]{1,0:T(8,128)S(1)} copy(f32[1024,512]{0,1:T(8,128)} %bitcast.108) | data formatting | bytes 4194304 | tf_op jit(solution)/shard_map/reshape | solution.py:61
  82.3 1.7 fusion
  84.0 6.6 %psum.15 = f32[1024]{0:T(1024)S(1)} all-reduce(f32[1024]{0:T(1024)S(1)} %fusion), channel_id=1, replica_groups=mesh['seq'=8,'head'=4] {'head'}, use_global_device_ids=true, to_apply=%region_5.6 | all-reduce | flops 1024 | bytes 8192 | tf_op jit(solution)/shard_map/psum | solution.py:66
  90.7 3.0 %fusion.2 = (bf16[1024,512]{1,0:T(8,128)(2,1)}, bf16[1024,512]{1,0:T(8,128)(2,1)}) fusion(bf16[1024,512]{1,0:T(8,128)(2,1)} %param.11, f32[1024,512]{1,0:T(8,128)S(1)} %copy.38, f32[1024]{0:T(1024)S(1)} %broadcast_multiply_fusion, f32[1024]{0:T(1024)S(1)} %add_rsqrt_fusion), kind=kLoop, calls=%fused_computation.9 | loop fusion | flops 3670016 | bytes 5251072 | tf_op jit(solution)/shard_map/convert_element_type | solution.py:71
  93.7 1.5 copy.56
  95.2 0.4 convolution_bitcast_fusion
  95.6 0.8 copy.46
  96.4 0.0 all-gather.7.cloned.1.call-update
  96.5 0.0 copy-start.9
  96.5 4.3 %select_convert_fusion = bf16[4,1024,1024]{2,1,0:T(8,128)(2,1)S(1)} fusion(bf16[1024,4,128]{0,2,1:T(8,128)(2,1)S(1)} %bitcast.105, pred[1024,1024]{1,0:T(8,128)(4,1)} %copy-done.10, bf16[1024,512]{1,0:T(8,128)(2,1)} %param.10), kind=kOutput, calls=%fused_computation.2 | convolution fusion | flops 1082130432 | bytes 11534336 | tf_op jit(solution)/shard_map/thd,shd->hts/dot_general | solution.py:32
  100.8 0.0 copy-done.9
  100.8 2.9 %fusion.32 = f32[4,1024,128]{1,2,0:T(8,128)S(1)} fusion(bf16[4,1024,1024]{2,1,0:T(8,128)(2,1)S(1)} %select_convert_fusion, bf16[1024,4,128]{0,2,1:T(8,128)(2,1)S(1)} %bitcast.113), kind=kOutput, calls=%fused_computation.48 | convolution fusion | flops 1073741824 | bytes 11534336 | tf_op jit(solution)/shard_map/hts,shd->thd/dot_general | solution.py:80
  103.8 0.3 copy-done.2
  104.1 1.4 fusion.4
  105.5 2.3 %copy.51 = bf16[1024,512]{1,0:T(8,128)(2,1)} copy(bf16[1024,512]{0,1:T(8,128)(2,1)} %bitcast.109) | data formatting | bytes 2097152
  107.8 6.0 %fusion.33 = f32[4,128,1024]{2,1,0:T(8,128)} fusion(bf16[1024,4,128]{0,2,1:T(8,128)(2,1)S(1)} %bitcast.107, bf16[4,1024,1024]{2,1,0:T(8,128)(2,1)} %copy-done.1), kind=kOutput, calls=%fused_computation.49 | convolution fusion | flops 1073741824 | bytes 11534336 | tf_op jit(solution)/shard_map/hts,the->she/dot_general | solution.py:88
  113.8 30.0 %all-gather.7.cloned.1.call-done = f32[32,128,128]{2,1,0:T(8,128)} async-done(((f32[4,128,128]{2,1,0:T(8,128)}), f32[32,128,128]{2,1,0:T(8,128)}) %all-gather.7.cloned.1.call-update) | async-done | bytes 2097168 | tf_op jit(solution)/shard_map/all_gather | solution.py:15
  143.7 8.5 %while.31 = (s32[]{:T(128)}, f32[4,128,128]{2,1,0:T(8,128)S(1)}, s32[]{:T(128)}, f32[8,4,128,128]{3,2,1,0:T(8,128)}, s32[]{:T(128)}, /*index=5*/s32[]{:T(128)}, s32[]{:T(128)}, s32[]{:T(128)}) while((s32[]{:T(128)}, f32[4,128,128]{2,1,0:T(8,128)S(1)}, s32[]{:T(128)}, f32[8,4,128,128]{3,2,1,0:T(8,128)}, s32[]{:T(128)}, ...), condition=%wide.region_7.8_spmd.clone, body=%wide.region_6.7_spmd.clone.sunk | while | flops 196616 | bytes 786595 | solution.py:24
  143.7 1.0 add_select_fusion.5
  144.8 1.0 add_select_fusion.5
  145.9 1.0 add_select_fusion.5
  146.9 1.0 add_select_fusion.5
  148.0 1.0 add_select_fusion.5
  149.1 1.0 add_select_fusion.5
  150.1 1.0 add_select_fusion.5
  151.2 1.0 add_select_fusion.5
  152.3 0.0 copy-start.3
  152.3 0.0 copy-start.6
  152.3 3.2 %fusion.7 = f32[4,128,1024]{2,1,0:T(8,128)} fusion(f32[4,128,128]{2,1,0:T(8,128)S(1)} %get-tuple-element.194, bf16[1024,512]{1,0:T(8,128)(2,1)} %param.10), kind=kOutput, calls=%fused_computation.21 | convolution fusion | flops 134283264 | bytes 3407872 | tf_op jit(solution)/shard_map/she,hde->shd/dot_general | solution.py:85
  155.4 0.0 copy-done.6
  155.5 1.5 add_convert_fusion
  156.9 2.4 %copy.53 = bf16[1024,512]{1,0:T(8,128)(2,1)} copy(bf16[1024,512]{0,1:T(8,128)(2,1)} %bitcast.110) | data formatting | bytes 2097152
  159.3 5.8 %fusion.3 = bf16[1024,4,128]{0,2,1:T(8,128)(2,1)} fusion(f32[4,128,1024]{2,1,0:T(8,128)S(1)} %copy-done.4, bf16[4,1024,1024]{2,1,0:T(8,128)(2,1)} %copy-done.2, bf16[1024,512]{1,0:T(8,128)(2,1)S(1)} %copy-done), kind=kOutput, calls=%fused_computation.11 | convolution fusion | flops 1074790400 | bytes 12582912 | tf_op jit(solution)/shard_map/hts,thd->shd/dot_general | solution.py:84
  165.1 2.3 %copy.52 = bf16[1024,512]{1,0:T(8,128)(2,1)} copy(bf16[1024,512]{0,1:T(8,128)(2,1)} %bitcast.111) | data formatting | bytes 2097152
  (10 shorter events, 0.0 us)
Async XLA Ops:
  7.2 6.3 %copy-start = (bf16[1024,512]{1,0:T(8,128)(2,1)S(1)}, bf16[1024,512]{1,0:T(8,128)(2,1)}, u32[]{:S(2)}) copy-start(bf16[1024,512]{1,0:T(8,128)(2,1)} %param.8) | copy-start | bytes 3145732
  7.2 2.5 %copy-start.7 = (bf16[1024,512]{1,0:T(8,128)(2,1)S(1)}, bf16[1024,512]{1,0:T(8,128)(2,1)}, u32[]{:S(2)}) copy-start(bf16[1024,512]{1,0:T(8,128)(2,1)} %param.10) | copy-start | bytes 3145732
  7.2 57.2 %all-gather.5.cloned.1.call-start = ((), (), s32[]{:S(2)}) async-start(), calls=%async_computation | async-start | bytes 2359296 | tf_op jit(solution)/shard_map/all_gather | solution.py:15
  9.6 3.8 %copy-start.5 = (bf16[1024,512]{1,0:T(8,128)(2,1)S(1)}, bf16[1024,512]{1,0:T(8,128)(2,1)}, u32[]{:S(2)}) copy-start(bf16[1024,512]{1,0:T(8,128)(2,1)} %param.9) | copy-start | bytes 3145732
  12.1 131.6 %all-gather.7.cloned.1.call-start = ((), (), s32[]{:S(2)}) async-start(), calls=%async_computation.1 | async-start | bytes 2359296 | tf_op jit(solution)/shard_map/all_gather | solution.py:15
  12.5 1.0 copy-start.10
  13.5 5.8 %copy-start.8 = (bf16[1024,512]{1,0:T(8,128)(2,1)S(1)}, bf16[1024,512]{1,0:T(8,128)(2,1)}, u32[]{:S(2)}) copy-start(bf16[1024,512]{1,0:T(8,128)(2,1)} %param.10) | copy-start | bytes 3145732
  16.0 3.2 %copy-start.1 = (bf16[4,1024,1024]{2,1,0:T(8,128)(2,1)}, bf16[4,1024,1024]{2,1,0:T(8,128)(2,1)S(1)}, u32[]{:S(2)}) copy-start(bf16[4,1024,1024]{2,1,0:T(8,128)(2,1)S(1)} %select_convert_fusion.1) | copy-start | bytes 25165828
  96.5 4.4 %copy-start.9 = (bf16[1024,512]{0,1:T(8,128)(2,1)S(1)}, bf16[1024,512]{0,1:T(8,128)(2,1)}, u32[]{:S(2)}) copy-start(bf16[1024,512]{0,1:T(8,128)(2,1)} %copy.100) | copy-start | bytes 3145732
  100.8 3.2 %copy-start.2 = (bf16[4,1024,1024]{2,1,0:T(8,128)(2,1)}, bf16[4,1024,1024]{2,1,0:T(8,128)(2,1)S(1)}, u32[]{:S(2)}) copy-start(bf16[4,1024,1024]{2,1,0:T(8,128)(2,1)S(1)} %select_convert_fusion) | copy-start | bytes 25165828
  152.3 3.2 %copy-start.3 = (f32[4,128,1024]{2,1,0:T(8,128)S(1)}, f32[4,128,1024]{2,1,0:T(8,128)}, u32[]{:S(2)}) copy-start(f32[4,128,1024]{2,1,0:T(8,128)} %fusion.33) | copy-start | bytes 6291460
  152.3 3.2 %copy-start.6 = (bf16[1024,512]{1,0:T(8,128)(2,1)S(1)}, bf16[1024,512]{1,0:T(8,128)(2,1)}, u32[]{:S(2)}) copy-start(bf16[1024,512]{1,0:T(8,128)(2,1)} %param.9) | copy-start | bytes 3145732
  156.9 2.4 %copy-start.4 = (f32[4,128,1024]{2,1,0:T(8,128)S(1)}, f32[4,128,1024]{2,1,0:T(8,128)}, u32[]{:S(2)}) copy-start(f32[4,128,1024]{2,1,0:T(8,128)} %fusion.7) | copy-start | bytes 6291460
Sparse Core Ops, SparseCore 0:
  12.2 52.1 all-gather.4
  96.6 47.0 all-gather.6
where the time goes:
time: 175 us; the launch traced here: 174 us
  waiting for transfers between devices  72.3 us (41%)
  matrix products  35.2 us (20%)
  other arithmetic  21.7 us (12%)
  local copies, waits for them, and re-layouts  18.2 us (10%)
  between operations  14.2 us (8%)
  blocking collectives  12.2 us (7%)
    all_gather x2, waiting for transfers between devices, entering(): everything = lax.all_gather(shard, axis)  72.2 us
    select_n x16, other arithmetic, step(): return jnp.where(reached, new, before)  16.6 us
    unnamed x25, local copies, waits for them, and re-layouts  11.5 us
    dot_general x2, matrix products, masked_scores(): jnp.einsum('thd,shd->hts', query_side, key_side, preferred_element_type=j...  6.87 us
    psum x1, blocking collectives, shards(): crossed = lax.psum(jnp.sum(grad_float * normed, axis=1), 'head')  6.61 us
    dot_general x1, matrix products, shards(): jnp.einsum('hts,the->she', scores, grad_mixed, preferred_element_type=jnp...  6.02 us
    dot_general x1, matrix products, shards(): jnp.einsum('hts,thd->shd', grad_scores, query_rows, preferred_element_typ...  5.8 us
    psum x1, blocking collectives, shards(): squares = lax.psum(jnp.sum(mixed_rows * mixed_rows, axis=1), 'head')  5.63 us
  transfers between devices with their start and end apart: 2, of which 2 were waited for; matrix products, arithmetic and copies ran while one was open for 13% of the time, Pallas kernels for 0%

commit v1 on v0

v1 whole, which is shorter than its diff:
```python
import functools

import jax
import jax.numpy as jnp
from jax import lax
from jax.experimental import pallas as pl
from jax.experimental.pallas import tpu as pltpu
from jax.sharding import PartitionSpec as P

HEAD_DIM = 128
EPSILON = 1e-06
CHUNK = 256
PAIR = 2 * HEAD_DIM
F32 = jnp.float32
BF16 = jnp.bfloat16


def dot(a, b, ca, cb):
    return lax.dot_general(a, b, (((ca,), (cb,)), ((), ())), preferred_element_type=F32)


def pair_state(left, right):
    full = dot(left, right, 0, 0)
    return jnp.concatenate(
        [full[:HEAD_DIM, :HEAD_DIM], full[HEAD_DIM:, HEAD_DIM:]], axis=0
    )


def store_halves(pairs, own_ref, oth_ref):
    odd = lax.rem(lax.axis_index("seq"), 2) == 1
    own_ref[...] = jnp.where(odd, pairs[1], pairs[0])
    oth_ref[...] = jnp.where(odd, pairs[0], pairs[1])


def merge_halves(own, oth):
    odd = lax.rem(lax.axis_index("seq"), 2) == 1
    return jnp.where(odd, oth, own), jnp.where(odd, own, oth)


def causal(count):
    rows = lax.broadcasted_iota(jnp.int32, (count, count), 0)
    cols = lax.broadcasted_iota(jnp.int32, (count, count), 1)
    return rows >= cols


def call(body, out_shape, args, flops, name, limit=48):
    size = sum(a.size * a.dtype.itemsize for a in args)
    size += sum(a.size * a.dtype.itemsize for a in out_shape)
    return pl.pallas_call(
        body,
        out_shape=out_shape,
        in_specs=[pl.BlockSpec(memory_space=pltpu.VMEM)] * len(args),
        out_specs=[pl.BlockSpec(memory_space=pltpu.VMEM)] * len(out_shape),
        compiler_params=pltpu.CompilerParams(vmem_limit_bytes=limit * 2**20),
        cost_estimate=pl.CostEstimate(flops=flops, bytes_accessed=size, transcendentals=0),
        name=name,
    )(*args)


def chain_scan(own, oth, size, reverse):
    def dev(level, side):
        place = 2 * level + side
        return size - 1 - place if reverse else place

    def permute(value, pairs):
        both = [(dev(*a), dev(*b)) for a, b in pairs]
        return lax.ppermute(value, "seq", both + [(b, a) for a, b in both])

    sides = (0, 1)
    inner = [((level, 0), (level, 1)) for level in range(4)]
    outer = [inner[0], inner[3]]
    straight = [((level, s), (level + 1, s)) for level in (0, 2) for s in sides]
    crossed = [((level, s), (level + 1, 1 - s)) for level in (0, 2) for s in sides]
    middle = [((1, s), (2, s)) for s in sides]
    middle_crossed = [((1, s), (2, 1 - s)) for s in sides]

    place = lax.axis_index("seq")
    if reverse:
        place = size - 1 - place
    level = place // 2

    a1 = permute(own, straight)
    a2 = permute(oth, crossed)
    a3 = permute(oth, inner)
    a4 = permute(own, inner)
    total = own + a3
    window = total + (a1 + a2)
    b1 = permute(window, middle + outer)
    b2 = permute(window, middle_crossed + outer)
    running = jnp.where(level == 2, b1, jnp.zeros_like(b1)) + total
    c1 = permute(running, straight)
    c2 = permute(running, crossed)
    return [a3, a4, b1, b2, c1, c2]


def chain_merge(refs, size, reverse):
    a3, a4, b1, b2, c1, c2 = [r[...] for r in refs]
    place = lax.axis_index("seq")
    if reverse:
        place = size - 1 - place
    level, side = place // 2, lax.rem(place, 2)
    zero = jnp.zeros_like(a3)

    def pick(a, b, c):
        before = jnp.where(lax.rem(level, 2) == 1, c, jnp.where(level == 2, b, zero))
        return before + jnp.where(side == 1, a, zero)

    return merge_halves(pick(a3, b1, c1), pick(a4, b2, c2))


def doubling_scan(own, oth, size, reverse):
    def shift(value, by):
        pairs = [(i, i + by) for i in range(size - by)]
        if reverse:
            pairs = [(b, a) for a, b in pairs]
        return lax.ppermute(value, "seq", pairs)

    odd = lax.rem(lax.axis_index("seq"), 2) == 1
    both = jnp.stack([jnp.where(odd, oth, own), jnp.where(odd, own, oth)])
    by = 1
    while by < size:
        both = both + shift(both, by)
        by *= 2
    both = shift(both, 1)
    return [both[0], both[1]]


def doubling_merge(refs, size, reverse):
    return refs[0][...], refs[1][...]


def state_kernel(k, v, own, oth):
    pairs = [
        pair_state(k[:, p * PAIR : (p + 1) * PAIR], v[:, p * PAIR : (p + 1) * PAIR])
        for p in range(2)
    ]
    store_halves(pairs, own, oth)


def intra_kernel(q, k, v, intra):
    rows = q.shape[0]
    keep = causal(CHUNK)
    for h in range(q.shape[1] // HEAD_DIM):
        cols = slice(h * HEAD_DIM, (h + 1) * HEAD_DIM)
        state = None
        for start in range(0, rows, CHUNK):
            at = slice(start, start + CHUNK)
            qi, ki, vi = q[at, cols], k[at, cols], v[at, cols]
            scores = jnp.where(keep, dot(qi, ki, 1, 1), 0.0).astype(BF16)
            out = dot(scores, vi, 1, 0)
            if state is not None:
                out = out + dot(qi, state.astype(BF16), 1, 0)
            intra[at, cols] = out
            if start + CHUNK < rows:
                new = dot(ki, vi, 0, 0)
                state = new if state is None else state + new


def row_sums(tile):
    return jnp.sum(tile.T, axis=0, keepdims=True)


def mixed_kernel(merge, n_parts, intra, q, g, *refs):
    parts, (mixed, stats, prefix) = refs[:n_parts], refs[n_parts:]
    pairs = merge(parts)
    heads = q.shape[1] // HEAD_DIM
    rounded = [p.astype(BF16) for p in pairs]
    for p in range(2):
        prefix[p * PAIR : (p + 1) * PAIR, :] = rounded[p]
    blocks = q.shape[0] // HEAD_DIM
    for start in range(0, q.shape[0], CHUNK):
        at = slice(start, start + CHUNK)
        square = cross = None
        for h in range(heads):
            cols = slice(h * HEAD_DIM, (h + 1) * HEAD_DIM)
            state = rounded[h // 2][(h % 2) * HEAD_DIM : (h % 2 + 1) * HEAD_DIM]
            m = intra[at, cols] + dot(q[at, cols], state, 1, 0)
            mixed[at, cols] = m
            s, c = m * m, m * g[at, cols].astype(F32)
            square = s if square is None else square + s
            cross = c if cross is None else cross + c
        for j in range(CHUNK // HEAD_DIM):
            part = slice(j * HEAD_DIM, (j + 1) * HEAD_DIM)
            i = start // HEAD_DIM + j
            stats[i : i + 1, :] = row_sums(square[part])
            stats[blocks + i : blocks + i + 1, :] = row_sums(cross[part])


def norm_kernel(width, n_stats, mixed, q, g, *refs):
    stat_refs, (out, gm, own, oth) = refs[:n_stats], refs[n_stats:]
    total = stat_refs[0][...]
    for r in stat_refs[1:]:
        total = total + r[...]
    blocks = q.shape[0] // HEAD_DIM
    inverse = lax.rsqrt(total[:blocks] / width + EPSILON)
    cross_mean = total[blocks:] * inverse / width
    scale = inverse * inverse * cross_mean
    shape = (HEAD_DIM, HEAD_DIM)
    for i in range(blocks):
        at = slice(i * HEAD_DIM, (i + 1) * HEAD_DIM)
        a = jnp.broadcast_to(inverse[i : i + 1], shape).T
        b = jnp.broadcast_to(scale[i : i + 1], shape).T
        for h in range(q.shape[1] // HEAD_DIM):
            cols = slice(h * HEAD_DIM, (h + 1) * HEAD_DIM)
            m = mixed[at, cols]
            out[at, cols] = (m * a).astype(BF16)
            gm[at, cols] = (g[at, cols].astype(F32) * a - m * b).astype(BF16)
    pairs = [
        pair_state(q[:, p * PAIR : (p + 1) * PAIR], gm[:, p * PAIR : (p + 1) * PAIR])
        for p in range(2)
    ]
    store_halves(pairs, own, oth)


def grads_kernel(q, k, v, gm, prefix, gq, gk, gv):
    rows = q.shape[0]
    keep = causal(CHUNK)
    starts = list(range(0, rows, CHUNK))
    for h in range(q.shape[1] // HEAD_DIM):
        cols = slice(h * HEAD_DIM, (h + 1) * HEAD_DIM)
        first = prefix[cols, :]
        sums = None
        states = []
        for start in starts[:-1]:
            at = slice(start, start + CHUNK)
            new = dot(k[at, cols], v[at, cols], 0, 0)
            sums = new if sums is None else sums + new
            states.append(sums.astype(BF16))
        after = None
        for n, start in reversed(list(enumerate(starts))):
            at = slice(start, start + CHUNK)
            qi, ki, vi, gi = q[at, cols], k[at, cols], v[at, cols], gm[at, cols]
            scores = jnp.where(keep, dot(qi, ki, 1, 1), 0.0).astype(BF16)
            grad_scores = jnp.where(keep, dot(gi, vi, 1, 1), 0.0).astype(BF16)
            gq_i = dot(grad_scores, ki, 1, 0) + dot(gi, first, 1, 1)
            if n:
                gq_i = gq_i + dot(gi, states[n - 1], 1, 1)
            gk_i = dot(grad_scores, qi, 0, 0)
            gv_i = dot(scores, gi, 0, 0)
            if after is not None:
                later = after.astype(BF16)
                gk_i = gk_i + dot(vi, later, 1, 1)
                gv_i = gv_i + dot(ki, later, 1, 0)
            gq[at, cols] = gq_i.astype(BF16)
            gk[at, cols] = gk_i
            gv[at, cols] = gv_i
            if n:
                new = dot(qi, gi, 0, 0)
                after = new if after is None else after + new


def last_kernel(merge, n_parts, k, v, gk_part, gv_part, *refs):
    parts, (gk, gv) = refs[:n_parts], refs[n_parts:]
    rounded = [p.astype(BF16) for p in merge(parts)]
    for start in range(0, k.shape[0], CHUNK):
        at = slice(start, start + CHUNK)
        for h in range(k.shape[1] // HEAD_DIM):
            cols = slice(h * HEAD_DIM, (h + 1) * HEAD_DIM)
            state = rounded[h // 2][(h % 2) * HEAD_DIM : (h % 2 + 1) * HEAD_DIM]
            gk[at, cols] = (gk_part[at, cols] + dot(v[at, cols], state, 1, 1)).astype(BF16)
            gv[at, cols] = (gv_part[at, cols] + dot(k[at, cols], state, 1, 0)).astype(BF16)


def all_parts(value, axis, size):
    power = size & (size - 1) == 0
    parts = [value]
    for by in range(1, size):
        pairs = [(i, i ^ by if power else (i + by) % size) for i in range(size)]
        parts.append(lax.ppermute(value, axis, pairs))
    return parts


def shards(sizes, queries, keys, values, grad_out):
    seq, heads = sizes
    rows, cols = queries.shape
    width = cols * heads
    scan, merge = (chain_scan, chain_merge) if seq == 8 else (doubling_scan, doubling_merge)
    half = jax.ShapeDtypeStruct((PAIR, HEAD_DIM), F32)
    wide = jax.ShapeDtypeStruct((rows, cols), F32)
    narrow = jax.ShapeDtypeStruct((rows, cols), BF16)
    stats_shape = jax.ShapeDtypeStruct((2 * rows // HEAD_DIM, HEAD_DIM), F32)
    state_flops = 2 * rows * cols * HEAD_DIM
    chunk_flops = 2 * rows * cols * CHUNK

    own, oth = call(state_kernel, [half, half], [keys, values], state_flops, "local_state")
    parts = scan(own, oth, seq, False)
    (intra,) = call(
        intra_kernel, [wide], [queries, keys, values], 2 * chunk_flops + 2 * state_flops, "intra"
    )
    n = len(parts)
    mixed, stats, prefix = call(
        functools.partial(mixed_kernel, lambda r: merge(r, seq, False), n),
        [wide, stats_shape, jax.ShapeDtypeStruct((cols, HEAD_DIM), BF16)],
        [intra, queries, grad_out, *parts],
        state_flops,
        "mixed",
    )
    stats_parts = all_parts(stats, "head", heads)
    output, grad_mixed, own, oth = call(
        functools.partial(norm_kernel, width, len(stats_parts)),
        [narrow, narrow, half, half],
        [mixed, queries, grad_out, *stats_parts],
        state_flops,
        "norm",
    )
    parts = scan(own, oth, seq, True)
    grad_q, gk_part, gv_part = call(
        grads_kernel,
        [narrow, wide, wide],
        [queries, keys, values, grad_mixed, prefix],
        5 * chunk_flops + 6 * state_flops,
        "grads",
    )
    grad_k, grad_v = call(
        functools.partial(last_kernel, lambda r: merge(r, seq, True), n),
        [narrow, narrow],
        [keys, values, gk_part, gv_part, *parts],
        2 * state_flops,
        "last",
    )
    return output, grad_q, grad_k, grad_v


def solution(mesh):
    sizes = (mesh.shape["seq"], mesh.shape["head"])
    spec = P("seq", "head")
    return jax.shard_map(
        functools.partial(shards, sizes),
        mesh=mesh,
        in_specs=(spec,) * 4,
        out_specs=(spec,) * 4,
        check_vma=False,
    )
```

time: 175 us -> 76.2 us (0.44)
  waiting for transfers between devices: 72.3 us -> 22.1 us
  matrix products: 35.2 us -> 0 us
  starting transfers between devices: 0.08 us -> 21.1 us
  Pallas kernels: 0 us -> 18.5 us
  other arithmetic: 21.7 us -> 4.18 us
  between operations: 14.2 us -> 0.73 us
  blocking collectives: 12.2 us -> 0 us
  local copies, waits for them, and re-layouts: 18.2 us -> 9.14 us
    all_gather x2 -> x0, waiting for transfers between devices: 72.2 us -> none  [entering(): everything = lax.all_gather(shard, axis)]
    dot_general x12 -> x0, matrix products: 35.2 us -> none  [the longest x2 6.87 us: masked_scores(): jnp.einsum('thd,shd->hts', query_side, key_side, preferred_element_type=j...]
    ppermute x0 -> x19, waiting for transfers between devices: none -> 22.1 us  [the longest x16 20.3 us: permute(): return lax.ppermute(value, 'seq', both + [(b, a) for a, b in both])]
    ppermute x0 -> x19, starting transfers between devices: none -> 21.1 us  [the longest x16 19.2 us: permute(): return lax.ppermute(value, 'seq', both + [(b, a) for a, b in both])]
    pallas_call x0 -> x6, Pallas kernels: none -> 18.5 us  [call(): pl.pallas_call(body, out_shape=out_shape, in_specs=[pl.BlockSpec(memory_s...]
    select_n x16 -> x0, other arithmetic: 16.6 us -> none  [step(): return jnp.where(reached, new, before)]
    psum x2 -> x0, blocking collectives: 12.2 us -> none  [the longest x1 6.61 us: shards(): crossed = lax.psum(jnp.sum(grad_float * normed, axis=1), 'head')]
    reshape x3 -> x0, local copies, waits for them, and re-layouts: 5.81 us -> none  [the longest x1 2.4 us: shards(): key_rows = keys.reshape(shaped)]
  transfers between devices with their start and end apart: 2 -> 19, of which waited for: 2 -> 11; matrix products, arithmetic and copies ran while one was open for 13% -> 2% of each run, Pallas kernels for 0% -> 13%
where the time goes in v1:
time: 76.2 us; the launch traced here: 75.8 us
  waiting for transfers between devices  22.1 us (29%)
  starting transfers between devices  21.1 us (28%)
  Pallas kernels  18.5 us (24%)
  local copies, waits for them, and re-layouts  9.14 us (12%)
  other arithmetic  4.18 us (5%)
    ppermute x16, waiting for transfers between devices, permute(): return lax.ppermute(value, 'seq', both + [(b, a) for a, b in both])  20.3 us
    ppermute x16, starting transfers between devices, permute(): return lax.ppermute(value, 'seq', both + [(b, a) for a, b in both])  19.2 us
    pallas_call x6, Pallas kernels, call(): pl.pallas_call(body, out_shape=out_shape, in_specs=[pl.BlockSpec(memory_s...  18.5 us
    unnamed x24, local copies, waits for them, and re-layouts  9.14 us
    add x2, other arithmetic, chain_scan(): window = total + (a1 + a2)  2.34 us
    ppermute x3, starting transfers between devices, all_parts(): parts.append(lax.ppermute(value, axis, pairs))  1.86 us
    add x2, other arithmetic, chain_scan(): running = jnp.where(level == 2, b1, jnp.zeros_like(b1)) + total  1.84 us
    ppermute x3, waiting for transfers between devices, all_parts(): parts.append(lax.ppermute(value, axis, pairs))  1.82 us
  transfers between devices with their start and end apart: 19, of which 11 were waited for; matrix products, arithmetic and copies ran while one was open for 2% of the time, Pallas kernels for 13%

profile of v1, /device:TPU:0, one launch (start us, length us, event | category | flops | bytes accessed | tf_op | source)
XLA Modules:
  0.0 75.8 jit_solution(5722376243468796576)
XLA Ops:
  0.6 0.0 copy-start
  0.6 1.2 %copy-done = bf16[1024,512]{1,0:T(8,128)(2,1)S(1)} copy-done((bf16[1024,512]{1,0:T(8,128)(2,1)S(1)}, bf16[1024,512]{1,0:T(8,128)(2,1)}, u32[]{:S(2)}) %copy-start) | copy-done | bytes 1048600
  1.9 1.2 %copy-done.2 = bf16[1024,512]{1,0:T(8,128)(2,1)S(1)} copy-done((bf16[1024,512]{1,0:T(8,128)(2,1)S(1)}, bf16[1024,512]{1,0:T(8,128)(2,1)}, u32[]{:S(2)}) %copy-start.2) | copy-done | bytes 1048600
  3.1 1.1 %local_state.1 = (f32[256,128]{1,0:T(8,128)}, f32[256,128]{1,0:T(8,128)S(1)}) custom-call(bf16[1024,512]{1,0:T(8,128)(2,1)S(1)} %copy-done, bf16[1024,512]{1,0:T(8,128)(2,1)S(1)} %copy-done.2), custom_call_target="tpu_custom_call" | custom-call | flops 134217728 | bytes 2359296 | tf_op jit(solution)/shard_map/local_state/pallas_call | solution.py:49
  4.2 4.0 %collective-permute-start.3 = (f32[256,128]{1,0:T(8,128)S(1)}, f32[256,128]{1,0:T(8,128)S(1)}, u32[]{:S(2)}, u32[]{:S(2)}) collective-permute-start(f32[256,128]{1,0:T(8,128)S(1)} %get-tuple-element.18), channel_id=1, source_target_pairs={{0,12},{4,8},{16,28},{20,24},{12,0},{8,4},{28,16},{24,20},{1,13},{... | collective-permute-start | bytes 393224 | tf_op jit(solution)/shard_map/ppermute | solution.py:67
  8.2 0.5 collective-permute-start
  8.7 0.0 collective-permute-start.2
  8.7 3.3 %collective-permute-done.3 = f32[256,128]{1,0:T(8,128)S(1)} collective-permute-done((f32[256,128]{1,0:T(8,128)S(1)}, f32[256,128]{1,0:T(8,128)S(1)}, u32[]{:S(2)}, u32[]{:S(2)}) %collective-permute-start.3) | collective-permute-done | bytes 131104 | tf_op jit(solution)/shard_map/ppermute | solution.py:67
  12.1 2.4 %collective-permute-done.refs_0_ = f32[256,128]{1,0:T(8,128)S(1)} collective-permute-done((f32[256,128]{1,0:T(8,128)S(1)}, f32[256,128]{1,0:T(8,128)S(1)}, u32[]{:S(2)}, u32[]{:S(2)}) %collective-permute-start) | collective-permute-done | bytes 131104 | tf_op jit(solution)/shard_map/ppermute | solution.py:67
  14.5 0.2 collective-permute-done.2
  14.7 1.6 %add_add_fusion.1 = (f32[256,128]{1,0:T(8,128)}, f32[256,128]{1,0:T(8,128)}) fusion(f32[256,128]{1,0:T(8,128)S(1)} %collective-permute-done.2, f32[256,128]{1,0:T(8,128)S(1)} %collective-permute-done.3, f32[256,128]{1,0:T(8,128)} %get-tuple-element.19, f32[256,128]{1,0:T(8,128)S(1)} %collective-permute-done.refs_0_), kind=kLoop, calls=%fused_computation.3 | loop fusion | flops 98304 | bytes 786432 | tf_op jit(solution)/shard_map/add | solution.py:87
  16.3 1.5 %collective-permute-start.4 = (f32[256,128]{1,0:T(8,128)}, f32[256,128]{1,0:T(8,128)S(1)}, u32[]{:S(2)}, u32[]{:S(2)}) collective-permute-start(f32[256,128]{1,0:T(8,128)} %get-tuple-element.34), channel_id=1, source_target_pairs={{8,16},{12,20},{0,4},{24,28},{16,8},{20,12},{4,0},{28,24},{9,17},{... | collective-permute-start | bytes 393224 | tf_op jit(solution)/shard_map/ppermute | solution.py:67
  17.8 0.6 collective-permute-start.1
  18.3 1.5 %collective-permute-start.5 = (f32[256,128]{1,0:T(8,128)}, f32[256,128]{1,0:T(8,128)S(1)}, u32[]{:S(2)}, u32[]{:S(2)}) collective-permute-start(f32[256,128]{1,0:T(8,128)} %get-tuple-element.34), channel_id=1, source_target_pairs={{8,20},{12,16},{0,4},{24,28},{20,8},{16,12},{4,0},{28,24},{9,21},{... | collective-permute-start | bytes 393224 | tf_op jit(solution)/shard_map/ppermute | solution.py:67
  19.8 3.1 %collective-permute-done.4.refs_2_ = f32[256,128]{1,0:T(8,128)S(1)} collective-permute-done((f32[256,128]{1,0:T(8,128)}, f32[256,128]{1,0:T(8,128)S(1)}, u32[]{:S(2)}, u32[]{:S(2)}) %collective-permute-start.4) | collective-permute-done | bytes 131104 | tf_op jit(solution)/shard_map/ppermute | solution.py:67
  22.9 0.9 %select_add_fusion.1 = f32[256,128]{1,0:T(8,128)S(1)} fusion(f32[256,128]{1,0:T(8,128)} %get-tuple-element.35, f32[256,128]{1,0:T(8,128)S(1)} %collective-permute-done.4.refs_2_, pred[]{:T(512)S(6)} %eq.6), kind=kLoop, calls=%fused_computation.2 | loop fusion | flops 65536 | bytes 393217 | tf_op jit(solution)/shard_map/add | solution.py:90
  23.8 0.0 copy-start.6
  23.8 1.7 %collective-permute-start.7 = (f32[256,128]{1,0:T(8,128)S(1)}, f32[256,128]{1,0:T(8,128)S(1)}, u32[]{:S(2)}, u32[]{:S(2)}) collective-permute-start(f32[256,128]{1,0:T(8,128)S(1)} %select_add_fusion.1), channel_id=1, source_target_pairs={{0,12},{4,8},{16,28},{20,24},{12,0},{8,4},{28,16},{24,20},{1,13},{... | collective-permute-start | bytes 393224 | tf_op jit(solution)/shard_map/ppermute | solution.py:67
  25.5 1.3 %collective-permute-start.6 = (f32[256,128]{1,0:T(8,128)S(1)}, f32[256,128]{1,0:T(8,128)S(1)}, u32[]{:S(2)}, u32[]{:S(2)}) collective-permute-start(f32[256,128]{1,0:T(8,128)S(1)} %select_add_fusion.1), channel_id=1, source_target_pairs={{0,8},{4,12},{16,24},{20,28},{8,0},{12,4},{24,16},{28,20},{1,9},{5... | collective-permute-start | bytes 393224 | tf_op jit(solution)/shard_map/ppermute | solution.py:67
  26.8 0.0 copy-done.1
  26.8 0.0 copy-done.3
  26.8 0.0 copy-done.4
  26.8 1.9 %intra.1 = f32[1024,512]{1,0:T(8,128)S(1)} custom-call(bf16[1024,512]{1,0:T(8,128)(2,1)S(1)} %copy-done.4, bf16[1024,512]{1,0:T(8,128)(2,1)S(1)} %copy-done.1, bf16[1024,512]{1,0:T(8,128)(2,1)S(1)} %copy-done.3), custom_call_target="tpu_custom_call" | custom-call | flops 805306368 | bytes 5242880 | tf_op jit(solution)/shard_map/intra/pallas_call | solution.py:49
  28.7 0.0 copy-start.5
  28.7 1.3 %copy-done.5 = f32[1024,512]{1,0:T(8,128)} copy-done((f32[1024,512]{1,0:T(8,128)}, f32[1024,512]{1,0:T(8,128)S(1)}, u32[]{:S(2)}) %copy-start.5) | copy-done | bytes 2097176
  30.1 0.0 collective-permute-done.1.refs_1_
  30.1 0.1 collective-permute-done.5.refs_3_
  30.2 0.0 collective-permute-done.7.refs_5_
  30.2 1.1 %collective-permute-done.6.refs_4_ = f32[256,128]{1,0:T(8,128)S(1)} collective-permute-done((f32[256,128]{1,0:T(8,128)S(1)}, f32[256,128]{1,0:T(8,128)S(1)}, u32[]{:S(2)}, u32[]{:S(2)}) %collective-permute-start.6) | collective-permute-done | bytes 131104 | tf_op jit(solution)/shard_map/ppermute | solution.py:67
  31.3 0.0 copy-done.6
  31.3 2.3 %mixed.1 = (f32[1024,512]{1,0:T(8,128)S(1)}, f32[16,128]{1,0:T(8,128)S(1)}, bf16[512,128]{1,0:T(8,128)(2,1)S(1)}) custom-call(f32[1024,512]{1,0:T(8,128)} %copy-done.5, bf16[1024,512]{1,0:T(8,128)(2,1)S(1)} %copy-done.4, bf16[1024,512]{1,0:T(8,128)(2,1)S(1)} %copy-done.6, f32[256,128]{1,0:T(8,128)S(1)} %collective-permute-done.refs_0_, ...), custom_call_target="tpu_custom_call" | custom-call | flops 134217728 | bytes 7217152 | tf_op jit(solution)/shard_map/mixed/pallas_call | solution.py:49
  33.6 0.0 copy-start.10
  33.7 0.6 copy-done.10
  34.3 0.0 collective-permute-start.10
  34.3 1.6 %collective-permute-start.9 = (f32[16,128]{1,0:T(8,128)S(1)}, f32[16,128]{1,0:T(8,128)S(1)}, u32[]{:S(2)}, u32[]{:S(2)}) collective-permute-start(f32[16,128]{1,0:T(8,128)S(1)} %get-tuple-element.21.refs_0_), channel_id=1, source_target_pairs={{0,2},{1,3},{2,0},{3,1},{4,6},{5,7},{6,4},{7,5},{8,10},{9,11},{10,... | collective-permute-start | bytes 24584 | tf_op jit(solution)/shard_map/ppermute | solution.py:269
  35.9 0.3 collective-permute-start.8
  36.2 1.2 %collective-permute-done.10.refs_3_ = f32[16,128]{1,0:T(8,128)S(1)} collective-permute-done((f32[16,128]{1,0:T(8,128)S(1)}, f32[16,128]{1,0:T(8,128)S(1)}, u32[]{:S(2)}, u32[]{:S(2)}) %collective-permute-start.10) | collective-permute-done | bytes 8224 | tf_op jit(solution)/shard_map/ppermute | solution.py:269
  37.4 0.6 collective-permute-done.9.refs_2_
  38.0 0.0 collective-permute-done.8.refs_1_
  38.0 1.8 %norm.1 = (bf16[1024,512]{1,0:T(8,128)(2,1)}, bf16[1024,512]{1,0:T(8,128)(2,1)S(1)}, f32[256,128]{1,0:T(8,128)S(1)}, f32[256,128]{1,0:T(8,128)S(1)}) custom-call(f32[1024,512]{1,0:T(8,128)S(1)} %get-tuple-element.20.mixed, bf16[1024,512]{1,0:T(8,128)(2,1)S(1)} %copy-done.4, bf16[1024,512]{1,0:T(8,128)(2,1)S(1)} %copy-done.6, ...), custom_call_target="tpu_custom_call" | custom-call | flops 134217728 | bytes 6586368 | tf_op jit(solution)/shard_map/norm/pallas_call | solution.py:49
  39.8 1.0 %copy-done.8 = bf16[1024,512]{1,0:T(8,128)(2,1)} copy-done((bf16[1024,512]{1,0:T(8,128)(2,1)}, bf16[1024,512]{1,0:T(8,128)(2,1)S(1)}, u32[]{:S(2)}) %copy-start.8) | copy-done | bytes 1048600
  40.8 1.4 %collective-permute-start.14 = (f32[256,128]{1,0:T(8,128)S(1)}, f32[256,128]{1,0:T(8,128)S(1)}, u32[]{:S(2)}, u32[]{:S(2)}) collective-permute-start(f32[256,128]{1,0:T(8,128)S(1)} %get-tuple-element.28), channel_id=1, source_target_pairs={{28,16},{24,20},{12,0},{8,4},{16,28},{20,24},{0,12},{4,8},{29,17},... | collective-permute-start | bytes 393224 | tf_op jit(solution)/shard_map/ppermute | solution.py:67
  42.2 1.7 %collective-permute-start.11 = (f32[256,128]{1,0:T(8,128)S(1)}, f32[256,128]{1,0:T(8,128)S(1)}, u32[]{:S(2)}, u32[]{:S(2)}) collective-permute-start(f32[256,128]{1,0:T(8,128)S(1)} %get-tuple-element.28), channel_id=1, source_target_pairs={{28,24},{20,16},{12,8},{4,0},{24,28},{16,20},{8,12},{0,4},{29,25},... | collective-permute-start | bytes 393224 | tf_op jit(solution)/shard_map/ppermute | solution.py:67
  43.9 0.3 collective-permute-start.13
  44.3 3.8 %collective-permute-done.14 = f32[256,128]{1,0:T(8,128)S(1)} collective-permute-done((f32[256,128]{1,0:T(8,128)S(1)}, f32[256,128]{1,0:T(8,128)S(1)}, u32[]{:S(2)}, u32[]{:S(2)}) %collective-permute-start.14) | collective-permute-done | bytes 131104 | tf_op jit(solution)/shard_map/ppermute | solution.py:67
  48.0 2.3 %collective-permute-done.11.refs_0_ = f32[256,128]{1,0:T(8,128)S(1)} collective-permute-done((f32[256,128]{1,0:T(8,128)S(1)}, f32[256,128]{1,0:T(8,128)S(1)}, u32[]{:S(2)}, u32[]{:S(2)}) %collective-permute-start.11) | collective-permute-done | bytes 131104 | tf_op jit(solution)/shard_map/ppermute | solution.py:67
  50.3 0.0 collective-permute-done.13
  50.3 0.7 add_add_fusion
  51.1 0.6 collective-permute-start.15
  51.7 1.4 %collective-permute-start.12 = (f32[256,128]{1,0:T(8,128)S(1)}, f32[256,128]{1,0:T(8,128)S(1)}, u32[]{:S(2)}, u32[]{:S(2)}) collective-permute-start(f32[256,128]{1,0:T(8,128)S(1)} %get-tuple-element.29), channel_id=1, source_target_pairs={{28,24},{20,16},{12,8},{4,0},{24,28},{16,20},{8,12},{0,4},{29,25},... | collective-permute-start | bytes 393224 | tf_op jit(solution)/shard_map/ppermute | solution.py:67
  53.1 0.6 collective-permute-start.16
  53.7 3.9 %collective-permute-done.15.refs_2_ = f32[256,128]{1,0:T(8,128)S(1)} collective-permute-done((f32[256,128]{1,0:T(8,128)}, f32[256,128]{1,0:T(8,128)S(1)}, u32[]{:S(2)}, u32[]{:S(2)}) %collective-permute-start.15) | collective-permute-done | bytes 131104 | tf_op jit(solution)/shard_map/ppermute | solution.py:67
  57.6 0.9 %select_add_fusion = f32[256,128]{1,0:T(8,128)S(1)} fusion(f32[256,128]{1,0:T(8,128)} %get-tuple-element.33, f32[256,128]{1,0:T(8,128)S(1)} %collective-permute-done.15.refs_2_, pred[]{:T(512)S(6)} %eq.7), kind=kLoop, calls=%fused_computation | loop fusion | flops 65536 | bytes 393217 | tf_op jit(solution)/shard_map/add | solution.py:90
  58.5 0.9 %collective-permute-start.18 = (f32[256,128]{1,0:T(8,128)S(1)}, f32[256,128]{1,0:T(8,128)S(1)}, u32[]{:S(2)}, u32[]{:S(2)}) collective-permute-start(f32[256,128]{1,0:T(8,128)S(1)} %select_add_fusion), channel_id=1, source_target_pairs={{28,16},{24,20},{12,0},{8,4},{16,28},{20,24},{0,12},{4,8},{29,17},... | collective-permute-start | bytes 393224 | tf_op jit(solution)/shard_map/ppermute | solution.py:67
  59.5 1.2 %collective-permute-start.17 = (f32[256,128]{1,0:T(8,128)S(1)}, f32[256,128]{1,0:T(8,128)S(1)}, u32[]{:S(2)}, u32[]{:S(2)}) collective-permute-start(f32[256,128]{1,0:T(8,128)S(1)} %select_add_fusion), channel_id=1, source_target_pairs={{28,20},{24,16},{12,4},{8,0},{20,28},{16,24},{4,12},{0,8},{29,21},... | collective-permute-start | bytes 393224 | tf_op jit(solution)/shard_map/ppermute | solution.py:67
  60.7 1.2 %copy-done.9 = bf16[1024,512]{1,0:T(8,128)(2,1)S(1)} copy-done((bf16[1024,512]{1,0:T(8,128)(2,1)S(1)}, bf16[1024,512]{1,0:T(8,128)(2,1)}, u32[]{:S(2)}) %copy-start.9) | copy-done | bytes 1048600
  61.9 0.9 %copy-done.11 = bf16[512,128]{1,0:T(8,128)(2,1)S(1)} copy-done((bf16[512,128]{1,0:T(8,128)(2,1)S(1)}, bf16[512,128]{1,0:T(8,128)(2,1)}, u32[]{:S(2)}) %copy-start.11) | copy-done | bytes 131096
  62.8 7.7 %grads.1 = (bf16[1024,512]{1,0:T(8,128)(2,1)}, f32[1024,512]{1,0:T(8,128)}, f32[1024,512]{1,0:T(8,128)}) custom-call(bf16[1024,512]{1,0:T(8,128)(2,1)S(1)} %copy-done.4, bf16[1024,512]{1,0:T(8,128)(2,1)S(1)} %copy-done.1, bf16[1024,512]{1,0:T(8,128)(2,1)S(1)} %copy-done.3, bf16[1024,512]{1,0:T(8,128)(2,1)S(1)} %copy-done.9, bf16[512,128]{1,0:T(8,128)(2,1)S(1)} %copy-done.11), custom_call_target="tpu_custom_call" | custom-call | flops 2147483648 | bytes 9568256 | tf_op jit(solution)/shard_map/grads/pallas_call | solution.py:49
  70.5 0.0 collective-permute-done.12.refs_1_
  70.5 0.0 collective-permute-done.16.refs_3_
  70.5 0.0 collective-permute-done.18.refs_5_
  70.5 0.0 collective-permute-done.17.refs_4_
  70.5 1.6 %copy-done.7 = f32[1024,512]{1,0:T(8,128)S(1)} copy-done((f32[1024,512]{1,0:T(8,128)S(1)}, f32[1024,512]{1,0:T(8,128)}, u32[]{:S(2)}) %copy-start.7) | copy-done | bytes 2097176
  72.1 3.7 %last.1 = (bf16[1024,512]{1,0:T(8,128)(2,1)}, bf16[1024,512]{1,0:T(8,128)(2,1)}) custom-call(bf16[1024,512]{1,0:T(8,128)(2,1)S(1)} %copy-done.1, bf16[1024,512]{1,0:T(8,128)(2,1)S(1)} %copy-done.3, f32[1024,512]{1,0:T(8,128)S(1)} %copy-done.7, f32[1024,512]{1,0:T(8,128)} %get-tuple-element.27.gv_part, f32[256,128]{1,0:T(8,128)S(1)} %collective-permute-done.11.refs_0_, ...), custom_call_target="tpu_custom_call" | custom-call | flops 268435456 | bytes 9175040 | tf_op jit(solution)/shard_map/last/pallas_call | solution.py:49
  (8 shorter events, 0.0 us)
Async XLA Ops:
  0.6 1.2 %copy-start = (bf16[1024,512]{1,0:T(8,128)(2,1)S(1)}, bf16[1024,512]{1,0:T(8,128)(2,1)}, u32[]{:S(2)}) copy-start(bf16[1024,512]{1,0:T(8,128)(2,1)} %k.7) | copy-start | bytes 3145732
  1.9 1.2 %copy-start.2 = (bf16[1024,512]{1,0:T(8,128)(2,1)S(1)}, bf16[1024,512]{1,0:T(8,128)(2,1)}, u32[]{:S(2)}) copy-start(bf16[1024,512]{1,0:T(8,128)(2,1)} %v.7) | copy-start | bytes 3145732
  3.1 23.7 %copy-start.1 = (bf16[1024,512]{1,0:T(8,128)(2,1)S(1)}, bf16[1024,512]{1,0:T(8,128)(2,1)}, u32[]{:S(2)}) copy-start(bf16[1024,512]{1,0:T(8,128)(2,1)} %k.7) | copy-start | bytes 3145732
  3.1 23.7 %copy-start.3 = (bf16[1024,512]{1,0:T(8,128)(2,1)S(1)}, bf16[1024,512]{1,0:T(8,128)(2,1)}, u32[]{:S(2)}) copy-start(bf16[1024,512]{1,0:T(8,128)(2,1)} %v.7) | copy-start | bytes 3145732
  3.1 23.7 %copy-start.4 = (bf16[1024,512]{1,0:T(8,128)(2,1)S(1)}, bf16[1024,512]{1,0:T(8,128)(2,1)}, u32[]{:S(2)}) copy-start(bf16[1024,512]{1,0:T(8,128)(2,1)} %q.7) | copy-start | bytes 3145732
  4.2 7.9 %collective-permute-start.3 = (f32[256,128]{1,0:T(8,128)S(1)}, f32[256,128]{1,0:T(8,128)S(1)}, u32[]{:S(2)}, u32[]{:S(2)}) collective-permute-start(f32[256,128]{1,0:T(8,128)S(1)} %get-tuple-element.18), channel_id=1, source_target_pairs={{0,12},{4,8},{16,28},{20,24},{12,0},{8,4},{28,16},{24,20},{1,13},{... | collective-permute-start | bytes 393224 | tf_op jit(solution)/shard_map/ppermute | solution.py:67
  8.2 6.3 %collective-permute-start = (f32[256,128]{1,0:T(8,128)S(1)}, f32[256,128]{1,0:T(8,128)S(1)}, u32[]{:S(2)}, u32[]{:S(2)}) collective-permute-start(f32[256,128]{1,0:T(8,128)S(1)} %get-tuple-element.18), channel_id=1, source_target_pairs={{0,4},{8,12},{16,20},{24,28},{4,0},{12,8},{20,16},{28,24},{1,5},{9... | collective-permute-start | bytes 393224 | tf_op jit(solution)/shard_map/ppermute | solution.py:67
  8.7 5.9 %collective-permute-start.2 = (f32[256,128]{1,0:T(8,128)}, f32[256,128]{1,0:T(8,128)S(1)}, u32[]{:S(2)}, u32[]{:S(2)}) collective-permute-start(f32[256,128]{1,0:T(8,128)} %get-tuple-element.19), channel_id=1, source_target_pairs={{0,8},{4,12},{16,24},{20,28},{8,0},{12,4},{24,16},{28,20},{1,9},{5... | collective-permute-start | bytes 393224 | tf_op jit(solution)/shard_map/ppermute | solution.py:67
  16.3 6.6 %collective-permute-start.4 = (f32[256,128]{1,0:T(8,128)}, f32[256,128]{1,0:T(8,128)S(1)}, u32[]{:S(2)}, u32[]{:S(2)}) collective-permute-start(f32[256,128]{1,0:T(8,128)} %get-tuple-element.34), channel_id=1, source_target_pairs={{8,16},{12,20},{0,4},{24,28},{16,8},{20,12},{4,0},{28,24},{9,17},{... | collective-permute-start | bytes 393224 | tf_op jit(solution)/shard_map/ppermute | solution.py:67
  17.8 12.3 %collective-permute-start.1 = (f32[256,128]{1,0:T(8,128)}, f32[256,128]{1,0:T(8,128)S(1)}, u32[]{:S(2)}, u32[]{:S(2)}) collective-permute-start(f32[256,128]{1,0:T(8,128)} %get-tuple-element.19), channel_id=1, source_target_pairs={{0,4},{8,12},{16,20},{24,28},{4,0},{12,8},{20,16},{28,24},{1,5},{9... | collective-permute-start | bytes 393224 | tf_op jit(solution)/shard_map/ppermute | solution.py:67
  18.3 11.9 %collective-permute-start.5 = (f32[256,128]{1,0:T(8,128)}, f32[256,128]{1,0:T(8,128)S(1)}, u32[]{:S(2)}, u32[]{:S(2)}) collective-permute-start(f32[256,128]{1,0:T(8,128)} %get-tuple-element.34), channel_id=1, source_target_pairs={{8,20},{12,16},{0,4},{24,28},{20,8},{16,12},{4,0},{28,24},{9,21},{... | collective-permute-start | bytes 393224 | tf_op jit(solution)/shard_map/ppermute | solution.py:67
  23.8 7.5 %copy-start.6 = (bf16[1024,512]{1,0:T(8,128)(2,1)S(1)}, bf16[1024,512]{1,0:T(8,128)(2,1)}, u32[]{:S(2)}) copy-start(bf16[1024,512]{1,0:T(8,128)(2,1)} %g.3) | copy-start | bytes 3145732
  23.8 6.4 %collective-permute-start.7 = (f32[256,128]{1,0:T(8,128)S(1)}, f32[256,128]{1,0:T(8,128)S(1)}, u32[]{:S(2)}, u32[]{:S(2)}) collective-permute-start(f32[256,128]{1,0:T(8,128)S(1)} %select_add_fusion.1), channel_id=1, source_target_pairs={{0,12},{4,8},{16,28},{20,24},{12,0},{8,4},{28,16},{24,20},{1,13},{... | collective-permute-start | bytes 393224 | tf_op jit(solution)/shard_map/ppermute | solution.py:67
  25.5 5.8 %collective-permute-start.6 = (f32[256,128]{1,0:T(8,128)S(1)}, f32[256,128]{1,0:T(8,128)S(1)}, u32[]{:S(2)}, u32[]{:S(2)}) collective-permute-start(f32[256,128]{1,0:T(8,128)S(1)} %select_add_fusion.1), channel_id=1, source_target_pairs={{0,8},{4,12},{16,24},{20,28},{8,0},{12,4},{24,16},{28,20},{1,9},{5... | collective-permute-start | bytes 393224 | tf_op jit(solution)/shard_map/ppermute | solution.py:67
  28.7 1.4 %copy-start.5 = (f32[1024,512]{1,0:T(8,128)}, f32[1024,512]{1,0:T(8,128)S(1)}, u32[]{:S(2)}) copy-start(f32[1024,512]{1,0:T(8,128)S(1)} %intra.1) | copy-start | bytes 6291460
  33.6 0.7 copy-start.10
  34.3 3.1 %collective-permute-start.10 = (f32[16,128]{1,0:T(8,128)S(1)}, f32[16,128]{1,0:T(8,128)S(1)}, u32[]{:S(2)}, u32[]{:S(2)}) collective-permute-start(f32[16,128]{1,0:T(8,128)S(1)} %get-tuple-element.21.refs_0_), channel_id=1, source_target_pairs={{0,3},{1,2},{2,1},{3,0},{4,7},{5,6},{6,5},{7,4},{8,11},{9,10},{10,... | collective-permute-start | bytes 24584 | tf_op jit(solution)/shard_map/ppermute | solution.py:269
  34.3 3.7 %collective-permute-start.9 = (f32[16,128]{1,0:T(8,128)S(1)}, f32[16,128]{1,0:T(8,128)S(1)}, u32[]{:S(2)}, u32[]{:S(2)}) collective-permute-start(f32[16,128]{1,0:T(8,128)S(1)} %get-tuple-element.21.refs_0_), channel_id=1, source_target_pairs={{0,2},{1,3},{2,0},{3,1},{4,6},{5,7},{6,4},{7,5},{8,10},{9,11},{10,... | collective-permute-start | bytes 24584 | tf_op jit(solution)/shard_map/ppermute | solution.py:269
  35.9 2.1 %collective-permute-start.8 = (f32[16,128]{1,0:T(8,128)S(1)}, f32[16,128]{1,0:T(8,128)S(1)}, u32[]{:S(2)}, u32[]{:S(2)}) collective-permute-start(f32[16,128]{1,0:T(8,128)S(1)} %get-tuple-element.21.refs_0_), channel_id=1, source_target_pairs={{0,1},{1,0},{2,3},{3,2},{4,5},{5,4},{6,7},{7,6},{8,9},{9,8},{10,11... | collective-permute-start | bytes 24584 | tf_op jit(solution)/shard_map/ppermute | solution.py:269
  39.8 1.0 %copy-start.8 = (bf16[1024,512]{1,0:T(8,128)(2,1)}, bf16[1024,512]{1,0:T(8,128)(2,1)S(1)}, u32[]{:S(2)}) copy-start(bf16[1024,512]{1,0:T(8,128)(2,1)S(1)} %get-tuple-element.23.gm) | copy-start | bytes 3145732
  40.8 7.2 %collective-permute-start.14 = (f32[256,128]{1,0:T(8,128)S(1)}, f32[256,128]{1,0:T(8,128)S(1)}, u32[]{:S(2)}, u32[]{:S(2)}) collective-permute-start(f32[256,128]{1,0:T(8,128)S(1)} %get-tuple-element.28), channel_id=1, source_target_pairs={{28,16},{24,20},{12,0},{8,4},{16,28},{20,24},{0,12},{4,8},{29,17},... | collective-permute-start | bytes 393224 | tf_op jit(solution)/shard_map/ppermute | solution.py:67
  42.2 8.2 %collective-permute-start.11 = (f32[256,128]{1,0:T(8,128)S(1)}, f32[256,128]{1,0:T(8,128)S(1)}, u32[]{:S(2)}, u32[]{:S(2)}) collective-permute-start(f32[256,128]{1,0:T(8,128)S(1)} %get-tuple-element.28), channel_id=1, source_target_pairs={{28,24},{20,16},{12,8},{4,0},{24,28},{16,20},{8,12},{0,4},{29,25},... | collective-permute-start | bytes 393224 | tf_op jit(solution)/shard_map/ppermute | solution.py:67
  43.9 6.4 %collective-permute-start.13 = (f32[256,128]{1,0:T(8,128)S(1)}, f32[256,128]{1,0:T(8,128)S(1)}, u32[]{:S(2)}, u32[]{:S(2)}) collective-permute-start(f32[256,128]{1,0:T(8,128)S(1)} %get-tuple-element.29), channel_id=1, source_target_pairs={{28,20},{24,16},{12,4},{8,0},{20,28},{16,24},{4,12},{0,8},{29,21},... | collective-permute-start | bytes 393224 | tf_op jit(solution)/shard_map/ppermute | solution.py:67
  51.1 6.6 %collective-permute-start.15 = (f32[256,128]{1,0:T(8,128)}, f32[256,128]{1,0:T(8,128)S(1)}, u32[]{:S(2)}, u32[]{:S(2)}) collective-permute-start(f32[256,128]{1,0:T(8,128)} %get-tuple-element.32), channel_id=1, source_target_pairs={{20,12},{16,8},{28,24},{4,0},{12,20},{8,16},{24,28},{0,4},{21,13},... | collective-permute-start | bytes 393224 | tf_op jit(solution)/shard_map/ppermute | solution.py:67
  51.7 18.8 %collective-permute-start.12 = (f32[256,128]{1,0:T(8,128)S(1)}, f32[256,128]{1,0:T(8,128)S(1)}, u32[]{:S(2)}, u32[]{:S(2)}) collective-permute-start(f32[256,128]{1,0:T(8,128)S(1)} %get-tuple-element.29), channel_id=1, source_target_pairs={{28,24},{20,16},{12,8},{4,0},{24,28},{16,20},{8,12},{0,4},{29,25},... | collective-permute-start | bytes 393224 | tf_op jit(solution)/shard_map/ppermute | solution.py:67
  53.1 17.4 %collective-permute-start.16 = (f32[256,128]{1,0:T(8,128)}, f32[256,128]{1,0:T(8,128)S(1)}, u32[]{:S(2)}, u32[]{:S(2)}) collective-permute-start(f32[256,128]{1,0:T(8,128)} %get-tuple-element.32), channel_id=1, source_target_pairs={{20,8},{16,12},{28,24},{4,0},{8,20},{12,16},{24,28},{0,4},{21,9},{... | collective-permute-start | bytes 393224 | tf_op jit(solution)/shard_map/ppermute | solution.py:67
  58.5 11.9 %collective-permute-start.18 = (f32[256,128]{1,0:T(8,128)S(1)}, f32[256,128]{1,0:T(8,128)S(1)}, u32[]{:S(2)}, u32[]{:S(2)}) collective-permute-start(f32[256,128]{1,0:T(8,128)S(1)} %select_add_fusion), channel_id=1, source_target_pairs={{28,16},{24,20},{12,0},{8,4},{16,28},{20,24},{0,12},{4,8},{29,17},... | collective-permute-start | bytes 393224 | tf_op jit(solution)/shard_map/ppermute | solution.py:67
  59.5 11.0 %collective-permute-start.17 = (f32[256,128]{1,0:T(8,128)S(1)}, f32[256,128]{1,0:T(8,128)S(1)}, u32[]{:S(2)}, u32[]{:S(2)}) collective-permute-start(f32[256,128]{1,0:T(8,128)S(1)} %select_add_fusion), channel_id=1, source_target_pairs={{28,20},{24,16},{12,4},{8,0},{20,28},{16,24},{4,12},{0,8},{29,21},... | collective-permute-start | bytes 393224 | tf_op jit(solution)/shard_map/ppermute | solution.py:67
  60.7 1.2 %copy-start.9 = (bf16[1024,512]{1,0:T(8,128)(2,1)S(1)}, bf16[1024,512]{1,0:T(8,128)(2,1)}, u32[]{:S(2)}) copy-start(bf16[1024,512]{1,0:T(8,128)(2,1)} %copy-done.8) | copy-start | bytes 3145732
  61.9 0.9 %copy-start.11 = (bf16[512,128]{1,0:T(8,128)(2,1)S(1)}, bf16[512,128]{1,0:T(8,128)(2,1)}, u32[]{:S(2)}) copy-start(bf16[512,128]{1,0:T(8,128)(2,1)} %copy-done.10) | copy-start | bytes 393220
  70.5 1.6 %copy-start.7 = (f32[1024,512]{1,0:T(8,128)S(1)}, f32[1024,512]{1,0:T(8,128)}, u32[]{:S(2)}) copy-start(f32[1024,512]{1,0:T(8,128)} %get-tuple-element.26.gk_part) | copy-start | bytes 6291460

commit v2 on v1

v2 whole, which is shorter than its diff:
```python
import functools

import jax
import jax.numpy as jnp
from jax import lax
from jax.experimental import pallas as pl
from jax.experimental.pallas import tpu as pltpu
from jax.sharding import PartitionSpec as P

HEAD_DIM = 128
EPSILON = 1e-06
CHUNK = 256
PAIR = 2 * HEAD_DIM
F32 = jnp.float32
BF16 = jnp.bfloat16


def dot(a, b, ca, cb):
    return lax.dot_general(a, b, (((ca,), (cb,)), ((), ())), preferred_element_type=F32)


def causal(count):
    rows = lax.broadcasted_iota(jnp.int32, (count, count), 0)
    cols = lax.broadcasted_iota(jnp.int32, (count, count), 1)
    return rows >= cols


def call(body, out_shape, args, flops, name, spaces=None, outs=None, scratch=(), limit=20):
    size = sum(a.size * a.dtype.itemsize for a in args)
    size += sum(a.size * a.dtype.itemsize for a in out_shape)
    spaces, outs = spaces or {}, outs or {}
    kernel = pl.pallas_call(
        body,
        out_shape=out_shape,
        in_specs=[
            pl.BlockSpec(memory_space=spaces.get(i, pltpu.VMEM)) for i in range(len(args))
        ],
        out_specs=[
            pl.BlockSpec(memory_space=outs.get(i, pltpu.VMEM)) for i in range(len(out_shape))
        ],
        scratch_shapes=list(scratch),
        compiler_params=pltpu.CompilerParams(vmem_limit_bytes=limit * 2**20),
        cost_estimate=pl.CostEstimate(flops=flops, bytes_accessed=size, transcendentals=0),
        name=name,
    )
    return list(kernel(*args))


def exchange(value, size, by):
    return lax.ppermute(value, "seq", [(i, i ^ by) for i in range(size)])


def sum_kernel(*refs):
    parts, out = refs[:4], refs[-1]
    out[...] = (parts[0][...] + parts[1][...]) + (parts[2][...] + parts[3][...])


def quad_scan(state, size, between):
    near = [exchange(state, size, by) for by in (3, 2, 1)]
    done = between(None)
    (total,) = call(
        sum_kernel,
        [jax.ShapeDtypeStruct(state.shape, F32)],
        [state, *near, *done[:1]],
        0,
        "quad_sum",
        spaces={4: pl.ANY},
    )
    far = exchange(total, size, 4)
    done = done + between(total)
    return near + [far], done


def quad_merge(refs, size, reverse):
    place = lax.axis_index("seq")
    if reverse:
        place = size - 1 - place
    inner = lax.rem(place, 4)
    zero = jnp.zeros(refs[0].shape, F32)
    total = jnp.where(place >= 4, refs[3][...], zero)
    for ref, by in zip(refs, (3, 2, 1)):
        total = total + jnp.where((inner ^ by) < inner, ref[...], zero)
    return total.astype(BF16)


def doubling_scan(state, size, reverse):
    def shift(value, by):
        pairs = [(i, i + by) for i in range(size - by)]
        if reverse:
            pairs = [(b, a) for a, b in pairs]
        return lax.ppermute(value, "seq", pairs)

    by = 1
    while by < size:
        state = state + shift(state, by)
        by *= 2
    return [shift(state, 1)]


def scan(state, size, reverse, between):
    if size == 8:
        return quad_scan(state, size, between)
    done = between(None)
    return doubling_scan(state, size, reverse), done + between(done[0])


def merge(refs, size, reverse):
    if size == 8:
        return quad_merge(refs, size, reverse)
    return refs[0][...].astype(BF16)


def state_kernel(k_hbm, v_hbm, state, k, v, sems):
    rows = k.shape[0]
    starts = range(0, rows, CHUNK)
    copies = []
    for n, start in enumerate(starts):
        at = slice(start, start + CHUNK)
        for j, (src, dst) in enumerate(((k_hbm, k), (v_hbm, v))):
            copies.append(pltpu.make_async_copy(src.at[at], dst.at[at], sems.at[j, n]))
            copies[-1].start()
    pairs = k.shape[1] // PAIR
    sums = [None] * pairs
    for n, start in enumerate(starts):
        at = slice(start, start + CHUNK)
        copies[2 * n].wait()
        copies[2 * n + 1].wait()
        for p in range(pairs):
            cols = slice(p * PAIR, (p + 1) * PAIR)
            new = dot(k[at, cols], v[at, cols], 0, 0)
            sums[p] = new if sums[p] is None else sums[p] + new
    for p in range(pairs):
        store_pair(state, p, sums[p])


def store_pair(state, p, full):
    state[p * PAIR : p * PAIR + HEAD_DIM, :] = full[:HEAD_DIM, :HEAD_DIM]
    state[p * PAIR + HEAD_DIM : (p + 1) * PAIR, :] = full[HEAD_DIM:, HEAD_DIM:]


def intra_kernel(q, k, v, intra):
    rows = q.shape[0]
    keep = causal(CHUNK)
    for h in range(q.shape[1] // HEAD_DIM):
        cols = slice(h * HEAD_DIM, (h + 1) * HEAD_DIM)
        state = None
        for start in range(0, rows, CHUNK):
            at = slice(start, start + CHUNK)
            qi, ki, vi = q[at, cols], k[at, cols], v[at, cols]
            scores = jnp.where(keep, dot(qi, ki, 1, 1), 0.0).astype(BF16)
            out = dot(scores, vi, 1, 0)
            if state is not None:
                out = out + dot(qi, state.astype(BF16), 1, 0)
            intra[at, cols] = out
            if start + CHUNK < rows:
                new = dot(ki, vi, 0, 0)
                state = new if state is None else state + new


def row_sums(tile):
    return jnp.sum(tile.T, axis=0, keepdims=True)


def mixed_kernel(merge, n_parts, intra, q, g, *refs):
    parts, (mixed, stats, prefix) = refs[:n_parts], refs[n_parts:]
    prefix[...] = merge(parts)
    heads = q.shape[1] // HEAD_DIM
    blocks = q.shape[0] // HEAD_DIM
    for start in range(0, q.shape[0], CHUNK):
        at = slice(start, start + CHUNK)
        square = cross = None
        for h in range(heads):
            cols = slice(h * HEAD_DIM, (h + 1) * HEAD_DIM)
            m = intra[at, cols] + dot(q[at, cols], prefix[cols, :], 1, 0)
            mixed[at, cols] = m
            s, c = m * m, m * g[at, cols].astype(F32)
            square = s if square is None else square + s
            cross = c if cross is None else cross + c
        for j in range(CHUNK // HEAD_DIM):
            part = slice(j * HEAD_DIM, (j + 1) * HEAD_DIM)
            i = start // HEAD_DIM + j
            stats[i : i + 1, :] = row_sums(square[part])
            stats[blocks + i : blocks + i + 1, :] = row_sums(cross[part])


def norm_kernel(width, n_stats, mixed, q, g, *refs):
    stat_refs, (gm, state, inverse_out) = refs[:n_stats], refs[n_stats:]
    total = stat_refs[0][...]
    for r in stat_refs[1:]:
        total = total + r[...]
    blocks = q.shape[0] // HEAD_DIM
    inverse = lax.rsqrt(total[:blocks] / width + EPSILON)
    inverse_out[...] = inverse
    cross_mean = total[blocks:] * inverse / width
    scale = inverse * inverse * cross_mean
    shape = (HEAD_DIM, HEAD_DIM)
    for i in range(blocks):
        at = slice(i * HEAD_DIM, (i + 1) * HEAD_DIM)
        a = jnp.broadcast_to(inverse[i : i + 1], shape).T
        b = jnp.broadcast_to(scale[i : i + 1], shape).T
        for h in range(q.shape[1] // HEAD_DIM):
            cols = slice(h * HEAD_DIM, (h + 1) * HEAD_DIM)
            m = mixed[at, cols]
            gm[at, cols] = (g[at, cols].astype(F32) * a - m * b).astype(BF16)
    for p in range(q.shape[1] // PAIR):
        cols = slice(p * PAIR, (p + 1) * PAIR)
        store_pair(state, p, dot(q[:, cols], gm[:, cols], 0, 0))


def head_grads(heads, q, k, v, gm, prefix, gq, gk, gv):
    rows = q.shape[0]
    keep = causal(CHUNK)
    starts = list(range(0, rows, CHUNK))
    for j, h in enumerate(heads):
        cols = slice(h * HEAD_DIM, (h + 1) * HEAD_DIM)
        part = slice(j * HEAD_DIM, (j + 1) * HEAD_DIM)
        sums = prefix[cols, :].astype(F32)
        states = [prefix[cols, :]]
        for start in starts[:-1]:
            at = slice(start, start + CHUNK)
            sums = sums + dot(k[at, cols], v[at, cols], 0, 0)
            states.append(sums.astype(BF16))
        after = None
        for n, start in reversed(list(enumerate(starts))):
            at = slice(start, start + CHUNK)
            qi, ki, vi, gi = q[at, cols], k[at, cols], v[at, cols], gm[at, cols]
            scores = jnp.where(keep, dot(qi, ki, 1, 1), 0.0).astype(BF16)
            grad_scores = jnp.where(keep, dot(gi, vi, 1, 1), 0.0).astype(BF16)
            gq_i = dot(grad_scores, ki, 1, 0) + dot(gi, states[n], 1, 1)
            gk_i = dot(grad_scores, qi, 0, 0)
            gv_i = dot(scores, gi, 0, 0)
            if after is not None:
                later = after.astype(BF16)
                gk_i = gk_i + dot(vi, later, 1, 1)
                gv_i = gv_i + dot(ki, later, 1, 0)
            gq[at, part] = gq_i.astype(BF16)
            gk[at, part] = gk_i
            gv[at, part] = gv_i
            if n:
                new = dot(qi, gi, 0, 0)
                after = new if after is None else after + new


def first_grads_kernel(heads, q, k, v, gm, prefix, mixed, inverse, gq, gk, gv, out):
    head_grads(heads, q, k, v, gm, prefix, gq, gk, gv)
    shape = (HEAD_DIM, HEAD_DIM)
    for i in range(q.shape[0] // HEAD_DIM):
        at = slice(i * HEAD_DIM, (i + 1) * HEAD_DIM)
        a = jnp.broadcast_to(inverse[i : i + 1, :], shape).T
        for h in range(q.shape[1] // HEAD_DIM):
            cols = slice(h * HEAD_DIM, (h + 1) * HEAD_DIM)
            out[at, cols] = (mixed[at, cols] * a).astype(BF16)


def second_grads_kernel(heads, q, k, v, gm, prefix, gq_first, token, gq, gk, gv):
    head_grads(heads, q, k, v, gm, prefix, gq.at[:, heads[0] * HEAD_DIM :], gk, gv)
    gq[:, : heads[0] * HEAD_DIM] = gq_first[...]


def last_kernel(merge, n_parts, k, v, gk0, gv0, gk1, gv1, *refs):
    parts, (gk_hbm, gv_hbm, gk, gv, sems) = refs[:n_parts], refs[n_parts:]
    suffix = merge(parts)
    heads = k.shape[1] // HEAD_DIM
    copies = []
    for n, start in enumerate(range(0, k.shape[0], CHUNK)):
        at = slice(start, start + CHUNK)
        for h in range(heads):
            cols = slice(h * HEAD_DIM, (h + 1) * HEAD_DIM)
            state = suffix[cols]
            first = h < heads // 2
            part = cols if first else slice(cols.start - gk0.shape[1], cols.stop - gk0.shape[1])
            gk_part, gv_part = (gk0, gv0) if first else (gk1, gv1)
            gk[at, cols] = (gk_part[at, part] + dot(v[at, cols], state, 1, 1)).astype(BF16)
            gv[at, cols] = (gv_part[at, part] + dot(k[at, cols], state, 1, 0)).astype(BF16)
        for j, (src, dst) in enumerate(((gk, gk_hbm), (gv, gv_hbm))):
            copies.append(pltpu.make_async_copy(src.at[at], dst.at[at], sems.at[j, n]))
            copies[-1].start()
    for copy in copies:
        copy.wait()


def all_parts(value, axis, size):
    power = size & (size - 1) == 0
    parts = [value]
    for by in reversed(range(1, size)):
        pairs = [(i, i ^ by if power else (i + by) % size) for i in range(size)]
        parts.append(lax.ppermute(value, axis, pairs))
    return parts


def shards(sizes, queries, keys, values, grad_out):
    seq, head_size = sizes
    rows, cols = queries.shape
    heads = list(range(cols // HEAD_DIM))
    halves = heads[: len(heads) // 2], heads[len(heads) // 2 :]
    chunks = rows // CHUNK
    width = cols * head_size
    state_shape = jax.ShapeDtypeStruct((cols, HEAD_DIM), F32)
    wide = jax.ShapeDtypeStruct((rows, cols), F32)
    narrow = jax.ShapeDtypeStruct((rows, cols), BF16)
    half_wide = jax.ShapeDtypeStruct((rows, cols // 2), F32)
    half_narrow = jax.ShapeDtypeStruct((rows, cols // 2), BF16)
    stats_shape = jax.ShapeDtypeStruct((2 * rows // HEAD_DIM, HEAD_DIM), F32)
    inverse_shape = jax.ShapeDtypeStruct((rows // HEAD_DIM, HEAD_DIM), F32)
    state_flops = 2 * rows * cols * HEAD_DIM
    chunk_flops = 2 * rows * cols * CHUNK
    slots = [pltpu.VMEM((rows, cols), BF16)] * 2 + [pltpu.SemaphoreType.DMA((2, chunks))]

    (state,) = call(
        state_kernel,
        [state_shape],
        [keys, values],
        state_flops,
        "local_state",
        spaces={0: pl.ANY, 1: pl.ANY},
        scratch=slots,
        limit=60,
    )

    def forward(token):
        if token is not None:
            return []
        return call(
            intra_kernel,
            [wide],
            [queries, keys, values],
            2 * chunk_flops + 2 * state_flops,
            "intra",
        )

    parts, (intra,) = scan(state, seq, False, forward)
    n = len(parts)
    mixed, stats, prefix = call(
        functools.partial(mixed_kernel, lambda r: merge(r, seq, False), n),
        [wide, stats_shape, jax.ShapeDtypeStruct((cols, HEAD_DIM), BF16)],
        [intra, queries, grad_out, *parts],
        state_flops,
        "mixed",
    )
    stats_parts = all_parts(stats, "head", head_size)
    grad_mixed, state, inverse = call(
        functools.partial(norm_kernel, width, len(stats_parts)),
        [narrow, state_shape, inverse_shape],
        [mixed, queries, grad_out, *stats_parts],
        state_flops,
        "norm",
    )
    grads_args = [queries, keys, values, grad_mixed, prefix]
    grads_flops = (5 * chunk_flops + 6 * state_flops) // 2
    first = []

    def backward(token):
        if token is None:
            first.extend(
                call(
                    functools.partial(first_grads_kernel, halves[0]),
                    [half_narrow, half_wide, half_wide, narrow],
                    grads_args + [mixed, inverse],
                    grads_flops,
                    "first_grads",
                )
            )
            return first[1:3] + first[3:]
        return call(
            functools.partial(second_grads_kernel, halves[1]),
            [narrow, half_wide, half_wide],
            grads_args + [first[0], token],
            grads_flops,
            "second_grads",
            spaces={6: pl.ANY},
        )

    parts, (gk0, gv0, output, grad_q, gk1, gv1) = scan(state, seq, True, backward)
    grad_k, grad_v = call(
        functools.partial(last_kernel, lambda r: merge(r, seq, True), n),
        [narrow, narrow],
        [keys, values, gk0, gv0, gk1, gv1, *parts],
        2 * state_flops,
        "last",
        outs={0: pl.ANY, 1: pl.ANY},
        scratch=slots,
    )
    return output, grad_q, grad_k, grad_v


def solution(mesh):
    sizes = (mesh.shape["seq"], mesh.shape["head"])
    spec = P("seq", "head")
    return jax.shard_map(
        functools.partial(shards, sizes),
        mesh=mesh,
        in_specs=(spec,) * 4,
        out_specs=(spec,) * 4,
        check_vma=False,
    )
```

time: 76.2 us -> 72.2 us (0.948)
  waiting for transfers between devices: 22.1 us -> 39 us
  local copies, waits for them, and re-layouts: 9.14 us -> 1.25 us
  starting transfers between devices: 21.1 us -> 15.1 us
  other arithmetic: 4.18 us -> 0 us
  Pallas kernels: 18.5 us -> 16 us
    ppermute x16 -> x8, waiting for transfers between devices: 20.3 us -> 36.9 us  [exchange(): return lax.ppermute(value, 'seq', [(i, i ^ by) for i in range(size)])]
    unnamed x24 -> x12, local copies, waits for them, and re-layouts: 9.14 us -> 1.25 us
    ppermute x16 -> x8, starting transfers between devices: 19.2 us -> 13.2 us  [exchange(): return lax.ppermute(value, 'seq', [(i, i ^ by) for i in range(size)])]
    add x4 -> x0, other arithmetic: 4.18 us -> none  [the longest x2 2.34 us: chain_scan(): window = total + (a1 + a2)]
    pallas_call x6 -> x9, Pallas kernels: 18.5 us -> 16 us  [call(): return list(kernel(*args))]
  transfers between devices with their start and end apart: 19 -> 11, of which waited for: 11 -> 8; matrix products, arithmetic and copies ran while one was open for 2% -> 0% of each run, Pallas kernels for 13% -> 13%
where the time goes in v2:
time: 72.2 us; the launch traced here: 72 us
  waiting for transfers between devices  39 us (54%)
  Pallas kernels  16 us (22%)
  starting transfers between devices  15.1 us (21%)
  local copies, waits for them, and re-layouts  1.25 us (2%)
    ppermute x8, waiting for transfers between devices, exchange(): return lax.ppermute(value, 'seq', [(i, i ^ by) for i in range(size)])  36.9 us
    pallas_call x9, Pallas kernels, call(): return list(kernel(*args))  16 us
    ppermute x8, starting transfers between devices, exchange(): return lax.ppermute(value, 'seq', [(i, i ^ by) for i in range(size)])  13.2 us
    ppermute x3, waiting for transfers between devices, all_parts(): parts.append(lax.ppermute(value, axis, pairs))  2.06 us
    ppermute x3, starting transfers between devices, all_parts(): parts.append(lax.ppermute(value, axis, pairs))  1.93 us
  transfers between devices with their start and end apart: 11, of which 8 were waited for; matrix products, arithmetic and copies ran while one was open for 0% of the time, Pallas kernels for 13%

profile of v2, /device:TPU:0, one launch (start us, length us, event | category | flops | bytes accessed | tf_op | source)
XLA Modules:
  0.0 72.0 jit_solution(6304685095159399857)
XLA Ops:
  0.6 0.0 copy-start.1
  0.6 0.0 copy-start
  0.7 2.8 %local_state.1.refs_0_ = f32[512,128]{1,0:T(8,128)} custom-call(bf16[1024,512]{1,0:T(8,128)(2,1)} %k.7, bf16[1024,512]{1,0:T(8,128)(2,1)} %v.7), custom_call_target="tpu_custom_call" | custom-call | flops 134217728 | bytes 2359296 | tf_op jit(solution)/shard_map/local_state/pallas_call | solution.py:46
  3.4 4.0 %collective-permute-start = (f32[512,128]{1,0:T(8,128)}, f32[512,128]{1,0:T(8,128)S(1)}, u32[]{:S(2)}, u32[]{:S(2)}) collective-permute-start(f32[512,128]{1,0:T(8,128)} %local_state.1.refs_0_), channel_id=1, source_target_pairs={{0,12},{4,8},{8,4},{12,0},{16,28},{20,24},{24,20},{28,16},{1,13},{... | collective-permute-start | bytes 786440 | tf_op jit(solution)/shard_map/ppermute | solution.py:50
  7.4 0.4 collective-permute-start.1
  7.9 0.2 collective-permute-start.2
  8.1 0.0 copy-done.1
  8.1 0.0 copy-done
  8.1 0.0 copy-start.2
  8.1 1.2 %copy-done.2 = bf16[1024,512]{1,0:T(8,128)(2,1)S(1)} copy-done((bf16[1024,512]{1,0:T(8,128)(2,1)S(1)}, bf16[1024,512]{1,0:T(8,128)(2,1)}, u32[]{:S(2)}) %copy-start.2) | copy-done | bytes 1048600
  9.3 0.0 copy-start.5
  9.3 1.9 %intra.1.refs_4_ = f32[1024,512]{1,0:T(8,128)S(1)} custom-call(bf16[1024,512]{1,0:T(8,128)(2,1)S(1)} %copy-done, bf16[1024,512]{1,0:T(8,128)(2,1)S(1)} %copy-done.1, bf16[1024,512]{1,0:T(8,128)(2,1)S(1)} %copy-done.2), custom_call_target="tpu_custom_call" | custom-call | flops 805306368 | bytes 5242880 | tf_op jit(solution)/shard_map/intra/pallas_call | solution.py:46
  11.2 0.0 copy-start.4
  11.2 3.6 %collective-permute-done.refs_1_.refs_0_ = f32[512,128]{1,0:T(8,128)S(1)} collective-permute-done((f32[512,128]{1,0:T(8,128)}, f32[512,128]{1,0:T(8,128)S(1)}, u32[]{:S(2)}, u32[]{:S(2)}) %collective-permute-start) | collective-permute-done | bytes 262176 | tf_op jit(solution)/shard_map/ppermute | solution.py:50
  14.8 5.0 %collective-permute-done.1.refs_2_.refs_1_ = f32[512,128]{1,0:T(8,128)S(1)} collective-permute-done((f32[512,128]{1,0:T(8,128)}, f32[512,128]{1,0:T(8,128)S(1)}, u32[]{:S(2)}, u32[]{:S(2)}) %collective-permute-start.1) | collective-permute-done | bytes 262176 | tf_op jit(solution)/shard_map/ppermute | solution.py:50
  19.8 0.0 collective-permute-done.2.refs_3_.refs_2_
  19.8 0.0 copy-done.5
  19.8 0.1 quad_sum.2
  19.9 2.7 %collective-permute-start.3 = (f32[512,128]{1,0:T(8,128)S(1)}, f32[512,128]{1,0:T(8,128)S(1)}, u32[]{:S(2)}, u32[]{:S(2)}) collective-permute-start(f32[512,128]{1,0:T(8,128)S(1)} %quad_sum.2), channel_id=1, source_target_pairs={{0,16},{4,20},{8,24},{12,28},{16,0},{20,4},{24,8},{28,12},{1,17},{... | collective-permute-start | bytes 786440 | tf_op jit(solution)/shard_map/ppermute | solution.py:50
  22.5 12.0 %collective-permute-done.3.refs_3_ = f32[512,128]{1,0:T(8,128)S(1)} collective-permute-done((f32[512,128]{1,0:T(8,128)S(1)}, f32[512,128]{1,0:T(8,128)S(1)}, u32[]{:S(2)}, u32[]{:S(2)}) %collective-permute-start.3) | collective-permute-done | bytes 262176 | tf_op jit(solution)/shard_map/ppermute | solution.py:50
  34.5 0.0 copy-done.4
  34.5 0.8 %mixed.1 = (f32[1024,512]{1,0:T(8,128)S(1)}, f32[16,128]{1,0:T(8,128)S(1)}, bf16[512,128]{1,0:T(8,128)(2,1)S(1)}) custom-call(f32[1024,512]{1,0:T(8,128)S(1)} %intra.1.refs_4_, bf16[1024,512]{1,0:T(8,128)(2,1)S(1)} %copy-done, bf16[1024,512]{1,0:T(8,128)(2,1)S(1)} %copy-done.4, f32[512,128]{1,0:T(8,128)S(1)} %collective-permute-done.refs_1_.refs_0_, ...), custom_call_target="tpu_custom_call" | custom-call | flops 134217728 | bytes 7479296 | tf_op jit(solution)/shard_map/mixed/pallas_call | solution.py:46
  35.4 0.3 collective-permute-start.4
  35.7 1.4 %collective-permute-start.5 = (f32[16,128]{1,0:T(8,128)S(1)}, f32[16,128]{1,0:T(8,128)S(1)}, u32[]{:S(2)}, u32[]{:S(2)}) collective-permute-start(f32[16,128]{1,0:T(8,128)S(1)} %get-tuple-element.20.refs_0_), channel_id=1, source_target_pairs={{0,2},{1,3},{2,0},{3,1},{4,6},{5,7},{6,4},{7,5},{8,10},{9,11},{10,... | collective-permute-start | bytes 24584 | tf_op jit(solution)/shard_map/ppermute | solution.py:287
  37.1 0.2 collective-permute-start.6
  37.3 1.2 %collective-permute-done.4.refs_1_ = f32[16,128]{1,0:T(8,128)S(1)} collective-permute-done((f32[16,128]{1,0:T(8,128)S(1)}, f32[16,128]{1,0:T(8,128)S(1)}, u32[]{:S(2)}, u32[]{:S(2)}) %collective-permute-start.4) | collective-permute-done | bytes 8224 | tf_op jit(solution)/shard_map/ppermute | solution.py:287
  38.5 0.8 %collective-permute-done.5.refs_2_ = f32[16,128]{1,0:T(8,128)S(1)} collective-permute-done((f32[16,128]{1,0:T(8,128)S(1)}, f32[16,128]{1,0:T(8,128)S(1)}, u32[]{:S(2)}, u32[]{:S(2)}) %collective-permute-start.5) | collective-permute-done | bytes 8224 | tf_op jit(solution)/shard_map/ppermute | solution.py:287
  39.3 0.0 collective-permute-done.6.refs_3_
  39.3 0.0 copy-start.3
  39.3 1.0 %norm.1 = (bf16[1024,512]{1,0:T(8,128)(2,1)S(1)}, f32[512,128]{1,0:T(8,128)S(1)}, f32[8,128]{1,0:T(8,128)S(1)}) custom-call(f32[1024,512]{1,0:T(8,128)S(1)} %get-tuple-element.19.mixed, bf16[1024,512]{1,0:T(8,128)(2,1)S(1)} %copy-done, bf16[1024,512]{1,0:T(8,128)(2,1)S(1)} %copy-done.4, f32[16,128]{1,0:T(8,128)S(1)} %get-tuple-element.20.refs_0_, ...), custom_call_target="tpu_custom_call" | custom-call | flops 134217728 | bytes 5541888 | tf_op jit(solution)/shard_map/norm/pallas_call | solution.py:46
  40.4 2.6 %collective-permute-start.7 = (f32[512,128]{1,0:T(8,128)S(1)}, f32[512,128]{1,0:T(8,128)S(1)}, u32[]{:S(2)}, u32[]{:S(2)}) collective-permute-start(f32[512,128]{1,0:T(8,128)S(1)} %get-tuple-element.26.refs_0_), channel_id=1, source_target_pairs={{0,12},{4,8},{8,4},{12,0},{16,28},{20,24},{24,20},{28,16},{1,13},{... | collective-permute-start | bytes 786440 | tf_op jit(solution)/shard_map/ppermute | solution.py:50
  42.9 0.5 collective-permute-start.8
  43.5 0.5 collective-permute-start.9
  43.9 0.0 copy-done.3
  43.9 3.9 %first_grads.1 = (bf16[1024,256]{1,0:T(8,128)(2,1)S(1)}, f32[1024,256]{1,0:T(8,128)S(1)}, f32[1024,256]{1,0:T(8,128)S(1)}, bf16[1024,512]{1,0:T(8,128)(2,1)}) custom-call(bf16[1024,512]{1,0:T(8,128)(2,1)S(1)} %copy-done, bf16[1024,512]{1,0:T(8,128)(2,1)S(1)} %copy-done.1, bf16[1024,512]{1,0:T(8,128)(2,1)S(1)} %copy-done.3, ...), custom_call_target="tpu_custom_call" | custom-call | flops 1073741824 | bytes 10096640 | tf_op jit(solution)/shard_map/first_grads/pallas_call | solution.py:46
  47.8 2.7 %collective-permute-done.7.refs_1_.refs_0_ = f32[512,128]{1,0:T(8,128)S(1)} collective-permute-done((f32[512,128]{1,0:T(8,128)S(1)}, f32[512,128]{1,0:T(8,128)S(1)}, u32[]{:S(2)}, u32[]{:S(2)}) %collective-permute-start.7) | collective-permute-done | bytes 262176 | tf_op jit(solution)/shard_map/ppermute | solution.py:50
  50.5 5.0 %collective-permute-done.8.refs_2_.refs_1_ = f32[512,128]{1,0:T(8,128)S(1)} collective-permute-done((f32[512,128]{1,0:T(8,128)S(1)}, f32[512,128]{1,0:T(8,128)S(1)}, u32[]{:S(2)}, u32[]{:S(2)}) %collective-permute-start.8) | collective-permute-done | bytes 262176 | tf_op jit(solution)/shard_map/ppermute | solution.py:50
  55.5 0.0 collective-permute-done.9.refs_3_.refs_2_
  55.5 0.1 quad_sum.3.token
  55.5 2.3 %collective-permute-start.10 = (f32[512,128]{1,0:T(8,128)S(1)}, f32[512,128]{1,0:T(8,128)S(1)}, u32[]{:S(2)}, u32[]{:S(2)}) collective-permute-start(f32[512,128]{1,0:T(8,128)S(1)} %quad_sum.3.token), channel_id=1, source_target_pairs={{0,16},{4,20},{8,24},{12,28},{16,0},{20,4},{24,8},{28,12},{1,17},{... | collective-permute-start | bytes 786440 | tf_op jit(solution)/shard_map/ppermute | solution.py:50
  57.9 3.8 %second_grads.1 = (bf16[1024,512]{1,0:T(8,128)(2,1)}, f32[1024,256]{1,0:T(8,128)S(1)}, f32[1024,256]{1,0:T(8,128)S(1)}) custom-call(bf16[1024,512]{1,0:T(8,128)(2,1)S(1)} %copy-done, bf16[1024,512]{1,0:T(8,128)(2,1)S(1)} %copy-done.1, bf16[1024,512]{1,0:T(8,128)(2,1)S(1)} %copy-done.3, bf16[1024,512]{1,0:T(8,128)(2,1)S(1)} %get-tuple-element.21.gm, ...), custom_call_target="tpu_custom_call" | custom-call | flops 1073741824 | bytes 8257536 | tf_op jit(solution)/shard_map/second_grads/pallas_call | solution.py:46
  61.7 8.6 %collective-permute-done.10.refs_3_ = f32[512,128]{1,0:T(8,128)S(1)} collective-permute-done((f32[512,128]{1,0:T(8,128)S(1)}, f32[512,128]{1,0:T(8,128)S(1)}, u32[]{:S(2)}, u32[]{:S(2)}) %collective-permute-start.10) | collective-permute-done | bytes 262176 | tf_op jit(solution)/shard_map/ppermute | solution.py:50
  70.3 1.8 %last.1 = (bf16[1024,512]{1,0:T(8,128)(2,1)}, bf16[1024,512]{1,0:T(8,128)(2,1)}) custom-call(bf16[1024,512]{1,0:T(8,128)(2,1)S(1)} %copy-done.1, bf16[1024,512]{1,0:T(8,128)(2,1)S(1)} %copy-done.3, f32[1024,256]{1,0:T(8,128)S(1)} %get-tuple-element.27.refs_4_.gk0, f32[1024,256]{1,0:T(8,128)S(1)} %get-tuple-element.29.gv0, ...), custom_call_target="tpu_custom_call" | custom-call | flops 268435456 | bytes 9437184 | tf_op jit(solution)/shard_map/last/pallas_call | solution.py:46
Async XLA Ops:
  0.6 7.5 %copy-start.1 = (bf16[1024,512]{1,0:T(8,128)(2,1)S(1)}, bf16[1024,512]{1,0:T(8,128)(2,1)}, u32[]{:S(2)}) copy-start(bf16[1024,512]{1,0:T(8,128)(2,1)} %k.7) | copy-start | bytes 3145732
  0.6 7.5 %copy-start = (bf16[1024,512]{1,0:T(8,128)(2,1)S(1)}, bf16[1024,512]{1,0:T(8,128)(2,1)}, u32[]{:S(2)}) copy-start(bf16[1024,512]{1,0:T(8,128)(2,1)} %q.9) | copy-start | bytes 3145732
  3.4 11.4 %collective-permute-start = (f32[512,128]{1,0:T(8,128)}, f32[512,128]{1,0:T(8,128)S(1)}, u32[]{:S(2)}, u32[]{:S(2)}) collective-permute-start(f32[512,128]{1,0:T(8,128)} %local_state.1.refs_0_), channel_id=1, source_target_pairs={{0,12},{4,8},{8,4},{12,0},{16,28},{20,24},{24,20},{28,16},{1,13},{... | collective-permute-start | bytes 786440 | tf_op jit(solution)/shard_map/ppermute | solution.py:50
  7.4 12.3 %collective-permute-start.1 = (f32[512,128]{1,0:T(8,128)}, f32[512,128]{1,0:T(8,128)S(1)}, u32[]{:S(2)}, u32[]{:S(2)}) collective-permute-start(f32[512,128]{1,0:T(8,128)} %local_state.1.refs_0_), channel_id=1, source_target_pairs={{0,8},{4,12},{8,0},{12,4},{16,24},{20,28},{24,16},{28,20},{1,9},{5... | collective-permute-start | bytes 786440 | tf_op jit(solution)/shard_map/ppermute | solution.py:50
  7.9 11.9 %collective-permute-start.2 = (f32[512,128]{1,0:T(8,128)}, f32[512,128]{1,0:T(8,128)S(1)}, u32[]{:S(2)}, u32[]{:S(2)}) collective-permute-start(f32[512,128]{1,0:T(8,128)} %local_state.1.refs_0_), channel_id=1, source_target_pairs={{0,4},{4,0},{8,12},{12,8},{16,20},{20,16},{24,28},{28,24},{1,5},{5... | collective-permute-start | bytes 786440 | tf_op jit(solution)/shard_map/ppermute | solution.py:50
  8.1 1.2 %copy-start.2 = (bf16[1024,512]{1,0:T(8,128)(2,1)S(1)}, bf16[1024,512]{1,0:T(8,128)(2,1)}, u32[]{:S(2)}) copy-start(bf16[1024,512]{1,0:T(8,128)(2,1)} %v.7) | copy-start | bytes 3145732
  9.3 10.5 %copy-start.5 = (f32[512,128]{1,0:T(8,128)S(1)}, f32[512,128]{1,0:T(8,128)}, u32[]{:S(2)}) copy-start(f32[512,128]{1,0:T(8,128)} %local_state.1.refs_0_) | copy-start | bytes 786436
  11.2 23.3 %copy-start.4 = (bf16[1024,512]{1,0:T(8,128)(2,1)S(1)}, bf16[1024,512]{1,0:T(8,128)(2,1)}, u32[]{:S(2)}) copy-start(bf16[1024,512]{1,0:T(8,128)(2,1)} %g.3) | copy-start | bytes 3145732
  19.9 14.7 %collective-permute-start.3 = (f32[512,128]{1,0:T(8,128)S(1)}, f32[512,128]{1,0:T(8,128)S(1)}, u32[]{:S(2)}, u32[]{:S(2)}) collective-permute-start(f32[512,128]{1,0:T(8,128)S(1)} %quad_sum.2), channel_id=1, source_target_pairs={{0,16},{4,20},{8,24},{12,28},{16,0},{20,4},{24,8},{28,12},{1,17},{... | collective-permute-start | bytes 786440 | tf_op jit(solution)/shard_map/ppermute | solution.py:50
  35.4 3.1 %collective-permute-start.4 = (f32[16,128]{1,0:T(8,128)S(1)}, f32[16,128]{1,0:T(8,128)S(1)}, u32[]{:S(2)}, u32[]{:S(2)}) collective-permute-start(f32[16,128]{1,0:T(8,128)S(1)} %get-tuple-element.20.refs_0_), channel_id=1, source_target_pairs={{0,3},{1,2},{2,1},{3,0},{4,7},{5,6},{6,5},{7,4},{8,11},{9,10},{10,... | collective-permute-start | bytes 24584 | tf_op jit(solution)/shard_map/ppermute | solution.py:287
  35.7 3.7 %collective-permute-start.5 = (f32[16,128]{1,0:T(8,128)S(1)}, f32[16,128]{1,0:T(8,128)S(1)}, u32[]{:S(2)}, u32[]{:S(2)}) collective-permute-start(f32[16,128]{1,0:T(8,128)S(1)} %get-tuple-element.20.refs_0_), channel_id=1, source_target_pairs={{0,2},{1,3},{2,0},{3,1},{4,6},{5,7},{6,4},{7,5},{8,10},{9,11},{10,... | collective-permute-start | bytes 24584 | tf_op jit(solution)/shard_map/ppermute | solution.py:287
  37.1 2.3 %collective-permute-start.6 = (f32[16,128]{1,0:T(8,128)S(1)}, f32[16,128]{1,0:T(8,128)S(1)}, u32[]{:S(2)}, u32[]{:S(2)}) collective-permute-start(f32[16,128]{1,0:T(8,128)S(1)} %get-tuple-element.20.refs_0_), channel_id=1, source_target_pairs={{0,1},{1,0},{2,3},{3,2},{4,5},{5,4},{6,7},{7,6},{8,9},{9,8},{10,11... | collective-permute-start | bytes 24584 | tf_op jit(solution)/shard_map/ppermute | solution.py:287
  39.3 4.6 %copy-start.3 = (bf16[1024,512]{1,0:T(8,128)(2,1)S(1)}, bf16[1024,512]{1,0:T(8,128)(2,1)}, u32[]{:S(2)}) copy-start(bf16[1024,512]{1,0:T(8,128)(2,1)} %v.7) | copy-start | bytes 3145732
  40.4 10.1 %collective-permute-start.7 = (f32[512,128]{1,0:T(8,128)S(1)}, f32[512,128]{1,0:T(8,128)S(1)}, u32[]{:S(2)}, u32[]{:S(2)}) collective-permute-start(f32[512,128]{1,0:T(8,128)S(1)} %get-tuple-element.26.refs_0_), channel_id=1, source_target_pairs={{0,12},{4,8},{8,4},{12,0},{16,28},{20,24},{24,20},{28,16},{1,13},{... | collective-permute-start | bytes 786440 | tf_op jit(solution)/shard_map/ppermute | solution.py:50
  42.9 12.5 %collective-permute-start.8 = (f32[512,128]{1,0:T(8,128)S(1)}, f32[512,128]{1,0:T(8,128)S(1)}, u32[]{:S(2)}, u32[]{:S(2)}) collective-permute-start(f32[512,128]{1,0:T(8,128)S(1)} %get-tuple-element.26.refs_0_), channel_id=1, source_target_pairs={{0,8},{4,12},{8,0},{12,4},{16,24},{20,28},{24,16},{28,20},{1,9},{5... | collective-permute-start | bytes 786440 | tf_op jit(solution)/shard_map/ppermute | solution.py:50
  43.5 12.0 %collective-permute-start.9 = (f32[512,128]{1,0:T(8,128)S(1)}, f32[512,128]{1,0:T(8,128)S(1)}, u32[]{:S(2)}, u32[]{:S(2)}) collective-permute-start(f32[512,128]{1,0:T(8,128)S(1)} %get-tuple-element.26.refs_0_), channel_id=1, source_target_pairs={{0,4},{4,0},{8,12},{12,8},{16,20},{20,16},{24,28},{28,24},{1,5},{5... | collective-permute-start | bytes 786440 | tf_op jit(solution)/shard_map/ppermute | solution.py:50
  55.5 14.7 %collective-permute-start.10 = (f32[512,128]{1,0:T(8,128)S(1)}, f32[512,128]{1,0:T(8,128)S(1)}, u32[]{:S(2)}, u32[]{:S(2)}) collective-permute-start(f32[512,128]{1,0:T(8,128)S(1)} %quad_sum.3.token), channel_id=1, source_target_pairs={{0,16},{4,20},{8,24},{12,28},{16,0},{20,4},{24,8},{28,12},{1,17},{... | collective-permute-start | bytes 786440 | tf_op jit(solution)/shard_map/ppermute | solution.py:50

commit v3 on v2

--- a/solution.py
+++ b/solution.py
@@ -50,46 +50,79 @@
     return lax.ppermute(value, "seq", [(i, i ^ by) for i in range(size)])
 
 
-def sum_kernel(*refs):
-    parts, out = refs[:4], refs[-1]
-    out[...] = (parts[0][...] + parts[1][...]) + (parts[2][...] + parts[3][...])
-
-
-def quad_scan(state, size, between):
-    near = [exchange(state, size, by) for by in (3, 2, 1)]
+def place_of(size, reverse):
+    place = lax.axis_index("seq")
+    return size - 1 - place if reverse else place
+
+
+def window_kernel(own, near3, near2, near1, *refs):
+    outs = refs[-2:]
+    total = (own[...] + near1[...]) + (near2[...] + near3[...])
+    for n, out in enumerate(outs):
+        out[...] = total[n * HEAD_DIM : (n + 1) * HEAD_DIM]
+
+
+def finish_kernel(size, reverse, n, own, near3, near2, near1, far, *refs):
+    mine, theirs = refs[-2:]
+    place = place_of(size, reverse)
+    at = slice(n * HEAD_DIM, (n + 1) * HEAD_DIM)
+    zero = jnp.zeros(far.shape, F32)
+    before = jnp.where(place >= 4, far[...], zero)
+    before = before + jnp.where(lax.rem(place, 4) >= 2, near2[at] + near3[at], zero)
+    second = lax.rem(place, 2) == 1
+    mine[...] = before + jnp.where(second, near1[at], zero)
+    theirs[...] = before + jnp.where(second, zero, own[at])
+
+
+def quad_scan(halves, size, reverse, between):
+    own, oth = halves
+    half = jax.ShapeDtypeStruct(own.shape, F32)
+    head = jax.ShapeDtypeStruct((HEAD_DIM, HEAD_DIM), F32)
+    near = [exchange(v, size, by) for v, by in ((oth, 3), (own, 2), (oth, 1))]
     done = between(None)
-    (total,) = call(
-        sum_kernel,
-        [jax.ShapeDtypeStruct(state.shape, F32)],
-        [state, *near, *done[:1]],
+    pieces = call(
+        window_kernel,
+        [head, head],
+        [own, *near, done[0]],
         0,
         "quad_sum",
         spaces={4: pl.ANY},
     )
-    far = exchange(total, size, 4)
-    done = done + between(total)
-    return near + [far], done
+    far = [exchange(piece, size, 4) for piece in pieces]
+    later = between(pieces[1])
+    mine, theirs = [], []
+    for n in range(2):
+        a, b = call(
+            functools.partial(finish_kernel, size, reverse, n),
+            [head, head],
+            [own, *near, far[n], *later[-1:]],
+            0,
+            "finish",
+            spaces={5: pl.ANY},
+        )
+        mine.append(a)
+        theirs.append(exchange(b, size, 1))
+    return mine + theirs, done + later
 
 
 def quad_merge(refs, size, reverse):
-    place = lax.axis_index("seq")
-    if reverse:
-        place = size - 1 - place
-    inner = lax.rem(place, 4)
-    zero = jnp.zeros(refs[0].shape, F32)
-    total = jnp.where(place >= 4, refs[3][...], zero)
-    for ref, by in zip(refs, (3, 2, 1)):
-        total = total + jnp.where((inner ^ by) < inner, ref[...], zero)
-    return total.astype(BF16)
-
-
-def doubling_scan(state, size, reverse):
+    odd = lax.rem(lax.axis_index("seq"), 2) == 1
+    mine, theirs = [r[...] for r in refs[:2]], [r[...] for r in refs[2:]]
+    heads = [jnp.where(odd, b, a) for a, b in zip(mine, theirs)]
+    heads += [jnp.where(odd, a, b) for a, b in zip(mine, theirs)]
+    return jnp.concatenate(heads, axis=0).astype(BF16)
+
+
+def doubling_scan(halves, size, reverse):
     def shift(value, by):
         pairs = [(i, i + by) for i in range(size - by)]
         if reverse:
             pairs = [(b, a) for a, b in pairs]
         return lax.ppermute(value, "seq", pairs)
 
+    odd = lax.rem(lax.axis_index("seq"), 2) == 1
+    own, oth = halves
+    state = jnp.concatenate([jnp.where(odd, oth, own), jnp.where(odd, own, oth)], axis=0)
     by = 1
     while by < size:
         state = state + shift(state, by)
@@ -97,11 +130,11 @@
     return [shift(state, 1)]
 
 
-def scan(state, size, reverse, between):
+def scan(halves, size, reverse, between):
     if size == 8:
-        return quad_scan(state, size, between)
+        return quad_scan(halves, size, reverse, between)
     done = between(None)
-    return doubling_scan(state, size, reverse), done + between(done[0])
+    return doubling_scan(halves, size, reverse), done + between(done[0])
 
 
 def merge(refs, size, reverse):
@@ -110,7 +143,7 @@
     return refs[0][...].astype(BF16)
 
 
-def state_kernel(k_hbm, v_hbm, state, k, v, sems):
+def state_kernel(k_hbm, v_hbm, own, oth, k, v, sems):
     rows = k.shape[0]
     starts = range(0, rows, CHUNK)
     copies = []
@@ -129,13 +162,16 @@
             cols = slice(p * PAIR, (p + 1) * PAIR)
             new = dot(k[at, cols], v[at, cols], 0, 0)
             sums[p] = new if sums[p] is None else sums[p] + new
-    for p in range(pairs):
-        store_pair(state, p, sums[p])
-
-
-def store_pair(state, p, full):
-    state[p * PAIR : p * PAIR + HEAD_DIM, :] = full[:HEAD_DIM, :HEAD_DIM]
-    state[p * PAIR + HEAD_DIM : (p + 1) * PAIR, :] = full[HEAD_DIM:, HEAD_DIM:]
+    store_halves(sums, own, oth)
+
+
+def store_halves(pairs, own, oth):
+    odd = lax.rem(lax.axis_index("seq"), 2) == 1
+    blocks = [
+        jnp.concatenate([p[:HEAD_DIM, :HEAD_DIM], p[HEAD_DIM:, HEAD_DIM:]], axis=0) for p in pairs
+    ]
+    own[...] = jnp.where(odd, blocks[1], blocks[0])
+    oth[...] = jnp.where(odd, blocks[0], blocks[1])
 
 
 def intra_kernel(q, k, v, intra):
@@ -184,7 +220,7 @@
 
 
 def norm_kernel(width, n_stats, mixed, q, g, *refs):
-    stat_refs, (gm, state, inverse_out) = refs[:n_stats], refs[n_stats:]
+    stat_refs, (gm, own, oth, inverse_out) = refs[:n_stats], refs[n_stats:]
     total = stat_refs[0][...]
     for r in stat_refs[1:]:
         total = total + r[...]
@@ -202,9 +238,8 @@
             cols = slice(h * HEAD_DIM, (h + 1) * HEAD_DIM)
             m = mixed[at, cols]
             gm[at, cols] = (g[at, cols].astype(F32) * a - m * b).astype(BF16)
-    for p in range(q.shape[1] // PAIR):
-        cols = slice(p * PAIR, (p + 1) * PAIR)
-        store_pair(state, p, dot(q[:, cols], gm[:, cols], 0, 0))
+    pairs = [slice(p * PAIR, (p + 1) * PAIR) for p in range(q.shape[1] // PAIR)]
+    store_halves([dot(q[:, cols], gm[:, cols], 0, 0) for cols in pairs], own, oth)
 
 
 def head_grads(heads, q, k, v, gm, prefix, gq, gk, gv):
@@ -295,7 +330,7 @@
     halves = heads[: len(heads) // 2], heads[len(heads) // 2 :]
     chunks = rows // CHUNK
     width = cols * head_size
-    state_shape = jax.ShapeDtypeStruct((cols, HEAD_DIM), F32)
+    half = jax.ShapeDtypeStruct((cols // 2, HEAD_DIM), F32)
     wide = jax.ShapeDtypeStruct((rows, cols), F32)
     narrow = jax.ShapeDtypeStruct((rows, cols), BF16)
     half_wide = jax.ShapeDtypeStruct((rows, cols // 2), F32)
@@ -306,9 +341,9 @@
     chunk_flops = 2 * rows * cols * CHUNK
     slots = [pltpu.VMEM((rows, cols), BF16)] * 2 + [pltpu.SemaphoreType.DMA((2, chunks))]
 
-    (state,) = call(
+    state = call(
         state_kernel,
-        [state_shape],
+        [half, half],
         [keys, values],
         state_flops,
         "local_state",
@@ -338,9 +373,9 @@
         "mixed",
     )
     stats_parts = all_parts(stats, "head", head_size)
-    grad_mixed, state, inverse = call(
+    grad_mixed, *state, inverse = call(
         functools.partial(norm_kernel, width, len(stats_parts)),
-        [narrow, state_shape, inverse_shape],
+        [narrow, half, half, inverse_shape],
         [mixed, queries, grad_out, *stats_parts],
         state_flops,
         "norm",

time: 72.2 us -> 59 us (0.82)
  waiting for transfers between devices: 39 us -> 23.2 us
  starting transfers between devices: 15.1 us -> 17.6 us
    ppermute x8 -> x14, waiting for transfers between devices: 36.9 us -> 21.3 us  [exchange(): return lax.ppermute(value, 'seq', [(i, i ^ by) for i in range(size)])]
    ppermute x8 -> x14, starting transfers between devices: 13.2 us -> 15.7 us  [exchange(): return lax.ppermute(value, 'seq', [(i, i ^ by) for i in range(size)])]
    pallas_call x9 -> x13, Pallas kernels: 16 us -> 16 us  [call(): return list(kernel(*args))]
  transfers between devices with their start and end apart: 11 -> 17, of which waited for: 8 -> 14; matrix products, arithmetic and copies ran while one was open for 0% -> 0% of each run, Pallas kernels for 13% -> 16%
where the time goes in v3:
time: 59 us; the launch traced here: 58.8 us
  waiting for transfers between devices  23.2 us (39%)
  starting transfers between devices  17.6 us (30%)
  Pallas kernels  16 us (27%)
  local copies, waits for them, and re-layouts  1.25 us (2%)
  between operations  0.75 us (1%)
    ppermute x14, waiting for transfers between devices, exchange(): return lax.ppermute(value, 'seq', [(i, i ^ by) for i in range(size)])  21.3 us
    pallas_call x13, Pallas kernels, call(): return list(kernel(*args))  16 us
    ppermute x14, starting transfers between devices, exchange(): return lax.ppermute(value, 'seq', [(i, i ^ by) for i in range(size)])  15.7 us
    ppermute x3, starting transfers between devices, all_parts(): parts.append(lax.ppermute(value, axis, pairs))  1.92 us
    ppermute x3, waiting for transfers between devices, all_parts(): parts.append(lax.ppermute(value, axis, pairs))  1.87 us
    unnamed x12, local copies, waits for them, and re-layouts  1.25 us
  transfers between devices with their start and end apart: 17, of which 14 were waited for; matrix products, arithmetic and copies ran while one was open for 0% of the time, Pallas kernels for 16%

profile of v3, /device:TPU:0, one launch (start us, length us, event | category | flops | bytes accessed | tf_op | source)
XLA Modules:
  0.0 58.8 jit_solution(17953628552321367139)
XLA Ops:
  0.6 0.0 copy-start.1
  0.6 0.0 copy-start
  0.7 2.8 %local_state.1 = (f32[256,128]{1,0:T(8,128)}, f32[256,128]{1,0:T(8,128)}) custom-call(bf16[1024,512]{1,0:T(8,128)(2,1)} %k.7, bf16[1024,512]{1,0:T(8,128)(2,1)} %v.7), custom_call_target="tpu_custom_call" | custom-call | flops 134217728 | bytes 2359296 | tf_op jit(solution)/shard_map/local_state/pallas_call | solution.py:46
  3.4 3.1 %collective-permute-start.1 = (f32[256,128]{1,0:T(8,128)}, f32[256,128]{1,0:T(8,128)S(1)}, u32[]{:S(2)}, u32[]{:S(2)}) collective-permute-start(f32[256,128]{1,0:T(8,128)} %get-tuple-element.34.own), channel_id=1, source_target_pairs={{0,8},{4,12},{8,0},{12,4},{16,24},{20,28},{24,16},{28,20},{1,9},{5... | collective-permute-start | bytes 393224 | tf_op jit(solution)/shard_map/ppermute | solution.py:50
  6.5 1.4 %collective-permute-start = (f32[256,128]{1,0:T(8,128)}, f32[256,128]{1,0:T(8,128)S(1)}, u32[]{:S(2)}, u32[]{:S(2)}) collective-permute-start(f32[256,128]{1,0:T(8,128)} %get-tuple-element.35), channel_id=1, source_target_pairs={{0,12},{4,8},{8,4},{12,0},{16,28},{20,24},{24,20},{28,16},{1,13},{... | collective-permute-start | bytes 393224 | tf_op jit(solution)/shard_map/ppermute | solution.py:50
  7.9 0.2 collective-permute-start.2
  8.1 0.0 copy-done.1
  8.1 0.0 copy-done
  8.1 0.0 copy-start.2
  8.1 1.2 %copy-done.2 = bf16[1024,512]{1,0:T(8,128)(2,1)S(1)} copy-done((bf16[1024,512]{1,0:T(8,128)(2,1)S(1)}, bf16[1024,512]{1,0:T(8,128)(2,1)}, u32[]{:S(2)}) %copy-start.2) | copy-done | bytes 1048600
  9.3 0.0 copy-start.5
  9.3 1.9 %intra.1.refs_0_ = f32[1024,512]{1,0:T(8,128)S(1)} custom-call(bf16[1024,512]{1,0:T(8,128)(2,1)S(1)} %copy-done, bf16[1024,512]{1,0:T(8,128)(2,1)S(1)} %copy-done.1, bf16[1024,512]{1,0:T(8,128)(2,1)S(1)} %copy-done.2), custom_call_target="tpu_custom_call" | custom-call | flops 805306368 | bytes 5242880 | tf_op jit(solution)/shard_map/intra/pallas_call | solution.py:46
  11.2 0.0 copy-start.4
  11.2 0.0 collective-permute-done.1.near2
  11.2 3.0 %collective-permute-done.near3 = f32[256,128]{1,0:T(8,128)S(1)} collective-permute-done((f32[256,128]{1,0:T(8,128)}, f32[256,128]{1,0:T(8,128)S(1)}, u32[]{:S(2)}, u32[]{:S(2)}) %collective-permute-start) | collective-permute-done | bytes 131104 | tf_op jit(solution)/shard_map/ppermute | solution.py:50
  14.2 1.4 %collective-permute-done.2.near1 = f32[256,128]{1,0:T(8,128)S(1)} collective-permute-done((f32[256,128]{1,0:T(8,128)}, f32[256,128]{1,0:T(8,128)S(1)}, u32[]{:S(2)}, u32[]{:S(2)}) %collective-permute-start.2) | collective-permute-done | bytes 131104 | tf_op jit(solution)/shard_map/ppermute | solution.py:50
  15.6 0.0 copy-done.5
  15.6 2.6 %collective-permute-start.4 = (f32[128,128]{1,0:T(8,128)S(1)}, f32[128,128]{1,0:T(8,128)S(1)}, u32[]{:S(2)}, u32[]{:S(2)}) collective-permute-start(f32[128,128]{1,0:T(8,128)S(1)} %get-tuple-element.38), channel_id=1, source_target_pairs={{0,16},{4,20},{8,24},{12,28},{16,0},{20,4},{24,8},{28,12},{1,17},{... | collective-permute-start | bytes 196616 | tf_op jit(solution)/shard_map/ppermute | solution.py:50
  18.3 0.3 collective-permute-start.3
  18.6 2.6 %collective-permute-done.4.far = f32[128,128]{1,0:T(8,128)S(1)} collective-permute-done((f32[128,128]{1,0:T(8,128)S(1)}, f32[128,128]{1,0:T(8,128)S(1)}, u32[]{:S(2)}, u32[]{:S(2)}) %collective-permute-start.4) | collective-permute-done | bytes 65568 | tf_op jit(solution)/shard_map/ppermute | solution.py:50
  21.2 0.6 %collective-permute-start.6 = (f32[128,128]{1,0:T(8,128)S(1)}, f32[128,128]{1,0:T(8,128)S(1)}, u32[]{:S(2)}, u32[]{:S(2)}) collective-permute-start(f32[128,128]{1,0:T(8,128)S(1)} %get-tuple-element.41), channel_id=1, source_target_pairs={{0,4},{4,0},{8,12},{12,8},{16,20},{20,16},{24,28},{28,24},{1,5},{5... | collective-permute-start | bytes 196616 | tf_op jit(solution)/shard_map/ppermute | solution.py:50
  21.9 1.8 %collective-permute-done.3.far = f32[128,128]{1,0:T(8,128)S(1)} collective-permute-done((f32[128,128]{1,0:T(8,128)S(1)}, f32[128,128]{1,0:T(8,128)S(1)}, u32[]{:S(2)}, u32[]{:S(2)}) %collective-permute-start.3) | collective-permute-done | bytes 65568 | tf_op jit(solution)/shard_map/ppermute | solution.py:50
  23.7 0.5 collective-permute-start.5
  24.2 1.4 %collective-permute-done.6.refs_3_ = f32[128,128]{1,0:T(8,128)S(1)} collective-permute-done((f32[128,128]{1,0:T(8,128)S(1)}, f32[128,128]{1,0:T(8,128)S(1)}, u32[]{:S(2)}, u32[]{:S(2)}) %collective-permute-start.6) | collective-permute-done | bytes 65568 | tf_op jit(solution)/shard_map/ppermute | solution.py:50
  25.6 2.5 %collective-permute-done.5.refs_2_ = f32[128,128]{1,0:T(8,128)S(1)} collective-permute-done((f32[128,128]{1,0:T(8,128)S(1)}, f32[128,128]{1,0:T(8,128)S(1)}, u32[]{:S(2)}, u32[]{:S(2)}) %collective-permute-start.5) | collective-permute-done | bytes 65568 | tf_op jit(solution)/shard_map/ppermute | solution.py:50
  28.0 0.0 copy-done.4
  28.0 0.8 %mixed.1 = (f32[1024,512]{1,0:T(8,128)S(1)}, f32[16,128]{1,0:T(8,128)S(1)}, bf16[512,128]{1,0:T(8,128)(2,1)S(1)}) custom-call(f32[1024,512]{1,0:T(8,128)S(1)} %intra.1.refs_0_, bf16[1024,512]{1,0:T(8,128)(2,1)S(1)} %copy-done, bf16[1024,512]{1,0:T(8,128)(2,1)S(1)} %copy-done.4, f32[128,128]{1,0:T(8,128)S(1)} %get-tuple-element.37.refs_0_, ...), custom_call_target="tpu_custom_call" | custom-call | flops 134217728 | bytes 6692864 | tf_op jit(solution)/shard_map/mixed/pallas_call | solution.py:46
  28.9 0.1 collective-permute-start.7
  28.9 1.6 %collective-permute-start.8 = (f32[16,128]{1,0:T(8,128)S(1)}, f32[16,128]{1,0:T(8,128)S(1)}, u32[]{:S(2)}, u32[]{:S(2)}) collective-permute-start(f32[16,128]{1,0:T(8,128)S(1)} %get-tuple-element.43.refs_0_), channel_id=1, source_target_pairs={{0,2},{1,3},{2,0},{3,1},{4,6},{5,7},{6,4},{7,5},{8,10},{9,11},{10,... | collective-permute-start | bytes 24584 | tf_op jit(solution)/shard_map/ppermute | solution.py:322
  30.5 0.3 collective-permute-start.9
  30.8 1.2 %collective-permute-done.7.refs_1_ = f32[16,128]{1,0:T(8,128)S(1)} collective-permute-done((f32[16,128]{1,0:T(8,128)S(1)}, f32[16,128]{1,0:T(8,128)S(1)}, u32[]{:S(2)}, u32[]{:S(2)}) %collective-permute-start.7) | collective-permute-done | bytes 8224 | tf_op jit(solution)/shard_map/ppermute | solution.py:322
  32.0 0.6 %collective-permute-done.8.refs_2_ = f32[16,128]{1,0:T(8,128)S(1)} collective-permute-done((f32[16,128]{1,0:T(8,128)S(1)}, f32[16,128]{1,0:T(8,128)S(1)}, u32[]{:S(2)}, u32[]{:S(2)}) %collective-permute-start.8) | collective-permute-done | bytes 8224 | tf_op jit(solution)/shard_map/ppermute | solution.py:322
  32.7 0.0 collective-permute-done.9.refs_3_
  32.7 0.0 copy-start.3
  32.7 1.0 %norm.1 = (bf16[1024,512]{1,0:T(8,128)(2,1)S(1)}, f32[256,128]{1,0:T(8,128)S(1)}, f32[256,128]{1,0:T(8,128)S(1)}, f32[8,128]{1,0:T(8,128)S(1)}) custom-call(f32[1024,512]{1,0:T(8,128)S(1)} %get-tuple-element.42.mixed, bf16[1024,512]{1,0:T(8,128)(2,1)S(1)} %copy-done, bf16[1024,512]{1,0:T(8,128)(2,1)S(1)} %copy-done.4, ...), custom_call_target="tpu_custom_call" | custom-call | flops 134217728 | bytes 5541888 | tf_op jit(solution)/shard_map/norm/pallas_call | solution.py:46
  33.7 1.7 %collective-permute-start.10 = (f32[256,128]{1,0:T(8,128)S(1)}, f32[256,128]{1,0:T(8,128)S(1)}, u32[]{:S(2)}, u32[]{:S(2)}) collective-permute-start(f32[256,128]{1,0:T(8,128)S(1)} %get-tuple-element.50), channel_id=1, source_target_pairs={{0,12},{4,8},{8,4},{12,0},{16,28},{20,24},{24,20},{28,16},{1,13},{... | collective-permute-start | bytes 393224 | tf_op jit(solution)/shard_map/ppermute | solution.py:50
  35.4 0.4 collective-permute-start.11
  35.8 1.5 %collective-permute-start.12 = (f32[256,128]{1,0:T(8,128)S(1)}, f32[256,128]{1,0:T(8,128)S(1)}, u32[]{:S(2)}, u32[]{:S(2)}) collective-permute-start(f32[256,128]{1,0:T(8,128)S(1)} %get-tuple-element.50), channel_id=1, source_target_pairs={{0,4},{4,0},{8,12},{12,8},{16,20},{20,16},{24,28},{28,24},{1,5},{5... | collective-permute-start | bytes 393224 | tf_op jit(solution)/shard_map/ppermute | solution.py:50
  37.3 0.0 copy-done.3
  37.3 3.9 %first_grads.1 = (bf16[1024,256]{1,0:T(8,128)(2,1)S(1)}, f32[1024,256]{1,0:T(8,128)S(1)}, f32[1024,256]{1,0:T(8,128)S(1)}, bf16[1024,512]{1,0:T(8,128)(2,1)}) custom-call(bf16[1024,512]{1,0:T(8,128)(2,1)S(1)} %copy-done, bf16[1024,512]{1,0:T(8,128)(2,1)S(1)} %copy-done.1, bf16[1024,512]{1,0:T(8,128)(2,1)S(1)} %copy-done.3, ...), custom_call_target="tpu_custom_call" | custom-call | flops 1073741824 | bytes 10096640 | tf_op jit(solution)/shard_map/first_grads/pallas_call | solution.py:46
  41.1 0.0 collective-permute-done.10.near3
  41.1 1.3 %collective-permute-done.11.near2 = f32[256,128]{1,0:T(8,128)S(1)} collective-permute-done((f32[256,128]{1,0:T(8,128)S(1)}, f32[256,128]{1,0:T(8,128)S(1)}, u32[]{:S(2)}, u32[]{:S(2)}) %collective-permute-start.11) | collective-permute-done | bytes 131104 | tf_op jit(solution)/shard_map/ppermute | solution.py:50
  42.4 0.9 %collective-permute-done.12.near1 = f32[256,128]{1,0:T(8,128)S(1)} collective-permute-done((f32[256,128]{1,0:T(8,128)S(1)}, f32[256,128]{1,0:T(8,128)S(1)}, u32[]{:S(2)}, u32[]{:S(2)}) %collective-permute-start.12) | collective-permute-done | bytes 131104 | tf_op jit(solution)/shard_map/ppermute | solution.py:50
  43.3 2.4 %collective-permute-start.14 = (f32[128,128]{1,0:T(8,128)S(1)}, f32[128,128]{1,0:T(8,128)S(1)}, u32[]{:S(2)}, u32[]{:S(2)}) collective-permute-start(f32[128,128]{1,0:T(8,128)S(1)} %get-tuple-element.52.token), channel_id=1, source_target_pairs={{0,16},{4,20},{8,24},{12,28},{16,0},{20,4},{24,8},{28,12},{1,17},{... | collective-permute-start | bytes 196616 | tf_op jit(solution)/shard_map/ppermute | solution.py:50
  45.7 0.6 %collective-permute-start.13 = (f32[128,128]{1,0:T(8,128)S(1)}, f32[128,128]{1,0:T(8,128)S(1)}, u32[]{:S(2)}, u32[]{:S(2)}) collective-permute-start(f32[128,128]{1,0:T(8,128)S(1)} %get-tuple-element.57), channel_id=1, source_target_pairs={{0,16},{4,20},{8,24},{12,28},{16,0},{20,4},{24,8},{28,12},{1,17},{... | collective-permute-start | bytes 196616 | tf_op jit(solution)/shard_map/ppermute | solution.py:50
  46.3 3.8 %second_grads.1 = (bf16[1024,512]{1,0:T(8,128)(2,1)}, f32[1024,256]{1,0:T(8,128)S(1)}, f32[1024,256]{1,0:T(8,128)S(1)}) custom-call(bf16[1024,512]{1,0:T(8,128)(2,1)S(1)} %copy-done, bf16[1024,512]{1,0:T(8,128)(2,1)S(1)} %copy-done.1, bf16[1024,512]{1,0:T(8,128)(2,1)S(1)} %copy-done.3, bf16[1024,512]{1,0:T(8,128)(2,1)S(1)} %get-tuple-element.44.gm, ...), custom_call_target="tpu_custom_call" | custom-call | flops 1073741824 | bytes 8060928 | tf_op jit(solution)/shard_map/second_grads/pallas_call | solution.py:46
  50.1 0.3 collective-permute-done.14.far
  50.5 0.3 collective-permute-start.16
  50.8 2.0 %collective-permute-done.13.far = f32[128,128]{1,0:T(8,128)S(1)} collective-permute-done((f32[128,128]{1,0:T(8,128)S(1)}, f32[128,128]{1,0:T(8,128)S(1)}, u32[]{:S(2)}, u32[]{:S(2)}) %collective-permute-start.13) | collective-permute-done | bytes 65568 | tf_op jit(solution)/shard_map/ppermute | solution.py:50
  52.8 0.1 collective-permute-start.15
  52.9 1.9 %collective-permute-done.16.refs_3_ = f32[128,128]{1,0:T(8,128)S(1)} collective-permute-done((f32[128,128]{1,0:T(8,128)S(1)}, f32[128,128]{1,0:T(8,128)S(1)}, u32[]{:S(2)}, u32[]{:S(2)}) %collective-permute-start.16) | collective-permute-done | bytes 65568 | tf_op jit(solution)/shard_map/ppermute | solution.py:50
  54.8 2.3 %collective-permute-done.15.refs_2_ = f32[128,128]{1,0:T(8,128)S(1)} collective-permute-done((f32[128,128]{1,0:T(8,128)S(1)}, f32[128,128]{1,0:T(8,128)S(1)}, u32[]{:S(2)}, u32[]{:S(2)}) %collective-permute-start.15) | collective-permute-done | bytes 65568 | tf_op jit(solution)/shard_map/ppermute | solution.py:50
  57.1 1.7 %last.1 = (bf16[1024,512]{1,0:T(8,128)(2,1)}, bf16[1024,512]{1,0:T(8,128)(2,1)}) custom-call(bf16[1024,512]{1,0:T(8,128)(2,1)S(1)} %copy-done.1, bf16[1024,512]{1,0:T(8,128)(2,1)S(1)} %copy-done.3, f32[1024,256]{1,0:T(8,128)S(1)} %get-tuple-element.51.refs_0_.gk0, f32[1024,256]{1,0:T(8,128)S(1)} %get-tuple-element.54.gv0, ...), custom_call_target="tpu_custom_call" | custom-call | flops 268435456 | bytes 8650752 | tf_op jit(solution)/shard_map/last/pallas_call | solution.py:46
  (6 shorter events, 0.2 us)
Async XLA Ops:
  0.6 7.4 %copy-start.1 = (bf16[1024,512]{1,0:T(8,128)(2,1)S(1)}, bf16[1024,512]{1,0:T(8,128)(2,1)}, u32[]{:S(2)}) copy-start(bf16[1024,512]{1,0:T(8,128)(2,1)} %k.7) | copy-start | bytes 3145732
  0.6 7.4 %copy-start = (bf16[1024,512]{1,0:T(8,128)(2,1)S(1)}, bf16[1024,512]{1,0:T(8,128)(2,1)}, u32[]{:S(2)}) copy-start(bf16[1024,512]{1,0:T(8,128)(2,1)} %q.9) | copy-start | bytes 3145732
  3.4 7.8 %collective-permute-start.1 = (f32[256,128]{1,0:T(8,128)}, f32[256,128]{1,0:T(8,128)S(1)}, u32[]{:S(2)}, u32[]{:S(2)}) collective-permute-start(f32[256,128]{1,0:T(8,128)} %get-tuple-element.34.own), channel_id=1, source_target_pairs={{0,8},{4,12},{8,0},{12,4},{16,24},{20,28},{24,16},{28,20},{1,9},{5... | collective-permute-start | bytes 393224 | tf_op jit(solution)/shard_map/ppermute | solution.py:50
  6.5 7.7 %collective-permute-start = (f32[256,128]{1,0:T(8,128)}, f32[256,128]{1,0:T(8,128)S(1)}, u32[]{:S(2)}, u32[]{:S(2)}) collective-permute-start(f32[256,128]{1,0:T(8,128)} %get-tuple-element.35), channel_id=1, source_target_pairs={{0,12},{4,8},{8,4},{12,0},{16,28},{20,24},{24,20},{28,16},{1,13},{... | collective-permute-start | bytes 393224 | tf_op jit(solution)/shard_map/ppermute | solution.py:50
  7.9 7.7 %collective-permute-start.2 = (f32[256,128]{1,0:T(8,128)}, f32[256,128]{1,0:T(8,128)S(1)}, u32[]{:S(2)}, u32[]{:S(2)}) collective-permute-start(f32[256,128]{1,0:T(8,128)} %get-tuple-element.35), channel_id=1, source_target_pairs={{0,4},{4,0},{8,12},{12,8},{16,20},{20,16},{24,28},{28,24},{1,5},{5... | collective-permute-start | bytes 393224 | tf_op jit(solution)/shard_map/ppermute | solution.py:50
  8.1 1.2 %copy-start.2 = (bf16[1024,512]{1,0:T(8,128)(2,1)S(1)}, bf16[1024,512]{1,0:T(8,128)(2,1)}, u32[]{:S(2)}) copy-start(bf16[1024,512]{1,0:T(8,128)(2,1)} %v.7) | copy-start | bytes 3145732
  9.3 6.3 %copy-start.5 = (f32[256,128]{1,0:T(8,128)S(1)}, f32[256,128]{1,0:T(8,128)}, u32[]{:S(2)}) copy-start(f32[256,128]{1,0:T(8,128)} %get-tuple-element.34.own) | copy-start | bytes 393220
  11.2 16.8 %copy-start.4 = (bf16[1024,512]{1,0:T(8,128)(2,1)S(1)}, bf16[1024,512]{1,0:T(8,128)(2,1)}, u32[]{:S(2)}) copy-start(bf16[1024,512]{1,0:T(8,128)(2,1)} %g.3) | copy-start | bytes 3145732
  15.6 5.6 %collective-permute-start.4 = (f32[128,128]{1,0:T(8,128)S(1)}, f32[128,128]{1,0:T(8,128)S(1)}, u32[]{:S(2)}, u32[]{:S(2)}) collective-permute-start(f32[128,128]{1,0:T(8,128)S(1)} %get-tuple-element.38), channel_id=1, source_target_pairs={{0,16},{4,20},{8,24},{12,28},{16,0},{20,4},{24,8},{28,12},{1,17},{... | collective-permute-start | bytes 196616 | tf_op jit(solution)/shard_map/ppermute | solution.py:50
  18.3 5.4 %collective-permute-start.3 = (f32[128,128]{1,0:T(8,128)S(1)}, f32[128,128]{1,0:T(8,128)S(1)}, u32[]{:S(2)}, u32[]{:S(2)}) collective-permute-start(f32[128,128]{1,0:T(8,128)S(1)} %get-tuple-element.36), channel_id=1, source_target_pairs={{0,16},{4,20},{8,24},{12,28},{16,0},{20,4},{24,8},{28,12},{1,17},{... | collective-permute-start | bytes 196616 | tf_op jit(solution)/shard_map/ppermute | solution.py:50
  21.2 4.3 %collective-permute-start.6 = (f32[128,128]{1,0:T(8,128)S(1)}, f32[128,128]{1,0:T(8,128)S(1)}, u32[]{:S(2)}, u32[]{:S(2)}) collective-permute-start(f32[128,128]{1,0:T(8,128)S(1)} %get-tuple-element.41), channel_id=1, source_target_pairs={{0,4},{4,0},{8,12},{12,8},{16,20},{20,16},{24,28},{28,24},{1,5},{5... | collective-permute-start | bytes 196616 | tf_op jit(solution)/shard_map/ppermute | solution.py:50
  23.7 4.3 %collective-permute-start.5 = (f32[128,128]{1,0:T(8,128)S(1)}, f32[128,128]{1,0:T(8,128)S(1)}, u32[]{:S(2)}, u32[]{:S(2)}) collective-permute-start(f32[128,128]{1,0:T(8,128)S(1)} %get-tuple-element.40), channel_id=1, source_target_pairs={{0,4},{4,0},{8,12},{12,8},{16,20},{20,16},{24,28},{28,24},{1,5},{5... | collective-permute-start | bytes 196616 | tf_op jit(solution)/shard_map/ppermute | solution.py:50
  28.9 3.2 %collective-permute-start.7 = (f32[16,128]{1,0:T(8,128)S(1)}, f32[16,128]{1,0:T(8,128)S(1)}, u32[]{:S(2)}, u32[]{:S(2)}) collective-permute-start(f32[16,128]{1,0:T(8,128)S(1)} %get-tuple-element.43.refs_0_), channel_id=1, source_target_pairs={{0,3},{1,2},{2,1},{3,0},{4,7},{5,6},{6,5},{7,4},{8,11},{9,10},{10,... | collective-permute-start | bytes 24584 | tf_op jit(solution)/shard_map/ppermute | solution.py:322
  28.9 3.7 %collective-permute-start.8 = (f32[16,128]{1,0:T(8,128)S(1)}, f32[16,128]{1,0:T(8,128)S(1)}, u32[]{:S(2)}, u32[]{:S(2)}) collective-permute-start(f32[16,128]{1,0:T(8,128)S(1)} %get-tuple-element.43.refs_0_), channel_id=1, source_target_pairs={{0,2},{1,3},{2,0},{3,1},{4,6},{5,7},{6,4},{7,5},{8,10},{9,11},{10,... | collective-permute-start | bytes 24584 | tf_op jit(solution)/shard_map/ppermute | solution.py:322
  30.5 2.1 %collective-permute-start.9 = (f32[16,128]{1,0:T(8,128)S(1)}, f32[16,128]{1,0:T(8,128)S(1)}, u32[]{:S(2)}, u32[]{:S(2)}) collective-permute-start(f32[16,128]{1,0:T(8,128)S(1)} %get-tuple-element.43.refs_0_), channel_id=1, source_target_pairs={{0,1},{1,0},{2,3},{3,2},{4,5},{5,4},{6,7},{7,6},{8,9},{9,8},{10,11... | collective-permute-start | bytes 24584 | tf_op jit(solution)/shard_map/ppermute | solution.py:322
  32.7 4.6 %copy-start.3 = (bf16[1024,512]{1,0:T(8,128)(2,1)S(1)}, bf16[1024,512]{1,0:T(8,128)(2,1)}, u32[]{:S(2)}) copy-start(bf16[1024,512]{1,0:T(8,128)(2,1)} %v.7) | copy-start | bytes 3145732
  33.7 7.4 %collective-permute-start.10 = (f32[256,128]{1,0:T(8,128)S(1)}, f32[256,128]{1,0:T(8,128)S(1)}, u32[]{:S(2)}, u32[]{:S(2)}) collective-permute-start(f32[256,128]{1,0:T(8,128)S(1)} %get-tuple-element.50), channel_id=1, source_target_pairs={{0,12},{4,8},{8,4},{12,0},{16,28},{20,24},{24,20},{28,16},{1,13},{... | collective-permute-start | bytes 393224 | tf_op jit(solution)/shard_map/ppermute | solution.py:50
  35.4 7.0 %collective-permute-start.11 = (f32[256,128]{1,0:T(8,128)S(1)}, f32[256,128]{1,0:T(8,128)S(1)}, u32[]{:S(2)}, u32[]{:S(2)}) collective-permute-start(f32[256,128]{1,0:T(8,128)S(1)} %get-tuple-element.49.own), channel_id=1, source_target_pairs={{0,8},{4,12},{8,0},{12,4},{16,24},{20,28},{24,16},{28,20},{1,9},{5... | collective-permute-start | bytes 393224 | tf_op jit(solution)/shard_map/ppermute | solution.py:50
  35.8 7.5 %collective-permute-start.12 = (f32[256,128]{1,0:T(8,128)S(1)}, f32[256,128]{1,0:T(8,128)S(1)}, u32[]{:S(2)}, u32[]{:S(2)}) collective-permute-start(f32[256,128]{1,0:T(8,128)S(1)} %get-tuple-element.50), channel_id=1, source_target_pairs={{0,4},{4,0},{8,12},{12,8},{16,20},{20,16},{24,28},{28,24},{1,5},{5... | collective-permute-start | bytes 393224 | tf_op jit(solution)/shard_map/ppermute | solution.py:50
  43.3 7.1 %collective-permute-start.14 = (f32[128,128]{1,0:T(8,128)S(1)}, f32[128,128]{1,0:T(8,128)S(1)}, u32[]{:S(2)}, u32[]{:S(2)}) collective-permute-start(f32[128,128]{1,0:T(8,128)S(1)} %get-tuple-element.52.token), channel_id=1, source_target_pairs={{0,16},{4,20},{8,24},{12,28},{16,0},{20,4},{24,8},{28,12},{1,17},{... | collective-permute-start | bytes 196616 | tf_op jit(solution)/shard_map/ppermute | solution.py:50
  45.7 7.1 %collective-permute-start.13 = (f32[128,128]{1,0:T(8,128)S(1)}, f32[128,128]{1,0:T(8,128)S(1)}, u32[]{:S(2)}, u32[]{:S(2)}) collective-permute-start(f32[128,128]{1,0:T(8,128)S(1)} %get-tuple-element.57), channel_id=1, source_target_pairs={{0,16},{4,20},{8,24},{12,28},{16,0},{20,4},{24,8},{28,12},{1,17},{... | collective-permute-start | bytes 196616 | tf_op jit(solution)/shard_map/ppermute | solution.py:50
  50.5 4.3 %collective-permute-start.16 = (f32[128,128]{1,0:T(8,128)S(1)}, f32[128,128]{1,0:T(8,128)S(1)}, u32[]{:S(2)}, u32[]{:S(2)}) collective-permute-start(f32[128,128]{1,0:T(8,128)S(1)} %get-tuple-element.61), channel_id=1, source_target_pairs={{0,4},{4,0},{8,12},{12,8},{16,20},{20,16},{24,28},{28,24},{1,5},{5... | collective-permute-start | bytes 196616 | tf_op jit(solution)/shard_map/ppermute | solution.py:50
  52.8 4.3 %collective-permute-start.15 = (f32[128,128]{1,0:T(8,128)S(1)}, f32[128,128]{1,0:T(8,128)S(1)}, u32[]{:S(2)}, u32[]{:S(2)}) collective-permute-start(f32[128,128]{1,0:T(8,128)S(1)} %get-tuple-element.60), channel_id=1, source_target_pairs={{0,4},{4,0},{8,12},{12,8},{16,20},{20,16},{24,28},{28,24},{1,5},{5... | collective-permute-start | bytes 196616 | tf_op jit(solution)/shard_map/ppermute | solution.py:50

commit v4 on v3

v4 whole, which is shorter than its diff:
```python
import functools

import jax
import jax.numpy as jnp
from jax import lax
from jax.experimental import pallas as pl
from jax.experimental.pallas import tpu as pltpu
from jax.sharding import PartitionSpec as P

HEAD_DIM = 128
EPSILON = 1e-06
CHUNK = 256
PAIR = 2 * HEAD_DIM
F32 = jnp.float32
BF16 = jnp.bfloat16


def dot(a, b, ca, cb):
    return lax.dot_general(a, b, (((ca,), (cb,)), ((), ())), preferred_element_type=F32)


def columns(own, head=0, count=1):
    odd = lax.rem(lax.axis_index("seq"), 2)
    side = odd if own else 1 - odd
    start = pl.multiple_of(side * PAIR + head * HEAD_DIM, HEAD_DIM)
    return pl.ds(start, count * HEAD_DIM)


def causal(count):
    rows = lax.broadcasted_iota(jnp.int32, (count, count), 0)
    cols = lax.broadcasted_iota(jnp.int32, (count, count), 1)
    return rows >= cols


def call(
    body, out_shape, args, flops, name, spaces=None, outs=None, scratch=(), limit=20, aliases=None
):
    size = sum(a.size * a.dtype.itemsize for a in args)
    size += sum(a.size * a.dtype.itemsize for a in out_shape)
    spaces, outs = spaces or {}, outs or {}
    kernel = pl.pallas_call(
        body,
        out_shape=out_shape,
        in_specs=[
            pl.BlockSpec(memory_space=spaces.get(i, pltpu.VMEM)) for i in range(len(args))
        ],
        out_specs=[
            pl.BlockSpec(memory_space=outs.get(i, pltpu.VMEM)) for i in range(len(out_shape))
        ],
        scratch_shapes=list(scratch),
        input_output_aliases=aliases or {},
        compiler_params=pltpu.CompilerParams(vmem_limit_bytes=limit * 2**20),
        cost_estimate=pl.CostEstimate(flops=flops, bytes_accessed=size, transcendentals=0),
        name=name,
    )
    return list(kernel(*args))


def exchange(value, size, by):
    return lax.ppermute(value, "seq", [(i, i ^ by) for i in range(size)])


def place_of(size, reverse):
    place = lax.axis_index("seq")
    return size - 1 - place if reverse else place


def window_kernel(own, near3, near2, near1, *refs):
    outs = refs[-2:]
    total = (own[...] + near1[...]) + (near2[...] + near3[...])
    for n, out in enumerate(outs):
        out[...] = total[n * HEAD_DIM : (n + 1) * HEAD_DIM]


def finish_kernel(size, reverse, n, own, near3, near2, near1, far, *refs):
    mine, theirs = refs[-2:]
    place = place_of(size, reverse)
    at = slice(n * HEAD_DIM, (n + 1) * HEAD_DIM)
    zero = jnp.zeros(far.shape, F32)
    before = jnp.where(place >= 4, far[...], zero)
    before = before + jnp.where(lax.rem(place, 4) >= 2, near2[at] + near3[at], zero)
    second = lax.rem(place, 2) == 1
    mine[...] = before + jnp.where(second, near1[at], zero)
    theirs[...] = before + jnp.where(second, zero, own[at])


def quad_scan(own, oth, size, reverse, between):
    half = jax.ShapeDtypeStruct(own.shape, F32)
    head = jax.ShapeDtypeStruct((HEAD_DIM, HEAD_DIM), F32)
    near = [exchange(v, size, by) for v, by in ((oth, 3), (own, 2), (oth, 1))]
    done = between(None)
    pieces = call(
        window_kernel,
        [head, head],
        [own, *near, done[0]],
        0,
        "quad_sum",
        spaces={4: pl.ANY},
    )
    far = [exchange(piece, size, 4) for piece in pieces]
    later = between(pieces[1])
    mine, theirs = [], []
    for n in range(2):
        a, b = call(
            functools.partial(finish_kernel, size, reverse, n),
            [head, head],
            [own, *near, far[n], *later[-1:]],
            0,
            "finish",
            spaces={5: pl.ANY},
        )
        mine.append(a)
        theirs.append(exchange(b, size, 1))
    return mine + theirs, done + later


def doubling_scan(own, oth, size, reverse):
    def shift(value, by):
        pairs = [(i, i + by) for i in range(size - by)]
        if reverse:
            pairs = [(b, a) for a, b in pairs]
        return lax.ppermute(value, "seq", pairs)

    odd = lax.rem(lax.axis_index("seq"), 2) == 1
    state = jnp.stack([jnp.where(odd, oth, own), jnp.where(odd, own, oth)])
    by = 1
    while by < size:
        state = state + shift(state, by)
        by *= 2
    state = shift(state, 1)
    own, oth = jnp.where(odd, state[1], state[0]), jnp.where(odd, state[0], state[1])
    return [half[n * HEAD_DIM : (n + 1) * HEAD_DIM] for half in (own, oth) for n in range(2)]


def scan(own, oth, size, reverse, between):
    if size == 8:
        return quad_scan(own, oth, size, reverse, between)
    done = between(None)
    return doubling_scan(own, oth, size, reverse), done + between(done[0])


def state_kernel(is_own, k_hbm, v_hbm, *refs):
    state, k, v, sems = refs[-4:]
    starts = range(0, k.shape[0], CHUNK)
    cols = columns(is_own, count=2)
    copies = []
    for n, start in enumerate(starts):
        at = slice(start, start + CHUNK)
        for j, (src, dst) in enumerate(((k_hbm, k), (v_hbm, v))):
            copies.append(pltpu.make_async_copy(src.at[at, cols], dst.at[at], sems.at[j, n]))
            copies[-1].start()
    total = None
    for n, start in enumerate(starts):
        at = slice(start, start + CHUNK)
        copies[2 * n].wait()
        copies[2 * n + 1].wait()
        new = dot(k[at], v[at], 0, 0)
        total = new if total is None else total + new
    store_blocks(total, state)


def store_blocks(full, state):
    state[:HEAD_DIM] = full[:HEAD_DIM, :HEAD_DIM]
    state[HEAD_DIM:] = full[HEAD_DIM:, HEAD_DIM:]


def intra_kernel(q, k, v, intra):
    rows = q.shape[0]
    keep = causal(CHUNK)
    for h in range(q.shape[1] // HEAD_DIM):
        cols = slice(h * HEAD_DIM, (h + 1) * HEAD_DIM)
        state = None
        for start in range(0, rows, CHUNK):
            at = slice(start, start + CHUNK)
            qi, ki, vi = q[at, cols], k[at, cols], v[at, cols]
            scores = jnp.where(keep, dot(qi, ki, 1, 1), 0.0).astype(BF16)
            out = dot(scores, vi, 1, 0)
            if state is not None:
                out = out + dot(qi, state.astype(BF16), 1, 0)
            intra[at, cols] = out
            if start + CHUNK < rows:
                new = dot(ki, vi, 0, 0)
                state = new if state is None else state + new


def row_sums(tile):
    return jnp.sum(tile.T, axis=0, keepdims=True)


def mixed_kernel(is_own, intra, q, g, state0, state1, *refs):
    (mixed, stats, prefix), before = refs[-3:], refs[:-3]
    blocks = q.shape[0] // HEAD_DIM
    for j, state in enumerate((state0, state1)):
        prefix[j * HEAD_DIM : (j + 1) * HEAD_DIM] = state[...].astype(BF16)
    for start in range(0, q.shape[0], CHUNK):
        at = slice(start, start + CHUNK)
        square = cross = None
        for j in range(2):
            cols, part = columns(is_own, j), slice(j * HEAD_DIM, (j + 1) * HEAD_DIM)
            m = intra[at, cols] + dot(q[at, cols], prefix[part], 1, 0)
            mixed[at, part] = m
            s, c = m * m, m * g[at, cols].astype(F32)
            square = s if square is None else square + s
            cross = c if cross is None else cross + c
        for n in range(CHUNK // HEAD_DIM):
            part = slice(n * HEAD_DIM, (n + 1) * HEAD_DIM)
            for first, value in ((0, square), (blocks, cross)):
                i = first + start // HEAD_DIM + n
                sums = row_sums(value[part])
                stats[i : i + 1] = sums + before[0][i : i + 1] if before else sums


def half_norm(is_own, inverse, scale, mixed, q, g, gm, state):
    shape = (HEAD_DIM, HEAD_DIM)
    for i in range(q.shape[0] // HEAD_DIM):
        at = slice(i * HEAD_DIM, (i + 1) * HEAD_DIM)
        a = jnp.broadcast_to(inverse[i : i + 1], shape).T
        b = jnp.broadcast_to(scale[i : i + 1], shape).T
        for j in range(2):
            part = slice(j * HEAD_DIM, (j + 1) * HEAD_DIM)
            value = g[at, columns(is_own, j)].astype(F32) * a - mixed[at, part] * b
            gm[at, part] = value.astype(BF16)
    store_blocks(dot(q[:, columns(is_own, count=2)], gm[...], 0, 0), state)


def first_norm_kernel(width, mixed, q, g, *refs):
    stats, (gm, state, inverse_out, scale_out) = refs[:-4], refs[-4:]
    total = stats[0][...]
    for r in stats[1:]:
        total = total + r[...]
    blocks = q.shape[0] // HEAD_DIM
    inverse = lax.rsqrt(total[:blocks] / width + EPSILON)
    cross_mean = total[blocks:] * inverse / width
    scale = inverse * inverse * cross_mean
    inverse_out[...] = inverse
    scale_out[...] = scale
    half_norm(False, inverse, scale, mixed, q, g, gm, state)


def second_norm_kernel(mixed, q, g, inverse, scale, gm, state):
    half_norm(True, inverse[...], scale[...], mixed, q, g, gm, state)


def head_grads(cols, part, q, k, v, gm, prefix, gq, gk, gv):
    keep = causal(CHUNK)
    starts = list(range(0, q.shape[0], CHUNK))
    sums = prefix[part].astype(F32)
    states = [prefix[part]]
    for start in starts[:-1]:
        at = slice(start, start + CHUNK)
        sums = sums + dot(k[at, cols], v[at, cols], 0, 0)
        states.append(sums.astype(BF16))
    after = None
    for n, start in reversed(list(enumerate(starts))):
        at = slice(start, start + CHUNK)
        qi, ki, vi, gi = q[at, cols], k[at, cols], v[at, cols], gm[at, part]
        scores = jnp.where(keep, dot(qi, ki, 1, 1), 0.0).astype(BF16)
        grad_scores = jnp.where(keep, dot(gi, vi, 1, 1), 0.0).astype(BF16)
        gq_i = dot(grad_scores, ki, 1, 0) + dot(gi, states[n], 1, 1)
        gk_i = dot(grad_scores, qi, 0, 0)
        gv_i = dot(scores, gi, 0, 0)
        if after is not None:
            later = after.astype(BF16)
            gk_i = gk_i + dot(vi, later, 1, 1)
            gv_i = gv_i + dot(ki, later, 1, 0)
        gq[at] = gq_i.astype(BF16)
        gk[at] = gk_i
        gv[at] = gv_i
        if n:
            new = dot(qi, gi, 0, 0)
            after = new if after is None else after + new


def first_grads_kernel(q, k, v, gm, prefix, oth_gm, oth_prefix, mixed, oth_mixed, inverse, *refs):
    gqs, gks, gvs, out = refs[:3], refs[3:6], refs[6:9], refs[9]
    for n, (is_own, j) in enumerate(((True, 0), (True, 1), (False, 0))):
        part = slice(j * HEAD_DIM, (j + 1) * HEAD_DIM)
        halves = (gm, prefix) if is_own else (oth_gm, oth_prefix)
        head_grads(columns(is_own, j), part, q, k, v, *halves, gqs[n], gks[n], gvs[n])
    shape = (HEAD_DIM, HEAD_DIM)
    for i in range(q.shape[0] // HEAD_DIM):
        at = slice(i * HEAD_DIM, (i + 1) * HEAD_DIM)
        a = jnp.broadcast_to(inverse[i : i + 1], shape).T
        for is_own, value in ((True, mixed), (False, oth_mixed)):
            for j in range(2):
                part = slice(j * HEAD_DIM, (j + 1) * HEAD_DIM)
                out[at, columns(is_own, j)] = (value[at, part] * a).astype(BF16)


def second_grads_kernel(q, k, v, oth_gm, oth_prefix, gq0, gq1, gq2, token, gq, gk, gv):
    gq[:, columns(True, 0)] = gq0[...]
    gq[:, columns(True, 1)] = gq1[...]
    gq[:, columns(False, 0)] = gq2[...]
    cols, part = columns(False, 1), slice(HEAD_DIM, PAIR)
    head_grads(cols, part, q, k, v, oth_gm, oth_prefix, gq.at[:, cols], gk, gv)


def last_kernel(heads, k, v, *refs):
    count = len(heads)
    gk_parts, gv_parts, states = (refs[i * count : (i + 1) * count] for i in range(3))
    gk_hbm, gv_hbm, gk, gv, sems = refs[-5:]
    rounded = [state[...].astype(BF16) for state in states]
    copies = []
    for n, start in enumerate(range(0, k.shape[0], CHUNK)):
        at = slice(start, start + CHUNK)
        for i, head in enumerate(heads):
            cols, part = columns(*head), slice(i * HEAD_DIM, (i + 1) * HEAD_DIM)
            gk[at, part] = (gk_parts[i][at] + dot(v[at, cols], rounded[i], 1, 1)).astype(BF16)
            gv[at, part] = (gv_parts[i][at] + dot(k[at, cols], rounded[i], 1, 0)).astype(BF16)
        cols = columns(*heads[0], count=count)
        for j, (src, dst) in enumerate(((gk, gk_hbm), (gv, gv_hbm))):
            copies.append(pltpu.make_async_copy(src.at[at], dst.at[at, cols], sems.at[j, n]))
            copies[-1].start()
    for copy in copies:
        copy.wait()


def all_parts(value, axis, size):
    power = size & (size - 1) == 0
    parts = [value]
    for by in reversed(range(1, size)):
        pairs = [(i, i ^ by if power else (i + by) % size) for i in range(size)]
        parts.append(lax.ppermute(value, axis, pairs))
    return parts


def shards(sizes, queries, keys, values, grad_out):
    seq, head_size = sizes
    rows, cols = queries.shape
    chunks = rows // CHUNK
    blocks = rows // HEAD_DIM
    width = cols * head_size

    def shape(count, lanes, kind):
        return jax.ShapeDtypeStruct((count, lanes), kind)

    half = shape(PAIR, HEAD_DIM, F32)
    narrow = shape(rows, cols, BF16)
    half_wide, half_narrow = shape(rows, PAIR, F32), shape(rows, PAIR, BF16)
    head_wide, head_narrow = shape(rows, HEAD_DIM, F32), shape(rows, HEAD_DIM, BF16)
    head_flops = 2 * rows * HEAD_DIM * HEAD_DIM
    chunk_flops = 2 * rows * CHUNK * HEAD_DIM

    def slots(count):
        return [pltpu.VMEM((rows, count * HEAD_DIM), BF16)] * 2 + [
            pltpu.SemaphoreType.DMA((2, chunks))
        ]

    def state_of(is_own, *token):
        return call(
            functools.partial(state_kernel, is_own),
            [half],
            [keys, values, *token],
            2 * head_flops,
            "local_state",
            spaces={0: pl.ANY, 1: pl.ANY, 2: pl.ANY},
            scratch=slots(2),
            limit=63,
        )[0]

    oth_state = state_of(False)
    own_state = state_of(True, oth_state)

    def forward(token):
        if token is not None:
            return []
        return call(
            intra_kernel,
            [shape(rows, cols, F32)],
            [queries, keys, values],
            8 * (chunk_flops + head_flops),
            "intra",
        )

    (mine0, mine1, theirs0, theirs1), (intra,) = scan(own_state, oth_state, seq, False, forward)

    def mix(is_own, *args):
        return call(
            functools.partial(mixed_kernel, is_own),
            [half_wide, shape(2 * blocks, HEAD_DIM, F32), shape(PAIR, HEAD_DIM, BF16)],
            [intra, queries, grad_out, *args],
            2 * head_flops,
            "mixed",
        )

    mixed, stats, prefix = mix(True, mine0, mine1)
    oth_mixed, stats, oth_prefix = mix(False, theirs0, theirs1, stats)
    oth_gm, oth_state, inverse, scale = call(
        functools.partial(first_norm_kernel, width),
        [half_narrow, half, shape(blocks, HEAD_DIM, F32), shape(blocks, HEAD_DIM, F32)],
        [oth_mixed, queries, grad_out, *all_parts(stats, "head", head_size)],
        2 * head_flops,
        "first_norm",
    )
    gm, own_state = call(
        second_norm_kernel,
        [half_narrow, half],
        [mixed, queries, grad_out, inverse, scale],
        2 * head_flops,
        "second_norm",
    )
    grads_flops = 5 * chunk_flops + 6 * head_flops
    first = []

    def backward(token):
        if token is None:
            first.extend(
                call(
                    first_grads_kernel,
                    [head_narrow] * 3 + [head_wide] * 6 + [narrow],
                    [queries, keys, values, gm, prefix, oth_gm, oth_prefix]
                    + [mixed, oth_mixed, inverse],
                    3 * grads_flops,
                    "first_grads",
                )
            )
            return first[3:]
        return call(
            second_grads_kernel,
            [narrow, head_wide, head_wide],
            [queries, keys, values, oth_gm, oth_prefix, *first[:3], token],
            grads_flops,
            "second_grads",
            spaces={8: pl.ANY},
        )

    (mine0, mine1, theirs0, theirs1), done = scan(own_state, oth_state, seq, True, backward)
    gk_parts, gv_parts, (output, grad_q) = done[:3], done[3:6], done[6:8]
    gk_parts, gv_parts = gk_parts + done[8:9], gv_parts + done[9:]

    def last(heads, states, *before):
        picked = [(0 if is_own else 2) + j for is_own, j in heads]
        args = [keys, values]
        args += [gk_parts[i] for i in picked] + [gv_parts[i] for i in picked] + states
        return call(
            functools.partial(last_kernel, heads),
            [narrow, narrow],
            args + list(before),
            2 * len(heads) * head_flops,
            "last",
            spaces={len(args) + i: pl.ANY for i in range(len(before))},
            outs={0: pl.ANY, 1: pl.ANY},
            scratch=slots(len(heads)),
            aliases={len(args) + i: i for i in range(len(before))},
        )

    grads = last(((True, 0), (True, 1)), [mine0, mine1])
    grads = last(((False, 1),), [theirs1], *grads)
    grad_k, grad_v = last(((False, 0),), [theirs0], *grads)
    return output, grad_q, grad_k, grad_v


def solution(mesh):
    sizes = (mesh.shape["seq"], mesh.shape["head"])
    spec = P("seq", "head")
    return jax.shard_map(
        functools.partial(shards, sizes),
        mesh=mesh,
        in_specs=(spec,) * 4,
        out_specs=(spec,) * 4,
        check_vma=False,
    )
```

time: 59 us -> 58.3 us (0.988)
  waiting for transfers between devices: 23.2 us -> 7.77 us
  starting transfers between devices: 17.6 us -> 24.9 us
  Pallas kernels: 16 us -> 20.8 us
  local copies, waits for them, and re-layouts: 1.25 us -> 3.71 us
    ppermute x14, waiting for transfers between devices: 21.3 us -> 5.92 us  [exchange(): return lax.ppermute(value, 'seq', [(i, i ^ by) for i in range(size)])]
    ppermute x14, starting transfers between devices: 15.7 us -> 23 us  [exchange(): return lax.ppermute(value, 'seq', [(i, i ^ by) for i in range(size)])]
    pallas_call x13 -> x18, Pallas kernels: 16 us -> 20.8 us  [call(): return list(kernel(*args))]
    unnamed x12 -> x18, local copies, waits for them, and re-layouts: 1.25 us -> 3.71 us
  transfers between devices with their start and end apart: 17 -> 17, of which waited for: 14 -> 9; matrix products, arithmetic and copies ran while one was open for 0% -> 0% of each run, Pallas kernels for 16% -> 27%
where the time goes in v4:
time: 58.3 us; the launch traced here: 58.1 us
  starting transfers between devices  24.9 us (43%)
  Pallas kernels  20.8 us (36%)
  waiting for transfers between devices  7.77 us (13%)
  local copies, waits for them, and re-layouts  3.71 us (6%)
  between operations  0.84 us (1%)
    ppermute x14, starting transfers between devices, exchange(): return lax.ppermute(value, 'seq', [(i, i ^ by) for i in range(size)])  23 us
    pallas_call x18, Pallas kernels, call(): return list(kernel(*args))  20.8 us
    ppermute x14, waiting for transfers between devices, exchange(): return lax.ppermute(value, 'seq', [(i, i ^ by) for i in range(size)])  5.92 us
    unnamed x18, local copies, waits for them, and re-layouts  3.71 us
    ppermute x3, starting transfers between devices, all_parts(): parts.append(lax.ppermute(value, axis, pairs))  1.94 us
    ppermute x3, waiting for transfers between devices, all_parts(): parts.append(lax.ppermute(value, axis, pairs))  1.84 us
  transfers between devices with their start and end apart: 17, of which 9 were waited for; matrix products, arithmetic and copies ran while one was open for 0% of the time, Pallas kernels for 27%

profile of v4, /device:TPU:0, one launch (start us, length us, event | category | flops | bytes accessed | tf_op | source)
XLA Modules:
  0.0 58.1 jit_solution(14211113956414884079)
XLA Ops:
  0.6 2.5 %local_state.2.refs_0_ = f32[256,128]{1,0:T(8,128)} custom-call(bf16[1024,512]{1,0:T(8,128)(2,1)} %k.11, bf16[1024,512]{1,0:T(8,128)(2,1)} %v.11), custom_call_target="tpu_custom_call" | custom-call | flops 67108864 | bytes 2228224 | tf_op jit(solution)/shard_map/local_state/pallas_call | solution.py:56
  3.1 0.0 copy-start.8
  3.1 4.0 %collective-permute-start = (f32[256,128]{1,0:T(8,128)}, f32[256,128]{1,0:T(8,128)S(1)}, u32[]{:S(2)}, u32[]{:S(2)}) collective-permute-start(f32[256,128]{1,0:T(8,128)} %local_state.2.refs_0_), channel_id=1, source_target_pairs={{0,12},{4,8},{8,4},{12,0},{16,28},{20,24},{24,20},{28,16},{1,13},{... | collective-permute-start | bytes 393224 | tf_op jit(solution)/shard_map/ppermute | solution.py:60
  7.2 2.5 %local_state.3.own = f32[256,128]{1,0:T(8,128)} custom-call(bf16[1024,512]{1,0:T(8,128)(2,1)} %k.11, bf16[1024,512]{1,0:T(8,128)(2,1)} %v.11, f32[256,128]{1,0:T(8,128)} %local_state.2.refs_0_), custom_call_target="tpu_custom_call" | custom-call | flops 67108864 | bytes 2359296 | tf_op jit(solution)/shard_map/local_state/pallas_call | solution.py:56
  9.7 0.5 collective-permute-start.1
  10.2 0.0 copy-done.8
  10.2 0.2 collective-permute-start.2
  10.3 0.0 copy-start
  10.4 1.2 %copy-done = bf16[1024,512]{1,0:T(8,128)(2,1)S(1)} copy-done((bf16[1024,512]{1,0:T(8,128)(2,1)S(1)}, bf16[1024,512]{1,0:T(8,128)(2,1)}, u32[]{:S(2)}) %copy-start) | copy-done | bytes 1048600
  11.6 0.0 copy-start.2
  11.6 1.2 %copy-done.2 = bf16[1024,512]{1,0:T(8,128)(2,1)S(1)} copy-done((bf16[1024,512]{1,0:T(8,128)(2,1)S(1)}, bf16[1024,512]{1,0:T(8,128)(2,1)}, u32[]{:S(2)}) %copy-start.2) | copy-done | bytes 1048600
  12.8 0.0 copy-start.4
  12.8 1.2 %copy-done.4 = bf16[1024,512]{1,0:T(8,128)(2,1)S(1)} copy-done((bf16[1024,512]{1,0:T(8,128)(2,1)S(1)}, bf16[1024,512]{1,0:T(8,128)(2,1)}, u32[]{:S(2)}) %copy-start.4) | copy-done | bytes 1048600
  14.0 0.0 copy-start.7
  14.0 1.9 %intra.1.refs_0_ = f32[1024,512]{1,0:T(8,128)S(1)} custom-call(bf16[1024,512]{1,0:T(8,128)(2,1)S(1)} %copy-done.4, bf16[1024,512]{1,0:T(8,128)(2,1)S(1)} %copy-done, bf16[1024,512]{1,0:T(8,128)(2,1)S(1)} %copy-done.2), custom_call_target="tpu_custom_call" | custom-call | flops 805306368 | bytes 5242880 | tf_op jit(solution)/shard_map/intra/pallas_call | solution.py:56
  15.9 0.0 copy-start.5
  15.9 0.0 copy-start.6
  16.0 0.0 collective-permute-done.near3
  16.0 0.0 collective-permute-done.1.near2
  16.0 0.0 collective-permute-done.2.near1
  16.0 0.0 copy-done.7
  16.0 3.0 %collective-permute-start.3 = (f32[128,128]{1,0:T(8,128)S(1)}, f32[128,128]{1,0:T(8,128)S(1)}, u32[]{:S(2)}, u32[]{:S(2)}) collective-permute-start(f32[128,128]{1,0:T(8,128)S(1)} %get-tuple-element.47), channel_id=1, source_target_pairs={{0,16},{4,20},{8,24},{12,28},{16,0},{20,4},{24,8},{28,12},{1,17},{... | collective-permute-start | bytes 196616 | tf_op jit(solution)/shard_map/ppermute | solution.py:60
  19.1 0.1 collective-permute-start.4
  19.1 2.4 %collective-permute-done.3.far = f32[128,128]{1,0:T(8,128)S(1)} collective-permute-done((f32[128,128]{1,0:T(8,128)S(1)}, f32[128,128]{1,0:T(8,128)S(1)}, u32[]{:S(2)}, u32[]{:S(2)}) %collective-permute-start.3) | collective-permute-done | bytes 65568 | tf_op jit(solution)/shard_map/ppermute | solution.py:60
  21.6 2.0 %collective-permute-start.5 = (f32[128,128]{1,0:T(8,128)S(1)}, f32[128,128]{1,0:T(8,128)S(1)}, u32[]{:S(2)}, u32[]{:S(2)}) collective-permute-start(f32[128,128]{1,0:T(8,128)S(1)} %get-tuple-element.52), channel_id=1, source_target_pairs={{0,4},{4,0},{8,12},{12,8},{16,20},{20,16},{24,28},{28,24},{1,5},{5... | collective-permute-start | bytes 196616 | tf_op jit(solution)/shard_map/ppermute | solution.py:60
  23.6 0.6 %collective-permute-done.4.far = f32[128,128]{1,0:T(8,128)S(1)} collective-permute-done((f32[128,128]{1,0:T(8,128)S(1)}, f32[128,128]{1,0:T(8,128)S(1)}, u32[]{:S(2)}, u32[]{:S(2)}) %collective-permute-start.4) | collective-permute-done | bytes 65568 | tf_op jit(solution)/shard_map/ppermute | solution.py:60
  24.3 1.8 %collective-permute-start.6 = (f32[128,128]{1,0:T(8,128)S(1)}, f32[128,128]{1,0:T(8,128)S(1)}, u32[]{:S(2)}, u32[]{:S(2)}) collective-permute-start(f32[128,128]{1,0:T(8,128)S(1)} %get-tuple-element.53), channel_id=1, source_target_pairs={{0,4},{4,0},{8,12},{12,8},{16,20},{20,16},{24,28},{28,24},{1,5},{5... | collective-permute-start | bytes 196616 | tf_op jit(solution)/shard_map/ppermute | solution.py:60
  26.0 0.0 copy-done.5
  26.0 0.0 copy-done.6
  26.0 0.5 mixed.2
  26.6 0.0 collective-permute-done.5.state0
  26.6 2.0 %collective-permute-done.6.state1 = f32[128,128]{1,0:T(8,128)S(1)} collective-permute-done((f32[128,128]{1,0:T(8,128)S(1)}, f32[128,128]{1,0:T(8,128)S(1)}, u32[]{:S(2)}, u32[]{:S(2)}) %collective-permute-start.6) | collective-permute-done | bytes 65568 | tf_op jit(solution)/shard_map/ppermute | solution.py:60
  28.6 0.6 mixed.3
  29.1 0.1 collective-permute-start.7
  29.2 1.8 %collective-permute-start.8 = (f32[16,128]{1,0:T(8,128)S(1)}, f32[16,128]{1,0:T(8,128)S(1)}, u32[]{:S(2)}, u32[]{:S(2)}) collective-permute-start(f32[16,128]{1,0:T(8,128)S(1)} %get-tuple-element.56.refs_0_), channel_id=1, source_target_pairs={{0,2},{1,3},{2,0},{3,1},{4,6},{5,7},{6,4},{7,5},{8,10},{9,11},{10,... | collective-permute-start | bytes 24584 | tf_op jit(solution)/shard_map/ppermute | solution.py:323
  31.0 0.1 collective-permute-start.9
  31.1 1.2 %collective-permute-done.7.refs_1_ = f32[16,128]{1,0:T(8,128)S(1)} collective-permute-done((f32[16,128]{1,0:T(8,128)S(1)}, f32[16,128]{1,0:T(8,128)S(1)}, u32[]{:S(2)}, u32[]{:S(2)}) %collective-permute-start.7) | collective-permute-done | bytes 8224 | tf_op jit(solution)/shard_map/ppermute | solution.py:323
  32.3 0.7 %collective-permute-done.8.refs_2_ = f32[16,128]{1,0:T(8,128)S(1)} collective-permute-done((f32[16,128]{1,0:T(8,128)S(1)}, f32[16,128]{1,0:T(8,128)S(1)}, u32[]{:S(2)}, u32[]{:S(2)}) %collective-permute-start.8) | collective-permute-done | bytes 8224 | tf_op jit(solution)/shard_map/ppermute | solution.py:323
  32.9 0.0 collective-permute-done.9.refs_3_
  32.9 0.8 %first_norm.1 = (bf16[1024,256]{1,0:T(8,128)(2,1)S(1)}, f32[256,128]{1,0:T(8,128)S(1)}, f32[8,128]{1,0:T(8,128)S(1)}, f32[8,128]{1,0:T(8,128)S(1)}) custom-call(f32[1024,256]{1,0:T(8,128)S(1)} %get-tuple-element.55.mixed.oth_mixed, bf16[1024,512]{1,0:T(8,128)(2,1)S(1)} %copy-done.5, bf16[1024,512]{1,0:T(8,128)(2,1)S(1)} %copy-done.6, ...), custom_call_target="tpu_custom_call" | custom-call | flops 67108864 | bytes 3842048 | tf_op jit(solution)/shard_map/first_norm/pallas_call | solution.py:56
  33.8 0.0 copy-start.1
  33.8 0.0 copy-start.3
  33.8 2.6 %collective-permute-start.10 = (f32[256,128]{1,0:T(8,128)S(1)}, f32[256,128]{1,0:T(8,128)S(1)}, u32[]{:S(2)}, u32[]{:S(2)}) collective-permute-start(f32[256,128]{1,0:T(8,128)S(1)} %get-tuple-element.68), channel_id=1, source_target_pairs={{0,12},{4,8},{8,4},{12,0},{16,28},{20,24},{24,20},{28,16},{1,13},{... | collective-permute-start | bytes 393224 | tf_op jit(solution)/shard_map/ppermute | solution.py:60
  36.3 0.9 %collective-permute-start.12 = (f32[256,128]{1,0:T(8,128)S(1)}, f32[256,128]{1,0:T(8,128)S(1)}, u32[]{:S(2)}, u32[]{:S(2)}) collective-permute-start(f32[256,128]{1,0:T(8,128)S(1)} %get-tuple-element.68), channel_id=1, source_target_pairs={{0,4},{4,0},{8,12},{12,8},{16,20},{20,16},{24,28},{28,24},{1,5},{5... | collective-permute-start | bytes 393224 | tf_op jit(solution)/shard_map/ppermute | solution.py:60
  37.3 0.8 %second_norm.1 = (bf16[1024,256]{1,0:T(8,128)(2,1)S(1)}, f32[256,128]{1,0:T(8,128)S(1)}) custom-call(f32[1024,256]{1,0:T(8,128)S(1)} %get-tuple-element.51.mixed, bf16[1024,512]{1,0:T(8,128)(2,1)S(1)} %copy-done.5, bf16[1024,512]{1,0:T(8,128)(2,1)S(1)} %copy-done.6, f32[8,128]{1,0:T(8,128)S(1)} %get-tuple-element.57.inverse, ...), custom_call_target="tpu_custom_call" | custom-call | flops 67108864 | bytes 3809280 | tf_op jit(solution)/shard_map/second_norm/pallas_call | solution.py:56
  38.0 0.1 collective-permute-start.11
  38.2 0.0 copy-done.1
  38.2 0.0 copy-done.3
  38.2 5.3 %first_grads.1 = (bf16[1024,128]{1,0:T(8,128)(2,1)S(1)}, bf16[1024,128]{1,0:T(8,128)(2,1)S(1)}, bf16[1024,128]{1,0:T(8,128)(2,1)S(1)}, f32[1024,128]{1,0:T(8,128...) custom-call(bf16[1024,512]{1,0:T(8,128)(2,1)S(1)} %copy-done.5, ...), custom_call_target="tpu_custom_call" | custom-call | flops 1610612736 | bytes 11407360 | tf_op jit(solution)/shard_map/first_grads/pallas_call | solution.py:56
  43.5 0.0 collective-permute-done.10.near3
  43.5 0.2 collective-permute-done.11.near2
  43.7 0.0 collective-permute-done.12.near1
  43.7 3.2 %collective-permute-start.15 = (f32[128,128]{1,0:T(8,128)S(1)}, f32[128,128]{1,0:T(8,128)S(1)}, u32[]{:S(2)}, u32[]{:S(2)}) collective-permute-start(f32[128,128]{1,0:T(8,128)S(1)} %get-tuple-element.70.token), channel_id=1, source_target_pairs={{0,16},{4,20},{8,24},{12,28},{16,0},{20,4},{24,8},{28,12},{1,17},{... | collective-permute-start | bytes 196616 | tf_op jit(solution)/shard_map/ppermute | solution.py:60
  46.9 0.1 collective-permute-start.13
  47.0 2.5 %second_grads.1 = (bf16[1024,512]{1,0:T(8,128)(2,1)}, f32[1024,128]{1,0:T(8,128)S(1)}, f32[1024,128]{1,0:T(8,128)S(1)}) custom-call(bf16[1024,512]{1,0:T(8,128)(2,1)S(1)} %copy-done.5, bf16[1024,512]{1,0:T(8,128)(2,1)S(1)} %copy-done.1, bf16[1024,512]{1,0:T(8,128)(2,1)S(1)} %copy-done.3, bf16[1024,256]{1,0:T(8,128)(2,1)S(1)} %get-tuple-element.61.oth_gm, ...), custom_call_target="tpu_custom_call" | custom-call | flops 536870912 | bytes 6684672 | tf_op jit(solution)/shard_map/second_grads/pallas_call | solution.py:56
  49.5 0.4 collective-permute-done.15.far
  49.9 2.7 %collective-permute-start.16 = (f32[128,128]{1,0:T(8,128)S(1)}, f32[128,128]{1,0:T(8,128)S(1)}, u32[]{:S(2)}, u32[]{:S(2)}) collective-permute-start(f32[128,128]{1,0:T(8,128)S(1)} %get-tuple-element.78), channel_id=1, source_target_pairs={{0,4},{4,0},{8,12},{12,8},{16,20},{20,16},{24,28},{28,24},{1,5},{5... | collective-permute-start | bytes 196616 | tf_op jit(solution)/shard_map/ppermute | solution.py:60
  52.6 0.1 collective-permute-done.13.far
  52.7 1.7 %collective-permute-start.14 = (f32[128,128]{1,0:T(8,128)S(1)}, f32[128,128]{1,0:T(8,128)S(1)}, u32[]{:S(2)}, u32[]{:S(2)}) collective-permute-start(f32[128,128]{1,0:T(8,128)S(1)} %get-tuple-element.76), channel_id=1, source_target_pairs={{0,4},{4,0},{8,12},{12,8},{16,20},{20,16},{24,28},{28,24},{1,5},{5... | collective-permute-start | bytes 196616 | tf_op jit(solution)/shard_map/ppermute | solution.py:60
  54.4 1.2 %last.3 = (bf16[1024,512]{1,0:T(8,128)(2,1)}, bf16[1024,512]{1,0:T(8,128)(2,1)}) custom-call(bf16[1024,512]{1,0:T(8,128)(2,1)S(1)} %copy-done.1, bf16[1024,512]{1,0:T(8,128)(2,1)S(1)} %copy-done.3, f32[1024,128]{1,0:T(8,128)S(1)} %get-tuple-element.69.refs_0_, f32[1024,128]{1,0:T(8,128)S(1)} %get-tuple-element.79.refs_1_, ...), custom_call_target="tpu_custom_call" | custom-call | flops 134217728 | bytes 6422528 | tf_op jit(solution)/shard_map/last/pallas_call | solution.py:56
  55.7 0.0 collective-permute-done.16.refs_2_
  55.7 1.0 %last.4 = (bf16[1024,512]{1,0:T(8,128)(2,1)}, bf16[1024,512]{1,0:T(8,128)(2,1)}) custom-call(bf16[1024,512]{1,0:T(8,128)(2,1)S(1)} %copy-done.1, bf16[1024,512]{1,0:T(8,128)(2,1)S(1)} %copy-done.3, f32[1024,128]{1,0:T(8,128)S(1)} %get-tuple-element.77.refs_0_, ...), custom_call_target="tpu_custom_call", output_to_operand_aliasing={{0}: (5, {}), {1}: (6, {})} | custom-call | flops 67108864 | bytes 7405568 | tf_op jit(solution)/shard_map/last/pallas_call | solution.py:56
  56.7 0.3 collective-permute-done.14.refs_2_
  57.0 1.0 %last.5 = (bf16[1024,512]{1,0:T(8,128)(2,1)}, bf16[1024,512]{1,0:T(8,128)(2,1)}) custom-call(bf16[1024,512]{1,0:T(8,128)(2,1)S(1)} %copy-done.1, bf16[1024,512]{1,0:T(8,128)(2,1)S(1)} %copy-done.3, f32[1024,128]{1,0:T(8,128)S(1)} %get-tuple-element.72.refs_0_, ...), custom_call_target="tpu_custom_call", output_to_operand_aliasing={{0}: (5, {}), {1}: (6, {})} | custom-call | flops 67108864 | bytes 7405568 | tf_op jit(solution)/shard_map/last/pallas_call | solution.py:56
  (6 shorter events, 0.2 us)
Async XLA Ops:
  3.1 7.0 %copy-start.8 = (f32[256,128]{1,0:T(8,128)S(1)}, f32[256,128]{1,0:T(8,128)}, u32[]{:S(2)}) copy-start(f32[256,128]{1,0:T(8,128)} %local_state.2.refs_0_) | copy-start | bytes 393220
  3.1 12.8 %collective-permute-start = (f32[256,128]{1,0:T(8,128)}, f32[256,128]{1,0:T(8,128)S(1)}, u32[]{:S(2)}, u32[]{:S(2)}) collective-permute-start(f32[256,128]{1,0:T(8,128)} %local_state.2.refs_0_), channel_id=1, source_target_pairs={{0,12},{4,8},{8,4},{12,0},{16,28},{20,24},{24,20},{28,16},{1,13},{... | collective-permute-start | bytes 393224 | tf_op jit(solution)/shard_map/ppermute | solution.py:60
  9.7 6.3 %collective-permute-start.1 = (f32[256,128]{1,0:T(8,128)}, f32[256,128]{1,0:T(8,128)S(1)}, u32[]{:S(2)}, u32[]{:S(2)}) collective-permute-start(f32[256,128]{1,0:T(8,128)} %local_state.3.own), channel_id=1, source_target_pairs={{0,8},{4,12},{8,0},{12,4},{16,24},{20,28},{24,16},{28,20},{1,9},{5... | collective-permute-start | bytes 393224 | tf_op jit(solution)/shard_map/ppermute | solution.py:60
  10.2 5.8 %collective-permute-start.2 = (f32[256,128]{1,0:T(8,128)S(1)}, f32[256,128]{1,0:T(8,128)S(1)}, u32[]{:S(2)}, u32[]{:S(2)}) collective-permute-start(f32[256,128]{1,0:T(8,128)S(1)} %copy-done.8), channel_id=1, source_target_pairs={{0,4},{4,0},{8,12},{12,8},{16,20},{20,16},{24,28},{28,24},{1,5},{5... | collective-permute-start | bytes 393224 | tf_op jit(solution)/shard_map/ppermute | solution.py:60
  10.3 1.2 %copy-start = (bf16[1024,512]{1,0:T(8,128)(2,1)S(1)}, bf16[1024,512]{1,0:T(8,128)(2,1)}, u32[]{:S(2)}) copy-start(bf16[1024,512]{1,0:T(8,128)(2,1)} %k.11) | copy-start | bytes 3145732
  11.6 1.2 %copy-start.2 = (bf16[1024,512]{1,0:T(8,128)(2,1)S(1)}, bf16[1024,512]{1,0:T(8,128)(2,1)}, u32[]{:S(2)}) copy-start(bf16[1024,512]{1,0:T(8,128)(2,1)} %v.11) | copy-start | bytes 3145732
  12.8 1.2 %copy-start.4 = (bf16[1024,512]{1,0:T(8,128)(2,1)S(1)}, bf16[1024,512]{1,0:T(8,128)(2,1)}, u32[]{:S(2)}) copy-start(bf16[1024,512]{1,0:T(8,128)(2,1)} %q.13) | copy-start | bytes 3145732
  14.0 2.0 %copy-start.7 = (f32[256,128]{1,0:T(8,128)S(1)}, f32[256,128]{1,0:T(8,128)}, u32[]{:S(2)}) copy-start(f32[256,128]{1,0:T(8,128)} %local_state.3.own) | copy-start | bytes 393220
  15.9 10.1 %copy-start.5 = (bf16[1024,512]{1,0:T(8,128)(2,1)S(1)}, bf16[1024,512]{1,0:T(8,128)(2,1)}, u32[]{:S(2)}) copy-start(bf16[1024,512]{1,0:T(8,128)(2,1)} %q.13) | copy-start | bytes 3145732
  15.9 10.1 %copy-start.6 = (bf16[1024,512]{1,0:T(8,128)(2,1)S(1)}, bf16[1024,512]{1,0:T(8,128)(2,1)}, u32[]{:S(2)}) copy-start(bf16[1024,512]{1,0:T(8,128)(2,1)} %g.7) | copy-start | bytes 3145732
  16.0 5.5 %collective-permute-start.3 = (f32[128,128]{1,0:T(8,128)S(1)}, f32[128,128]{1,0:T(8,128)S(1)}, u32[]{:S(2)}, u32[]{:S(2)}) collective-permute-start(f32[128,128]{1,0:T(8,128)S(1)} %get-tuple-element.47), channel_id=1, source_target_pairs={{0,16},{4,20},{8,24},{12,28},{16,0},{20,4},{24,8},{28,12},{1,17},{... | collective-permute-start | bytes 196616 | tf_op jit(solution)/shard_map/ppermute | solution.py:60
  19.1 5.2 %collective-permute-start.4 = (f32[128,128]{1,0:T(8,128)S(1)}, f32[128,128]{1,0:T(8,128)S(1)}, u32[]{:S(2)}, u32[]{:S(2)}) collective-permute-start(f32[128,128]{1,0:T(8,128)S(1)} %get-tuple-element.49), channel_id=1, source_target_pairs={{0,16},{4,20},{8,24},{12,28},{16,0},{20,4},{24,8},{28,12},{1,17},{... | collective-permute-start | bytes 196616 | tf_op jit(solution)/shard_map/ppermute | solution.py:60
  21.6 5.0 %collective-permute-start.5 = (f32[128,128]{1,0:T(8,128)S(1)}, f32[128,128]{1,0:T(8,128)S(1)}, u32[]{:S(2)}, u32[]{:S(2)}) collective-permute-start(f32[128,128]{1,0:T(8,128)S(1)} %get-tuple-element.52), channel_id=1, source_target_pairs={{0,4},{4,0},{8,12},{12,8},{16,20},{20,16},{24,28},{28,24},{1,5},{5... | collective-permute-start | bytes 196616 | tf_op jit(solution)/shard_map/ppermute | solution.py:60
  24.3 4.3 %collective-permute-start.6 = (f32[128,128]{1,0:T(8,128)S(1)}, f32[128,128]{1,0:T(8,128)S(1)}, u32[]{:S(2)}, u32[]{:S(2)}) collective-permute-start(f32[128,128]{1,0:T(8,128)S(1)} %get-tuple-element.53), channel_id=1, source_target_pairs={{0,4},{4,0},{8,12},{12,8},{16,20},{20,16},{24,28},{28,24},{1,5},{5... | collective-permute-start | bytes 196616 | tf_op jit(solution)/shard_map/ppermute | solution.py:60
  29.1 3.1 %collective-permute-start.7 = (f32[16,128]{1,0:T(8,128)S(1)}, f32[16,128]{1,0:T(8,128)S(1)}, u32[]{:S(2)}, u32[]{:S(2)}) collective-permute-start(f32[16,128]{1,0:T(8,128)S(1)} %get-tuple-element.56.refs_0_), channel_id=1, source_target_pairs={{0,3},{1,2},{2,1},{3,0},{4,7},{5,6},{6,5},{7,4},{8,11},{9,10},{10,... | collective-permute-start | bytes 24584 | tf_op jit(solution)/shard_map/ppermute | solution.py:323
  29.2 3.7 %collective-permute-start.8 = (f32[16,128]{1,0:T(8,128)S(1)}, f32[16,128]{1,0:T(8,128)S(1)}, u32[]{:S(2)}, u32[]{:S(2)}) collective-permute-start(f32[16,128]{1,0:T(8,128)S(1)} %get-tuple-element.56.refs_0_), channel_id=1, source_target_pairs={{0,2},{1,3},{2,0},{3,1},{4,6},{5,7},{6,4},{7,5},{8,10},{9,11},{10,... | collective-permute-start | bytes 24584 | tf_op jit(solution)/shard_map/ppermute | solution.py:323
  31.0 1.9 %collective-permute-start.9 = (f32[16,128]{1,0:T(8,128)S(1)}, f32[16,128]{1,0:T(8,128)S(1)}, u32[]{:S(2)}, u32[]{:S(2)}) collective-permute-start(f32[16,128]{1,0:T(8,128)S(1)} %get-tuple-element.56.refs_0_), channel_id=1, source_target_pairs={{0,1},{1,0},{2,3},{3,2},{4,5},{5,4},{6,7},{7,6},{8,9},{9,8},{10,11... | collective-permute-start | bytes 24584 | tf_op jit(solution)/shard_map/ppermute | solution.py:323
  33.8 4.4 %copy-start.1 = (bf16[1024,512]{1,0:T(8,128)(2,1)S(1)}, bf16[1024,512]{1,0:T(8,128)(2,1)}, u32[]{:S(2)}) copy-start(bf16[1024,512]{1,0:T(8,128)(2,1)} %k.11) | copy-start | bytes 3145732
  33.8 4.4 %copy-start.3 = (bf16[1024,512]{1,0:T(8,128)(2,1)S(1)}, bf16[1024,512]{1,0:T(8,128)(2,1)}, u32[]{:S(2)}) copy-start(bf16[1024,512]{1,0:T(8,128)(2,1)} %v.11) | copy-start | bytes 3145732
  33.8 9.7 %collective-permute-start.10 = (f32[256,128]{1,0:T(8,128)S(1)}, f32[256,128]{1,0:T(8,128)S(1)}, u32[]{:S(2)}, u32[]{:S(2)}) collective-permute-start(f32[256,128]{1,0:T(8,128)S(1)} %get-tuple-element.68), channel_id=1, source_target_pairs={{0,12},{4,8},{8,4},{12,0},{16,28},{20,24},{24,20},{28,16},{1,13},{... | collective-permute-start | bytes 393224 | tf_op jit(solution)/shard_map/ppermute | solution.py:60
  36.3 7.3 %collective-permute-start.12 = (f32[256,128]{1,0:T(8,128)S(1)}, f32[256,128]{1,0:T(8,128)S(1)}, u32[]{:S(2)}, u32[]{:S(2)}) collective-permute-start(f32[256,128]{1,0:T(8,128)S(1)} %get-tuple-element.68), channel_id=1, source_target_pairs={{0,4},{4,0},{8,12},{12,8},{16,20},{20,16},{24,28},{28,24},{1,5},{5... | collective-permute-start | bytes 393224 | tf_op jit(solution)/shard_map/ppermute | solution.py:60
  38.0 5.6 %collective-permute-start.11 = (f32[256,128]{1,0:T(8,128)S(1)}, f32[256,128]{1,0:T(8,128)S(1)}, u32[]{:S(2)}, u32[]{:S(2)}) collective-permute-start(f32[256,128]{1,0:T(8,128)S(1)} %get-tuple-element.67.own), channel_id=1, source_target_pairs={{0,8},{4,12},{8,0},{12,4},{16,24},{20,28},{24,16},{28,20},{1,9},{5... | collective-permute-start | bytes 393224 | tf_op jit(solution)/shard_map/ppermute | solution.py:60
  43.7 6.1 %collective-permute-start.15 = (f32[128,128]{1,0:T(8,128)S(1)}, f32[128,128]{1,0:T(8,128)S(1)}, u32[]{:S(2)}, u32[]{:S(2)}) collective-permute-start(f32[128,128]{1,0:T(8,128)S(1)} %get-tuple-element.70.token), channel_id=1, source_target_pairs={{0,16},{4,20},{8,24},{12,28},{16,0},{20,4},{24,8},{28,12},{1,17},{... | collective-permute-start | bytes 196616 | tf_op jit(solution)/shard_map/ppermute | solution.py:60
  46.9 5.8 %collective-permute-start.13 = (f32[128,128]{1,0:T(8,128)S(1)}, f32[128,128]{1,0:T(8,128)S(1)}, u32[]{:S(2)}, u32[]{:S(2)}) collective-permute-start(f32[128,128]{1,0:T(8,128)S(1)} %get-tuple-element.74), channel_id=1, source_target_pairs={{0,16},{4,20},{8,24},{12,28},{16,0},{20,4},{24,8},{28,12},{1,17},{... | collective-permute-start | bytes 196616 | tf_op jit(solution)/shard_map/ppermute | solution.py:60
  49.9 5.8 %collective-permute-start.16 = (f32[128,128]{1,0:T(8,128)S(1)}, f32[128,128]{1,0:T(8,128)S(1)}, u32[]{:S(2)}, u32[]{:S(2)}) collective-permute-start(f32[128,128]{1,0:T(8,128)S(1)} %get-tuple-element.78), channel_id=1, source_target_pairs={{0,4},{4,0},{8,12},{12,8},{16,20},{20,16},{24,28},{28,24},{1,5},{5... | collective-permute-start | bytes 196616 | tf_op jit(solution)/shard_map/ppermute | solution.py:60
  52.7 4.3 %collective-permute-start.14 = (f32[128,128]{1,0:T(8,128)S(1)}, f32[128,128]{1,0:T(8,128)S(1)}, u32[]{:S(2)}, u32[]{:S(2)}) collective-permute-start(f32[128,128]{1,0:T(8,128)S(1)} %get-tuple-element.76), channel_id=1, source_target_pairs={{0,4},{4,0},{8,12},{12,8},{16,20},{20,16},{24,28},{28,24},{1,5},{5... | collective-permute-start | bytes 196616 | tf_op jit(solution)/shard_map/ppermute | solution.py:60

commit v5 on v4

--- a/solution.py
+++ b/solution.py
@@ -1,4 +1,5 @@
 import functools
+import math
 
 import jax
 import jax.numpy as jnp
@@ -36,7 +37,7 @@
     body, out_shape, args, flops, name, spaces=None, outs=None, scratch=(), limit=20, aliases=None
 ):
     size = sum(a.size * a.dtype.itemsize for a in args)
-    size += sum(a.size * a.dtype.itemsize for a in out_shape)
+    size += sum(math.prod(a.shape) * a.dtype.itemsize for a in out_shape)
     spaces, outs = spaces or {}, outs or {}
     kernel = pl.pallas_call(
         body,
@@ -139,29 +140,33 @@
     return doubling_scan(own, oth, size, reverse), done + between(done[0])
 
 
-def state_kernel(is_own, k_hbm, v_hbm, *refs):
-    state, k, v, sems = refs[-4:]
+def store_halves(fulls, own, oth):
+    odd = lax.rem(lax.axis_index("seq"), 2) == 1
+    blocks = [
+        jnp.concatenate([f[:HEAD_DIM, :HEAD_DIM], f[HEAD_DIM:, HEAD_DIM:]], axis=0) for f in fulls
+    ]
+    own[...] = jnp.where(odd, blocks[1], blocks[0])
+    oth[...] = jnp.where(odd, blocks[0], blocks[1])
+
+
+def state_kernel(k_hbm, v_hbm, own, oth, k, v, sems):
     starts = range(0, k.shape[0], CHUNK)
-    cols = columns(is_own, count=2)
     copies = []
     for n, start in enumerate(starts):
         at = slice(start, start + CHUNK)
         for j, (src, dst) in enumerate(((k_hbm, k), (v_hbm, v))):
-            copies.append(pltpu.make_async_copy(src.at[at, cols], dst.at[at], sems.at[j, n]))
+            copies.append(pltpu.make_async_copy(src.at[at], dst.at[at], sems.at[j, n]))
             copies[-1].start()
-    total = None
+    totals = [None, None]
     for n, start in enumerate(starts):
         at = slice(start, start + CHUNK)
         copies[2 * n].wait()
         copies[2 * n + 1].wait()
-        new = dot(k[at], v[at], 0, 0)
-        total = new if total is None else total + new
-    store_blocks(total, state)
-
-
-def store_blocks(full, state):
-    state[:HEAD_DIM] = full[:HEAD_DIM, :HEAD_DIM]
-    state[HEAD_DIM:] = full[HEAD_DIM:, HEAD_DIM:]
+        for p in range(2):
+            cols = slice(p * PAIR, (p + 1) * PAIR)
+            new = dot(k[at, cols], v[at, cols], 0, 0)
+            totals[p] = new if totals[p] is None else totals[p] + new
+    store_halves(totals, own, oth)
 
 
 def intra_kernel(q, k, v, intra):
@@ -210,21 +215,8 @@
                 stats[i : i + 1] = sums + before[0][i : i + 1] if before else sums
 
 
-def half_norm(is_own, inverse, scale, mixed, q, g, gm, state):
-    shape = (HEAD_DIM, HEAD_DIM)
-    for i in range(q.shape[0] // HEAD_DIM):
-        at = slice(i * HEAD_DIM, (i + 1) * HEAD_DIM)
-        a = jnp.broadcast_to(inverse[i : i + 1], shape).T
-        b = jnp.broadcast_to(scale[i : i + 1], shape).T
-        for j in range(2):
-            part = slice(j * HEAD_DIM, (j + 1) * HEAD_DIM)
-            value = g[at, columns(is_own, j)].astype(F32) * a - mixed[at, part] * b
-            gm[at, part] = value.astype(BF16)
-    store_blocks(dot(q[:, columns(is_own, count=2)], gm[...], 0, 0), state)
-
-
-def first_norm_kernel(width, mixed, q, g, *refs):
-    stats, (gm, state, inverse_out, scale_out) = refs[:-4], refs[-4:]
+def norm_kernel(width, mixed, oth_mixed, q, g, *refs):
+    stats, (gm, oth_gm, own, oth, inverse_out) = refs[:-5], refs[-5:]
     total = stats[0][...]
     for r in stats[1:]:
         total = total + r[...]
@@ -233,12 +225,21 @@
     cross_mean = total[blocks:] * inverse / width
     scale = inverse * inverse * cross_mean
     inverse_out[...] = inverse
-    scale_out[...] = scale
-    half_norm(False, inverse, scale, mixed, q, g, gm, state)
-
-
-def second_norm_kernel(mixed, q, g, inverse, scale, gm, state):
-    half_norm(True, inverse[...], scale[...], mixed, q, g, gm, state)
+    shape = (HEAD_DIM, HEAD_DIM)
+    halves = ((False, oth_mixed, oth_gm, oth), (True, mixed, gm, own))
+    for i in range(blocks):
+        at = slice(i * HEAD_DIM, (i + 1) * HEAD_DIM)
+        a = jnp.broadcast_to(inverse[i : i + 1], shape).T
+        b = jnp.broadcast_to(scale[i : i + 1], shape).T
+        for is_own, value, out, unused in halves:
+            for j in range(2):
+                part = slice(j * HEAD_DIM, (j + 1) * HEAD_DIM)
+                grad = g[at, columns(is_own, j)].astype(F32)
+                out[at, part] = (grad * a - value[at, part] * b).astype(BF16)
+    for is_own, unused, out, state in halves:
+        full = dot(q[:, columns(is_own, count=2)], out[...], 0, 0)
+        state[:HEAD_DIM] = full[:HEAD_DIM, :HEAD_DIM]
+        state[HEAD_DIM:] = full[HEAD_DIM:, HEAD_DIM:]
 
 
 def head_grads(cols, part, q, k, v, gm, prefix, gq, gk, gv):
@@ -271,12 +272,11 @@
             after = new if after is None else after + new
 
 
-def first_grads_kernel(q, k, v, gm, prefix, oth_gm, oth_prefix, mixed, oth_mixed, inverse, *refs):
-    gqs, gks, gvs, out = refs[:3], refs[3:6], refs[6:9], refs[9]
-    for n, (is_own, j) in enumerate(((True, 0), (True, 1), (False, 0))):
+def first_grads_kernel(q, k, v, gm, prefix, mixed, oth_mixed, inverse, *refs):
+    gqs, gks, gvs, out = refs[:2], refs[2:4], refs[4:6], refs[6]
+    for j in range(2):
         part = slice(j * HEAD_DIM, (j + 1) * HEAD_DIM)
-        halves = (gm, prefix) if is_own else (oth_gm, oth_prefix)
-        head_grads(columns(is_own, j), part, q, k, v, *halves, gqs[n], gks[n], gvs[n])
+        head_grads(columns(True, j), part, q, k, v, gm, prefix, gqs[j], gks[j], gvs[j])
     shape = (HEAD_DIM, HEAD_DIM)
     for i in range(q.shape[0] // HEAD_DIM):
         at = slice(i * HEAD_DIM, (i + 1) * HEAD_DIM)
@@ -287,12 +287,13 @@
                 out[at, columns(is_own, j)] = (value[at, part] * a).astype(BF16)
 
 
-def second_grads_kernel(q, k, v, oth_gm, oth_prefix, gq0, gq1, gq2, token, gq, gk, gv):
+def second_grads_kernel(q, k, v, gm, prefix, gq0, gq1, token, gq, *refs):
+    gks, gvs = refs[:2], refs[2:]
     gq[:, columns(True, 0)] = gq0[...]
     gq[:, columns(True, 1)] = gq1[...]
-    gq[:, columns(False, 0)] = gq2[...]
-    cols, part = columns(False, 1), slice(HEAD_DIM, PAIR)
-    head_grads(cols, part, q, k, v, oth_gm, oth_prefix, gq.at[:, cols], gk, gv)
+    for j in range(2):
+        cols, part = columns(False, j), slice(j * HEAD_DIM, (j + 1) * HEAD_DIM)
+        head_grads(cols, part, q, k, v, gm, prefix, gq.at[:, cols], gks[j], gvs[j])
 
 
 def last_kernel(heads, k, v, *refs):
@@ -346,20 +347,15 @@
             pltpu.SemaphoreType.DMA((2, chunks))
         ]
 
-    def state_of(is_own, *token):
-        return call(
-            functools.partial(state_kernel, is_own),
-            [half],
-            [keys, values, *token],
-            2 * head_flops,
-            "local_state",
-            spaces={0: pl.ANY, 1: pl.ANY, 2: pl.ANY},
-            scratch=slots(2),
-            limit=63,
-        )[0]
-
-    oth_state = state_of(False)
-    own_state = state_of(True, oth_state)
+    own_state, oth_state, keys, values = call(
+        state_kernel,
+        [half, half, pltpu.VMEM((rows, cols), BF16), pltpu.VMEM((rows, cols), BF16)],
+        [pltpu.with_memory_space_constraint(a, pltpu.HBM) for a in (keys, values)],
+        4 * head_flops,
+        "local_state",
+        spaces={0: pltpu.HBM, 1: pltpu.HBM},
+        scratch=[pltpu.SemaphoreType.DMA((2, chunks))],
+    )
 
     def forward(token):
         if token is not None:
@@ -385,21 +381,14 @@
 
     mixed, stats, prefix = mix(True, mine0, mine1)
     oth_mixed, stats, oth_prefix = mix(False, theirs0, theirs1, stats)
-    oth_gm, oth_state, inverse, scale = call(
-        functools.partial(first_norm_kernel, width),
-        [half_narrow, half, shape(blocks, HEAD_DIM, F32), shape(blocks, HEAD_DIM, F32)],
-        [oth_mixed, queries, grad_out, *all_parts(stats, "head", head_size)],
-        2 * head_flops,
-        "first_norm",
+    gm, oth_gm, own_state, oth_state, inverse = call(
+        functools.partial(norm_kernel, width),
+        [half_narrow, half_narrow, half, half, shape(blocks, HEAD_DIM, F32)],
+        [mixed, oth_mixed, queries, grad_out, *all_parts(stats, "head", head_size)],
+        4 * head_flops,
+        "norm",
     )
-    gm, own_state = call(
-        second_norm_kernel,
-        [half_narrow, half],
-        [mixed, queries, grad_out, inverse, scale],
-        2 * head_flops,
-        "second_norm",
-    )
-    grads_flops = 5 * chunk_flops + 6 * head_flops
+    grads_flops = 2 * (5 * chunk_flops + 6 * head_flops)
     first = []
 
     def backward(token):
@@ -407,26 +396,25 @@
             first.extend(
                 call(
                     first_grads_kernel,
-                    [head_narrow] * 3 + [head_wide] * 6 + [narrow],
-                    [queries, keys, values, gm, prefix, oth_gm, oth_prefix]
-                    + [mixed, oth_mixed, inverse],
-                    3 * grads_flops,
+                    [head_narrow] * 2 + [head_wide] * 4 + [narrow],
+                    [queries, keys, values, gm, prefix, mixed, oth_mixed, inverse],
+                    grads_flops,
                     "first_grads",
                 )
             )
-            return first[3:]
+            return first[2:]
         return call(
             second_grads_kernel,
-            [narrow, head_wide, head_wide],
-            [queries, keys, values, oth_gm, oth_prefix, *first[:3], token],
+            [narrow] + [head_wide] * 4,
+            [queries, keys, values, oth_gm, oth_prefix, *first[:2], token],
             grads_flops,
             "second_grads",
-            spaces={8: pl.ANY},
+            spaces={7: pl.ANY},
         )
 
     (mine0, mine1, theirs0, theirs1), done = scan(own_state, oth_state, seq, True, backward)
-    gk_parts, gv_parts, (output, grad_q) = done[:3], done[3:6], done[6:8]
-    gk_parts, gv_parts = gk_parts + done[8:9], gv_parts + done[9:]
+    gk_parts, gv_parts, (output, grad_q) = done[:2], done[2:4], done[4:6]
+    gk_parts, gv_parts = gk_parts + done[6:8], gv_parts + done[8:]
 
     def last(heads, states, *before):
         picked = [(0 if is_own else 2) + j for is_own, j in heads]
@@ -445,8 +433,7 @@
         )
 
     grads = last(((True, 0), (True, 1)), [mine0, mine1])
-    grads = last(((False, 1),), [theirs1], *grads)
-    grad_k, grad_v = last(((False, 0),), [theirs0], *grads)
+    grad_k, grad_v = last(((False, 0), (False, 1)), [theirs0, theirs1], *grads)
     return output, grad_q, grad_k, grad_v
 
 

time: 58.3 us -> 57.2 us (0.981)
  waiting for transfers between devices: 7.77 us -> 14.3 us
  Pallas kernels: 20.8 us -> 16.3 us
  local copies, waits for them, and re-layouts: 3.71 us -> 0.01 us
  starting transfers between devices: 24.9 us -> 25.7 us
    ppermute x14, waiting for transfers between devices: 5.92 us -> 12.4 us  [exchange(): return lax.ppermute(value, 'seq', [(i, i ^ by) for i in range(size)])]
    pallas_call x18 -> x15, Pallas kernels: 20.8 us -> 16.3 us  [call(): return list(kernel(*args))]
    unnamed x18 -> x4, local copies, waits for them, and re-layouts: 3.71 us -> 0.01 us
    ppermute x14, starting transfers between devices: 23 us -> 23.8 us  [exchange(): return lax.ppermute(value, 'seq', [(i, i ^ by) for i in range(size)])]
  transfers between devices with their start and end apart: 17 -> 17, of which waited for: 9 -> 8; matrix products, arithmetic and copies ran while one was open for 0% -> 0% of each run, Pallas kernels for 27% -> 20%
where the time goes in v5:
time: 57.2 us; the launch traced here: 57 us
  starting transfers between devices  25.7 us (45%)
  Pallas kernels  16.3 us (28%)
  waiting for transfers between devices  14.3 us (25%)
  between operations  0.76 us (1%)
    ppermute x14, starting transfers between devices, exchange(): return lax.ppermute(value, 'seq', [(i, i ^ by) for i in range(size)])  23.8 us
    pallas_call x15, Pallas kernels, call(): return list(kernel(*args))  16.3 us
    ppermute x14, waiting for transfers between devices, exchange(): return lax.ppermute(value, 'seq', [(i, i ^ by) for i in range(size)])  12.4 us
    ppermute x3, starting transfers between devices, all_parts(): parts.append(lax.ppermute(value, axis, pairs))  1.93 us
    ppermute x3, waiting for transfers between devices, all_parts(): parts.append(lax.ppermute(value, axis, pairs))  1.87 us
  transfers between devices with their start and end apart: 17, of which 8 were waited for; matrix products, arithmetic and copies ran while one was open for 0% of the time, Pallas kernels for 20%

profile of v5, /device:TPU:0, one launch (start us, length us, event | category | flops | bytes accessed | tf_op | source)
XLA Modules:
  0.0 57.0 jit_solution(4719737256887020436)
XLA Ops:
  0.6 0.0 copy-start
  0.6 2.0 %local_state.1 = (f32[256,128]{1,0:T(8,128)S(1)}, f32[256,128]{1,0:T(8,128)S(1)}, bf16[1024,512]{1,0:T(8,128)(2,1)S(1)}, bf16[1024,512]{1,0:T(8,128)(2,1)S(1)}) custom-call(bf16[1024,512]{1,0:T(8,128)(2,1)} %k_hbm.1, bf16[1024,512]{1,0:T(8,128)(2,1)} %v_hbm.1), custom_call_target="tpu_custom_call" | custom-call | flops 134217728 | bytes 4456448 | tf_op jit(solution)/shard_map/local_state/pallas_call | solution.py:57
  2.7 4.0 %collective-permute-start = (f32[256,128]{1,0:T(8,128)S(1)}, f32[256,128]{1,0:T(8,128)S(1)}, u32[]{:S(2)}, u32[]{:S(2)}) collective-permute-start(f32[256,128]{1,0:T(8,128)S(1)} %get-tuple-element.50), channel_id=1, source_target_pairs={{0,12},{4,8},{8,4},{12,0},{16,28},{20,24},{24,20},{28,16},{1,13},{... | collective-permute-start | bytes 393224 | tf_op jit(solution)/shard_map/ppermute | solution.py:61
  6.7 0.4 collective-permute-start.1
  7.1 0.2 collective-permute-start.2
  7.3 0.0 copy-done
  7.3 1.9 %intra.1.refs_0_ = f32[1024,512]{1,0:T(8,128)S(1)} custom-call(bf16[1024,512]{1,0:T(8,128)(2,1)S(1)} %copy-done, bf16[1024,512]{1,0:T(8,128)(2,1)S(1)} %get-tuple-element.47.k, bf16[1024,512]{1,0:T(8,128)(2,1)S(1)} %get-tuple-element.48.v), custom_call_target="tpu_custom_call" | custom-call | flops 805306368 | bytes 5242880 | tf_op jit(solution)/shard_map/intra/pallas_call | solution.py:57
  9.2 0.0 copy-start.1
  9.3 1.7 %collective-permute-done.near3 = f32[256,128]{1,0:T(8,128)S(1)} collective-permute-done((f32[256,128]{1,0:T(8,128)S(1)}, f32[256,128]{1,0:T(8,128)S(1)}, u32[]{:S(2)}, u32[]{:S(2)}) %collective-permute-start) | collective-permute-done | bytes 131104 | tf_op jit(solution)/shard_map/ppermute | solution.py:61
  11.0 2.1 %collective-permute-done.1.near2 = f32[256,128]{1,0:T(8,128)S(1)} collective-permute-done((f32[256,128]{1,0:T(8,128)S(1)}, f32[256,128]{1,0:T(8,128)S(1)}, u32[]{:S(2)}, u32[]{:S(2)}) %collective-permute-start.1) | collective-permute-done | bytes 131104 | tf_op jit(solution)/shard_map/ppermute | solution.py:61
  13.1 0.0 collective-permute-done.2.near1
  13.2 2.7 %collective-permute-start.3 = (f32[128,128]{1,0:T(8,128)S(1)}, f32[128,128]{1,0:T(8,128)S(1)}, u32[]{:S(2)}, u32[]{:S(2)}) collective-permute-start(f32[128,128]{1,0:T(8,128)S(1)} %get-tuple-element.51), channel_id=1, source_target_pairs={{0,16},{4,20},{8,24},{12,28},{16,0},{20,4},{24,8},{28,12},{1,17},{... | collective-permute-start | bytes 196616 | tf_op jit(solution)/shard_map/ppermute | solution.py:61
  15.8 0.3 collective-permute-start.4
  16.2 2.4 %collective-permute-done.3.far = f32[128,128]{1,0:T(8,128)S(1)} collective-permute-done((f32[128,128]{1,0:T(8,128)S(1)}, f32[128,128]{1,0:T(8,128)S(1)}, u32[]{:S(2)}, u32[]{:S(2)}) %collective-permute-start.3) | collective-permute-done | bytes 65568 | tf_op jit(solution)/shard_map/ppermute | solution.py:61
  18.6 2.9 %collective-permute-start.5 = (f32[128,128]{1,0:T(8,128)S(1)}, f32[128,128]{1,0:T(8,128)S(1)}, u32[]{:S(2)}, u32[]{:S(2)}) collective-permute-start(f32[128,128]{1,0:T(8,128)S(1)} %get-tuple-element.56), channel_id=1, source_target_pairs={{0,4},{4,0},{8,12},{12,8},{16,20},{20,16},{24,28},{28,24},{1,5},{5... | collective-permute-start | bytes 196616 | tf_op jit(solution)/shard_map/ppermute | solution.py:61
  21.5 0.0 collective-permute-done.4.far
  21.5 2.5 %collective-permute-start.6 = (f32[128,128]{1,0:T(8,128)S(1)}, f32[128,128]{1,0:T(8,128)S(1)}, u32[]{:S(2)}, u32[]{:S(2)}) collective-permute-start(f32[128,128]{1,0:T(8,128)S(1)} %get-tuple-element.57), channel_id=1, source_target_pairs={{0,4},{4,0},{8,12},{12,8},{16,20},{20,16},{24,28},{28,24},{1,5},{5... | collective-permute-start | bytes 196616 | tf_op jit(solution)/shard_map/ppermute | solution.py:61
  24.0 0.0 copy-done.1
  24.0 0.5 mixed.2
  24.6 0.0 collective-permute-done.5.state0
  24.6 1.7 %collective-permute-done.6.state1 = f32[128,128]{1,0:T(8,128)S(1)} collective-permute-done((f32[128,128]{1,0:T(8,128)S(1)}, f32[128,128]{1,0:T(8,128)S(1)}, u32[]{:S(2)}, u32[]{:S(2)}) %collective-permute-start.6) | collective-permute-done | bytes 65568 | tf_op jit(solution)/shard_map/ppermute | solution.py:61
  26.3 0.5 mixed.3
  26.8 0.1 collective-permute-start.7
  27.0 1.5 %collective-permute-start.8 = (f32[16,128]{1,0:T(8,128)S(1)}, f32[16,128]{1,0:T(8,128)S(1)}, u32[]{:S(2)}, u32[]{:S(2)}) collective-permute-start(f32[16,128]{1,0:T(8,128)S(1)} %get-tuple-element.60.refs_0_), channel_id=1, source_target_pairs={{0,2},{1,3},{2,0},{3,1},{4,6},{5,7},{6,4},{7,5},{8,10},{9,11},{10,... | collective-permute-start | bytes 24584 | tf_op jit(solution)/shard_map/ppermute | solution.py:324
  28.5 0.3 collective-permute-start.9
  28.8 1.2 %collective-permute-done.7.refs_1_ = f32[16,128]{1,0:T(8,128)S(1)} collective-permute-done((f32[16,128]{1,0:T(8,128)S(1)}, f32[16,128]{1,0:T(8,128)S(1)}, u32[]{:S(2)}, u32[]{:S(2)}) %collective-permute-start.7) | collective-permute-done | bytes 8224 | tf_op jit(solution)/shard_map/ppermute | solution.py:324
  30.0 0.7 %collective-permute-done.8.refs_2_ = f32[16,128]{1,0:T(8,128)S(1)} collective-permute-done((f32[16,128]{1,0:T(8,128)S(1)}, f32[16,128]{1,0:T(8,128)S(1)}, u32[]{:S(2)}, u32[]{:S(2)}) %collective-permute-start.8) | collective-permute-done | bytes 8224 | tf_op jit(solution)/shard_map/ppermute | solution.py:324
  30.6 0.0 collective-permute-done.9.refs_3_
  30.6 1.0 %norm.1 = (bf16[1024,256]{1,0:T(8,128)(2,1)S(1)}, bf16[1024,256]{1,0:T(8,128)(2,1)S(1)}, f32[256,128]{1,0:T(8,128)S(1)}, f32[256,128]{1,0:T(8,128)S(1)}, f32[8,128]{1,0:T(8,128)S(1)}) custom-call(f32[1024,256]{1,0:T(8,128)S(1)} %get-tuple-element.55.mixed, f32[1024,256]{1,0:T(8,128)S(1)} %get-tuple-element.59.oth_mixed, bf16[1024,512]{1,0:T(8,128)(2,1)S(1)} %copy-done, ...), custom_call_target="tpu_custom_call" | custom-call | flops 134217728 | bytes 5541888 | tf_op jit(solution)/shard_map/norm/pallas_call | solution.py:57
  31.7 2.6 %collective-permute-start.10 = (f32[256,128]{1,0:T(8,128)S(1)}, f32[256,128]{1,0:T(8,128)S(1)}, u32[]{:S(2)}, u32[]{:S(2)}) collective-permute-start(f32[256,128]{1,0:T(8,128)S(1)} %get-tuple-element.70), channel_id=1, source_target_pairs={{0,12},{4,8},{8,4},{12,0},{16,28},{20,24},{24,20},{28,16},{1,13},{... | collective-permute-start | bytes 393224 | tf_op jit(solution)/shard_map/ppermute | solution.py:61
  34.3 0.9 %collective-permute-start.11 = (f32[256,128]{1,0:T(8,128)S(1)}, f32[256,128]{1,0:T(8,128)S(1)}, u32[]{:S(2)}, u32[]{:S(2)}) collective-permute-start(f32[256,128]{1,0:T(8,128)S(1)} %get-tuple-element.69.own), channel_id=1, source_target_pairs={{0,8},{4,12},{8,0},{12,4},{16,24},{20,28},{24,16},{28,20},{1,9},{5... | collective-permute-start | bytes 393224 | tf_op jit(solution)/shard_map/ppermute | solution.py:61
  35.2 0.0 collective-permute-start.12
  35.2 3.9 %first_grads.1 = (bf16[1024,128]{1,0:T(8,128)(2,1)S(1)}, bf16[1024,128]{1,0:T(8,128)(2,1)S(1)}, f32[1024,128]{1,0:T(8,128)S(1)}, f32[1024,128]{1,0:T(8,128)S(1)}...) custom-call(bf16[1024,512]{1,0:T(8,128)(2,1)S(1)} %copy-done, ...), custom_call_target="tpu_custom_call" | custom-call | flops 1073741824 | bytes 9506816 | tf_op jit(solution)/shard_map/first_grads/pallas_call | solution.py:57
  39.2 0.0 collective-permute-done.10.near3
  39.2 2.7 %collective-permute-done.11.near2 = f32[256,128]{1,0:T(8,128)S(1)} collective-permute-done((f32[256,128]{1,0:T(8,128)S(1)}, f32[256,128]{1,0:T(8,128)S(1)}, u32[]{:S(2)}, u32[]{:S(2)}) %collective-permute-start.11) | collective-permute-done | bytes 131104 | tf_op jit(solution)/shard_map/ppermute | solution.py:61
  41.9 0.0 collective-permute-done.12.near1
  41.9 2.4 %collective-permute-start.13 = (f32[128,128]{1,0:T(8,128)S(1)}, f32[128,128]{1,0:T(8,128)S(1)}, u32[]{:S(2)}, u32[]{:S(2)}) collective-permute-start(f32[128,128]{1,0:T(8,128)S(1)} %get-tuple-element.78), channel_id=1, source_target_pairs={{0,16},{4,20},{8,24},{12,28},{16,0},{20,4},{24,8},{28,12},{1,17},{... | collective-permute-start | bytes 196616 | tf_op jit(solution)/shard_map/ppermute | solution.py:61
  44.3 0.6 %collective-permute-start.15 = (f32[128,128]{1,0:T(8,128)S(1)}, f32[128,128]{1,0:T(8,128)S(1)}, u32[]{:S(2)}, u32[]{:S(2)}) collective-permute-start(f32[128,128]{1,0:T(8,128)S(1)} %get-tuple-element.72.token), channel_id=1, source_target_pairs={{0,16},{4,20},{8,24},{12,28},{16,0},{20,4},{24,8},{28,12},{1,17},{... | collective-permute-start | bytes 196616 | tf_op jit(solution)/shard_map/ppermute | solution.py:61
  44.9 3.7 %second_grads.1 = (bf16[1024,512]{1,0:T(8,128)(2,1)}, f32[1024,128]{1,0:T(8,128)S(1)}, f32[1024,128]{1,0:T(8,128)S(1)}, f32[1024,128]{1,0:T(8,128)S(1)}, f32[1024,128]{1,0:T(8,128)S(1)}) custom-call(bf16[1024,512]{1,0:T(8,128)(2,1)S(1)} %copy-done, bf16[1024,512]{1,0:T(8,128)(2,1)S(1)} %get-tuple-element.47.k, bf16[1024,512]{1,0:T(8,128)(2,1)S(1)} %get-tuple-element.48.v, ...), custom_call_target="tpu_custom_call" | custom-call | flops 1073741824 | bytes 7471104 | tf_op jit(solution)/shard_map/second_grads/pallas_call | solution.py:57
  48.6 0.0 collective-permute-done.13.far
  48.6 2.8 %collective-permute-start.14 = (f32[128,128]{1,0:T(8,128)S(1)}, f32[128,128]{1,0:T(8,128)S(1)}, u32[]{:S(2)}, u32[]{:S(2)}) collective-permute-start(f32[128,128]{1,0:T(8,128)S(1)} %get-tuple-element.79), channel_id=1, source_target_pairs={{0,4},{4,0},{8,12},{12,8},{16,20},{20,16},{24,28},{28,24},{1,5},{5... | collective-permute-start | bytes 196616 | tf_op jit(solution)/shard_map/ppermute | solution.py:61
  51.4 0.0 collective-permute-done.15.far
  51.5 1.4 %collective-permute-start.16 = (f32[128,128]{1,0:T(8,128)S(1)}, f32[128,128]{1,0:T(8,128)S(1)}, u32[]{:S(2)}, u32[]{:S(2)}) collective-permute-start(f32[128,128]{1,0:T(8,128)S(1)} %get-tuple-element.80), channel_id=1, source_target_pairs={{0,4},{4,0},{8,12},{12,8},{16,20},{20,16},{24,28},{28,24},{1,5},{5... | collective-permute-start | bytes 196616 | tf_op jit(solution)/shard_map/ppermute | solution.py:61
  52.9 1.2 %last.2 = (bf16[1024,512]{1,0:T(8,128)(2,1)}, bf16[1024,512]{1,0:T(8,128)(2,1)}) custom-call(bf16[1024,512]{1,0:T(8,128)(2,1)S(1)} %get-tuple-element.47.k, bf16[1024,512]{1,0:T(8,128)(2,1)S(1)} %get-tuple-element.48.v, f32[1024,128]{1,0:T(8,128)S(1)} %get-tuple-element.71.refs_0_, f32[1024,128]{1,0:T(8,128)S(1)} %get-tuple-element.81.refs_1_, ...), custom_call_target="tpu_custom_call" | custom-call | flops 134217728 | bytes 6422528 | tf_op jit(solution)/shard_map/last/pallas_call | solution.py:57
  54.1 0.0 collective-permute-done.14.refs_4_
  54.1 1.7 %collective-permute-done.16.refs_5_ = f32[128,128]{1,0:T(8,128)S(1)} collective-permute-done((f32[128,128]{1,0:T(8,128)S(1)}, f32[128,128]{1,0:T(8,128)S(1)}, u32[]{:S(2)}, u32[]{:S(2)}) %collective-permute-start.16) | collective-permute-done | bytes 65568 | tf_op jit(solution)/shard_map/ppermute | solution.py:61
  55.8 1.2 %last.3 = (bf16[1024,512]{1,0:T(8,128)(2,1)}, bf16[1024,512]{1,0:T(8,128)(2,1)}) custom-call(bf16[1024,512]{1,0:T(8,128)(2,1)S(1)} %get-tuple-element.47.k, bf16[1024,512]{1,0:T(8,128)(2,1)S(1)} %get-tuple-element.48.v, f32[1024,128]{1,0:T(8,128)S(1)} %get-tuple-element.74.refs_0_, ...), custom_call_target="tpu_custom_call", output_to_operand_aliasing={{0}: (8, {}), {1}: (9, {})} | custom-call | flops 134217728 | bytes 8519680 | tf_op jit(solution)/shard_map/last/pallas_call | solution.py:57
  (6 shorter events, 0.2 us)
Async XLA Ops:
  0.6 6.7 %copy-start = (bf16[1024,512]{1,0:T(8,128)(2,1)S(1)}, bf16[1024,512]{1,0:T(8,128)(2,1)}, u32[]{:S(2)}) copy-start(bf16[1024,512]{1,0:T(8,128)(2,1)} %q.11) | copy-start | bytes 3145732
  2.7 8.3 %collective-permute-start = (f32[256,128]{1,0:T(8,128)S(1)}, f32[256,128]{1,0:T(8,128)S(1)}, u32[]{:S(2)}, u32[]{:S(2)}) collective-permute-start(f32[256,128]{1,0:T(8,128)S(1)} %get-tuple-element.50), channel_id=1, source_target_pairs={{0,12},{4,8},{8,4},{12,0},{16,28},{20,24},{24,20},{28,16},{1,13},{... | collective-permute-start | bytes 393224 | tf_op jit(solution)/shard_map/ppermute | solution.py:61
  6.7 6.5 %collective-permute-start.1 = (f32[256,128]{1,0:T(8,128)S(1)}, f32[256,128]{1,0:T(8,128)S(1)}, u32[]{:S(2)}, u32[]{:S(2)}) collective-permute-start(f32[256,128]{1,0:T(8,128)S(1)} %get-tuple-element.49.own), channel_id=1, source_target_pairs={{0,8},{4,12},{8,0},{12,4},{16,24},{20,28},{24,16},{28,20},{1,9},{5... | collective-permute-start | bytes 393224 | tf_op jit(solution)/shard_map/ppermute | solution.py:61
  7.1 6.0 %collective-permute-start.2 = (f32[256,128]{1,0:T(8,128)S(1)}, f32[256,128]{1,0:T(8,128)S(1)}, u32[]{:S(2)}, u32[]{:S(2)}) collective-permute-start(f32[256,128]{1,0:T(8,128)S(1)} %get-tuple-element.50), channel_id=1, source_target_pairs={{0,4},{4,0},{8,12},{12,8},{16,20},{20,16},{24,28},{28,24},{1,5},{5... | collective-permute-start | bytes 393224 | tf_op jit(solution)/shard_map/ppermute | solution.py:61
  9.2 14.8 %copy-start.1 = (bf16[1024,512]{1,0:T(8,128)(2,1)S(1)}, bf16[1024,512]{1,0:T(8,128)(2,1)}, u32[]{:S(2)}) copy-start(bf16[1024,512]{1,0:T(8,128)(2,1)} %g.5) | copy-start | bytes 3145732
  13.2 5.4 %collective-permute-start.3 = (f32[128,128]{1,0:T(8,128)S(1)}, f32[128,128]{1,0:T(8,128)S(1)}, u32[]{:S(2)}, u32[]{:S(2)}) collective-permute-start(f32[128,128]{1,0:T(8,128)S(1)} %get-tuple-element.51), channel_id=1, source_target_pairs={{0,16},{4,20},{8,24},{12,28},{16,0},{20,4},{24,8},{28,12},{1,17},{... | collective-permute-start | bytes 196616 | tf_op jit(solution)/shard_map/ppermute | solution.py:61
  15.8 5.6 %collective-permute-start.4 = (f32[128,128]{1,0:T(8,128)S(1)}, f32[128,128]{1,0:T(8,128)S(1)}, u32[]{:S(2)}, u32[]{:S(2)}) collective-permute-start(f32[128,128]{1,0:T(8,128)S(1)} %get-tuple-element.53), channel_id=1, source_target_pairs={{0,16},{4,20},{8,24},{12,28},{16,0},{20,4},{24,8},{28,12},{1,17},{... | collective-permute-start | bytes 196616 | tf_op jit(solution)/shard_map/ppermute | solution.py:61
  18.6 6.0 %collective-permute-start.5 = (f32[128,128]{1,0:T(8,128)S(1)}, f32[128,128]{1,0:T(8,128)S(1)}, u32[]{:S(2)}, u32[]{:S(2)}) collective-permute-start(f32[128,128]{1,0:T(8,128)S(1)} %get-tuple-element.56), channel_id=1, source_target_pairs={{0,4},{4,0},{8,12},{12,8},{16,20},{20,16},{24,28},{28,24},{1,5},{5... | collective-permute-start | bytes 196616 | tf_op jit(solution)/shard_map/ppermute | solution.py:61
  21.5 4.8 %collective-permute-start.6 = (f32[128,128]{1,0:T(8,128)S(1)}, f32[128,128]{1,0:T(8,128)S(1)}, u32[]{:S(2)}, u32[]{:S(2)}) collective-permute-start(f32[128,128]{1,0:T(8,128)S(1)} %get-tuple-element.57), channel_id=1, source_target_pairs={{0,4},{4,0},{8,12},{12,8},{16,20},{20,16},{24,28},{28,24},{1,5},{5... | collective-permute-start | bytes 196616 | tf_op jit(solution)/shard_map/ppermute | solution.py:61
  26.8 3.1 %collective-permute-start.7 = (f32[16,128]{1,0:T(8,128)S(1)}, f32[16,128]{1,0:T(8,128)S(1)}, u32[]{:S(2)}, u32[]{:S(2)}) collective-permute-start(f32[16,128]{1,0:T(8,128)S(1)} %get-tuple-element.60.refs_0_), channel_id=1, source_target_pairs={{0,3},{1,2},{2,1},{3,0},{4,7},{5,6},{6,5},{7,4},{8,11},{9,10},{10,... | collective-permute-start | bytes 24584 | tf_op jit(solution)/shard_map/ppermute | solution.py:324
  27.0 3.7 %collective-permute-start.8 = (f32[16,128]{1,0:T(8,128)S(1)}, f32[16,128]{1,0:T(8,128)S(1)}, u32[]{:S(2)}, u32[]{:S(2)}) collective-permute-start(f32[16,128]{1,0:T(8,128)S(1)} %get-tuple-element.60.refs_0_), channel_id=1, source_target_pairs={{0,2},{1,3},{2,0},{3,1},{4,6},{5,7},{6,4},{7,5},{8,10},{9,11},{10,... | collective-permute-start | bytes 24584 | tf_op jit(solution)/shard_map/ppermute | solution.py:324
  28.5 2.1 %collective-permute-start.9 = (f32[16,128]{1,0:T(8,128)S(1)}, f32[16,128]{1,0:T(8,128)S(1)}, u32[]{:S(2)}, u32[]{:S(2)}) collective-permute-start(f32[16,128]{1,0:T(8,128)S(1)} %get-tuple-element.60.refs_0_), channel_id=1, source_target_pairs={{0,1},{1,0},{2,3},{3,2},{4,5},{5,4},{6,7},{7,6},{8,9},{9,8},{10,11... | collective-permute-start | bytes 24584 | tf_op jit(solution)/shard_map/ppermute | solution.py:324
  31.7 7.5 %collective-permute-start.10 = (f32[256,128]{1,0:T(8,128)S(1)}, f32[256,128]{1,0:T(8,128)S(1)}, u32[]{:S(2)}, u32[]{:S(2)}) collective-permute-start(f32[256,128]{1,0:T(8,128)S(1)} %get-tuple-element.70), channel_id=1, source_target_pairs={{0,12},{4,8},{8,4},{12,0},{16,28},{20,24},{24,20},{28,16},{1,13},{... | collective-permute-start | bytes 393224 | tf_op jit(solution)/shard_map/ppermute | solution.py:61
  34.3 7.6 %collective-permute-start.11 = (f32[256,128]{1,0:T(8,128)S(1)}, f32[256,128]{1,0:T(8,128)S(1)}, u32[]{:S(2)}, u32[]{:S(2)}) collective-permute-start(f32[256,128]{1,0:T(8,128)S(1)} %get-tuple-element.69.own), channel_id=1, source_target_pairs={{0,8},{4,12},{8,0},{12,4},{16,24},{20,28},{24,16},{28,20},{1,9},{5... | collective-permute-start | bytes 393224 | tf_op jit(solution)/shard_map/ppermute | solution.py:61
  35.2 6.7 %collective-permute-start.12 = (f32[256,128]{1,0:T(8,128)S(1)}, f32[256,128]{1,0:T(8,128)S(1)}, u32[]{:S(2)}, u32[]{:S(2)}) collective-permute-start(f32[256,128]{1,0:T(8,128)S(1)} %get-tuple-element.70), channel_id=1, source_target_pairs={{0,4},{4,0},{8,12},{12,8},{16,20},{20,16},{24,28},{28,24},{1,5},{5... | collective-permute-start | bytes 393224 | tf_op jit(solution)/shard_map/ppermute | solution.py:61
  41.9 6.7 %collective-permute-start.13 = (f32[128,128]{1,0:T(8,128)S(1)}, f32[128,128]{1,0:T(8,128)S(1)}, u32[]{:S(2)}, u32[]{:S(2)}) collective-permute-start(f32[128,128]{1,0:T(8,128)S(1)} %get-tuple-element.78), channel_id=1, source_target_pairs={{0,16},{4,20},{8,24},{12,28},{16,0},{20,4},{24,8},{28,12},{1,17},{... | collective-permute-start | bytes 196616 | tf_op jit(solution)/shard_map/ppermute | solution.py:61
  44.3 7.1 %collective-permute-start.15 = (f32[128,128]{1,0:T(8,128)S(1)}, f32[128,128]{1,0:T(8,128)S(1)}, u32[]{:S(2)}, u32[]{:S(2)}) collective-permute-start(f32[128,128]{1,0:T(8,128)S(1)} %get-tuple-element.72.token), channel_id=1, source_target_pairs={{0,16},{4,20},{8,24},{12,28},{16,0},{20,4},{24,8},{28,12},{1,17},{... | collective-permute-start | bytes 196616 | tf_op jit(solution)/shard_map/ppermute | solution.py:61
  48.6 5.5 %collective-permute-start.14 = (f32[128,128]{1,0:T(8,128)S(1)}, f32[128,128]{1,0:T(8,128)S(1)}, u32[]{:S(2)}, u32[]{:S(2)}) collective-permute-start(f32[128,128]{1,0:T(8,128)S(1)} %get-tuple-element.79), channel_id=1, source_target_pairs={{0,4},{4,0},{8,12},{12,8},{16,20},{20,16},{24,28},{28,24},{1,5},{5... | collective-permute-start | bytes 196616 | tf_op jit(solution)/shard_map/ppermute | solution.py:61
  51.5 4.3 %collective-permute-start.16 = (f32[128,128]{1,0:T(8,128)S(1)}, f32[128,128]{1,0:T(8,128)S(1)}, u32[]{:S(2)}, u32[]{:S(2)}) collective-permute-start(f32[128,128]{1,0:T(8,128)S(1)} %get-tuple-element.80), channel_id=1, source_target_pairs={{0,4},{4,0},{8,12},{12,8},{16,20},{20,16},{24,28},{28,24},{1,5},{5... | collective-permute-start | bytes 196616 | tf_op jit(solution)/shard_map/ppermute | solution.py:61

commit v6 on v0

v6 whole, which is shorter than its diff:
```python
import functools
import math

import jax
import jax.numpy as jnp
from jax import lax
from jax.experimental import pallas as pl
from jax.experimental.pallas import tpu as pltpu
from jax.sharding import PartitionSpec as P

HEAD_DIM = 128
EPSILON = 1e-06
CHUNK = 256
PAIR = 2 * HEAD_DIM
QUAD = 4
F32 = jnp.float32
BF16 = jnp.bfloat16


def dot(a, b, ca, cb):
    return lax.dot_general(a, b, (((ca,), (cb,)), ((), ())), preferred_element_type=F32)


def head_slice(h):
    return slice(h * HEAD_DIM, (h + 1) * HEAD_DIM)


def chunk_slices(rows):
    return [slice(start, start + CHUNK) for start in range(0, rows, CHUNK)]


def causal(transposed=False):
    rows = lax.broadcasted_iota(jnp.int32, (CHUNK, CHUNK), 0)
    cols = lax.broadcasted_iota(jnp.int32, (CHUNK, CHUNK), 1)
    return cols >= rows if transposed else rows >= cols


def call(body, out_shape, args, flops, name, spaces=None, outs=None, scratch=()):
    size = sum(a.size * a.dtype.itemsize for a in args)
    size += sum(math.prod(a.shape) * a.dtype.itemsize for a in out_shape)
    spaces, outs = spaces or {}, outs or {}
    kernel = pl.pallas_call(
        body,
        out_shape=out_shape,
        in_specs=[
            pl.BlockSpec(memory_space=spaces.get(i, pltpu.VMEM)) for i in range(len(args))
        ],
        out_specs=[
            pl.BlockSpec(memory_space=outs.get(i, pltpu.VMEM)) for i in range(len(out_shape))
        ],
        scratch_shapes=list(scratch),
        compiler_params=pltpu.CompilerParams(vmem_limit_bytes=20 * 2**20),
        cost_estimate=pl.CostEstimate(flops=flops, bytes_accessed=size, transcendentals=0),
        name=name,
    )
    return list(kernel(*args))


def head_of(n):
    number = lax.rem(lax.axis_index("seq"), QUAD) ^ n
    return pl.ds(pl.multiple_of(number * HEAD_DIM, HEAD_DIM), HEAD_DIM)


def exchange(value, size, by):
    return lax.ppermute(value, "seq", [(i, i ^ by) for i in range(size)])


def quad_kernel(piece0, piece1, piece2, piece3, *refs):
    refs[-1][...] = (piece0[...] + piece1[...]) + (piece2[...] + piece3[...])


def finish_kernel(reverse, piece0, piece1, piece2, piece3, far, *refs):
    place = lax.axis_index("seq")
    number = lax.rem(place, QUAD)
    pieces = [p[...] for p in (piece0, piece1, piece2, piece3)]
    zero = jnp.zeros(far.shape, F32)
    second = place < QUAD if reverse else place >= QUAD
    before = jnp.where(second, far[...], zero)
    for to, out in enumerate(refs[-QUAD:]):
        total = before
        for n, piece in enumerate(pieces):
            ahead = (number ^ n) > (number ^ to) if reverse else (number ^ n) < (number ^ to)
            if n != to:
                total = total + jnp.where(ahead, piece, zero)
        out[...] = total


def quad_scan(pieces, size, reverse, between):
    head = jax.ShapeDtypeStruct((HEAD_DIM, HEAD_DIM), F32)
    got = {by: exchange(pieces[by], size, by) for by in (3, 2, 1)}
    pieces = [pieces[0], got[1], got[2], got[3]]
    first = between(0, None)
    (total,) = call(
        quad_kernel, [head], [*pieces, *first[-1:]], 0, "quad_sum", spaces={4: pl.ANY}
    )
    far = exchange(total, size, QUAD)
    second = between(1, total)
    finished = call(
        functools.partial(finish_kernel, reverse),
        [head] * QUAD,
        [*pieces, far, *second[-1:]],
        0,
        "finish",
        spaces={5: pl.ANY},
    )
    got = {by: exchange(finished[by], size, by) for by in (3, 2, 1)}
    third = between(2, finished[0])
    return [finished[0], got[1], got[2], got[3]], first + second + third


def doubling_scan(pieces, size, reverse, between):
    def shift(value, by):
        pairs = [(i, i + by) for i in range(size - by)]
        if reverse:
            pairs = [(b, a) for a, b in pairs]
        return lax.ppermute(value, "seq", pairs)

    def reorder(state):
        number = lax.rem(lax.axis_index("seq"), QUAD)
        return jnp.take(state, number ^ jnp.arange(QUAD), axis=0)

    state = reorder(jnp.stack(pieces))
    by = 1
    while by < size:
        state = state + shift(state, by)
        by *= 2
    state = reorder(shift(state, 1))
    done = []
    for phase in range(3):
        done += between(phase, done[-1] if done else None)
    return [state[n] for n in range(QUAD)], done


def store_pieces(states, pieces, scratch):
    for h, state in enumerate(states):
        scratch[head_slice(h), :] = state
    for n, piece in enumerate(pieces):
        piece[...] = scratch[head_of(n), :]


def load_pieces(pieces, rounded):
    for n, piece in enumerate(pieces):
        rounded[head_of(n), :] = piece[...].astype(BF16)


def pair_blocks(left, right, contract):
    blocks = []
    for p in range(right.shape[1] // PAIR):
        cols = slice(p * PAIR, (p + 1) * PAIR)
        full = dot(left[:, cols] if contract == 0 else left[cols, :], right[:, cols], contract, 0)
        blocks += [full[:HEAD_DIM, :HEAD_DIM], full[HEAD_DIM:, HEAD_DIM:]]
    return blocks


def add_all(a, b):
    return b if a is None else [x + y for x, y in zip(a, b)]


def state_kernel(k_hbm, v_hbm, *refs):
    pieces, (k, v, scratch, sems) = refs[:QUAD], refs[QUAD:]
    chunks = chunk_slices(k.shape[0])
    copies = []
    for n, at in enumerate(chunks):
        for j, (src, dst) in enumerate(((k_hbm, k), (v_hbm, v))):
            copies.append(pltpu.make_async_copy(src.at[at], dst.at[at], sems.at[j, n]))
            copies[-1].start()
    total = None
    for n, at in enumerate(chunks):
        copies[2 * n].wait()
        copies[2 * n + 1].wait()
        total = add_all(total, pair_blocks(k[at, :], v[at, :], 0))
    store_pieces(total, pieces, scratch)


def intra_kernel(q, k, v, intra, states, q_t):
    keep = causal()
    cols = q.shape[1]
    q_t[...] = q[...].T
    for h in range(cols // HEAD_DIM):
        part = head_slice(h)
        state = None
        for n, at in enumerate(chunk_slices(q.shape[0])):
            qi, ki, vi = q[at, part], k[at, part], v[at, part]
            scores = jnp.where(keep, dot(qi, ki, 1, 1), 0.0).astype(BF16)
            out = dot(scores, vi, 1, 0)
            if n:
                out = out + dot(qi, state.astype(BF16), 1, 0)
                states[(n - 1) * cols + part.start : (n - 1) * cols + part.stop, :] = state
            intra[at, part] = out
            new = dot(ki, vi, 0, 0)
            state = state + new if n else new


def row_sums(tile):
    return jnp.sum(tile.T, axis=0, keepdims=True)


def mixed_kernel(intra, q, g, *refs):
    pieces, (mixed, stats, prefix) = refs[:QUAD], refs[QUAD:]
    load_pieces(pieces, prefix)
    blocks = q.shape[0] // HEAD_DIM
    for at in chunk_slices(q.shape[0]):
        square = cross = None
        for h in range(q.shape[1] // HEAD_DIM):
            part = head_slice(h)
            m = intra[at, part] + dot(q[at, part], prefix[part, :], 1, 0)
            mixed[at, part] = m
            s, c = m * m, m * g[at, part].astype(F32)
            square = s if square is None else square + s
            cross = c if cross is None else cross + c
        for n in range(CHUNK // HEAD_DIM):
            i = at.start // HEAD_DIM + n
            stats[i : i + 1, :] = row_sums(square[head_slice(n)])
            stats[blocks + i : blocks + i + 1, :] = row_sums(cross[head_slice(n)])


def norm_kernel(width, mixed, q_t, g, *refs):
    stats, (gm, inverse_out, states, *pieces, scratch) = refs[: -4 - QUAD], refs[-4 - QUAD :]
    total = stats[0][...]
    for r in stats[1:]:
        total = total + r[...]
    rows, cols = mixed.shape
    blocks = rows // HEAD_DIM
    inverse = lax.rsqrt(total[:blocks] / width + EPSILON)
    cross_mean = total[blocks:] * inverse / width
    scale = inverse * inverse * cross_mean
    inverse_out[...] = inverse
    shape = (HEAD_DIM, HEAD_DIM)
    after = None
    for n, at in reversed(list(enumerate(chunk_slices(rows)))):
        for i in range(at.start // HEAD_DIM, at.stop // HEAD_DIM):
            block = head_slice(i)
            a = jnp.broadcast_to(inverse[i : i + 1], shape).T
            b = jnp.broadcast_to(scale[i : i + 1], shape).T
            for h in range(cols // HEAD_DIM):
                part = head_slice(h)
                grad = g[block, part].astype(F32)
                gm[block, part] = (grad * a - mixed[block, part] * b).astype(BF16)
        after = add_all(after, pair_blocks(q_t[:, at], gm[at, :], 1))
        if n:
            for h, state in enumerate(after):
                first = (n - 1) * cols + h * HEAD_DIM
                states[first : first + HEAD_DIM, :] = state
    store_pieces(after, pieces, scratch)


def head_grads(h, q, k, v, gm, prefix, states, after, gq, gk, gv):
    cols, part = q.shape[1], head_slice(h)
    keep, keep_t = causal(), causal(True)
    chunks = chunk_slices(q.shape[0])
    first = prefix[part, :].astype(F32)
    for n, at in enumerate(chunks):
        qi, ki, vi, gi = q[at, part], k[at, part], v[at, part], gm[at, part]
        scores_t = jnp.where(keep_t, dot(ki, qi, 1, 1), 0.0).astype(BF16)
        grad_scores = jnp.where(keep, dot(gi, vi, 1, 1), 0.0).astype(BF16)
        grad_scores_t = jnp.where(keep_t, dot(vi, gi, 1, 1), 0.0).astype(BF16)
        entering = first
        if n:
            entering = first + states[pl.ds((n - 1) * cols + part.start, HEAD_DIM), :]
        gq_i = dot(grad_scores, ki, 1, 0) + dot(gi, entering.astype(BF16), 1, 1)
        gk_i = dot(grad_scores_t, qi, 1, 0)
        gv_i = dot(scores_t, gi, 1, 0)
        if n < len(chunks) - 1:
            later = after[pl.ds(n * cols + part.start, HEAD_DIM), :].astype(BF16)
            gk_i = gk_i + dot(vi, later, 1, 1)
            gv_i = gv_i + dot(ki, later, 1, 0)
        gq[at, :] = gq_i.astype(BF16)
        gk[at, :] = gk_i
        gv[at, :] = gv_i


def grads_kernel(heads, q, k, v, gm, prefix, states, after, *refs):
    count = len(heads)
    outs = refs[-3 * count :]
    gqs, gks, gvs = (outs[i * count : (i + 1) * count] for i in range(3))
    for j, h in enumerate(heads):
        head_grads(h, q, k, v, gm, prefix, states, after, gqs[j], gks[j], gvs[j])


def output_kernel(mixed, inverse, *refs):
    (gqs, (out, gq)) = refs[:QUAD], refs[-2:]
    shape = (HEAD_DIM, HEAD_DIM)
    for i in range(mixed.shape[0] // HEAD_DIM):
        a = jnp.broadcast_to(inverse[i : i + 1, :], shape).T
        for h in range(mixed.shape[1] // HEAD_DIM):
            out[head_slice(i), head_slice(h)] = (
                mixed[head_slice(i), head_slice(h)] * a
            ).astype(BF16)
    for h in range(QUAD):
        gq[:, head_slice(h)] = gqs[h][...]


def last_kernel(k, v, *refs):
    gks, gvs, pieces = (refs[i * QUAD : (i + 1) * QUAD] for i in range(3))
    gk_hbm, gv_hbm, gk, gv, suffix, sems = refs[-6:]
    load_pieces(pieces, suffix)
    copies = []
    for n, at in enumerate(chunk_slices(k.shape[0])):
        for h in range(QUAD):
            part = head_slice(h)
            state = suffix[part, :]
            gk[at, part] = (gks[h][at, :] + dot(v[at, part], state, 1, 1)).astype(BF16)
            gv[at, part] = (gvs[h][at, :] + dot(k[at, part], state, 1, 0)).astype(BF16)
        for j, (src, dst) in enumerate(((gk, gk_hbm), (gv, gv_hbm))):
            copies.append(pltpu.make_async_copy(src.at[at], dst.at[at], sems.at[j, n]))
            copies[-1].start()
    for copy in copies:
        copy.wait()


def all_parts(value, axis, size):
    power = size & (size - 1) == 0
    parts = [value]
    for by in reversed(range(1, size)):
        pairs = [(i, i ^ by if power else (i + by) % size) for i in range(size)]
        parts.append(lax.ppermute(value, axis, pairs))
    return parts


def shards(sizes, queries, keys, values, grad_out):
    seq, head_size = sizes
    rows, cols = queries.shape
    chunks = rows // CHUNK
    blocks = rows // HEAD_DIM
    scan = quad_scan if seq == 2 * QUAD else doubling_scan

    def shape(count, lanes, kind=F32):
        return jax.ShapeDtypeStruct((count, lanes), kind)

    wide, narrow = shape(rows, cols), shape(rows, cols, BF16)
    head_wide, head_narrow = shape(rows, HEAD_DIM), shape(rows, HEAD_DIM, BF16)
    pieces_shape = [shape(HEAD_DIM, HEAD_DIM)] * QUAD
    states_shape = shape((chunks - 1) * cols, HEAD_DIM)
    pieces_scratch = pltpu.VMEM((cols, HEAD_DIM), F32)
    head_flops = 2 * rows * HEAD_DIM * HEAD_DIM
    chunk_flops = 2 * rows * CHUNK * HEAD_DIM

    *pieces, keys, values = call(
        state_kernel,
        pieces_shape + [pltpu.VMEM((rows, cols), BF16)] * 2,
        [pltpu.with_memory_space_constraint(a, pltpu.HBM) for a in (keys, values)],
        QUAD * head_flops,
        "local_state",
        spaces={0: pltpu.HBM, 1: pltpu.HBM},
        scratch=[pieces_scratch, pltpu.SemaphoreType.DMA((2, chunks))],
    )

    def forward(phase, token):
        if phase:
            return []
        return call(
            intra_kernel,
            [wide, states_shape, shape(cols, rows, BF16)],
            [queries, keys, values],
            QUAD * (2 * chunk_flops + 2 * head_flops),
            "intra",
        )

    prefixes, (intra, states, queries_t) = scan(pieces, seq, False, forward)
    mixed, stats, prefix = call(
        mixed_kernel,
        [wide, shape(2 * blocks, HEAD_DIM), shape(cols, HEAD_DIM, BF16)],
        [intra, queries, grad_out, *prefixes],
        QUAD * head_flops,
        "mixed",
    )
    gm, inverse, after, *pieces = call(
        functools.partial(norm_kernel, cols * head_size),
        [narrow, shape(blocks, HEAD_DIM), states_shape] + pieces_shape,
        [mixed, queries_t, grad_out, *all_parts(stats, "head", head_size)],
        QUAD * head_flops,
        "norm",
        scratch=[pieces_scratch],
    )
    gqs, gks, gvs = [], [], []

    def backward(phase, token):
        heads = ((0,), (1, 2), (3,))[phase]
        count = len(heads)
        args = [queries, keys, values, gm, prefix, states, after]
        done = call(
            functools.partial(grads_kernel, heads),
            [head_narrow] * count + [head_wide] * (2 * count),
            args + ([] if token is None else [token]),
            count * (6 * chunk_flops + 3 * head_flops),
            "grads",
            spaces={len(args): pl.ANY},
        )
        gqs.extend(done[:count])
        gks.extend(done[count : 2 * count])
        gvs.extend(done[2 * count :])
        if phase == 2:
            done += call(
                output_kernel,
                [narrow, narrow],
                [mixed, inverse, *gqs],
                0,
                "outputs",
            )
        return done

    suffixes, done = scan(pieces, seq, True, backward)
    output, grad_q = done[-2:]
    grad_k, grad_v = call(
        last_kernel,
        [narrow, narrow],
        [keys, values, *gks, *gvs, *suffixes],
        2 * QUAD * head_flops,
        "last",
        outs={0: pl.ANY, 1: pl.ANY},
        scratch=[pltpu.VMEM((rows, cols), BF16)] * 2
        + [pltpu.VMEM((cols, HEAD_DIM), BF16), pltpu.SemaphoreType.DMA((2, chunks))],
    )
    return output, grad_q, grad_k, grad_v


def solution(mesh):
    sizes = (mesh.shape["seq"], mesh.shape["head"])
    spec = P("seq", "head")
    return jax.shard_map(
        functools.partial(shards, sizes),
        mesh=mesh,
        in_specs=(spec,) * 4,
        out_specs=(spec,) * 4,
        check_vma=False,
    )
```

time: 175 us -> 53.3 us (0.30)
  waiting for transfers between devices: 72.3 us -> 16 us
  matrix products: 35.2 us -> 0 us
  starting transfers between devices: 0.08 us -> 22.3 us
  other arithmetic: 21.7 us -> 0 us
  local copies, waits for them, and re-layouts: 18.2 us -> 0.01 us
  Pallas kernels: 0 us -> 14.1 us
  between operations: 14.2 us -> 0.74 us
  blocking collectives: 12.2 us -> 0 us
    all_gather x2 -> x0, waiting for transfers between devices: 72.2 us -> none  [entering(): everything = lax.all_gather(shard, axis)]
    dot_general x12 -> x0, matrix products: 35.2 us -> none  [the longest x2 6.87 us: masked_scores(): jnp.einsum('thd,shd->hts', query_side, key_side, preferred_element_type=j...]
    ppermute x0 -> x17, starting transfers between devices: none -> 22.3 us  [the longest x14 20.4 us: exchange(): return lax.ppermute(value, 'seq', [(i, i ^ by) for i in range(size)])]
    select_n x16 -> x0, other arithmetic: 16.6 us -> none  [step(): return jnp.where(reached, new, before)]
    ppermute x0 -> x17, waiting for transfers between devices: none -> 16 us  [the longest x14 13.2 us: exchange(): return lax.ppermute(value, 'seq', [(i, i ^ by) for i in range(size)])]
    pallas_call x0 -> x13, Pallas kernels: none -> 14.1 us  [call(): return list(kernel(*args))]
    psum x2 -> x0, blocking collectives: 12.2 us -> none  [the longest x1 6.61 us: shards(): crossed = lax.psum(jnp.sum(grad_float * normed, axis=1), 'head')]
    unnamed x25 -> x4, local copies, waits for them, and re-layouts: 11.5 us -> 0.01 us
  transfers between devices with their start and end apart: 2 -> 17, of which waited for: 2 -> 11; matrix products, arithmetic and copies ran while one was open for 13% -> 0% of each run, Pallas kernels for 0% -> 16%
where the time goes in v6:
time: 53.3 us; the launch traced here: 53.1 us
  starting transfers between devices  22.3 us (42%)
  waiting for transfers between devices  16 us (30%)
  Pallas kernels  14.1 us (26%)
  between operations  0.74 us (1%)
    ppermute x14, starting transfers between devices, exchange(): return lax.ppermute(value, 'seq', [(i, i ^ by) for i in range(size)])  20.4 us
    pallas_call x13, Pallas kernels, call(): return list(kernel(*args))  14.1 us
    ppermute x14, waiting for transfers between devices, exchange(): return lax.ppermute(value, 'seq', [(i, i ^ by) for i in range(size)])  13.2 us
    ppermute x3, waiting for transfers between devices, all_parts(): parts.append(lax.ppermute(value, axis, pairs))  2.8 us
    ppermute x3, starting transfers between devices, all_parts(): parts.append(lax.ppermute(value, axis, pairs))  1.93 us
  transfers between devices with their start and end apart: 17, of which 11 were waited for; matrix products, arithmetic and copies ran while one was open for 0% of the time, Pallas kernels for 16%

profile of v6, /device:TPU:0, one launch (start us, length us, event | category | flops | bytes accessed | tf_op | source)
XLA Modules:
  0.0 53.1 jit_solution(5048038519797335005)
XLA Ops:
  0.6 0.0 copy-start
  0.6 2.0 %local_state.1 = (f32[128,128]{1,0:T(8,128)S(1)}, f32[128,128]{1,0:T(8,128)S(1)}, f32[128,128]{1,0:T(8,128)S(1)}, f32[128,128]{1,0:T(8,128)S(1)}, bf16[1024,512]...) custom-call(bf16[1024,512]{1,0:T(8,128)(2,1)} %k_hbm.1, bf16[1024,512]{1,0:T(8,128)(2,1)} %v_hbm.1), custom_call_target="tpu_custom_call" | custom-call | flops 134217728 | bytes 4456448 | tf_op jit(solution)/shard_map/local_state/pallas_call | solution.py:56
  2.6 3.0 %collective-permute-start = (f32[128,128]{1,0:T(8,128)S(1)}, f32[128,128]{1,0:T(8,128)S(1)}, u32[]{:S(2)}, u32[]{:S(2)}) collective-permute-start(f32[128,128]{1,0:T(8,128)S(1)} %get-tuple-element.51), channel_id=1, source_target_pairs={{0,4},{4,0},{8,12},{12,8},{16,20},{20,16},{24,28},{28,24},{1,5},{5... | collective-permute-start | bytes 196616 | tf_op jit(solution)/shard_map/ppermute | solution.py:65
  5.6 1.6 %collective-permute-start.1 = (f32[128,128]{1,0:T(8,128)S(1)}, f32[128,128]{1,0:T(8,128)S(1)}, u32[]{:S(2)}, u32[]{:S(2)}) collective-permute-start(f32[128,128]{1,0:T(8,128)S(1)} %get-tuple-element.52), channel_id=1, source_target_pairs={{0,8},{4,12},{8,0},{12,4},{16,24},{20,28},{24,16},{28,20},{1,9},{5... | collective-permute-start | bytes 196616 | tf_op jit(solution)/shard_map/ppermute | solution.py:65
  7.2 0.0 collective-permute-start.2
  7.2 0.0 copy-done
  7.2 0.0 copy-start.1
  7.2 1.9 %intra.1 = (f32[1024,512]{1,0:T(8,128)S(1)}, f32[1536,128]{1,0:T(8,128)S(1)}, bf16[512,1024]{1,0:T(8,128)(2,1)S(1)}) custom-call(bf16[1024,512]{1,0:T(8,128)(2,1)S(1)} %copy-done, bf16[1024,512]{1,0:T(8,128)(2,1)S(1)} %get-tuple-element.47.k, bf16[1024,512]{1,0:T(8,128)(2,1)S(1)} %get-tuple-element.48.v), custom_call_target="tpu_custom_call" | custom-call | flops 805306368 | bytes 7077888 | tf_op jit(solution)/shard_map/intra/pallas_call | solution.py:56
  9.1 0.0 collective-permute-done.piece1
  9.1 1.3 %collective-permute-done.1.piece2 = f32[128,128]{1,0:T(8,128)S(1)} collective-permute-done((f32[128,128]{1,0:T(8,128)S(1)}, f32[128,128]{1,0:T(8,128)S(1)}, u32[]{:S(2)}, u32[]{:S(2)}) %collective-permute-start.1) | collective-permute-done | bytes 65568 | tf_op jit(solution)/shard_map/ppermute | solution.py:65
  10.4 1.9 %collective-permute-done.2.piece3 = f32[128,128]{1,0:T(8,128)S(1)} collective-permute-done((f32[128,128]{1,0:T(8,128)S(1)}, f32[128,128]{1,0:T(8,128)S(1)}, u32[]{:S(2)}, u32[]{:S(2)}) %collective-permute-start.2) | collective-permute-done | bytes 65568 | tf_op jit(solution)/shard_map/ppermute | solution.py:65
  12.4 2.7 %collective-permute-start.3 = (f32[128,128]{1,0:T(8,128)S(1)}, f32[128,128]{1,0:T(8,128)S(1)}, u32[]{:S(2)}, u32[]{:S(2)}) collective-permute-start(f32[128,128]{1,0:T(8,128)S(1)} %quad_sum.2), channel_id=1, source_target_pairs={{0,16},{4,20},{8,24},{12,28},{16,0},{20,4},{24,8},{28,12},{1,17},{... | collective-permute-start | bytes 196616 | tf_op jit(solution)/shard_map/ppermute | solution.py:65
  15.0 3.2 %collective-permute-done.3.far = f32[128,128]{1,0:T(8,128)S(1)} collective-permute-done((f32[128,128]{1,0:T(8,128)S(1)}, f32[128,128]{1,0:T(8,128)S(1)}, u32[]{:S(2)}, u32[]{:S(2)}) %collective-permute-start.3) | collective-permute-done | bytes 65568 | tf_op jit(solution)/shard_map/ppermute | solution.py:65
  18.2 0.1 finish.2
  18.3 0.7 %collective-permute-start.4 = (f32[128,128]{1,0:T(8,128)S(1)}, f32[128,128]{1,0:T(8,128)S(1)}, u32[]{:S(2)}, u32[]{:S(2)}) collective-permute-start(f32[128,128]{1,0:T(8,128)S(1)} %get-tuple-element.56), channel_id=1, source_target_pairs={{0,4},{4,0},{8,12},{12,8},{16,20},{20,16},{24,28},{28,24},{1,5},{5... | collective-permute-start | bytes 196616 | tf_op jit(solution)/shard_map/ppermute | solution.py:65
  19.0 0.1 collective-permute-start.5
  19.1 2.7 %collective-permute-start.6 = (f32[128,128]{1,0:T(8,128)S(1)}, f32[128,128]{1,0:T(8,128)S(1)}, u32[]{:S(2)}, u32[]{:S(2)}) collective-permute-start(f32[128,128]{1,0:T(8,128)S(1)} %get-tuple-element.58), channel_id=1, source_target_pairs={{0,12},{4,8},{8,4},{12,0},{16,28},{20,24},{24,20},{28,16},{1,13},{... | collective-permute-start | bytes 196616 | tf_op jit(solution)/shard_map/ppermute | solution.py:65
  21.8 0.8 %collective-permute-done.4.refs_1_ = f32[128,128]{1,0:T(8,128)S(1)} collective-permute-done((f32[128,128]{1,0:T(8,128)S(1)}, f32[128,128]{1,0:T(8,128)S(1)}, u32[]{:S(2)}, u32[]{:S(2)}) %collective-permute-start.4) | collective-permute-done | bytes 65568 | tf_op jit(solution)/shard_map/ppermute | solution.py:65
  22.6 0.6 %collective-permute-done.5.refs_2_ = f32[128,128]{1,0:T(8,128)S(1)} collective-permute-done((f32[128,128]{1,0:T(8,128)S(1)}, f32[128,128]{1,0:T(8,128)S(1)}, u32[]{:S(2)}, u32[]{:S(2)}) %collective-permute-start.5) | collective-permute-done | bytes 65568 | tf_op jit(solution)/shard_map/ppermute | solution.py:65
  23.2 1.5 %collective-permute-done.6.refs_3_ = f32[128,128]{1,0:T(8,128)S(1)} collective-permute-done((f32[128,128]{1,0:T(8,128)S(1)}, f32[128,128]{1,0:T(8,128)S(1)}, u32[]{:S(2)}, u32[]{:S(2)}) %collective-permute-start.6) | collective-permute-done | bytes 65568 | tf_op jit(solution)/shard_map/ppermute | solution.py:65
  24.8 0.0 copy-done.1
  24.8 0.7 %mixed.1 = (f32[1024,512]{1,0:T(8,128)S(1)}, f32[16,128]{1,0:T(8,128)S(1)}, bf16[512,128]{1,0:T(8,128)(2,1)S(1)}) custom-call(f32[1024,512]{1,0:T(8,128)S(1)} %get-tuple-element.49.intra, bf16[1024,512]{1,0:T(8,128)(2,1)S(1)} %copy-done, bf16[1024,512]{1,0:T(8,128)(2,1)S(1)} %copy-done.1, f32[128,128]{1,0:T(8,128)S(1)} %get-tuple-element.55.refs_0_, ...), custom_call_target="tpu_custom_call" | custom-call | flops 134217728 | bytes 6692864 | tf_op jit(solution)/shard_map/mixed/pallas_call | solution.py:56
  25.5 0.1 collective-permute-start.9
  25.6 1.6 %collective-permute-start.8 = (f32[16,128]{1,0:T(8,128)S(1)}, f32[16,128]{1,0:T(8,128)S(1)}, u32[]{:S(2)}, u32[]{:S(2)}) collective-permute-start(f32[16,128]{1,0:T(8,128)S(1)} %get-tuple-element.60.refs_0_), channel_id=1, source_target_pairs={{0,2},{1,3},{2,0},{3,1},{4,6},{5,7},{6,4},{7,5},{8,10},{9,11},{10,... | collective-permute-start | bytes 24584 | tf_op jit(solution)/shard_map/ppermute | solution.py:316
  27.2 0.3 collective-permute-start.7
  27.5 0.0 collective-permute-done.9.refs_3_
  27.5 1.9 %collective-permute-done.8.refs_2_ = f32[16,128]{1,0:T(8,128)S(1)} collective-permute-done((f32[16,128]{1,0:T(8,128)S(1)}, f32[16,128]{1,0:T(8,128)S(1)}, u32[]{:S(2)}, u32[]{:S(2)}) %collective-permute-start.8) | collective-permute-done | bytes 8224 | tf_op jit(solution)/shard_map/ppermute | solution.py:316
  29.3 0.9 %collective-permute-done.7.refs_1_ = f32[16,128]{1,0:T(8,128)S(1)} collective-permute-done((f32[16,128]{1,0:T(8,128)S(1)}, f32[16,128]{1,0:T(8,128)S(1)}, u32[]{:S(2)}, u32[]{:S(2)}) %collective-permute-start.7) | collective-permute-done | bytes 8224 | tf_op jit(solution)/shard_map/ppermute | solution.py:316
  30.3 0.8 %norm.1 = (bf16[1024,512]{1,0:T(8,128)(2,1)S(1)}, f32[8,128]{1,0:T(8,128)S(1)}, f32[1536,128]{1,0:T(8,128)S(1)}, f32[128,128]{1,0:T(8,128)S(1)}, f32[128,128]{1,...) custom-call(f32[1024,512]{1,0:T(8,128)S(1)} %get-tuple-element.59.mixed, ...), custom_call_target="tpu_custom_call" | custom-call | flops 134217728 | bytes 6328320 | tf_op jit(solution)/shard_map/norm/pallas_call | solution.py:56
  31.0 0.8 %collective-permute-start.10 = (f32[128,128]{1,0:T(8,128)S(1)}, f32[128,128]{1,0:T(8,128)S(1)}, u32[]{:S(2)}, u32[]{:S(2)}) collective-permute-start(f32[128,128]{1,0:T(8,128)S(1)} %get-tuple-element.68), channel_id=1, source_target_pairs={{0,4},{4,0},{8,12},{12,8},{16,20},{20,16},{24,28},{28,24},{1,5},{5... | collective-permute-start | bytes 196616 | tf_op jit(solution)/shard_map/ppermute | solution.py:65
  31.9 2.0 %collective-permute-start.11 = (f32[128,128]{1,0:T(8,128)S(1)}, f32[128,128]{1,0:T(8,128)S(1)}, u32[]{:S(2)}, u32[]{:S(2)}) collective-permute-start(f32[128,128]{1,0:T(8,128)S(1)} %get-tuple-element.69), channel_id=1, source_target_pairs={{0,8},{4,12},{8,0},{12,4},{16,24},{20,28},{24,16},{28,20},{1,9},{5... | collective-permute-start | bytes 196616 | tf_op jit(solution)/shard_map/ppermute | solution.py:65
  33.9 0.7 %collective-permute-start.12 = (f32[128,128]{1,0:T(8,128)S(1)}, f32[128,128]{1,0:T(8,128)S(1)}, u32[]{:S(2)}, u32[]{:S(2)}) collective-permute-start(f32[128,128]{1,0:T(8,128)S(1)} %get-tuple-element.70), channel_id=1, source_target_pairs={{0,12},{4,8},{8,4},{12,0},{16,28},{20,24},{24,20},{28,16},{1,13},{... | collective-permute-start | bytes 196616 | tf_op jit(solution)/shard_map/ppermute | solution.py:65
  34.6 1.3 %grads.3 = (bf16[1024,128]{1,0:T(8,128)(2,1)S(1)}, f32[1024,128]{1,0:T(8,128)S(1)}, f32[1024,128]{1,0:T(8,128)S(1)}) custom-call(bf16[1024,512]{1,0:T(8,128)(2,1)S(1)} %copy-done, bf16[1024,512]{1,0:T(8,128)(2,1)S(1)} %get-tuple-element.47.k, bf16[1024,512]{1,0:T(8,128)(2,1)S(1)} %get-tuple-element.48.v, bf16[1024,512]{1,0:T(8,128)(2,1)S(1)} %get-tuple-element.62.gm, ...), custom_call_target="tpu_custom_call" | custom-call | flops 503316480 | bytes 7208960 | tf_op jit(solution)/shard_map/grads/pallas_call | solution.py:56
  35.9 0.0 collective-permute-done.10.piece1
  36.0 0.2 collective-permute-done.11.piece2
  36.2 2.9 %collective-permute-done.12.piece3 = f32[128,128]{1,0:T(8,128)S(1)} collective-permute-done((f32[128,128]{1,0:T(8,128)S(1)}, f32[128,128]{1,0:T(8,128)S(1)}, u32[]{:S(2)}, u32[]{:S(2)}) %collective-permute-start.12) | collective-permute-done | bytes 65568 | tf_op jit(solution)/shard_map/ppermute | solution.py:65
  39.1 2.4 %collective-permute-start.13 = (f32[128,128]{1,0:T(8,128)S(1)}, f32[128,128]{1,0:T(8,128)S(1)}, u32[]{:S(2)}, u32[]{:S(2)}) collective-permute-start(f32[128,128]{1,0:T(8,128)S(1)} %quad_sum.3.refs_0_), channel_id=1, source_target_pairs={{0,16},{4,20},{8,24},{12,28},{16,0},{20,4},{24,8},{28,12},{1,17},{... | collective-permute-start | bytes 196616 | tf_op jit(solution)/shard_map/ppermute | solution.py:65
  41.6 2.5 %grads.4 = (bf16[1024,128]{1,0:T(8,128)(2,1)S(1)}, bf16[1024,128]{1,0:T(8,128)(2,1)S(1)}, f32[1024,128]{1,0:T(8,128)S(1)}, f32[1024,128]{1,0:T(8,128)S(1)}, f32[...) custom-call(bf16[1024,512]{1,0:T(8,128)(2,1)S(1)} %copy-done, bf16[1024,512]{1,0:T(8,128)(2,1)S(1)} %get-tuple-element.47.k, ...), custom_call_target="tpu_custom_call" | custom-call | flops 1006632960 | bytes 8585216 | tf_op jit(solution)/shard_map/grads/pallas_call | solution.py:56
  44.0 0.8 %collective-permute-done.13.far = f32[128,128]{1,0:T(8,128)S(1)} collective-permute-done((f32[128,128]{1,0:T(8,128)S(1)}, f32[128,128]{1,0:T(8,128)S(1)}, u32[]{:S(2)}, u32[]{:S(2)}) %collective-permute-start.13) | collective-permute-done | bytes 65568 | tf_op jit(solution)/shard_map/ppermute | solution.py:65
  44.8 0.1 finish.3
  44.9 0.9 %collective-permute-start.14 = (f32[128,128]{1,0:T(8,128)S(1)}, f32[128,128]{1,0:T(8,128)S(1)}, u32[]{:S(2)}, u32[]{:S(2)}) collective-permute-start(f32[128,128]{1,0:T(8,128)S(1)} %get-tuple-element.85), channel_id=1, source_target_pairs={{0,4},{4,0},{8,12},{12,8},{16,20},{20,16},{24,28},{28,24},{1,5},{5... | collective-permute-start | bytes 196616 | tf_op jit(solution)/shard_map/ppermute | solution.py:65
  45.8 0.4 collective-permute-start.15
  46.2 2.3 %collective-permute-start.16 = (f32[128,128]{1,0:T(8,128)S(1)}, f32[128,128]{1,0:T(8,128)S(1)}, u32[]{:S(2)}, u32[]{:S(2)}) collective-permute-start(f32[128,128]{1,0:T(8,128)S(1)} %get-tuple-element.87), channel_id=1, source_target_pairs={{0,12},{4,8},{8,4},{12,0},{16,28},{20,24},{24,20},{28,16},{1,13},{... | collective-permute-start | bytes 196616 | tf_op jit(solution)/shard_map/ppermute | solution.py:65
  48.4 1.3 %grads.5 = (bf16[1024,128]{1,0:T(8,128)(2,1)S(1)}, f32[1024,128]{1,0:T(8,128)S(1)}, f32[1024,128]{1,0:T(8,128)S(1)}) custom-call(bf16[1024,512]{1,0:T(8,128)(2,1)S(1)} %copy-done, bf16[1024,512]{1,0:T(8,128)(2,1)S(1)} %get-tuple-element.47.k, bf16[1024,512]{1,0:T(8,128)(2,1)S(1)} %get-tuple-element.48.v, bf16[1024,512]{1,0:T(8,128)(2,1)S(1)} %get-tuple-element.62.gm, ...), custom_call_target="tpu_custom_call" | custom-call | flops 503316480 | bytes 7274496 | tf_op jit(solution)/shard_map/grads/pallas_call | solution.py:56
  49.8 1.7 %outputs.1 = (bf16[1024,512]{1,0:T(8,128)(2,1)}, bf16[1024,512]{1,0:T(8,128)(2,1)}) custom-call(f32[1024,512]{1,0:T(8,128)S(1)} %get-tuple-element.59.mixed, f32[8,128]{1,0:T(8,128)S(1)} %get-tuple-element.61.inverse, bf16[1024,128]{1,0:T(8,128)(2,1)S(1)} %get-tuple-element.66.refs_0_, bf16[1024,128]{1,0:T(8,128)(2,1)S(1)} %get-tuple-element.72.refs_1_, ...), custom_call_target="tpu_custom_call" | custom-call | bytes 5246976 | tf_op jit(solution)/shard_map/outputs/pallas_call | solution.py:56
  51.4 0.0 collective-permute-done.14.refs_9_
  51.4 0.0 collective-permute-done.15.refs_10_
  51.4 0.0 collective-permute-done.16.refs_11_
  51.5 1.7 %last.1 = (bf16[1024,512]{1,0:T(8,128)(2,1)}, bf16[1024,512]{1,0:T(8,128)(2,1)}) custom-call(bf16[1024,512]{1,0:T(8,128)(2,1)S(1)} %get-tuple-element.47.k, bf16[1024,512]{1,0:T(8,128)(2,1)S(1)} %get-tuple-element.48.v, f32[1024,128]{1,0:T(8,128)S(1)} %get-tuple-element.79.refs_0_, f32[1024,128]{1,0:T(8,128)S(1)} %get-tuple-element.80.refs_1_, ...), custom_call_target="tpu_custom_call" | custom-call | flops 268435456 | bytes 8650752 | tf_op jit(solution)/shard_map/last/pallas_call | solution.py:56
  (2 shorter events, 0.0 us)
Async XLA Ops:
  0.6 6.6 %copy-start = (bf16[1024,512]{1,0:T(8,128)(2,1)S(1)}, bf16[1024,512]{1,0:T(8,128)(2,1)}, u32[]{:S(2)}) copy-start(bf16[1024,512]{1,0:T(8,128)(2,1)} %q.9) | copy-start | bytes 3145732
  2.6 6.5 %collective-permute-start = (f32[128,128]{1,0:T(8,128)S(1)}, f32[128,128]{1,0:T(8,128)S(1)}, u32[]{:S(2)}, u32[]{:S(2)}) collective-permute-start(f32[128,128]{1,0:T(8,128)S(1)} %get-tuple-element.51), channel_id=1, source_target_pairs={{0,4},{4,0},{8,12},{12,8},{16,20},{20,16},{24,28},{28,24},{1,5},{5... | collective-permute-start | bytes 196616 | tf_op jit(solution)/shard_map/ppermute | solution.py:65
  5.6 4.8 %collective-permute-start.1 = (f32[128,128]{1,0:T(8,128)S(1)}, f32[128,128]{1,0:T(8,128)S(1)}, u32[]{:S(2)}, u32[]{:S(2)}) collective-permute-start(f32[128,128]{1,0:T(8,128)S(1)} %get-tuple-element.52), channel_id=1, source_target_pairs={{0,8},{4,12},{8,0},{12,4},{16,24},{20,28},{24,16},{28,20},{1,9},{5... | collective-permute-start | bytes 196616 | tf_op jit(solution)/shard_map/ppermute | solution.py:65
  7.2 5.2 %collective-permute-start.2 = (f32[128,128]{1,0:T(8,128)S(1)}, f32[128,128]{1,0:T(8,128)S(1)}, u32[]{:S(2)}, u32[]{:S(2)}) collective-permute-start(f32[128,128]{1,0:T(8,128)S(1)} %get-tuple-element.53), channel_id=1, source_target_pairs={{0,12},{4,8},{8,4},{12,0},{16,28},{20,24},{24,20},{28,16},{1,13},{... | collective-permute-start | bytes 196616 | tf_op jit(solution)/shard_map/ppermute | solution.py:65
  7.2 17.6 %copy-start.1 = (bf16[1024,512]{1,0:T(8,128)(2,1)S(1)}, bf16[1024,512]{1,0:T(8,128)(2,1)}, u32[]{:S(2)}) copy-start(bf16[1024,512]{1,0:T(8,128)(2,1)} %g.3) | copy-start | bytes 3145732
  12.4 5.8 %collective-permute-start.3 = (f32[128,128]{1,0:T(8,128)S(1)}, f32[128,128]{1,0:T(8,128)S(1)}, u32[]{:S(2)}, u32[]{:S(2)}) collective-permute-start(f32[128,128]{1,0:T(8,128)S(1)} %quad_sum.2), channel_id=1, source_target_pairs={{0,16},{4,20},{8,24},{12,28},{16,0},{20,4},{24,8},{28,12},{1,17},{... | collective-permute-start | bytes 196616 | tf_op jit(solution)/shard_map/ppermute | solution.py:65
  18.3 4.3 %collective-permute-start.4 = (f32[128,128]{1,0:T(8,128)S(1)}, f32[128,128]{1,0:T(8,128)S(1)}, u32[]{:S(2)}, u32[]{:S(2)}) collective-permute-start(f32[128,128]{1,0:T(8,128)S(1)} %get-tuple-element.56), channel_id=1, source_target_pairs={{0,4},{4,0},{8,12},{12,8},{16,20},{20,16},{24,28},{28,24},{1,5},{5... | collective-permute-start | bytes 196616 | tf_op jit(solution)/shard_map/ppermute | solution.py:65
  19.0 4.3 %collective-permute-start.5 = (f32[128,128]{1,0:T(8,128)S(1)}, f32[128,128]{1,0:T(8,128)S(1)}, u32[]{:S(2)}, u32[]{:S(2)}) collective-permute-start(f32[128,128]{1,0:T(8,128)S(1)} %get-tuple-element.57), channel_id=1, source_target_pairs={{0,8},{4,12},{8,0},{12,4},{16,24},{20,28},{24,16},{28,20},{1,9},{5... | collective-permute-start | bytes 196616 | tf_op jit(solution)/shard_map/ppermute | solution.py:65
  19.1 5.7 %collective-permute-start.6 = (f32[128,128]{1,0:T(8,128)S(1)}, f32[128,128]{1,0:T(8,128)S(1)}, u32[]{:S(2)}, u32[]{:S(2)}) collective-permute-start(f32[128,128]{1,0:T(8,128)S(1)} %get-tuple-element.58), channel_id=1, source_target_pairs={{0,12},{4,8},{8,4},{12,0},{16,28},{20,24},{24,20},{28,16},{1,13},{... | collective-permute-start | bytes 196616 | tf_op jit(solution)/shard_map/ppermute | solution.py:65
  25.5 1.9 %collective-permute-start.9 = (f32[16,128]{1,0:T(8,128)S(1)}, f32[16,128]{1,0:T(8,128)S(1)}, u32[]{:S(2)}, u32[]{:S(2)}) collective-permute-start(f32[16,128]{1,0:T(8,128)S(1)} %get-tuple-element.60.refs_0_), channel_id=1, source_target_pairs={{0,1},{1,0},{2,3},{3,2},{4,5},{5,4},{6,7},{7,6},{8,9},{9,8},{10,11... | collective-permute-start | bytes 24584 | tf_op jit(solution)/shard_map/ppermute | solution.py:316
  25.6 3.7 %collective-permute-start.8 = (f32[16,128]{1,0:T(8,128)S(1)}, f32[16,128]{1,0:T(8,128)S(1)}, u32[]{:S(2)}, u32[]{:S(2)}) collective-permute-start(f32[16,128]{1,0:T(8,128)S(1)} %get-tuple-element.60.refs_0_), channel_id=1, source_target_pairs={{0,2},{1,3},{2,0},{3,1},{4,6},{5,7},{6,4},{7,5},{8,10},{9,11},{10,... | collective-permute-start | bytes 24584 | tf_op jit(solution)/shard_map/ppermute | solution.py:316
  27.2 3.1 %collective-permute-start.7 = (f32[16,128]{1,0:T(8,128)S(1)}, f32[16,128]{1,0:T(8,128)S(1)}, u32[]{:S(2)}, u32[]{:S(2)}) collective-permute-start(f32[16,128]{1,0:T(8,128)S(1)} %get-tuple-element.60.refs_0_), channel_id=1, source_target_pairs={{0,3},{1,2},{2,1},{3,0},{4,7},{5,6},{6,5},{7,4},{8,11},{9,10},{10,... | collective-permute-start | bytes 24584 | tf_op jit(solution)/shard_map/ppermute | solution.py:316
  31.0 4.9 %collective-permute-start.10 = (f32[128,128]{1,0:T(8,128)S(1)}, f32[128,128]{1,0:T(8,128)S(1)}, u32[]{:S(2)}, u32[]{:S(2)}) collective-permute-start(f32[128,128]{1,0:T(8,128)S(1)} %get-tuple-element.68), channel_id=1, source_target_pairs={{0,4},{4,0},{8,12},{12,8},{16,20},{20,16},{24,28},{28,24},{1,5},{5... | collective-permute-start | bytes 196616 | tf_op jit(solution)/shard_map/ppermute | solution.py:65
  31.9 4.3 %collective-permute-start.11 = (f32[128,128]{1,0:T(8,128)S(1)}, f32[128,128]{1,0:T(8,128)S(1)}, u32[]{:S(2)}, u32[]{:S(2)}) collective-permute-start(f32[128,128]{1,0:T(8,128)S(1)} %get-tuple-element.69), channel_id=1, source_target_pairs={{0,8},{4,12},{8,0},{12,4},{16,24},{20,28},{24,16},{28,20},{1,9},{5... | collective-permute-start | bytes 196616 | tf_op jit(solution)/shard_map/ppermute | solution.py:65
  33.9 5.2 %collective-permute-start.12 = (f32[128,128]{1,0:T(8,128)S(1)}, f32[128,128]{1,0:T(8,128)S(1)}, u32[]{:S(2)}, u32[]{:S(2)}) collective-permute-start(f32[128,128]{1,0:T(8,128)S(1)} %get-tuple-element.70), channel_id=1, source_target_pairs={{0,12},{4,8},{8,4},{12,0},{16,28},{20,24},{24,20},{28,16},{1,13},{... | collective-permute-start | bytes 196616 | tf_op jit(solution)/shard_map/ppermute | solution.py:65
  39.1 5.7 %collective-permute-start.13 = (f32[128,128]{1,0:T(8,128)S(1)}, f32[128,128]{1,0:T(8,128)S(1)}, u32[]{:S(2)}, u32[]{:S(2)}) collective-permute-start(f32[128,128]{1,0:T(8,128)S(1)} %quad_sum.3.refs_0_), channel_id=1, source_target_pairs={{0,16},{4,20},{8,24},{12,28},{16,0},{20,4},{24,8},{28,12},{1,17},{... | collective-permute-start | bytes 196616 | tf_op jit(solution)/shard_map/ppermute | solution.py:65
  44.9 6.6 %collective-permute-start.14 = (f32[128,128]{1,0:T(8,128)S(1)}, f32[128,128]{1,0:T(8,128)S(1)}, u32[]{:S(2)}, u32[]{:S(2)}) collective-permute-start(f32[128,128]{1,0:T(8,128)S(1)} %get-tuple-element.85), channel_id=1, source_target_pairs={{0,4},{4,0},{8,12},{12,8},{16,20},{20,16},{24,28},{28,24},{1,5},{5... | collective-permute-start | bytes 196616 | tf_op jit(solution)/shard_map/ppermute | solution.py:65
  45.8 5.7 %collective-permute-start.15 = (f32[128,128]{1,0:T(8,128)S(1)}, f32[128,128]{1,0:T(8,128)S(1)}, u32[]{:S(2)}, u32[]{:S(2)}) collective-permute-start(f32[128,128]{1,0:T(8,128)S(1)} %get-tuple-element.86), channel_id=1, source_target_pairs={{0,8},{4,12},{8,0},{12,4},{16,24},{20,28},{24,16},{28,20},{1,9},{5... | collective-permute-start | bytes 196616 | tf_op jit(solution)/shard_map/ppermute | solution.py:65
  46.2 5.3 %collective-permute-start.16 = (f32[128,128]{1,0:T(8,128)S(1)}, f32[128,128]{1,0:T(8,128)S(1)}, u32[]{:S(2)}, u32[]{:S(2)}) collective-permute-start(f32[128,128]{1,0:T(8,128)S(1)} %get-tuple-element.87), channel_id=1, source_target_pairs={{0,12},{4,8},{8,4},{12,0},{16,28},{20,24},{24,20},{28,16},{1,13},{... | collective-permute-start | bytes 196616 | tf_op jit(solution)/shard_map/ppermute | solution.py:65

commit v7 on v6

--- a/solution.py
+++ b/solution.py
@@ -13,6 +13,7 @@
 CHUNK = 256
 PAIR = 2 * HEAD_DIM
 QUAD = 4
+ORDER = (0, 3, 2, 1)
 F32 = jnp.float32
 BF16 = jnp.bfloat16
 
@@ -65,11 +66,11 @@
     return lax.ppermute(value, "seq", [(i, i ^ by) for i in range(size)])
 
 
-def quad_kernel(piece0, piece1, piece2, piece3, *refs):
+def quad_kernel(piece0, piece3, piece2, piece1, *refs):
     refs[-1][...] = (piece0[...] + piece1[...]) + (piece2[...] + piece3[...])
 
 
-def finish_kernel(reverse, piece0, piece1, piece2, piece3, far, *refs):
+def finish_kernel(reverse, piece0, piece3, piece2, piece1, far, *refs):
     place = lax.axis_index("seq")
     number = lax.rem(place, QUAD)
     pieces = [p[...] for p in (piece0, piece1, piece2, piece3)]
@@ -88,7 +89,7 @@
 def quad_scan(pieces, size, reverse, between):
     head = jax.ShapeDtypeStruct((HEAD_DIM, HEAD_DIM), F32)
     got = {by: exchange(pieces[by], size, by) for by in (3, 2, 1)}
-    pieces = [pieces[0], got[1], got[2], got[3]]
+    pieces = [pieces[0], got[3], got[2], got[1]]
     first = between(0, None)
     (total,) = call(
         quad_kernel, [head], [*pieces, *first[-1:]], 0, "quad_sum", spaces={4: pl.ANY}
@@ -105,7 +106,7 @@
     )
     got = {by: exchange(finished[by], size, by) for by in (3, 2, 1)}
     third = between(2, finished[0])
-    return [finished[0], got[1], got[2], got[3]], first + second + third
+    return [finished[0], got[3], got[2], got[1]], first + second + third
 
 
 def doubling_scan(pieces, size, reverse, between):
@@ -128,7 +129,7 @@
     done = []
     for phase in range(3):
         done += between(phase, done[-1] if done else None)
-    return [state[n] for n in range(QUAD)], done
+    return [state[n] for n in ORDER], done
 
 
 def store_pieces(states, pieces, scratch):
@@ -139,7 +140,7 @@
 
 
 def load_pieces(pieces, rounded):
-    for n, piece in enumerate(pieces):
+    for n, piece in zip(ORDER, pieces):
         rounded[head_of(n), :] = piece[...].astype(BF16)
 
 
@@ -277,8 +278,8 @@
         head_grads(h, q, k, v, gm, prefix, states, after, gqs[j], gks[j], gvs[j])
 
 
-def output_kernel(mixed, inverse, *refs):
-    (gqs, (out, gq)) = refs[:QUAD], refs[-2:]
+def output_kernel(mixed, inverse, token, out, written):
+    written[...] = inverse[...]
     shape = (HEAD_DIM, HEAD_DIM)
     for i in range(mixed.shape[0] // HEAD_DIM):
         a = jnp.broadcast_to(inverse[i : i + 1, :], shape).T
@@ -286,8 +287,11 @@
             out[head_slice(i), head_slice(h)] = (
                 mixed[head_slice(i), head_slice(h)] * a
             ).astype(BF16)
+
+
+def merge_kernel(*refs):
     for h in range(QUAD):
-        gq[:, head_slice(h)] = gqs[h][...]
+        refs[-1][:, head_slice(h)] = refs[h][...]
 
 
 def last_kernel(k, v, *refs):
@@ -311,7 +315,7 @@
 def all_parts(value, axis, size):
     power = size & (size - 1) == 0
     parts = [value]
-    for by in reversed(range(1, size)):
+    for by in range(1, size):
         pairs = [(i, i ^ by if power else (i + by) % size) for i in range(size)]
         parts.append(lax.ppermute(value, axis, pairs))
     return parts
@@ -372,10 +376,10 @@
         "norm",
         scratch=[pieces_scratch],
     )
-    gqs, gks, gvs = [], [], []
+    gqs, gks, gvs, results = [], [], [], []
 
     def backward(phase, token):
-        heads = ((0,), (1, 2), (3,))[phase]
+        heads = ((0, 1), (2,), (3,))[phase]
         count = len(heads)
         args = [queries, keys, values, gm, prefix, states, after]
         done = call(
@@ -389,18 +393,23 @@
         gqs.extend(done[:count])
         gks.extend(done[count : 2 * count])
         gvs.extend(done[2 * count :])
-        if phase == 2:
+        if phase == 1:
             done += call(
                 output_kernel,
-                [narrow, narrow],
-                [mixed, inverse, *gqs],
+                [narrow, shape(blocks, HEAD_DIM)],
+                [mixed, inverse, done[-1]],
                 0,
-                "outputs",
+                "output",
+                spaces={2: pl.ANY},
             )
+            results.append(done[-2])
+        if phase == 2:
+            done += call(merge_kernel, [narrow], gqs, 0, "grad_query")
+            results.append(done[-1])
         return done
 
     suffixes, done = scan(pieces, seq, True, backward)
-    output, grad_q = done[-2:]
+    output, grad_q = results
     grad_k, grad_v = call(
         last_kernel,
         [narrow, narrow],

time: 53.3 us -> 51 us (0.957)
  waiting for transfers between devices: 16 us -> 12.6 us
  Pallas kernels: 14.1 us -> 14.8 us
    ppermute x14, waiting for transfers between devices: 13.2 us -> 10.8 us  [exchange(): return lax.ppermute(value, 'seq', [(i, i ^ by) for i in range(size)])]
    ppermute x3, waiting for transfers between devices: 2.8 us -> 1.87 us  [all_parts(): parts.append(lax.ppermute(value, axis, pairs))]
    pallas_call x13 -> x14, Pallas kernels: 14.1 us -> 14.8 us  [call(): return list(kernel(*args))]
  transfers between devices with their start and end apart: 17 -> 17, of which waited for: 11 -> 13; matrix products, arithmetic and copies ran while one was open for 0% -> 0% of each run, Pallas kernels for 16% -> 19%
where the time goes in v7:
time: 51 us; the launch traced here: 50.8 us
  starting transfers between devices  22.7 us (45%)
  Pallas kernels  14.8 us (29%)
  waiting for transfers between devices  12.6 us (25%)
  between operations  0.74 us (1%)
    ppermute x14, starting transfers between devices, exchange(): return lax.ppermute(value, 'seq', [(i, i ^ by) for i in range(size)])  20.8 us
    pallas_call x14, Pallas kernels, call(): return list(kernel(*args))  14.8 us
    ppermute x14, waiting for transfers between devices, exchange(): return lax.ppermute(value, 'seq', [(i, i ^ by) for i in range(size)])  10.8 us
    ppermute x3, starting transfers between devices, all_parts(): parts.append(lax.ppermute(value, axis, pairs))  1.92 us
    ppermute x3, waiting for transfers between devices, all_parts(): parts.append(lax.ppermute(value, axis, pairs))  1.87 us
  transfers between devices with their start and end apart: 17, of which 13 were waited for; matrix products, arithmetic and copies ran while one was open for 0% of the time, Pallas kernels for 19%

profile of v7, /device:TPU:0, one launch (start us, length us, event | category | flops | bytes accessed | tf_op | source)
XLA Modules:
  0.0 50.8 jit_solution(9635297093701307126)
XLA Ops:
  0.6 0.0 copy-start
  0.6 2.0 %local_state.1 = (f32[128,128]{1,0:T(8,128)S(1)}, f32[128,128]{1,0:T(8,128)S(1)}, f32[128,128]{1,0:T(8,128)S(1)}, f32[128,128]{1,0:T(8,128)S(1)}, bf16[1024,512]...) custom-call(bf16[1024,512]{1,0:T(8,128)(2,1)} %k_hbm.1, bf16[1024,512]{1,0:T(8,128)(2,1)} %v_hbm.1), custom_call_target="tpu_custom_call" | custom-call | flops 134217728 | bytes 4456448 | tf_op jit(solution)/shard_map/local_state/pallas_call | solution.py:57
  2.6 4.0 %collective-permute-start = (f32[128,128]{1,0:T(8,128)S(1)}, f32[128,128]{1,0:T(8,128)S(1)}, u32[]{:S(2)}, u32[]{:S(2)}) collective-permute-start(f32[128,128]{1,0:T(8,128)S(1)} %get-tuple-element.51), channel_id=1, source_target_pairs={{0,12},{4,8},{8,4},{12,0},{16,28},{20,24},{24,20},{28,16},{1,13},{... | collective-permute-start | bytes 196616 | tf_op jit(solution)/shard_map/ppermute | solution.py:66
  6.6 0.5 collective-permute-start.1
  7.1 0.2 collective-permute-start.2
  7.3 0.0 copy-done
  7.3 0.0 copy-start.1
  7.3 1.9 %intra.1 = (f32[1024,512]{1,0:T(8,128)S(1)}, f32[1536,128]{1,0:T(8,128)S(1)}, bf16[512,1024]{1,0:T(8,128)(2,1)S(1)}) custom-call(bf16[1024,512]{1,0:T(8,128)(2,1)S(1)} %copy-done, bf16[1024,512]{1,0:T(8,128)(2,1)S(1)} %get-tuple-element.47.k, bf16[1024,512]{1,0:T(8,128)(2,1)S(1)} %get-tuple-element.48.v), custom_call_target="tpu_custom_call" | custom-call | flops 805306368 | bytes 7077888 | tf_op jit(solution)/shard_map/intra/pallas_call | solution.py:57
  9.2 0.0 collective-permute-done.piece3
  9.2 1.7 %collective-permute-done.1.piece2 = f32[128,128]{1,0:T(8,128)S(1)} collective-permute-done((f32[128,128]{1,0:T(8,128)S(1)}, f32[128,128]{1,0:T(8,128)S(1)}, u32[]{:S(2)}, u32[]{:S(2)}) %collective-permute-start.1) | collective-permute-done | bytes 65568 | tf_op jit(solution)/shard_map/ppermute | solution.py:66
  10.9 0.5 collective-permute-done.2.piece1
  11.4 2.7 %collective-permute-start.3 = (f32[128,128]{1,0:T(8,128)S(1)}, f32[128,128]{1,0:T(8,128)S(1)}, u32[]{:S(2)}, u32[]{:S(2)}) collective-permute-start(f32[128,128]{1,0:T(8,128)S(1)} %quad_sum.2), channel_id=1, source_target_pairs={{0,16},{4,20},{8,24},{12,28},{16,0},{20,4},{24,8},{28,12},{1,17},{... | collective-permute-start | bytes 196616 | tf_op jit(solution)/shard_map/ppermute | solution.py:66
  14.0 2.6 %collective-permute-done.3.far = f32[128,128]{1,0:T(8,128)S(1)} collective-permute-done((f32[128,128]{1,0:T(8,128)S(1)}, f32[128,128]{1,0:T(8,128)S(1)}, u32[]{:S(2)}, u32[]{:S(2)}) %collective-permute-start.3) | collective-permute-done | bytes 65568 | tf_op jit(solution)/shard_map/ppermute | solution.py:66
  16.6 0.1 finish.2
  16.7 1.6 %collective-permute-start.4 = (f32[128,128]{1,0:T(8,128)S(1)}, f32[128,128]{1,0:T(8,128)S(1)}, u32[]{:S(2)}, u32[]{:S(2)}) collective-permute-start(f32[128,128]{1,0:T(8,128)S(1)} %get-tuple-element.56), channel_id=1, source_target_pairs={{0,12},{4,8},{8,4},{12,0},{16,28},{20,24},{24,20},{28,16},{1,13},{... | collective-permute-start | bytes 196616 | tf_op jit(solution)/shard_map/ppermute | solution.py:66
  18.3 0.4 collective-permute-start.5
  18.6 1.6 %collective-permute-start.6 = (f32[128,128]{1,0:T(8,128)S(1)}, f32[128,128]{1,0:T(8,128)S(1)}, u32[]{:S(2)}, u32[]{:S(2)}) collective-permute-start(f32[128,128]{1,0:T(8,128)S(1)} %get-tuple-element.58), channel_id=1, source_target_pairs={{0,4},{4,0},{8,12},{12,8},{16,20},{20,16},{24,28},{28,24},{1,5},{5... | collective-permute-start | bytes 196616 | tf_op jit(solution)/shard_map/ppermute | solution.py:66
  20.2 1.7 %collective-permute-done.4.refs_1_ = f32[128,128]{1,0:T(8,128)S(1)} collective-permute-done((f32[128,128]{1,0:T(8,128)S(1)}, f32[128,128]{1,0:T(8,128)S(1)}, u32[]{:S(2)}, u32[]{:S(2)}) %collective-permute-start.4) | collective-permute-done | bytes 65568 | tf_op jit(solution)/shard_map/ppermute | solution.py:66
  21.9 0.6 %collective-permute-done.5.refs_2_ = f32[128,128]{1,0:T(8,128)S(1)} collective-permute-done((f32[128,128]{1,0:T(8,128)S(1)}, f32[128,128]{1,0:T(8,128)S(1)}, u32[]{:S(2)}, u32[]{:S(2)}) %collective-permute-start.5) | collective-permute-done | bytes 65568 | tf_op jit(solution)/shard_map/ppermute | solution.py:66
  22.5 0.4 collective-permute-done.6.refs_3_
  22.9 0.0 copy-done.1
  22.9 0.7 %mixed.1 = (f32[1024,512]{1,0:T(8,128)S(1)}, f32[16,128]{1,0:T(8,128)S(1)}, bf16[512,128]{1,0:T(8,128)(2,1)S(1)}) custom-call(f32[1024,512]{1,0:T(8,128)S(1)} %get-tuple-element.49.intra, bf16[1024,512]{1,0:T(8,128)(2,1)S(1)} %copy-done, bf16[1024,512]{1,0:T(8,128)(2,1)S(1)} %copy-done.1, f32[128,128]{1,0:T(8,128)S(1)} %get-tuple-element.55.refs_0_, ...), custom_call_target="tpu_custom_call" | custom-call | flops 134217728 | bytes 6692864 | tf_op jit(solution)/shard_map/mixed/pallas_call | solution.py:57
  23.6 0.1 collective-permute-start.9
  23.7 1.8 %collective-permute-start.8 = (f32[16,128]{1,0:T(8,128)S(1)}, f32[16,128]{1,0:T(8,128)S(1)}, u32[]{:S(2)}, u32[]{:S(2)}) collective-permute-start(f32[16,128]{1,0:T(8,128)S(1)} %get-tuple-element.60.refs_0_), channel_id=1, source_target_pairs={{0,2},{1,3},{2,0},{3,1},{4,6},{5,7},{6,4},{7,5},{8,10},{9,11},{10,... | collective-permute-start | bytes 24584 | tf_op jit(solution)/shard_map/ppermute | solution.py:320
  25.5 0.1 collective-permute-start.7
  25.6 1.2 %collective-permute-done.9.refs_3_ = f32[16,128]{1,0:T(8,128)S(1)} collective-permute-done((f32[16,128]{1,0:T(8,128)S(1)}, f32[16,128]{1,0:T(8,128)S(1)}, u32[]{:S(2)}, u32[]{:S(2)}) %collective-permute-start.9) | collective-permute-done | bytes 8224 | tf_op jit(solution)/shard_map/ppermute | solution.py:320
  26.8 0.7 %collective-permute-done.8.refs_2_ = f32[16,128]{1,0:T(8,128)S(1)} collective-permute-done((f32[16,128]{1,0:T(8,128)S(1)}, f32[16,128]{1,0:T(8,128)S(1)}, u32[]{:S(2)}, u32[]{:S(2)}) %collective-permute-start.8) | collective-permute-done | bytes 8224 | tf_op jit(solution)/shard_map/ppermute | solution.py:320
  27.4 0.0 collective-permute-done.7.refs_1_
  27.4 0.8 %norm.1 = (bf16[1024,512]{1,0:T(8,128)(2,1)S(1)}, f32[8,128]{1,0:T(8,128)S(1)}, f32[1536,128]{1,0:T(8,128)S(1)}, f32[128,128]{1,0:T(8,128)S(1)}, f32[128,128]{1,...) custom-call(f32[1024,512]{1,0:T(8,128)S(1)} %get-tuple-element.59.mixed, ...), custom_call_target="tpu_custom_call" | custom-call | flops 134217728 | bytes 6328320 | tf_op jit(solution)/shard_map/norm/pallas_call | solution.py:57
  28.2 2.7 %collective-permute-start.10 = (f32[128,128]{1,0:T(8,128)S(1)}, f32[128,128]{1,0:T(8,128)S(1)}, u32[]{:S(2)}, u32[]{:S(2)}) collective-permute-start(f32[128,128]{1,0:T(8,128)S(1)} %get-tuple-element.67), channel_id=1, source_target_pairs={{0,12},{4,8},{8,4},{12,0},{16,28},{20,24},{24,20},{28,16},{1,13},{... | collective-permute-start | bytes 196616 | tf_op jit(solution)/shard_map/ppermute | solution.py:66
  30.9 0.5 collective-permute-start.11
  31.4 0.4 collective-permute-start.12
  31.8 2.5 %grads.3 = (bf16[1024,128]{1,0:T(8,128)(2,1)S(1)}, bf16[1024,128]{1,0:T(8,128)(2,1)S(1)}, f32[1024,128]{1,0:T(8,128)S(1)}, f32[1024,128]{1,0:T(8,128)S(1)}, f32[...) custom-call(bf16[1024,512]{1,0:T(8,128)(2,1)S(1)} %copy-done, bf16[1024,512]{1,0:T(8,128)(2,1)S(1)} %get-tuple-element.47.k, ...), custom_call_target="tpu_custom_call" | custom-call | flops 1006632960 | bytes 8519680 | tf_op jit(solution)/shard_map/grads/pallas_call | solution.py:57
  34.3 0.0 collective-permute-done.10.piece3
  34.3 0.9 %collective-permute-done.11.piece2 = f32[128,128]{1,0:T(8,128)S(1)} collective-permute-done((f32[128,128]{1,0:T(8,128)S(1)}, f32[128,128]{1,0:T(8,128)S(1)}, u32[]{:S(2)}, u32[]{:S(2)}) %collective-permute-start.11) | collective-permute-done | bytes 65568 | tf_op jit(solution)/shard_map/ppermute | solution.py:66
  35.2 0.5 collective-permute-done.12.piece1
  35.7 2.8 %collective-permute-start.13 = (f32[128,128]{1,0:T(8,128)S(1)}, f32[128,128]{1,0:T(8,128)S(1)}, u32[]{:S(2)}, u32[]{:S(2)}) collective-permute-start(f32[128,128]{1,0:T(8,128)S(1)} %quad_sum.3.refs_0_), channel_id=1, source_target_pairs={{0,16},{4,20},{8,24},{12,28},{16,0},{20,4},{24,8},{28,12},{1,17},{... | collective-permute-start | bytes 196616 | tf_op jit(solution)/shard_map/ppermute | solution.py:66
  38.5 1.3 %grads.4 = (bf16[1024,128]{1,0:T(8,128)(2,1)S(1)}, f32[1024,128]{1,0:T(8,128)S(1)}, f32[1024,128]{1,0:T(8,128)S(1)}) custom-call(bf16[1024,512]{1,0:T(8,128)(2,1)S(1)} %copy-done, bf16[1024,512]{1,0:T(8,128)(2,1)S(1)} %get-tuple-element.47.k, bf16[1024,512]{1,0:T(8,128)(2,1)S(1)} %get-tuple-element.48.v, bf16[1024,512]{1,0:T(8,128)(2,1)S(1)} %get-tuple-element.62.gm, ...), custom_call_target="tpu_custom_call" | custom-call | flops 503316480 | bytes 7274496 | tf_op jit(solution)/shard_map/grads/pallas_call | solution.py:57
  39.8 1.2 %output.1 = (bf16[1024,512]{1,0:T(8,128)(2,1)}, f32[8,128]{1,0:T(8,128)S(1)}) custom-call(f32[1024,512]{1,0:T(8,128)S(1)} %get-tuple-element.59.mixed, f32[8,128]{1,0:T(8,128)S(1)} %get-tuple-element.61.inverse, f32[1024,128]{1,0:T(8,128)S(1)} %get-tuple-element.71.token.refs_6_), custom_call_target="tpu_custom_call" | custom-call | bytes 3678208 | tf_op jit(solution)/shard_map/output/pallas_call | solution.py:57
  41.0 0.4 collective-permute-done.13.far
  41.4 0.1 finish.3
  41.5 2.1 %collective-permute-start.14 = (f32[128,128]{1,0:T(8,128)S(1)}, f32[128,128]{1,0:T(8,128)S(1)}, u32[]{:S(2)}, u32[]{:S(2)}) collective-permute-start(f32[128,128]{1,0:T(8,128)S(1)} %get-tuple-element.85), channel_id=1, source_target_pairs={{0,12},{4,8},{8,4},{12,0},{16,28},{20,24},{24,20},{28,16},{1,13},{... | collective-permute-start | bytes 196616 | tf_op jit(solution)/shard_map/ppermute | solution.py:66
  43.6 1.3 %collective-permute-start.15 = (f32[128,128]{1,0:T(8,128)S(1)}, f32[128,128]{1,0:T(8,128)S(1)}, u32[]{:S(2)}, u32[]{:S(2)}) collective-permute-start(f32[128,128]{1,0:T(8,128)S(1)} %get-tuple-element.86), channel_id=1, source_target_pairs={{0,8},{4,12},{8,0},{12,4},{16,24},{20,28},{24,16},{28,20},{1,9},{5... | collective-permute-start | bytes 196616 | tf_op jit(solution)/shard_map/ppermute | solution.py:66
  44.9 0.1 collective-permute-start.16
  45.0 1.3 %grads.5 = (bf16[1024,128]{1,0:T(8,128)(2,1)S(1)}, f32[1024,128]{1,0:T(8,128)S(1)}, f32[1024,128]{1,0:T(8,128)S(1)}) custom-call(bf16[1024,512]{1,0:T(8,128)(2,1)S(1)} %copy-done, bf16[1024,512]{1,0:T(8,128)(2,1)S(1)} %get-tuple-element.47.k, bf16[1024,512]{1,0:T(8,128)(2,1)S(1)} %get-tuple-element.48.v, bf16[1024,512]{1,0:T(8,128)(2,1)S(1)} %get-tuple-element.62.gm, ...), custom_call_target="tpu_custom_call" | custom-call | flops 503316480 | bytes 7274496 | tf_op jit(solution)/shard_map/grads/pallas_call | solution.py:57
  46.4 1.2 %grad_query.1 = bf16[1024,512]{1,0:T(8,128)(2,1)} custom-call(bf16[1024,128]{1,0:T(8,128)(2,1)S(1)} %get-tuple-element.73.refs_0_, bf16[1024,128]{1,0:T(8,128)(2,1)S(1)} %get-tuple-element.74.refs_1_, bf16[1024,128]{1,0:T(8,128)(2,1)S(1)} %get-tuple-element.75.refs_2_, bf16[1024,128]{1,0:T(8,128)(2,1)S(1)} %get-tuple-element.78.refs_3_), custom_call_target="tpu_custom_call" | custom-call | bytes 2097152 | tf_op jit(solution)/shard_map/grad_query/pallas_call | solution.py:57
  47.5 0.0 collective-permute-done.14.refs_9_
  47.5 0.3 collective-permute-done.15.refs_10_
  47.9 1.3 %collective-permute-done.16.refs_11_ = f32[128,128]{1,0:T(8,128)S(1)} collective-permute-done((f32[128,128]{1,0:T(8,128)S(1)}, f32[128,128]{1,0:T(8,128)S(1)}, u32[]{:S(2)}, u32[]{:S(2)}) %collective-permute-start.16) | collective-permute-done | bytes 65568 | tf_op jit(solution)/shard_map/ppermute | solution.py:66
  49.2 1.7 %last.1 = (bf16[1024,512]{1,0:T(8,128)(2,1)}, bf16[1024,512]{1,0:T(8,128)(2,1)}) custom-call(bf16[1024,512]{1,0:T(8,128)(2,1)S(1)} %get-tuple-element.47.k, bf16[1024,512]{1,0:T(8,128)(2,1)S(1)} %get-tuple-element.48.v, f32[1024,128]{1,0:T(8,128)S(1)} %get-tuple-element.79.refs_0_, f32[1024,128]{1,0:T(8,128)S(1)} %get-tuple-element.80.refs_1_, ...), custom_call_target="tpu_custom_call" | custom-call | flops 268435456 | bytes 8650752 | tf_op jit(solution)/shard_map/last/pallas_call | solution.py:57
  (2 shorter events, 0.0 us)
Async XLA Ops:
  0.6 6.7 %copy-start = (bf16[1024,512]{1,0:T(8,128)(2,1)S(1)}, bf16[1024,512]{1,0:T(8,128)(2,1)}, u32[]{:S(2)}) copy-start(bf16[1024,512]{1,0:T(8,128)(2,1)} %q.9) | copy-start | bytes 3145732
  2.6 6.6 %collective-permute-start = (f32[128,128]{1,0:T(8,128)S(1)}, f32[128,128]{1,0:T(8,128)S(1)}, u32[]{:S(2)}, u32[]{:S(2)}) collective-permute-start(f32[128,128]{1,0:T(8,128)S(1)} %get-tuple-element.51), channel_id=1, source_target_pairs={{0,12},{4,8},{8,4},{12,0},{16,28},{20,24},{24,20},{28,16},{1,13},{... | collective-permute-start | bytes 196616 | tf_op jit(solution)/shard_map/ppermute | solution.py:66
  6.6 4.3 %collective-permute-start.1 = (f32[128,128]{1,0:T(8,128)S(1)}, f32[128,128]{1,0:T(8,128)S(1)}, u32[]{:S(2)}, u32[]{:S(2)}) collective-permute-start(f32[128,128]{1,0:T(8,128)S(1)} %get-tuple-element.52), channel_id=1, source_target_pairs={{0,8},{4,12},{8,0},{12,4},{16,24},{20,28},{24,16},{28,20},{1,9},{5... | collective-permute-start | bytes 196616 | tf_op jit(solution)/shard_map/ppermute | solution.py:66
  7.1 4.3 %collective-permute-start.2 = (f32[128,128]{1,0:T(8,128)S(1)}, f32[128,128]{1,0:T(8,128)S(1)}, u32[]{:S(2)}, u32[]{:S(2)}) collective-permute-start(f32[128,128]{1,0:T(8,128)S(1)} %get-tuple-element.53), channel_id=1, source_target_pairs={{0,4},{4,0},{8,12},{12,8},{16,20},{20,16},{24,28},{28,24},{1,5},{5... | collective-permute-start | bytes 196616 | tf_op jit(solution)/shard_map/ppermute | solution.py:66
  7.3 15.6 %copy-start.1 = (bf16[1024,512]{1,0:T(8,128)(2,1)S(1)}, bf16[1024,512]{1,0:T(8,128)(2,1)}, u32[]{:S(2)}) copy-start(bf16[1024,512]{1,0:T(8,128)(2,1)} %g.3) | copy-start | bytes 3145732
  11.4 5.2 %collective-permute-start.3 = (f32[128,128]{1,0:T(8,128)S(1)}, f32[128,128]{1,0:T(8,128)S(1)}, u32[]{:S(2)}, u32[]{:S(2)}) collective-permute-start(f32[128,128]{1,0:T(8,128)S(1)} %quad_sum.2), channel_id=1, source_target_pairs={{0,16},{4,20},{8,24},{12,28},{16,0},{20,4},{24,8},{28,12},{1,17},{... | collective-permute-start | bytes 196616 | tf_op jit(solution)/shard_map/ppermute | solution.py:66
  16.7 5.2 %collective-permute-start.4 = (f32[128,128]{1,0:T(8,128)S(1)}, f32[128,128]{1,0:T(8,128)S(1)}, u32[]{:S(2)}, u32[]{:S(2)}) collective-permute-start(f32[128,128]{1,0:T(8,128)S(1)} %get-tuple-element.56), channel_id=1, source_target_pairs={{0,12},{4,8},{8,4},{12,0},{16,28},{20,24},{24,20},{28,16},{1,13},{... | collective-permute-start | bytes 196616 | tf_op jit(solution)/shard_map/ppermute | solution.py:66
  18.3 4.3 %collective-permute-start.5 = (f32[128,128]{1,0:T(8,128)S(1)}, f32[128,128]{1,0:T(8,128)S(1)}, u32[]{:S(2)}, u32[]{:S(2)}) collective-permute-start(f32[128,128]{1,0:T(8,128)S(1)} %get-tuple-element.57), channel_id=1, source_target_pairs={{0,8},{4,12},{8,0},{12,4},{16,24},{20,28},{24,16},{28,20},{1,9},{5... | collective-permute-start | bytes 196616 | tf_op jit(solution)/shard_map/ppermute | solution.py:66
  18.6 4.3 %collective-permute-start.6 = (f32[128,128]{1,0:T(8,128)S(1)}, f32[128,128]{1,0:T(8,128)S(1)}, u32[]{:S(2)}, u32[]{:S(2)}) collective-permute-start(f32[128,128]{1,0:T(8,128)S(1)} %get-tuple-element.58), channel_id=1, source_target_pairs={{0,4},{4,0},{8,12},{12,8},{16,20},{20,16},{24,28},{28,24},{1,5},{5... | collective-permute-start | bytes 196616 | tf_op jit(solution)/shard_map/ppermute | solution.py:66
  23.6 3.1 %collective-permute-start.9 = (f32[16,128]{1,0:T(8,128)S(1)}, f32[16,128]{1,0:T(8,128)S(1)}, u32[]{:S(2)}, u32[]{:S(2)}) collective-permute-start(f32[16,128]{1,0:T(8,128)S(1)} %get-tuple-element.60.refs_0_), channel_id=1, source_target_pairs={{0,3},{1,2},{2,1},{3,0},{4,7},{5,6},{6,5},{7,4},{8,11},{9,10},{10,... | collective-permute-start | bytes 24584 | tf_op jit(solution)/shard_map/ppermute | solution.py:320
  23.7 3.7 %collective-permute-start.8 = (f32[16,128]{1,0:T(8,128)S(1)}, f32[16,128]{1,0:T(8,128)S(1)}, u32[]{:S(2)}, u32[]{:S(2)}) collective-permute-start(f32[16,128]{1,0:T(8,128)S(1)} %get-tuple-element.60.refs_0_), channel_id=1, source_target_pairs={{0,2},{1,3},{2,0},{3,1},{4,6},{5,7},{6,4},{7,5},{8,10},{9,11},{10,... | collective-permute-start | bytes 24584 | tf_op jit(solution)/shard_map/ppermute | solution.py:320
  25.5 2.0 %collective-permute-start.7 = (f32[16,128]{1,0:T(8,128)S(1)}, f32[16,128]{1,0:T(8,128)S(1)}, u32[]{:S(2)}, u32[]{:S(2)}) collective-permute-start(f32[16,128]{1,0:T(8,128)S(1)} %get-tuple-element.60.refs_0_), channel_id=1, source_target_pairs={{0,1},{1,0},{2,3},{3,2},{4,5},{5,4},{6,7},{7,6},{8,9},{9,8},{10,11... | collective-permute-start | bytes 24584 | tf_op jit(solution)/shard_map/ppermute | solution.py:320
  28.2 6.0 %collective-permute-start.10 = (f32[128,128]{1,0:T(8,128)S(1)}, f32[128,128]{1,0:T(8,128)S(1)}, u32[]{:S(2)}, u32[]{:S(2)}) collective-permute-start(f32[128,128]{1,0:T(8,128)S(1)} %get-tuple-element.67), channel_id=1, source_target_pairs={{0,12},{4,8},{8,4},{12,0},{16,28},{20,24},{24,20},{28,16},{1,13},{... | collective-permute-start | bytes 196616 | tf_op jit(solution)/shard_map/ppermute | solution.py:66
  30.9 4.3 %collective-permute-start.11 = (f32[128,128]{1,0:T(8,128)S(1)}, f32[128,128]{1,0:T(8,128)S(1)}, u32[]{:S(2)}, u32[]{:S(2)}) collective-permute-start(f32[128,128]{1,0:T(8,128)S(1)} %get-tuple-element.68), channel_id=1, source_target_pairs={{0,8},{4,12},{8,0},{12,4},{16,24},{20,28},{24,16},{28,20},{1,9},{5... | collective-permute-start | bytes 196616 | tf_op jit(solution)/shard_map/ppermute | solution.py:66
  31.4 4.3 %collective-permute-start.12 = (f32[128,128]{1,0:T(8,128)S(1)}, f32[128,128]{1,0:T(8,128)S(1)}, u32[]{:S(2)}, u32[]{:S(2)}) collective-permute-start(f32[128,128]{1,0:T(8,128)S(1)} %get-tuple-element.69), channel_id=1, source_target_pairs={{0,4},{4,0},{8,12},{12,8},{16,20},{20,16},{24,28},{28,24},{1,5},{5... | collective-permute-start | bytes 196616 | tf_op jit(solution)/shard_map/ppermute | solution.py:66
  35.7 5.7 %collective-permute-start.13 = (f32[128,128]{1,0:T(8,128)S(1)}, f32[128,128]{1,0:T(8,128)S(1)}, u32[]{:S(2)}, u32[]{:S(2)}) collective-permute-start(f32[128,128]{1,0:T(8,128)S(1)} %quad_sum.3.refs_0_), channel_id=1, source_target_pairs={{0,16},{4,20},{8,24},{12,28},{16,0},{20,4},{24,8},{28,12},{1,17},{... | collective-permute-start | bytes 196616 | tf_op jit(solution)/shard_map/ppermute | solution.py:66
  41.5 6.0 %collective-permute-start.14 = (f32[128,128]{1,0:T(8,128)S(1)}, f32[128,128]{1,0:T(8,128)S(1)}, u32[]{:S(2)}, u32[]{:S(2)}) collective-permute-start(f32[128,128]{1,0:T(8,128)S(1)} %get-tuple-element.85), channel_id=1, source_target_pairs={{0,12},{4,8},{8,4},{12,0},{16,28},{20,24},{24,20},{28,16},{1,13},{... | collective-permute-start | bytes 196616 | tf_op jit(solution)/shard_map/ppermute | solution.py:66
  43.6 4.3 %collective-permute-start.15 = (f32[128,128]{1,0:T(8,128)S(1)}, f32[128,128]{1,0:T(8,128)S(1)}, u32[]{:S(2)}, u32[]{:S(2)}) collective-permute-start(f32[128,128]{1,0:T(8,128)S(1)} %get-tuple-element.86), channel_id=1, source_target_pairs={{0,8},{4,12},{8,0},{12,4},{16,24},{20,28},{24,16},{28,20},{1,9},{5... | collective-permute-start | bytes 196616 | tf_op jit(solution)/shard_map/ppermute | solution.py:66
  44.9 4.3 %collective-permute-start.16 = (f32[128,128]{1,0:T(8,128)S(1)}, f32[128,128]{1,0:T(8,128)S(1)}, u32[]{:S(2)}, u32[]{:S(2)}) collective-permute-start(f32[128,128]{1,0:T(8,128)S(1)} %get-tuple-element.87), channel_id=1, source_target_pairs={{0,4},{4,0},{8,12},{12,8},{16,20},{20,16},{24,28},{28,24},{1,5},{5... | collective-permute-start | bytes 196616 | tf_op jit(solution)/shard_map/ppermute | solution.py:66

commit v8 on v7

--- a/solution.py
+++ b/solution.py
@@ -197,7 +197,7 @@
 
 
 def mixed_kernel(intra, q, g, *refs):
-    pieces, (mixed, stats, prefix) = refs[:QUAD], refs[QUAD:]
+    pieces, (mixed, prefix, stats, *copies) = refs[:QUAD], refs[QUAD:]
     load_pieces(pieces, prefix)
     blocks = q.shape[0] // HEAD_DIM
     for at in chunk_slices(q.shape[0]):
@@ -213,6 +213,8 @@
             i = at.start // HEAD_DIM + n
             stats[i : i + 1, :] = row_sums(square[head_slice(n)])
             stats[blocks + i : blocks + i + 1, :] = row_sums(cross[head_slice(n)])
+    for copy in copies:
+        copy[...] = stats[...]
 
 
 def norm_kernel(width, mixed, q_t, g, *refs):
@@ -245,7 +247,7 @@
     store_pieces(after, pieces, scratch)
 
 
-def head_grads(h, q, k, v, gm, prefix, states, after, gq, gk, gv):
+def head_grads(h, q, k, v, gm, prefix, states, after, gq, gk, gv, finished=None):
     cols, part = q.shape[1], head_slice(h)
     keep, keep_t = causal(), causal(True)
     chunks = chunk_slices(q.shape[0])
@@ -268,30 +270,48 @@
         gq[at, :] = gq_i.astype(BF16)
         gk[at, :] = gk_i
         gv[at, :] = gv_i
-
-
-def grads_kernel(heads, q, k, v, gm, prefix, states, after, *refs):
-    count = len(heads)
-    outs = refs[-3 * count :]
-    gqs, gks, gvs = (outs[i * count : (i + 1) * count] for i in range(3))
-    for j, h in enumerate(heads):
-        head_grads(h, q, k, v, gm, prefix, states, after, gqs[j], gks[j], gvs[j])
-
-
-def output_kernel(mixed, inverse, token, out, written):
-    written[...] = inverse[...]
+        if finished is not None:
+            finished(n, at)
+
+
+def first_grads_kernel(q, k, v, gm, prefix, states, after, *refs):
+    gqs, gks, gvs = refs[:2], refs[2:4], refs[4:]
+    for h in range(2):
+        head_grads(h, q, k, v, gm, prefix, states, after, gqs[h], gks[h], gvs[h])
+
+
+def second_grads_kernel(q, k, v, gm, prefix, states, after, mixed, inverse, *refs):
+    gq, gk, gv, out_hbm, out, sems = refs[-6:]
     shape = (HEAD_DIM, HEAD_DIM)
-    for i in range(mixed.shape[0] // HEAD_DIM):
-        a = jnp.broadcast_to(inverse[i : i + 1, :], shape).T
-        for h in range(mixed.shape[1] // HEAD_DIM):
-            out[head_slice(i), head_slice(h)] = (
-                mixed[head_slice(i), head_slice(h)] * a
-            ).astype(BF16)
-
-
-def merge_kernel(*refs):
-    for h in range(QUAD):
-        refs[-1][:, head_slice(h)] = refs[h][...]
+    copies = []
+    for n, at in enumerate(chunk_slices(q.shape[0])):
+        for i in range(at.start // HEAD_DIM, at.stop // HEAD_DIM):
+            a = jnp.broadcast_to(inverse[i : i + 1, :], shape).T
+            for h in range(q.shape[1] // HEAD_DIM):
+                block = (head_slice(i), head_slice(h))
+                out[block] = (mixed[block] * a).astype(BF16)
+        copies.append(pltpu.make_async_copy(out.at[at], out_hbm.at[at], sems.at[n]))
+        copies[-1].start()
+    head_grads(2, q, k, v, gm, prefix, states, after, gq, gk, gv)
+    for copy in copies:
+        copy.wait()
+
+
+def third_grads_kernel(q, k, v, gm, prefix, states, after, *refs):
+    gqs, (gk, gv, gq_hbm, gq, sems) = refs[:3], refs[-5:]
+    copies = []
+
+    def send(src, h, at, sem):
+        copies.append(pltpu.make_async_copy(src.at[at], gq_hbm.at[at, head_slice(h)], sem))
+        copies[-1].start()
+
+    for h in range(3):
+        send(gqs[h], h, slice(0, q.shape[0]), sems.at[h])
+    head_grads(
+        3, q, k, v, gm, prefix, states, after, gq, gk, gv, lambda n, at: send(gq, 3, at, sems.at[3 + n])
+    )
+    for copy in copies:
+        copy.wait()
 
 
 def last_kernel(k, v, *refs):
@@ -312,12 +332,13 @@
         copy.wait()
 
 
-def all_parts(value, axis, size):
+def all_parts(values, axis):
+    size = len(values)
     power = size & (size - 1) == 0
-    parts = [value]
-    for by in range(1, size):
+    parts = [values[0]]
+    for by in reversed(range(1, size)):
         pairs = [(i, i ^ by if power else (i + by) % size) for i in range(size)]
-        parts.append(lax.ppermute(value, axis, pairs))
+        parts.append(lax.ppermute(values[by], axis, pairs))
     return parts
 
 
@@ -361,9 +382,9 @@
         )
 
     prefixes, (intra, states, queries_t) = scan(pieces, seq, False, forward)
-    mixed, stats, prefix = call(
+    mixed, prefix, *stats = call(
         mixed_kernel,
-        [wide, shape(2 * blocks, HEAD_DIM), shape(cols, HEAD_DIM, BF16)],
+        [wide, shape(cols, HEAD_DIM, BF16)] + [shape(2 * blocks, HEAD_DIM)] * head_size,
         [intra, queries, grad_out, *prefixes],
         QUAD * head_flops,
         "mixed",
@@ -371,44 +392,60 @@
     gm, inverse, after, *pieces = call(
         functools.partial(norm_kernel, cols * head_size),
         [narrow, shape(blocks, HEAD_DIM), states_shape] + pieces_shape,
-        [mixed, queries_t, grad_out, *all_parts(stats, "head", head_size)],
+        [mixed, queries_t, grad_out, *all_parts(stats, "head")],
         QUAD * head_flops,
         "norm",
         scratch=[pieces_scratch],
     )
+    args = [queries, keys, values, gm, prefix, states, after]
+    grads_flops = 6 * chunk_flops + 3 * head_flops
+
+    def backward(phase, token):
+        if phase == 0:
+            parts = call(
+                first_grads_kernel,
+                [head_narrow] * 2 + [head_wide] * 4,
+                args,
+                2 * grads_flops,
+                "first_grads",
+            )
+        elif phase == 1:
+            parts = call(
+                second_grads_kernel,
+                [head_narrow] + [head_wide] * 2 + [narrow],
+                args + [mixed, inverse, token],
+                grads_flops,
+                "second_grads",
+                spaces={len(args) + 2: pl.ANY},
+                outs={3: pl.ANY},
+                scratch=[pltpu.VMEM((rows, cols), BF16), pltpu.SemaphoreType.DMA((chunks,))],
+            )
+        else:
+            parts = call(
+                third_grads_kernel,
+                [head_wide] * 2 + [narrow],
+                args + gqs + [token],
+                grads_flops,
+                "third_grads",
+                spaces={len(args) + 3: pl.ANY},
+                outs={2: pl.ANY},
+                scratch=[
+                    pltpu.VMEM((rows, HEAD_DIM), BF16),
+                    pltpu.SemaphoreType.DMA((3 + chunks,)),
+                ],
+            )
+        if phase < 2:
+            count = 2 - phase
+            gqs.extend(parts[:count])
+            parts = parts[count:]
+        count = 2 if phase == 0 else 1
+        gks.extend(parts[:count])
+        gvs.extend(parts[count : 2 * count])
+        results.extend(parts[2 * count :])
+        return gks[-1:]
+
     gqs, gks, gvs, results = [], [], [], []
-
-    def backward(phase, token):
-        heads = ((0, 1), (2,), (3,))[phase]
-        count = len(heads)
-        args = [queries, keys, values, gm, prefix, states, after]
-        done = call(
-            functools.partial(grads_kernel, heads),
-            [head_narrow] * count + [head_wide] * (2 * count),
-            args + ([] if token is None else [token]),
-            count * (6 * chunk_flops + 3 * head_flops),
-            "grads",
-            spaces={len(args): pl.ANY},
-        )
-        gqs.extend(done[:count])
-        gks.extend(done[count : 2 * count])
-        gvs.extend(done[2 * count :])
-        if phase == 1:
-            done += call(
-                output_kernel,
-                [narrow, shape(blocks, HEAD_DIM)],
-                [mixed, inverse, done[-1]],
-                0,
-                "output",
-                spaces={2: pl.ANY},
-            )
-            results.append(done[-2])
-        if phase == 2:
-            done += call(merge_kernel, [narrow], gqs, 0, "grad_query")
-            results.append(done[-1])
-        return done
-
-    suffixes, done = scan(pieces, seq, True, backward)
+    suffixes, unused = scan(pieces, seq, True, backward)
     output, grad_q = results
     grad_k, grad_v = call(
         last_kernel,

time: 51 us -> 51.1 us (level)
  waiting for transfers between devices: 12.6 us -> 13.4 us
  Pallas kernels: 14.8 us -> 14.1 us
    ppermute x14, waiting for transfers between devices: 10.8 us -> 11.6 us  [exchange(): return lax.ppermute(value, 'seq', [(i, i ^ by) for i in range(size)])]
    pallas_call x14 -> x12, Pallas kernels: 14.8 us -> 14.1 us  [call(): return list(kernel(*args))]
  transfers between devices with their start and end apart: 17 -> 17, of which waited for: 13 -> 13; matrix products, arithmetic and copies ran while one was open for 0% -> 0% of each run, Pallas kernels for 19% -> 17%
where the time goes in v8:
time: 51.1 us; the launch traced here: 51 us
  starting transfers between devices  22.7 us (44%)
  Pallas kernels  14.1 us (28%)
  waiting for transfers between devices  13.4 us (26%)
  between operations  0.74 us (1%)
    ppermute x14, starting transfers between devices, exchange(): return lax.ppermute(value, 'seq', [(i, i ^ by) for i in range(size)])  20.8 us
    pallas_call x12, Pallas kernels, call(): return list(kernel(*args))  14.1 us
    ppermute x14, waiting for transfers between devices, exchange(): return lax.ppermute(value, 'seq', [(i, i ^ by) for i in range(size)])  11.6 us
    ppermute x3, starting transfers between devices, all_parts(): parts.append(lax.ppermute(values[by], axis, pairs))  1.92 us
    ppermute x3, waiting for transfers between devices, all_parts(): parts.append(lax.ppermute(values[by], axis, pairs))  1.87 us
  transfers between devices with their start and end apart: 17, of which 13 were waited for; matrix products, arithmetic and copies ran while one was open for 0% of the time, Pallas kernels for 17%

profile of v8, /device:TPU:0, one launch (start us, length us, event | category | flops | bytes accessed | tf_op | source)
XLA Modules:
  0.0 51.0 jit_solution(13689917689208988402)
XLA Ops:
  0.6 0.0 copy-start
  0.6 2.0 %local_state.1 = (f32[128,128]{1,0:T(8,128)S(1)}, f32[128,128]{1,0:T(8,128)S(1)}, f32[128,128]{1,0:T(8,128)S(1)}, f32[128,128]{1,0:T(8,128)S(1)}, bf16[1024,512]...) custom-call(bf16[1024,512]{1,0:T(8,128)(2,1)} %k_hbm.1, bf16[1024,512]{1,0:T(8,128)(2,1)} %v_hbm.1), custom_call_target="tpu_custom_call" | custom-call | flops 134217728 | bytes 4456448 | tf_op jit(solution)/shard_map/local_state/pallas_call | solution.py:57
  2.6 4.0 %collective-permute-start = (f32[128,128]{1,0:T(8,128)S(1)}, f32[128,128]{1,0:T(8,128)S(1)}, u32[]{:S(2)}, u32[]{:S(2)}) collective-permute-start(f32[128,128]{1,0:T(8,128)S(1)} %get-tuple-element.53), channel_id=1, source_target_pairs={{0,12},{4,8},{8,4},{12,0},{16,28},{20,24},{24,20},{28,16},{1,13},{... | collective-permute-start | bytes 196616 | tf_op jit(solution)/shard_map/ppermute | solution.py:66
  6.6 0.5 collective-permute-start.1
  7.1 0.2 collective-permute-start.2
  7.3 0.0 copy-done
  7.3 0.0 copy-start.1
  7.3 2.0 %intra.1 = (f32[1024,512]{1,0:T(8,128)S(1)}, f32[1536,128]{1,0:T(8,128)S(1)}, bf16[512,1024]{1,0:T(8,128)(2,1)S(1)}) custom-call(bf16[1024,512]{1,0:T(8,128)(2,1)S(1)} %copy-done, bf16[1024,512]{1,0:T(8,128)(2,1)S(1)} %get-tuple-element.49.k, bf16[1024,512]{1,0:T(8,128)(2,1)S(1)} %get-tuple-element.50.v), custom_call_target="tpu_custom_call" | custom-call | flops 805306368 | bytes 7077888 | tf_op jit(solution)/shard_map/intra/pallas_call | solution.py:57
  9.2 0.0 collective-permute-done.piece3
  9.2 1.7 %collective-permute-done.1.piece2 = f32[128,128]{1,0:T(8,128)S(1)} collective-permute-done((f32[128,128]{1,0:T(8,128)S(1)}, f32[128,128]{1,0:T(8,128)S(1)}, u32[]{:S(2)}, u32[]{:S(2)}) %collective-permute-start.1) | collective-permute-done | bytes 65568 | tf_op jit(solution)/shard_map/ppermute | solution.py:66
  10.9 0.5 collective-permute-done.2.piece1
  11.4 2.7 %collective-permute-start.3 = (f32[128,128]{1,0:T(8,128)S(1)}, f32[128,128]{1,0:T(8,128)S(1)}, u32[]{:S(2)}, u32[]{:S(2)}) collective-permute-start(f32[128,128]{1,0:T(8,128)S(1)} %quad_sum.2), channel_id=1, source_target_pairs={{0,16},{4,20},{8,24},{12,28},{16,0},{20,4},{24,8},{28,12},{1,17},{... | collective-permute-start | bytes 196616 | tf_op jit(solution)/shard_map/ppermute | solution.py:66
  14.0 2.6 %collective-permute-done.3.far = f32[128,128]{1,0:T(8,128)S(1)} collective-permute-done((f32[128,128]{1,0:T(8,128)S(1)}, f32[128,128]{1,0:T(8,128)S(1)}, u32[]{:S(2)}, u32[]{:S(2)}) %collective-permute-start.3) | collective-permute-done | bytes 65568 | tf_op jit(solution)/shard_map/ppermute | solution.py:66
  16.6 0.1 finish.2
  16.7 1.6 %collective-permute-start.4 = (f32[128,128]{1,0:T(8,128)S(1)}, f32[128,128]{1,0:T(8,128)S(1)}, u32[]{:S(2)}, u32[]{:S(2)}) collective-permute-start(f32[128,128]{1,0:T(8,128)S(1)} %get-tuple-element.58), channel_id=1, source_target_pairs={{0,12},{4,8},{8,4},{12,0},{16,28},{20,24},{24,20},{28,16},{1,13},{... | collective-permute-start | bytes 196616 | tf_op jit(solution)/shard_map/ppermute | solution.py:66
  18.3 0.4 collective-permute-start.5
  18.6 1.6 %collective-permute-start.6 = (f32[128,128]{1,0:T(8,128)S(1)}, f32[128,128]{1,0:T(8,128)S(1)}, u32[]{:S(2)}, u32[]{:S(2)}) collective-permute-start(f32[128,128]{1,0:T(8,128)S(1)} %get-tuple-element.60), channel_id=1, source_target_pairs={{0,4},{4,0},{8,12},{12,8},{16,20},{20,16},{24,28},{28,24},{1,5},{5... | collective-permute-start | bytes 196616 | tf_op jit(solution)/shard_map/ppermute | solution.py:66
  20.2 1.7 %collective-permute-done.4.refs_1_ = f32[128,128]{1,0:T(8,128)S(1)} collective-permute-done((f32[128,128]{1,0:T(8,128)S(1)}, f32[128,128]{1,0:T(8,128)S(1)}, u32[]{:S(2)}, u32[]{:S(2)}) %collective-permute-start.4) | collective-permute-done | bytes 65568 | tf_op jit(solution)/shard_map/ppermute | solution.py:66
  21.9 0.6 %collective-permute-done.5.refs_2_ = f32[128,128]{1,0:T(8,128)S(1)} collective-permute-done((f32[128,128]{1,0:T(8,128)S(1)}, f32[128,128]{1,0:T(8,128)S(1)}, u32[]{:S(2)}, u32[]{:S(2)}) %collective-permute-start.5) | collective-permute-done | bytes 65568 | tf_op jit(solution)/shard_map/ppermute | solution.py:66
  22.5 0.4 collective-permute-done.6.refs_3_
  22.9 0.0 copy-done.1
  22.9 0.8 %mixed.1 = (f32[1024,512]{1,0:T(8,128)S(1)}, bf16[512,128]{1,0:T(8,128)(2,1)S(1)}, f32[16,128]{1,0:T(8,128)S(1)}, f32[16,128]{1,0:T(8,128)S(1)}, f32[16,128]{1,0:T(8,128)S(1)}, /*index=5*/f32[16,128]{1,0:T(8,128)S(1)}) custom-call(f32[1024,512]{1,0:T(8,128)S(1)} %get-tuple-element.51.intra, bf16[1024,512]{1,0:T(8,128)(2,1)S(1)} %copy-done, ...), custom_call_target="tpu_custom_call" | custom-call | flops 134217728 | bytes 6717440 | tf_op jit(solution)/shard_map/mixed/pallas_call | solution.py:57
  23.7 0.1 collective-permute-start.7
  23.8 1.8 %collective-permute-start.8 = (f32[16,128]{1,0:T(8,128)S(1)}, f32[16,128]{1,0:T(8,128)S(1)}, u32[]{:S(2)}, u32[]{:S(2)}) collective-permute-start(f32[16,128]{1,0:T(8,128)S(1)} %get-tuple-element.64), channel_id=1, source_target_pairs={{0,2},{1,3},{2,0},{3,1},{4,6},{5,7},{6,4},{7,5},{8,10},{9,11},{10,... | collective-permute-start | bytes 24584 | tf_op jit(solution)/shard_map/ppermute | solution.py:341
  25.5 0.1 collective-permute-start.9
  25.6 1.2 %collective-permute-done.7.refs_1_ = f32[16,128]{1,0:T(8,128)S(1)} collective-permute-done((f32[16,128]{1,0:T(8,128)S(1)}, f32[16,128]{1,0:T(8,128)S(1)}, u32[]{:S(2)}, u32[]{:S(2)}) %collective-permute-start.7) | collective-permute-done | bytes 8224 | tf_op jit(solution)/shard_map/ppermute | solution.py:341
  26.8 0.7 %collective-permute-done.8.refs_2_ = f32[16,128]{1,0:T(8,128)S(1)} collective-permute-done((f32[16,128]{1,0:T(8,128)S(1)}, f32[16,128]{1,0:T(8,128)S(1)}, u32[]{:S(2)}, u32[]{:S(2)}) %collective-permute-start.8) | collective-permute-done | bytes 8224 | tf_op jit(solution)/shard_map/ppermute | solution.py:341
  27.5 0.0 collective-permute-done.9.refs_3_
  27.5 0.8 %norm.1 = (bf16[1024,512]{1,0:T(8,128)(2,1)S(1)}, f32[8,128]{1,0:T(8,128)S(1)}, f32[1536,128]{1,0:T(8,128)S(1)}, f32[128,128]{1,0:T(8,128)S(1)}, f32[128,128]{1,...) custom-call(f32[1024,512]{1,0:T(8,128)S(1)} %get-tuple-element.61.mixed, ...), custom_call_target="tpu_custom_call" | custom-call | flops 134217728 | bytes 6328320 | tf_op jit(solution)/shard_map/norm/pallas_call | solution.py:57
  28.3 2.7 %collective-permute-start.10 = (f32[128,128]{1,0:T(8,128)S(1)}, f32[128,128]{1,0:T(8,128)S(1)}, u32[]{:S(2)}, u32[]{:S(2)}) collective-permute-start(f32[128,128]{1,0:T(8,128)S(1)} %get-tuple-element.72), channel_id=1, source_target_pairs={{0,12},{4,8},{8,4},{12,0},{16,28},{20,24},{24,20},{28,16},{1,13},{... | collective-permute-start | bytes 196616 | tf_op jit(solution)/shard_map/ppermute | solution.py:66
  31.0 0.5 collective-permute-start.11
  31.5 0.4 collective-permute-start.12
  31.9 2.5 %first_grads.1 = (bf16[1024,128]{1,0:T(8,128)(2,1)S(1)}, bf16[1024,128]{1,0:T(8,128)(2,1)S(1)}, f32[1024,128]{1,0:T(8,128)S(1)}, f32[1024,128]{1,0:T(8,128)S(1)}...) custom-call(bf16[1024,512]{1,0:T(8,128)(2,1)S(1)} %copy-done, bf16[1024,512]{1,0:T(8,128)(2,1)S(1)} %get-tuple-element.49.k, ...), custom_call_target="tpu_custom_call" | custom-call | flops 1006632960 | bytes 8519680 | tf_op jit(solution)/shard_map/first_grads/pallas_call | solution.py:57
  34.4 0.0 collective-permute-done.10.piece3
  34.4 0.9 %collective-permute-done.11.piece2 = f32[128,128]{1,0:T(8,128)S(1)} collective-permute-done((f32[128,128]{1,0:T(8,128)S(1)}, f32[128,128]{1,0:T(8,128)S(1)}, u32[]{:S(2)}, u32[]{:S(2)}) %collective-permute-start.11) | collective-permute-done | bytes 65568 | tf_op jit(solution)/shard_map/ppermute | solution.py:66
  35.3 0.5 collective-permute-done.12.piece1
  35.7 2.8 %collective-permute-start.13 = (f32[128,128]{1,0:T(8,128)S(1)}, f32[128,128]{1,0:T(8,128)S(1)}, u32[]{:S(2)}, u32[]{:S(2)}) collective-permute-start(f32[128,128]{1,0:T(8,128)S(1)} %quad_sum.3.refs_0_), channel_id=1, source_target_pairs={{0,16},{4,20},{8,24},{12,28},{16,0},{20,4},{24,8},{28,12},{1,17},{... | collective-permute-start | bytes 196616 | tf_op jit(solution)/shard_map/ppermute | solution.py:66
  38.5 2.2 %second_grads.1 = (bf16[1024,128]{1,0:T(8,128)(2,1)S(1)}, f32[1024,128]{1,0:T(8,128)S(1)}, f32[1024,128]{1,0:T(8,128)S(1)}, bf16[1024,512]{1,0:T(8,128)(2,1)}) custom-call(bf16[1024,512]{1,0:T(8,128)(2,1)S(1)} %copy-done, bf16[1024,512]{1,0:T(8,128)(2,1)S(1)} %get-tuple-element.49.k, bf16[1024,512]{1,0:T(8,128)(2,1)S(1)} %get-tuple-element.50.v, ...), custom_call_target="tpu_custom_call" | custom-call | flops 503316480 | bytes 10424320 | tf_op jit(solution)/shard_map/second_grads/pallas_call | solution.py:57
  40.8 0.7 %collective-permute-done.13.far = f32[128,128]{1,0:T(8,128)S(1)} collective-permute-done((f32[128,128]{1,0:T(8,128)S(1)}, f32[128,128]{1,0:T(8,128)S(1)}, u32[]{:S(2)}, u32[]{:S(2)}) %collective-permute-start.13) | collective-permute-done | bytes 65568 | tf_op jit(solution)/shard_map/ppermute | solution.py:66
  41.5 0.1 finish.3
  41.6 1.8 %collective-permute-start.14 = (f32[128,128]{1,0:T(8,128)S(1)}, f32[128,128]{1,0:T(8,128)S(1)}, u32[]{:S(2)}, u32[]{:S(2)}) collective-permute-start(f32[128,128]{1,0:T(8,128)S(1)} %get-tuple-element.89), channel_id=1, source_target_pairs={{0,12},{4,8},{8,4},{12,0},{16,28},{20,24},{24,20},{28,16},{1,13},{... | collective-permute-start | bytes 196616 | tf_op jit(solution)/shard_map/ppermute | solution.py:66
  43.4 1.6 %collective-permute-start.15 = (f32[128,128]{1,0:T(8,128)S(1)}, f32[128,128]{1,0:T(8,128)S(1)}, u32[]{:S(2)}, u32[]{:S(2)}) collective-permute-start(f32[128,128]{1,0:T(8,128)S(1)} %get-tuple-element.90), channel_id=1, source_target_pairs={{0,8},{4,12},{8,0},{12,4},{16,24},{20,28},{24,16},{28,20},{1,9},{5... | collective-permute-start | bytes 196616 | tf_op jit(solution)/shard_map/ppermute | solution.py:66
  45.0 0.1 collective-permute-start.16
  45.1 2.0 %third_grads.1 = (f32[1024,128]{1,0:T(8,128)S(1)}, f32[1024,128]{1,0:T(8,128)S(1)}, bf16[1024,512]{1,0:T(8,128)(2,1)}) custom-call(bf16[1024,512]{1,0:T(8,128)(2,1)S(1)} %copy-done, bf16[1024,512]{1,0:T(8,128)(2,1)S(1)} %get-tuple-element.49.k, bf16[1024,512]{1,0:T(8,128)(2,1)S(1)} %get-tuple-element.50.v, bf16[1024,512]{1,0:T(8,128)(2,1)S(1)} %get-tuple-element.66.gm, ...), custom_call_target="tpu_custom_call" | custom-call | flops 503316480 | bytes 8847360 | tf_op jit(solution)/shard_map/third_grads/pallas_call | solution.py:57
  47.1 0.0 collective-permute-done.14.refs_9_
  47.1 0.8 %collective-permute-done.15.refs_10_ = f32[128,128]{1,0:T(8,128)S(1)} collective-permute-done((f32[128,128]{1,0:T(8,128)S(1)}, f32[128,128]{1,0:T(8,128)S(1)}, u32[]{:S(2)}, u32[]{:S(2)}) %collective-permute-start.15) | collective-permute-done | bytes 65568 | tf_op jit(solution)/shard_map/ppermute | solution.py:66
  47.9 1.3 %collective-permute-done.16.refs_11_ = f32[128,128]{1,0:T(8,128)S(1)} collective-permute-done((f32[128,128]{1,0:T(8,128)S(1)}, f32[128,128]{1,0:T(8,128)S(1)}, u32[]{:S(2)}, u32[]{:S(2)}) %collective-permute-start.16) | collective-permute-done | bytes 65568 | tf_op jit(solution)/shard_map/ppermute | solution.py:66
  49.2 1.7 %last.1 = (bf16[1024,512]{1,0:T(8,128)(2,1)}, bf16[1024,512]{1,0:T(8,128)(2,1)}) custom-call(bf16[1024,512]{1,0:T(8,128)(2,1)S(1)} %get-tuple-element.49.k, bf16[1024,512]{1,0:T(8,128)(2,1)S(1)} %get-tuple-element.50.v, f32[1024,128]{1,0:T(8,128)S(1)} %get-tuple-element.83.refs_0_, f32[1024,128]{1,0:T(8,128)S(1)} %get-tuple-element.75.refs_0_.refs_1_, ...), custom_call_target="tpu_custom_call" | custom-call | flops 268435456 | bytes 8650752 | tf_op jit(solution)/shard_map/last/pallas_call | solution.py:57
  (2 shorter events, 0.0 us)
Async XLA Ops:
  0.6 6.7 %copy-start = (bf16[1024,512]{1,0:T(8,128)(2,1)S(1)}, bf16[1024,512]{1,0:T(8,128)(2,1)}, u32[]{:S(2)}) copy-start(bf16[1024,512]{1,0:T(8,128)(2,1)} %q.9) | copy-start | bytes 3145732
  2.6 6.6 %collective-permute-start = (f32[128,128]{1,0:T(8,128)S(1)}, f32[128,128]{1,0:T(8,128)S(1)}, u32[]{:S(2)}, u32[]{:S(2)}) collective-permute-start(f32[128,128]{1,0:T(8,128)S(1)} %get-tuple-element.53), channel_id=1, source_target_pairs={{0,12},{4,8},{8,4},{12,0},{16,28},{20,24},{24,20},{28,16},{1,13},{... | collective-permute-start | bytes 196616 | tf_op jit(solution)/shard_map/ppermute | solution.py:66
  6.6 4.3 %collective-permute-start.1 = (f32[128,128]{1,0:T(8,128)S(1)}, f32[128,128]{1,0:T(8,128)S(1)}, u32[]{:S(2)}, u32[]{:S(2)}) collective-permute-start(f32[128,128]{1,0:T(8,128)S(1)} %get-tuple-element.54), channel_id=1, source_target_pairs={{0,8},{4,12},{8,0},{12,4},{16,24},{20,28},{24,16},{28,20},{1,9},{5... | collective-permute-start | bytes 196616 | tf_op jit(solution)/shard_map/ppermute | solution.py:66
  7.1 4.3 %collective-permute-start.2 = (f32[128,128]{1,0:T(8,128)S(1)}, f32[128,128]{1,0:T(8,128)S(1)}, u32[]{:S(2)}, u32[]{:S(2)}) collective-permute-start(f32[128,128]{1,0:T(8,128)S(1)} %get-tuple-element.55), channel_id=1, source_target_pairs={{0,4},{4,0},{8,12},{12,8},{16,20},{20,16},{24,28},{28,24},{1,5},{5... | collective-permute-start | bytes 196616 | tf_op jit(solution)/shard_map/ppermute | solution.py:66
  7.3 15.6 %copy-start.1 = (bf16[1024,512]{1,0:T(8,128)(2,1)S(1)}, bf16[1024,512]{1,0:T(8,128)(2,1)}, u32[]{:S(2)}) copy-start(bf16[1024,512]{1,0:T(8,128)(2,1)} %g.3) | copy-start | bytes 3145732
  11.4 5.2 %collective-permute-start.3 = (f32[128,128]{1,0:T(8,128)S(1)}, f32[128,128]{1,0:T(8,128)S(1)}, u32[]{:S(2)}, u32[]{:S(2)}) collective-permute-start(f32[128,128]{1,0:T(8,128)S(1)} %quad_sum.2), channel_id=1, source_target_pairs={{0,16},{4,20},{8,24},{12,28},{16,0},{20,4},{24,8},{28,12},{1,17},{... | collective-permute-start | bytes 196616 | tf_op jit(solution)/shard_map/ppermute | solution.py:66
  16.7 5.2 %collective-permute-start.4 = (f32[128,128]{1,0:T(8,128)S(1)}, f32[128,128]{1,0:T(8,128)S(1)}, u32[]{:S(2)}, u32[]{:S(2)}) collective-permute-start(f32[128,128]{1,0:T(8,128)S(1)} %get-tuple-element.58), channel_id=1, source_target_pairs={{0,12},{4,8},{8,4},{12,0},{16,28},{20,24},{24,20},{28,16},{1,13},{... | collective-permute-start | bytes 196616 | tf_op jit(solution)/shard_map/ppermute | solution.py:66
  18.3 4.3 %collective-permute-start.5 = (f32[128,128]{1,0:T(8,128)S(1)}, f32[128,128]{1,0:T(8,128)S(1)}, u32[]{:S(2)}, u32[]{:S(2)}) collective-permute-start(f32[128,128]{1,0:T(8,128)S(1)} %get-tuple-element.59), channel_id=1, source_target_pairs={{0,8},{4,12},{8,0},{12,4},{16,24},{20,28},{24,16},{28,20},{1,9},{5... | collective-permute-start | bytes 196616 | tf_op jit(solution)/shard_map/ppermute | solution.py:66
  18.6 4.3 %collective-permute-start.6 = (f32[128,128]{1,0:T(8,128)S(1)}, f32[128,128]{1,0:T(8,128)S(1)}, u32[]{:S(2)}, u32[]{:S(2)}) collective-permute-start(f32[128,128]{1,0:T(8,128)S(1)} %get-tuple-element.60), channel_id=1, source_target_pairs={{0,4},{4,0},{8,12},{12,8},{16,20},{20,16},{24,28},{28,24},{1,5},{5... | collective-permute-start | bytes 196616 | tf_op jit(solution)/shard_map/ppermute | solution.py:66
  23.7 3.1 %collective-permute-start.7 = (f32[16,128]{1,0:T(8,128)S(1)}, f32[16,128]{1,0:T(8,128)S(1)}, u32[]{:S(2)}, u32[]{:S(2)}) collective-permute-start(f32[16,128]{1,0:T(8,128)S(1)} %get-tuple-element.63), channel_id=1, source_target_pairs={{0,3},{1,2},{2,1},{3,0},{4,7},{5,6},{6,5},{7,4},{8,11},{9,10},{10,... | collective-permute-start | bytes 24584 | tf_op jit(solution)/shard_map/ppermute | solution.py:341
  23.8 3.7 %collective-permute-start.8 = (f32[16,128]{1,0:T(8,128)S(1)}, f32[16,128]{1,0:T(8,128)S(1)}, u32[]{:S(2)}, u32[]{:S(2)}) collective-permute-start(f32[16,128]{1,0:T(8,128)S(1)} %get-tuple-element.64), channel_id=1, source_target_pairs={{0,2},{1,3},{2,0},{3,1},{4,6},{5,7},{6,4},{7,5},{8,10},{9,11},{10,... | collective-permute-start | bytes 24584 | tf_op jit(solution)/shard_map/ppermute | solution.py:341
  25.5 2.0 %collective-permute-start.9 = (f32[16,128]{1,0:T(8,128)S(1)}, f32[16,128]{1,0:T(8,128)S(1)}, u32[]{:S(2)}, u32[]{:S(2)}) collective-permute-start(f32[16,128]{1,0:T(8,128)S(1)} %get-tuple-element.65), channel_id=1, source_target_pairs={{0,1},{1,0},{2,3},{3,2},{4,5},{5,4},{6,7},{7,6},{8,9},{9,8},{10,11... | collective-permute-start | bytes 24584 | tf_op jit(solution)/shard_map/ppermute | solution.py:341
  28.3 6.1 %collective-permute-start.10 = (f32[128,128]{1,0:T(8,128)S(1)}, f32[128,128]{1,0:T(8,128)S(1)}, u32[]{:S(2)}, u32[]{:S(2)}) collective-permute-start(f32[128,128]{1,0:T(8,128)S(1)} %get-tuple-element.72), channel_id=1, source_target_pairs={{0,12},{4,8},{8,4},{12,0},{16,28},{20,24},{24,20},{28,16},{1,13},{... | collective-permute-start | bytes 196616 | tf_op jit(solution)/shard_map/ppermute | solution.py:66
  31.0 4.3 %collective-permute-start.11 = (f32[128,128]{1,0:T(8,128)S(1)}, f32[128,128]{1,0:T(8,128)S(1)}, u32[]{:S(2)}, u32[]{:S(2)}) collective-permute-start(f32[128,128]{1,0:T(8,128)S(1)} %get-tuple-element.73), channel_id=1, source_target_pairs={{0,8},{4,12},{8,0},{12,4},{16,24},{20,28},{24,16},{28,20},{1,9},{5... | collective-permute-start | bytes 196616 | tf_op jit(solution)/shard_map/ppermute | solution.py:66
  31.5 4.3 %collective-permute-start.12 = (f32[128,128]{1,0:T(8,128)S(1)}, f32[128,128]{1,0:T(8,128)S(1)}, u32[]{:S(2)}, u32[]{:S(2)}) collective-permute-start(f32[128,128]{1,0:T(8,128)S(1)} %get-tuple-element.74), channel_id=1, source_target_pairs={{0,4},{4,0},{8,12},{12,8},{16,20},{20,16},{24,28},{28,24},{1,5},{5... | collective-permute-start | bytes 196616 | tf_op jit(solution)/shard_map/ppermute | solution.py:66
  35.7 5.7 %collective-permute-start.13 = (f32[128,128]{1,0:T(8,128)S(1)}, f32[128,128]{1,0:T(8,128)S(1)}, u32[]{:S(2)}, u32[]{:S(2)}) collective-permute-start(f32[128,128]{1,0:T(8,128)S(1)} %quad_sum.3.refs_0_), channel_id=1, source_target_pairs={{0,16},{4,20},{8,24},{12,28},{16,0},{20,4},{24,8},{28,12},{1,17},{... | collective-permute-start | bytes 196616 | tf_op jit(solution)/shard_map/ppermute | solution.py:66
  41.6 5.5 %collective-permute-start.14 = (f32[128,128]{1,0:T(8,128)S(1)}, f32[128,128]{1,0:T(8,128)S(1)}, u32[]{:S(2)}, u32[]{:S(2)}) collective-permute-start(f32[128,128]{1,0:T(8,128)S(1)} %get-tuple-element.89), channel_id=1, source_target_pairs={{0,12},{4,8},{8,4},{12,0},{16,28},{20,24},{24,20},{28,16},{1,13},{... | collective-permute-start | bytes 196616 | tf_op jit(solution)/shard_map/ppermute | solution.py:66
  43.4 4.5 %collective-permute-start.15 = (f32[128,128]{1,0:T(8,128)S(1)}, f32[128,128]{1,0:T(8,128)S(1)}, u32[]{:S(2)}, u32[]{:S(2)}) collective-permute-start(f32[128,128]{1,0:T(8,128)S(1)} %get-tuple-element.90), channel_id=1, source_target_pairs={{0,8},{4,12},{8,0},{12,4},{16,24},{20,28},{24,16},{28,20},{1,9},{5... | collective-permute-start | bytes 196616 | tf_op jit(solution)/shard_map/ppermute | solution.py:66
  45.0 4.3 %collective-permute-start.16 = (f32[128,128]{1,0:T(8,128)S(1)}, f32[128,128]{1,0:T(8,128)S(1)}, u32[]{:S(2)}, u32[]{:S(2)}) collective-permute-start(f32[128,128]{1,0:T(8,128)S(1)} %get-tuple-element.91), channel_id=1, source_target_pairs={{0,4},{4,0},{8,12},{12,8},{16,20},{20,16},{24,28},{28,24},{1,5},{5... | collective-permute-start | bytes 196616 | tf_op jit(solution)/shard_map/ppermute | solution.py:66

commit v9 on v8

--- a/solution.py
+++ b/solution.py
@@ -13,7 +13,10 @@
 CHUNK = 256
 PAIR = 2 * HEAD_DIM
 QUAD = 4
-ORDER = (0, 3, 2, 1)
+ORDERS = {
+    False: (((3, 2, 1), (3, 2, 1)), ((3, 2, 1), (3, 2, 1))),
+    True: (((3, 1, 2), (3, 1, 2)), ((3, 1, 2), (3, 1, 2))),
+}
 F32 = jnp.float32
 BF16 = jnp.bfloat16
 
@@ -57,44 +60,65 @@
     return list(kernel(*args))
 
 
-def head_of(n):
-    number = lax.rem(lax.axis_index("seq"), QUAD) ^ n
-    return pl.ds(pl.multiple_of(number * HEAD_DIM, HEAD_DIM), HEAD_DIM)
-
-
-def exchange(value, size, by):
-    return lax.ppermute(value, "seq", [(i, i ^ by) for i in range(size)])
-
-
-def quad_kernel(piece0, piece3, piece2, piece1, *refs):
-    refs[-1][...] = (piece0[...] + piece1[...]) + (piece2[...] + piece3[...])
-
-
-def finish_kernel(reverse, piece0, piece3, piece2, piece1, far, *refs):
+def partner(order, slot):
+    if slot == 0:
+        return 0
+    even, odd = (choice[slot - 1] for choice in order)
+    if even == odd:
+        return even
+    return jnp.where(lax.rem(lax.axis_index("head"), 2) == 1, odd, even)
+
+
+def number_at(order, slot):
+    return lax.rem(lax.axis_index("seq"), QUAD) ^ partner(order, slot)
+
+
+def rows_at(order, slot):
+    return pl.ds(pl.multiple_of(number_at(order, slot) * HEAD_DIM, HEAD_DIM), HEAD_DIM)
+
+
+def exchange(value, sizes, by):
+    size, heads = sizes
+    pairs = [
+        (i * heads + h, (i ^ by[h % 2]) * heads + h) for i in range(size) for h in range(heads)
+    ]
+    return lax.ppermute(value, ("seq", "head"), pairs)
+
+
+def exchange_all(pieces, sizes, order):
+    even, odd = order
+    return pieces[:1] + [exchange(p, sizes, by) for p, by in zip(pieces[1:], zip(even, odd))]
+
+
+def quad_kernel(*refs):
+    refs[-1][...] = (refs[0][...] + refs[1][...]) + (refs[2][...] + refs[3][...])
+
+
+def finish_kernel(reverse, *refs):
+    into, out_of = ORDERS[reverse]
     place = lax.axis_index("seq")
-    number = lax.rem(place, QUAD)
-    pieces = [p[...] for p in (piece0, piece1, piece2, piece3)]
-    zero = jnp.zeros(far.shape, F32)
+    zero = jnp.zeros(refs[0].shape, F32)
     second = place < QUAD if reverse else place >= QUAD
-    before = jnp.where(second, far[...], zero)
+    before = jnp.where(second, refs[QUAD][...], zero)
     for to, out in enumerate(refs[-QUAD:]):
+        here = number_at(out_of, to)
         total = before
-        for n, piece in enumerate(pieces):
-            ahead = (number ^ n) > (number ^ to) if reverse else (number ^ n) < (number ^ to)
-            if n != to:
-                total = total + jnp.where(ahead, piece, zero)
+        for slot in range(QUAD):
+            number = number_at(into, slot)
+            ahead = number > here if reverse else number < here
+            total = total + jnp.where(ahead, refs[slot][...], zero)
         out[...] = total
 
 
-def quad_scan(pieces, size, reverse, between):
+def quad_scan(pieces, sizes, reverse, between):
     head = jax.ShapeDtypeStruct((HEAD_DIM, HEAD_DIM), F32)
-    got = {by: exchange(pieces[by], size, by) for by in (3, 2, 1)}
-    pieces = [pieces[0], got[3], got[2], got[1]]
+    into, out_of = ORDERS[reverse]
+    pieces = exchange_all(pieces, sizes, into)
     first = between(0, None)
     (total,) = call(
         quad_kernel, [head], [*pieces, *first[-1:]], 0, "quad_sum", spaces={4: pl.ANY}
     )
-    far = exchange(total, size, QUAD)
+    far = exchange(total, sizes, (QUAD, QUAD))
     second = between(1, total)
     finished = call(
         functools.partial(finish_kernel, reverse),
@@ -104,44 +128,44 @@
         "finish",
         spaces={5: pl.ANY},
     )
-    got = {by: exchange(finished[by], size, by) for by in (3, 2, 1)}
     third = between(2, finished[0])
-    return [finished[0], got[3], got[2], got[1]], first + second + third
-
-
-def doubling_scan(pieces, size, reverse, between):
+    return exchange_all(finished, sizes, out_of), first + second + third
+
+
+def doubling_scan(pieces, sizes, reverse, between):
+    size = sizes[0]
+
     def shift(value, by):
         pairs = [(i, i + by) for i in range(size - by)]
         if reverse:
             pairs = [(b, a) for a, b in pairs]
         return lax.ppermute(value, "seq", pairs)
 
-    def reorder(state):
-        number = lax.rem(lax.axis_index("seq"), QUAD)
-        return jnp.take(state, number ^ jnp.arange(QUAD), axis=0)
-
-    state = reorder(jnp.stack(pieces))
+    into, out_of = (
+        jnp.stack([number_at(order, slot) for slot in range(QUAD)]) for order in ORDERS[reverse]
+    )
+    state = jnp.stack(pieces)[jnp.argsort(into)]
     by = 1
     while by < size:
         state = state + shift(state, by)
         by *= 2
-    state = reorder(shift(state, 1))
+    state = shift(state, 1)[out_of]
     done = []
     for phase in range(3):
         done += between(phase, done[-1] if done else None)
-    return [state[n] for n in ORDER], done
-
-
-def store_pieces(states, pieces, scratch):
+    return [state[n] for n in range(QUAD)], done
+
+
+def store_pieces(states, order, pieces, scratch):
     for h, state in enumerate(states):
         scratch[head_slice(h), :] = state
-    for n, piece in enumerate(pieces):
-        piece[...] = scratch[head_of(n), :]
-
-
-def load_pieces(pieces, rounded):
-    for n, piece in zip(ORDER, pieces):
-        rounded[head_of(n), :] = piece[...].astype(BF16)
+    for slot, piece in enumerate(pieces):
+        piece[...] = scratch[rows_at(order, slot), :]
+
+
+def load_pieces(pieces, order, rounded):
+    for slot, piece in enumerate(pieces):
+        rounded[rows_at(order, slot), :] = piece[...].astype(BF16)
 
 
 def pair_blocks(left, right, contract):
@@ -170,7 +194,7 @@
         copies[2 * n].wait()
         copies[2 * n + 1].wait()
         total = add_all(total, pair_blocks(k[at, :], v[at, :], 0))
-    store_pieces(total, pieces, scratch)
+    store_pieces(total, ORDERS[False][0], pieces, scratch)
 
 
 def intra_kernel(q, k, v, intra, states, q_t):
@@ -198,7 +222,7 @@
 
 def mixed_kernel(intra, q, g, *refs):
     pieces, (mixed, prefix, stats, *copies) = refs[:QUAD], refs[QUAD:]
-    load_pieces(pieces, prefix)
+    load_pieces(pieces, ORDERS[False][1], prefix)
     blocks = q.shape[0] // HEAD_DIM
     for at in chunk_slices(q.shape[0]):
         square = cross = None
@@ -244,7 +268,7 @@
             for h, state in enumerate(after):
                 first = (n - 1) * cols + h * HEAD_DIM
                 states[first : first + HEAD_DIM, :] = state
-    store_pieces(after, pieces, scratch)
+    store_pieces(after, ORDERS[True][0], pieces, scratch)
 
 
 def head_grads(h, q, k, v, gm, prefix, states, after, gq, gk, gv, finished=None):
@@ -317,7 +341,7 @@
 def last_kernel(k, v, *refs):
     gks, gvs, pieces = (refs[i * QUAD : (i + 1) * QUAD] for i in range(3))
     gk_hbm, gv_hbm, gk, gv, suffix, sems = refs[-6:]
-    load_pieces(pieces, suffix)
+    load_pieces(pieces, ORDERS[True][1], suffix)
     copies = []
     for n, at in enumerate(chunk_slices(k.shape[0])):
         for h in range(QUAD):
@@ -381,7 +405,7 @@
             "intra",
         )
 
-    prefixes, (intra, states, queries_t) = scan(pieces, seq, False, forward)
+    prefixes, (intra, states, queries_t) = scan(pieces, sizes, False, forward)
     mixed, prefix, *stats = call(
         mixed_kernel,
         [wide, shape(cols, HEAD_DIM, BF16)] + [shape(2 * blocks, HEAD_DIM)] * head_size,
@@ -445,7 +469,7 @@
         return gks[-1:]
 
     gqs, gks, gvs, results = [], [], [], []
-    suffixes, unused = scan(pieces, seq, True, backward)
+    suffixes, unused = scan(pieces, sizes, True, backward)
     output, grad_q = results
     grad_k, grad_v = call(
         last_kernel,

time: 51.1 us -> 50.1 us (0.980)
  waiting for transfers between devices: 13.4 us -> 11.9 us
    ppermute x14, waiting for transfers between devices: 11.6 us -> 9.99 us  [exchange(): return lax.ppermute(value, ('seq', 'head'), pairs)]
    ppermute x14, starting transfers between devices: 20.8 us -> 21.3 us  [exchange(): return lax.ppermute(value, ('seq', 'head'), pairs)]
  transfers between devices with their start and end apart: 17 -> 17, of which waited for: 13 -> 12; matrix products, arithmetic and copies ran while one was open for 0% -> 0% of each run, Pallas kernels for 17% -> 17%
where the time goes in v9:
time: 50.1 us; the launch traced here: 49.9 us
  starting transfers between devices  23.2 us (46%)
  Pallas kernels  14.1 us (28%)
  waiting for transfers between devices  11.9 us (24%)
  between operations  0.75 us (1%)
    ppermute x14, starting transfers between devices, exchange(): return lax.ppermute(value, ('seq', 'head'), pairs)  21.3 us
    pallas_call x12, Pallas kernels, call(): return list(kernel(*args))  14.1 us
    ppermute x14, waiting for transfers between devices, exchange(): return lax.ppermute(value, ('seq', 'head'), pairs)  9.99 us
    ppermute x3, starting transfers between devices, all_parts(): parts.append(lax.ppermute(values[by], axis, pairs))  1.92 us
    ppermute x3, waiting for transfers between devices, all_parts(): parts.append(lax.ppermute(values[by], axis, pairs))  1.87 us
  transfers between devices with their start and end apart: 17, of which 12 were waited for; matrix products, arithmetic and copies ran while one was open for 0% of the time, Pallas kernels for 17%

profile of v9, /device:TPU:0, one launch (start us, length us, event | category | flops | bytes accessed | tf_op | source)
XLA Modules:
  0.0 49.9 jit_solution(6569113828086884450)
XLA Ops:
  0.6 0.0 copy-start
  0.6 2.0 %local_state.1 = (f32[128,128]{1,0:T(8,128)S(1)}, f32[128,128]{1,0:T(8,128)S(1)}, f32[128,128]{1,0:T(8,128)S(1)}, f32[128,128]{1,0:T(8,128)S(1)}, bf16[1024,512]...) custom-call(bf16[1024,512]{1,0:T(8,128)(2,1)} %k_hbm.1, bf16[1024,512]{1,0:T(8,128)(2,1)} %v_hbm.1), custom_call_target="tpu_custom_call" | custom-call | flops 134217728 | bytes 4456448 | tf_op jit(solution)/shard_map/local_state/pallas_call | solution.py:60
  2.6 4.0 %collective-permute-start = (f32[128,128]{1,0:T(8,128)S(1)}, f32[128,128]{1,0:T(8,128)S(1)}, u32[]{:S(2)}, u32[]{:S(2)}) collective-permute-start(f32[128,128]{1,0:T(8,128)S(1)} %get-tuple-element.53), channel_id=1, source_target_pairs={{0,12},{1,13},{2,14},{3,15},{4,8},{5,9},{6,10},{7,11},{8,4},{9,5},... | collective-permute-start | bytes 196616 | tf_op jit(solution)/shard_map/ppermute | solution.py:85
  6.6 0.5 collective-permute-start.1
  7.1 0.2 collective-permute-start.2
  7.3 0.0 copy-done
  7.3 0.0 copy-start.1
  7.3 2.0 %intra.1 = (f32[1024,512]{1,0:T(8,128)S(1)}, f32[1536,128]{1,0:T(8,128)S(1)}, bf16[512,1024]{1,0:T(8,128)(2,1)S(1)}) custom-call(bf16[1024,512]{1,0:T(8,128)(2,1)S(1)} %copy-done, bf16[1024,512]{1,0:T(8,128)(2,1)S(1)} %get-tuple-element.49.k, bf16[1024,512]{1,0:T(8,128)(2,1)S(1)} %get-tuple-element.50.v), custom_call_target="tpu_custom_call" | custom-call | flops 805306368 | bytes 7077888 | tf_op jit(solution)/shard_map/intra/pallas_call | solution.py:60
  9.2 0.0 collective-permute-done.refs_1_
  9.2 1.7 %collective-permute-done.1.refs_2_ = f32[128,128]{1,0:T(8,128)S(1)} collective-permute-done((f32[128,128]{1,0:T(8,128)S(1)}, f32[128,128]{1,0:T(8,128)S(1)}, u32[]{:S(2)}, u32[]{:S(2)}) %collective-permute-start.1) | collective-permute-done | bytes 65568 | tf_op jit(solution)/shard_map/ppermute | solution.py:85
  10.9 0.5 collective-permute-done.2.refs_3_
  11.4 2.7 %collective-permute-start.3 = (f32[128,128]{1,0:T(8,128)S(1)}, f32[128,128]{1,0:T(8,128)S(1)}, u32[]{:S(2)}, u32[]{:S(2)}) collective-permute-start(f32[128,128]{1,0:T(8,128)S(1)} %quad_sum.2), channel_id=1, source_target_pairs={{0,16},{1,17},{2,18},{3,19},{4,20},{5,21},{6,22},{7,23},{8,24},{9,... | collective-permute-start | bytes 196616 | tf_op jit(solution)/shard_map/ppermute | solution.py:85
  14.0 2.6 %collective-permute-done.3.refs_4_ = f32[128,128]{1,0:T(8,128)S(1)} collective-permute-done((f32[128,128]{1,0:T(8,128)S(1)}, f32[128,128]{1,0:T(8,128)S(1)}, u32[]{:S(2)}, u32[]{:S(2)}) %collective-permute-start.3) | collective-permute-done | bytes 65568 | tf_op jit(solution)/shard_map/ppermute | solution.py:85
  16.6 0.1 finish.2
  16.7 1.6 %collective-permute-start.4 = (f32[128,128]{1,0:T(8,128)S(1)}, f32[128,128]{1,0:T(8,128)S(1)}, u32[]{:S(2)}, u32[]{:S(2)}) collective-permute-start(f32[128,128]{1,0:T(8,128)S(1)} %get-tuple-element.58), channel_id=1, source_target_pairs={{0,12},{1,13},{2,14},{3,15},{4,8},{5,9},{6,10},{7,11},{8,4},{9,5},... | collective-permute-start | bytes 196616 | tf_op jit(solution)/shard_map/ppermute | solution.py:85
  18.3 0.4 collective-permute-start.5
  18.6 1.6 %collective-permute-start.6 = (f32[128,128]{1,0:T(8,128)S(1)}, f32[128,128]{1,0:T(8,128)S(1)}, u32[]{:S(2)}, u32[]{:S(2)}) collective-permute-start(f32[128,128]{1,0:T(8,128)S(1)} %get-tuple-element.60), channel_id=1, source_target_pairs={{0,4},{1,5},{2,6},{3,7},{4,0},{5,1},{6,2},{7,3},{8,12},{9,13},{10,... | collective-permute-start | bytes 196616 | tf_op jit(solution)/shard_map/ppermute | solution.py:85
  20.2 1.7 %collective-permute-done.4.refs_1_ = f32[128,128]{1,0:T(8,128)S(1)} collective-permute-done((f32[128,128]{1,0:T(8,128)S(1)}, f32[128,128]{1,0:T(8,128)S(1)}, u32[]{:S(2)}, u32[]{:S(2)}) %collective-permute-start.4) | collective-permute-done | bytes 65568 | tf_op jit(solution)/shard_map/ppermute | solution.py:85
  21.9 0.6 %collective-permute-done.5.refs_2_ = f32[128,128]{1,0:T(8,128)S(1)} collective-permute-done((f32[128,128]{1,0:T(8,128)S(1)}, f32[128,128]{1,0:T(8,128)S(1)}, u32[]{:S(2)}, u32[]{:S(2)}) %collective-permute-start.5) | collective-permute-done | bytes 65568 | tf_op jit(solution)/shard_map/ppermute | solution.py:85
  22.5 0.4 collective-permute-done.6.refs_3_
  22.9 0.0 copy-done.1
  22.9 0.8 %mixed.1 = (f32[1024,512]{1,0:T(8,128)S(1)}, bf16[512,128]{1,0:T(8,128)(2,1)S(1)}, f32[16,128]{1,0:T(8,128)S(1)}, f32[16,128]{1,0:T(8,128)S(1)}, f32[16,128]{1,0:T(8,128)S(1)}, /*index=5*/f32[16,128]{1,0:T(8,128)S(1)}) custom-call(f32[1024,512]{1,0:T(8,128)S(1)} %get-tuple-element.51.intra, bf16[1024,512]{1,0:T(8,128)(2,1)S(1)} %copy-done, ...), custom_call_target="tpu_custom_call" | custom-call | flops 134217728 | bytes 6717440 | tf_op jit(solution)/shard_map/mixed/pallas_call | solution.py:60
  23.7 0.1 collective-permute-start.7
  23.8 1.8 %collective-permute-start.8 = (f32[16,128]{1,0:T(8,128)S(1)}, f32[16,128]{1,0:T(8,128)S(1)}, u32[]{:S(2)}, u32[]{:S(2)}) collective-permute-start(f32[16,128]{1,0:T(8,128)S(1)} %get-tuple-element.64), channel_id=1, source_target_pairs={{0,2},{1,3},{2,0},{3,1},{4,6},{5,7},{6,4},{7,5},{8,10},{9,11},{10,... | collective-permute-start | bytes 24584 | tf_op jit(solution)/shard_map/ppermute | solution.py:365
  25.5 0.1 collective-permute-start.9
  25.6 1.2 %collective-permute-done.7.refs_1_ = f32[16,128]{1,0:T(8,128)S(1)} collective-permute-done((f32[16,128]{1,0:T(8,128)S(1)}, f32[16,128]{1,0:T(8,128)S(1)}, u32[]{:S(2)}, u32[]{:S(2)}) %collective-permute-start.7) | collective-permute-done | bytes 8224 | tf_op jit(solution)/shard_map/ppermute | solution.py:365
  26.8 0.7 %collective-permute-done.8.refs_2_ = f32[16,128]{1,0:T(8,128)S(1)} collective-permute-done((f32[16,128]{1,0:T(8,128)S(1)}, f32[16,128]{1,0:T(8,128)S(1)}, u32[]{:S(2)}, u32[]{:S(2)}) %collective-permute-start.8) | collective-permute-done | bytes 8224 | tf_op jit(solution)/shard_map/ppermute | solution.py:365
  27.5 0.0 collective-permute-done.9.refs_3_
  27.5 0.8 %norm.1 = (bf16[1024,512]{1,0:T(8,128)(2,1)S(1)}, f32[8,128]{1,0:T(8,128)S(1)}, f32[1536,128]{1,0:T(8,128)S(1)}, f32[128,128]{1,0:T(8,128)S(1)}, f32[128,128]{1,...) custom-call(f32[1024,512]{1,0:T(8,128)S(1)} %get-tuple-element.61.mixed, ...), custom_call_target="tpu_custom_call" | custom-call | flops 134217728 | bytes 6328320 | tf_op jit(solution)/shard_map/norm/pallas_call | solution.py:60
  28.3 2.7 %collective-permute-start.10 = (f32[128,128]{1,0:T(8,128)S(1)}, f32[128,128]{1,0:T(8,128)S(1)}, u32[]{:S(2)}, u32[]{:S(2)}) collective-permute-start(f32[128,128]{1,0:T(8,128)S(1)} %get-tuple-element.72), channel_id=1, source_target_pairs={{0,12},{1,13},{2,14},{3,15},{4,8},{5,9},{6,10},{7,11},{8,4},{9,5},... | collective-permute-start | bytes 196616 | tf_op jit(solution)/shard_map/ppermute | solution.py:85
  31.0 0.5 %collective-permute-start.11 = (f32[128,128]{1,0:T(8,128)S(1)}, f32[128,128]{1,0:T(8,128)S(1)}, u32[]{:S(2)}, u32[]{:S(2)}) collective-permute-start(f32[128,128]{1,0:T(8,128)S(1)} %get-tuple-element.73), channel_id=1, source_target_pairs={{0,4},{1,5},{2,6},{3,7},{4,0},{5,1},{6,2},{7,3},{8,12},{9,13},{10,... | collective-permute-start | bytes 196616 | tf_op jit(solution)/shard_map/ppermute | solution.py:85
  31.5 0.4 collective-permute-start.12
  31.9 2.5 %first_grads.1 = (bf16[1024,128]{1,0:T(8,128)(2,1)S(1)}, bf16[1024,128]{1,0:T(8,128)(2,1)S(1)}, f32[1024,128]{1,0:T(8,128)S(1)}, f32[1024,128]{1,0:T(8,128)S(1)}...) custom-call(bf16[1024,512]{1,0:T(8,128)(2,1)S(1)} %copy-done, bf16[1024,512]{1,0:T(8,128)(2,1)S(1)} %get-tuple-element.49.k, ...), custom_call_target="tpu_custom_call" | custom-call | flops 1006632960 | bytes 8519680 | tf_op jit(solution)/shard_map/first_grads/pallas_call | solution.py:60
  34.4 0.0 collective-permute-done.10.refs_1_
  34.4 0.9 %collective-permute-done.11.refs_2_ = f32[128,128]{1,0:T(8,128)S(1)} collective-permute-done((f32[128,128]{1,0:T(8,128)S(1)}, f32[128,128]{1,0:T(8,128)S(1)}, u32[]{:S(2)}, u32[]{:S(2)}) %collective-permute-start.11) | collective-permute-done | bytes 65568 | tf_op jit(solution)/shard_map/ppermute | solution.py:85
  35.3 0.5 %collective-permute-done.12.refs_3_ = f32[128,128]{1,0:T(8,128)S(1)} collective-permute-done((f32[128,128]{1,0:T(8,128)S(1)}, f32[128,128]{1,0:T(8,128)S(1)}, u32[]{:S(2)}, u32[]{:S(2)}) %collective-permute-start.12) | collective-permute-done | bytes 65568 | tf_op jit(solution)/shard_map/ppermute | solution.py:85
  35.8 3.3 %collective-permute-start.13 = (f32[128,128]{1,0:T(8,128)S(1)}, f32[128,128]{1,0:T(8,128)S(1)}, u32[]{:S(2)}, u32[]{:S(2)}) collective-permute-start(f32[128,128]{1,0:T(8,128)S(1)} %quad_sum.3.refs_0_), channel_id=1, source_target_pairs={{0,16},{1,17},{2,18},{3,19},{4,20},{5,21},{6,22},{7,23},{8,24},{9,... | collective-permute-start | bytes 196616 | tf_op jit(solution)/shard_map/ppermute | solution.py:85
  39.1 2.2 %second_grads.1 = (bf16[1024,128]{1,0:T(8,128)(2,1)S(1)}, f32[1024,128]{1,0:T(8,128)S(1)}, f32[1024,128]{1,0:T(8,128)S(1)}, bf16[1024,512]{1,0:T(8,128)(2,1)}) custom-call(bf16[1024,512]{1,0:T(8,128)(2,1)S(1)} %copy-done, bf16[1024,512]{1,0:T(8,128)(2,1)S(1)} %get-tuple-element.49.k, bf16[1024,512]{1,0:T(8,128)(2,1)S(1)} %get-tuple-element.50.v, ...), custom_call_target="tpu_custom_call" | custom-call | flops 503316480 | bytes 10424320 | tf_op jit(solution)/shard_map/second_grads/pallas_call | solution.py:60
  41.3 0.8 %collective-permute-done.13.refs_4_ = f32[128,128]{1,0:T(8,128)S(1)} collective-permute-done((f32[128,128]{1,0:T(8,128)S(1)}, f32[128,128]{1,0:T(8,128)S(1)}, u32[]{:S(2)}, u32[]{:S(2)}) %collective-permute-start.13) | collective-permute-done | bytes 65568 | tf_op jit(solution)/shard_map/ppermute | solution.py:85
  42.1 0.1 finish.3
  42.2 0.5 collective-permute-start.14
  42.7 1.3 %collective-permute-start.15 = (f32[128,128]{1,0:T(8,128)S(1)}, f32[128,128]{1,0:T(8,128)S(1)}, u32[]{:S(2)}, u32[]{:S(2)}) collective-permute-start(f32[128,128]{1,0:T(8,128)S(1)} %get-tuple-element.90), channel_id=1, source_target_pairs={{0,4},{1,5},{2,6},{3,7},{4,0},{5,1},{6,2},{7,3},{8,12},{9,13},{10,... | collective-permute-start | bytes 196616 | tf_op jit(solution)/shard_map/ppermute | solution.py:85
  44.0 1.8 %collective-permute-start.16 = (f32[128,128]{1,0:T(8,128)S(1)}, f32[128,128]{1,0:T(8,128)S(1)}, u32[]{:S(2)}, u32[]{:S(2)}) collective-permute-start(f32[128,128]{1,0:T(8,128)S(1)} %get-tuple-element.91), channel_id=1, source_target_pairs={{0,8},{1,9},{2,10},{3,11},{4,12},{5,13},{6,14},{7,15},{8,0},{9,1},... | collective-permute-start | bytes 196616 | tf_op jit(solution)/shard_map/ppermute | solution.py:85
  45.8 2.0 %third_grads.1 = (f32[1024,128]{1,0:T(8,128)S(1)}, f32[1024,128]{1,0:T(8,128)S(1)}, bf16[1024,512]{1,0:T(8,128)(2,1)}) custom-call(bf16[1024,512]{1,0:T(8,128)(2,1)S(1)} %copy-done, bf16[1024,512]{1,0:T(8,128)(2,1)S(1)} %get-tuple-element.49.k, bf16[1024,512]{1,0:T(8,128)(2,1)S(1)} %get-tuple-element.50.v, bf16[1024,512]{1,0:T(8,128)(2,1)S(1)} %get-tuple-element.66.gm, ...), custom_call_target="tpu_custom_call" | custom-call | flops 503316480 | bytes 8847360 | tf_op jit(solution)/shard_map/third_grads/pallas_call | solution.py:60
  47.8 0.0 collective-permute-done.14.refs_9_
  47.8 0.0 collective-permute-done.15.refs_10_
  47.8 0.4 collective-permute-done.16.refs_11_
  48.2 1.7 %last.1 = (bf16[1024,512]{1,0:T(8,128)(2,1)}, bf16[1024,512]{1,0:T(8,128)(2,1)}) custom-call(bf16[1024,512]{1,0:T(8,128)(2,1)S(1)} %get-tuple-element.49.k, bf16[1024,512]{1,0:T(8,128)(2,1)S(1)} %get-tuple-element.50.v, f32[1024,128]{1,0:T(8,128)S(1)} %get-tuple-element.83.refs_0_, f32[1024,128]{1,0:T(8,128)S(1)} %get-tuple-element.75.refs_4_.refs_1_, ...), custom_call_target="tpu_custom_call" | custom-call | flops 268435456 | bytes 8650752 | tf_op jit(solution)/shard_map/last/pallas_call | solution.py:60
  (2 shorter events, 0.0 us)
Async XLA Ops:
  0.6 6.7 %copy-start = (bf16[1024,512]{1,0:T(8,128)(2,1)S(1)}, bf16[1024,512]{1,0:T(8,128)(2,1)}, u32[]{:S(2)}) copy-start(bf16[1024,512]{1,0:T(8,128)(2,1)} %q.9) | copy-start | bytes 3145732
  2.6 6.6 %collective-permute-start = (f32[128,128]{1,0:T(8,128)S(1)}, f32[128,128]{1,0:T(8,128)S(1)}, u32[]{:S(2)}, u32[]{:S(2)}) collective-permute-start(f32[128,128]{1,0:T(8,128)S(1)} %get-tuple-element.53), channel_id=1, source_target_pairs={{0,12},{1,13},{2,14},{3,15},{4,8},{5,9},{6,10},{7,11},{8,4},{9,5},... | collective-permute-start | bytes 196616 | tf_op jit(solution)/shard_map/ppermute | solution.py:85
  6.6 4.3 %collective-permute-start.1 = (f32[128,128]{1,0:T(8,128)S(1)}, f32[128,128]{1,0:T(8,128)S(1)}, u32[]{:S(2)}, u32[]{:S(2)}) collective-permute-start(f32[128,128]{1,0:T(8,128)S(1)} %get-tuple-element.54), channel_id=1, source_target_pairs={{0,8},{1,9},{2,10},{3,11},{4,12},{5,13},{6,14},{7,15},{8,0},{9,1},... | collective-permute-start | bytes 196616 | tf_op jit(solution)/shard_map/ppermute | solution.py:85
  7.1 4.3 %collective-permute-start.2 = (f32[128,128]{1,0:T(8,128)S(1)}, f32[128,128]{1,0:T(8,128)S(1)}, u32[]{:S(2)}, u32[]{:S(2)}) collective-permute-start(f32[128,128]{1,0:T(8,128)S(1)} %get-tuple-element.55), channel_id=1, source_target_pairs={{0,4},{1,5},{2,6},{3,7},{4,0},{5,1},{6,2},{7,3},{8,12},{9,13},{10,... | collective-permute-start | bytes 196616 | tf_op jit(solution)/shard_map/ppermute | solution.py:85
  7.3 15.6 %copy-start.1 = (bf16[1024,512]{1,0:T(8,128)(2,1)S(1)}, bf16[1024,512]{1,0:T(8,128)(2,1)}, u32[]{:S(2)}) copy-start(bf16[1024,512]{1,0:T(8,128)(2,1)} %g.3) | copy-start | bytes 3145732
  11.4 5.2 %collective-permute-start.3 = (f32[128,128]{1,0:T(8,128)S(1)}, f32[128,128]{1,0:T(8,128)S(1)}, u32[]{:S(2)}, u32[]{:S(2)}) collective-permute-start(f32[128,128]{1,0:T(8,128)S(1)} %quad_sum.2), channel_id=1, source_target_pairs={{0,16},{1,17},{2,18},{3,19},{4,20},{5,21},{6,22},{7,23},{8,24},{9,... | collective-permute-start | bytes 196616 | tf_op jit(solution)/shard_map/ppermute | solution.py:85
  16.7 5.2 %collective-permute-start.4 = (f32[128,128]{1,0:T(8,128)S(1)}, f32[128,128]{1,0:T(8,128)S(1)}, u32[]{:S(2)}, u32[]{:S(2)}) collective-permute-start(f32[128,128]{1,0:T(8,128)S(1)} %get-tuple-element.58), channel_id=1, source_target_pairs={{0,12},{1,13},{2,14},{3,15},{4,8},{5,9},{6,10},{7,11},{8,4},{9,5},... | collective-permute-start | bytes 196616 | tf_op jit(solution)/shard_map/ppermute | solution.py:85
  18.3 4.3 %collective-permute-start.5 = (f32[128,128]{1,0:T(8,128)S(1)}, f32[128,128]{1,0:T(8,128)S(1)}, u32[]{:S(2)}, u32[]{:S(2)}) collective-permute-start(f32[128,128]{1,0:T(8,128)S(1)} %get-tuple-element.59), channel_id=1, source_target_pairs={{0,8},{1,9},{2,10},{3,11},{4,12},{5,13},{6,14},{7,15},{8,0},{9,1},... | collective-permute-start | bytes 196616 | tf_op jit(solution)/shard_map/ppermute | solution.py:85
  18.6 4.3 %collective-permute-start.6 = (f32[128,128]{1,0:T(8,128)S(1)}, f32[128,128]{1,0:T(8,128)S(1)}, u32[]{:S(2)}, u32[]{:S(2)}) collective-permute-start(f32[128,128]{1,0:T(8,128)S(1)} %get-tuple-element.60), channel_id=1, source_target_pairs={{0,4},{1,5},{2,6},{3,7},{4,0},{5,1},{6,2},{7,3},{8,12},{9,13},{10,... | collective-permute-start | bytes 196616 | tf_op jit(solution)/shard_map/ppermute | solution.py:85
  23.7 3.1 %collective-permute-start.7 = (f32[16,128]{1,0:T(8,128)S(1)}, f32[16,128]{1,0:T(8,128)S(1)}, u32[]{:S(2)}, u32[]{:S(2)}) collective-permute-start(f32[16,128]{1,0:T(8,128)S(1)} %get-tuple-element.63), channel_id=1, source_target_pairs={{0,3},{1,2},{2,1},{3,0},{4,7},{5,6},{6,5},{7,4},{8,11},{9,10},{10,... | collective-permute-start | bytes 24584 | tf_op jit(solution)/shard_map/ppermute | solution.py:365
  23.8 3.7 %collective-permute-start.8 = (f32[16,128]{1,0:T(8,128)S(1)}, f32[16,128]{1,0:T(8,128)S(1)}, u32[]{:S(2)}, u32[]{:S(2)}) collective-permute-start(f32[16,128]{1,0:T(8,128)S(1)} %get-tuple-element.64), channel_id=1, source_target_pairs={{0,2},{1,3},{2,0},{3,1},{4,6},{5,7},{6,4},{7,5},{8,10},{9,11},{10,... | collective-permute-start | bytes 24584 | tf_op jit(solution)/shard_map/ppermute | solution.py:365
  25.5 2.0 %collective-permute-start.9 = (f32[16,128]{1,0:T(8,128)S(1)}, f32[16,128]{1,0:T(8,128)S(1)}, u32[]{:S(2)}, u32[]{:S(2)}) collective-permute-start(f32[16,128]{1,0:T(8,128)S(1)} %get-tuple-element.65), channel_id=1, source_target_pairs={{0,1},{1,0},{2,3},{3,2},{4,5},{5,4},{6,7},{7,6},{8,9},{9,8},{10,11... | collective-permute-start | bytes 24584 | tf_op jit(solution)/shard_map/ppermute | solution.py:365
  28.3 6.1 %collective-permute-start.10 = (f32[128,128]{1,0:T(8,128)S(1)}, f32[128,128]{1,0:T(8,128)S(1)}, u32[]{:S(2)}, u32[]{:S(2)}) collective-permute-start(f32[128,128]{1,0:T(8,128)S(1)} %get-tuple-element.72), channel_id=1, source_target_pairs={{0,12},{1,13},{2,14},{3,15},{4,8},{5,9},{6,10},{7,11},{8,4},{9,5},... | collective-permute-start | bytes 196616 | tf_op jit(solution)/shard_map/ppermute | solution.py:85
  31.0 4.3 %collective-permute-start.11 = (f32[128,128]{1,0:T(8,128)S(1)}, f32[128,128]{1,0:T(8,128)S(1)}, u32[]{:S(2)}, u32[]{:S(2)}) collective-permute-start(f32[128,128]{1,0:T(8,128)S(1)} %get-tuple-element.73), channel_id=1, source_target_pairs={{0,4},{1,5},{2,6},{3,7},{4,0},{5,1},{6,2},{7,3},{8,12},{9,13},{10,... | collective-permute-start | bytes 196616 | tf_op jit(solution)/shard_map/ppermute | solution.py:85
  31.5 4.3 %collective-permute-start.12 = (f32[128,128]{1,0:T(8,128)S(1)}, f32[128,128]{1,0:T(8,128)S(1)}, u32[]{:S(2)}, u32[]{:S(2)}) collective-permute-start(f32[128,128]{1,0:T(8,128)S(1)} %get-tuple-element.74), channel_id=1, source_target_pairs={{0,8},{1,9},{2,10},{3,11},{4,12},{5,13},{6,14},{7,15},{8,0},{9,1},... | collective-permute-start | bytes 196616 | tf_op jit(solution)/shard_map/ppermute | solution.py:85
  35.8 6.3 %collective-permute-start.13 = (f32[128,128]{1,0:T(8,128)S(1)}, f32[128,128]{1,0:T(8,128)S(1)}, u32[]{:S(2)}, u32[]{:S(2)}) collective-permute-start(f32[128,128]{1,0:T(8,128)S(1)} %quad_sum.3.refs_0_), channel_id=1, source_target_pairs={{0,16},{1,17},{2,18},{3,19},{4,20},{5,21},{6,22},{7,23},{8,24},{9,... | collective-permute-start | bytes 196616 | tf_op jit(solution)/shard_map/ppermute | solution.py:85
  42.2 5.5 %collective-permute-start.14 = (f32[128,128]{1,0:T(8,128)S(1)}, f32[128,128]{1,0:T(8,128)S(1)}, u32[]{:S(2)}, u32[]{:S(2)}) collective-permute-start(f32[128,128]{1,0:T(8,128)S(1)} %get-tuple-element.89), channel_id=1, source_target_pairs={{0,12},{1,13},{2,14},{3,15},{4,8},{5,9},{6,10},{7,11},{8,4},{9,5},... | collective-permute-start | bytes 196616 | tf_op jit(solution)/shard_map/ppermute | solution.py:85
  42.7 5.1 %collective-permute-start.15 = (f32[128,128]{1,0:T(8,128)S(1)}, f32[128,128]{1,0:T(8,128)S(1)}, u32[]{:S(2)}, u32[]{:S(2)}) collective-permute-start(f32[128,128]{1,0:T(8,128)S(1)} %get-tuple-element.90), channel_id=1, source_target_pairs={{0,4},{1,5},{2,6},{3,7},{4,0},{5,1},{6,2},{7,3},{8,12},{9,13},{10,... | collective-permute-start | bytes 196616 | tf_op jit(solution)/shard_map/ppermute | solution.py:85
  44.0 4.3 %collective-permute-start.16 = (f32[128,128]{1,0:T(8,128)S(1)}, f32[128,128]{1,0:T(8,128)S(1)}, u32[]{:S(2)}, u32[]{:S(2)}) collective-permute-start(f32[128,128]{1,0:T(8,128)S(1)} %get-tuple-element.91), channel_id=1, source_target_pairs={{0,8},{1,9},{2,10},{3,11},{4,12},{5,13},{6,14},{7,15},{8,0},{9,1},... | collective-permute-start | bytes 196616 | tf_op jit(solution)/shard_map/ppermute | solution.py:85

commit v10 on v9

--- a/solution.py
+++ b/solution.py
@@ -73,8 +73,23 @@
     return lax.rem(lax.axis_index("seq"), QUAD) ^ partner(order, slot)
 
 
+def pair_of(number):
+    return lax.rem(number, 2) ^ (number // 2)
+
+
+def head_at(order, slot):
+    number = number_at(order, slot)
+    return 2 * pair_of(number) + number // 2
+
+
 def rows_at(order, slot):
-    return pl.ds(pl.multiple_of(number_at(order, slot) * HEAD_DIM, HEAD_DIM), HEAD_DIM)
+    return pl.ds(pl.multiple_of(head_at(order, slot) * HEAD_DIM, HEAD_DIM), HEAD_DIM)
+
+
+def by_pair(body, mine, other):
+    pair = pair_of(lax.rem(lax.axis_index("seq"), QUAD))
+    pl.when(pair == 0)(functools.partial(body, mine, other))
+    pl.when(pair == 1)(functools.partial(body, other, mine))
 
 
 def exchange(value, sizes, by):
@@ -142,7 +157,7 @@
         return lax.ppermute(value, "seq", pairs)
 
     into, out_of = (
-        jnp.stack([number_at(order, slot) for slot in range(QUAD)]) for order in ORDERS[reverse]
+        jnp.stack([head_at(order, slot) for slot in range(QUAD)]) for order in ORDERS[reverse]
     )
     state = jnp.stack(pieces)[jnp.argsort(into)]
     by = 1
@@ -163,8 +178,8 @@
         piece[...] = scratch[rows_at(order, slot), :]
 
 
-def load_pieces(pieces, order, rounded):
-    for slot, piece in enumerate(pieces):
+def load_pieces(pieces, order, rounded, first=0):
+    for slot, piece in enumerate(pieces, first):
         rounded[rows_at(order, slot), :] = piece[...].astype(BF16)
 
 
@@ -220,55 +235,77 @@
     return jnp.sum(tile.T, axis=0, keepdims=True)
 
 
-def mixed_kernel(intra, q, g, *refs):
-    pieces, (mixed, prefix, stats, *copies) = refs[:QUAD], refs[QUAD:]
-    load_pieces(pieces, ORDERS[False][1], prefix)
+def mixed_kernel(is_own, intra, q, g, *refs):
+    pieces, refs = refs[:2], refs[2:]
+    before, refs = ([], refs) if is_own else (refs[:2], refs[2:])
+    mixed, prefix, *stats, scratch = refs
+    load_pieces(pieces, ORDERS[False][1], scratch, 0 if is_own else 2)
     blocks = q.shape[0] // HEAD_DIM
-    for at in chunk_slices(q.shape[0]):
-        square = cross = None
-        for h in range(q.shape[1] // HEAD_DIM):
-            part = head_slice(h)
-            m = intra[at, part] + dot(q[at, part], prefix[part, :], 1, 0)
-            mixed[at, part] = m
-            s, c = m * m, m * g[at, part].astype(F32)
-            square = s if square is None else square + s
-            cross = c if cross is None else cross + c
-        for n in range(CHUNK // HEAD_DIM):
-            i = at.start // HEAD_DIM + n
-            stats[i : i + 1, :] = row_sums(square[head_slice(n)])
-            stats[blocks + i : blocks + i + 1, :] = row_sums(cross[head_slice(n)])
-    for copy in copies:
-        copy[...] = stats[...]
-
-
-def norm_kernel(width, mixed, q_t, g, *refs):
+
+    def pair(p):
+        for at in chunk_slices(q.shape[0]):
+            square = cross = None
+            for j in range(2):
+                part, whole = head_slice(j), head_slice(2 * p + j)
+                m = intra[at, whole] + dot(q[at, whole], scratch[whole, :], 1, 0)
+                mixed[at, part] = m
+                s, c = m * m, m * g[at, whole].astype(F32)
+                square = s if square is None else square + s
+                cross = c if cross is None else cross + c
+            for n in range(CHUNK // HEAD_DIM):
+                for first, value in ((0, square), (blocks, cross)):
+                    i = first + at.start // HEAD_DIM + n
+                    sums = row_sums(value[head_slice(n)])
+                    if before:
+                        sums = sums + before[0][i : i + 1, :]
+                    stats[0][i : i + 1, :] = sums
+        part = slice(p * PAIR, (p + 1) * PAIR)
+        prefix[part, :] = scratch[part, :]
+        if before:
+            part = slice((1 - p) * PAIR, (2 - p) * PAIR)
+            prefix[part, :] = before[1][part, :]
+
+    by_pair(lambda mine, other: pair(0 if mine else 1), is_own, not is_own)
+    for copy in stats[1:]:
+        copy[...] = stats[0][...]
+
+
+def norm_kernel(width, mixed, oth_mixed, q_t, g, *refs):
     stats, (gm, inverse_out, states, *pieces, scratch) = refs[: -4 - QUAD], refs[-4 - QUAD :]
     total = stats[0][...]
     for r in stats[1:]:
         total = total + r[...]
-    rows, cols = mixed.shape
+    rows, cols = gm.shape
     blocks = rows // HEAD_DIM
     inverse = lax.rsqrt(total[:blocks] / width + EPSILON)
     cross_mean = total[blocks:] * inverse / width
     scale = inverse * inverse * cross_mean
     inverse_out[...] = inverse
     shape = (HEAD_DIM, HEAD_DIM)
-    after = None
-    for n, at in reversed(list(enumerate(chunk_slices(rows)))):
-        for i in range(at.start // HEAD_DIM, at.stop // HEAD_DIM):
-            block = head_slice(i)
-            a = jnp.broadcast_to(inverse[i : i + 1], shape).T
-            b = jnp.broadcast_to(scale[i : i + 1], shape).T
-            for h in range(cols // HEAD_DIM):
-                part = head_slice(h)
-                grad = g[block, part].astype(F32)
-                gm[block, part] = (grad * a - mixed[block, part] * b).astype(BF16)
-        after = add_all(after, pair_blocks(q_t[:, at], gm[at, :], 1))
-        if n:
-            for h, state in enumerate(after):
-                first = (n - 1) * cols + h * HEAD_DIM
-                states[first : first + HEAD_DIM, :] = state
-    store_pieces(after, ORDERS[True][0], pieces, scratch)
+
+    def body(*pairs):
+        after = None
+        for n, at in reversed(list(enumerate(chunk_slices(rows)))):
+            for i in range(at.start // HEAD_DIM, at.stop // HEAD_DIM):
+                block = head_slice(i)
+                a = jnp.broadcast_to(inverse[i : i + 1], shape).T
+                b = jnp.broadcast_to(scale[i : i + 1], shape).T
+                for h in range(cols // HEAD_DIM):
+                    part = head_slice(h)
+                    value = pairs[h // 2][block, head_slice(h % 2)]
+                    grad = g[block, part].astype(F32)
+                    gm[block, part] = (grad * a - value * b).astype(BF16)
+            after = add_all(after, pair_blocks(q_t[:, at], gm[at, :], 1))
+            if n:
+                for h, state in enumerate(after):
+                    first = (n - 1) * cols + h * HEAD_DIM
+                    states[first : first + HEAD_DIM, :] = state
+        for h, state in enumerate(after):
+            scratch[head_slice(h), :] = state
+
+    by_pair(body, mixed, oth_mixed)
+    for slot, piece in enumerate(pieces):
+        piece[...] = scratch[rows_at(ORDERS[True][0], slot), :]
 
 
 def head_grads(h, q, k, v, gm, prefix, states, after, gq, gk, gv, finished=None):
@@ -304,21 +341,25 @@
         head_grads(h, q, k, v, gm, prefix, states, after, gqs[h], gks[h], gvs[h])
 
 
-def second_grads_kernel(q, k, v, gm, prefix, states, after, mixed, inverse, *refs):
+def second_grads_kernel(q, k, v, gm, prefix, states, after, mixed, oth_mixed, inverse, *refs):
     gq, gk, gv, out_hbm, out, sems = refs[-6:]
     shape = (HEAD_DIM, HEAD_DIM)
-    copies = []
-    for n, at in enumerate(chunk_slices(q.shape[0])):
-        for i in range(at.start // HEAD_DIM, at.stop // HEAD_DIM):
-            a = jnp.broadcast_to(inverse[i : i + 1, :], shape).T
-            for h in range(q.shape[1] // HEAD_DIM):
-                block = (head_slice(i), head_slice(h))
-                out[block] = (mixed[block] * a).astype(BF16)
-        copies.append(pltpu.make_async_copy(out.at[at], out_hbm.at[at], sems.at[n]))
-        copies[-1].start()
-    head_grads(2, q, k, v, gm, prefix, states, after, gq, gk, gv)
-    for copy in copies:
-        copy.wait()
+
+    def body(*pairs):
+        copies = []
+        for n, at in enumerate(chunk_slices(q.shape[0])):
+            for i in range(at.start // HEAD_DIM, at.stop // HEAD_DIM):
+                a = jnp.broadcast_to(inverse[i : i + 1, :], shape).T
+                for h in range(q.shape[1] // HEAD_DIM):
+                    value = pairs[h // 2][head_slice(i), head_slice(h % 2)]
+                    out[head_slice(i), head_slice(h)] = (value * a).astype(BF16)
+            copies.append(pltpu.make_async_copy(out.at[at], out_hbm.at[at], sems.at[n]))
+            copies[-1].start()
+        head_grads(2, q, k, v, gm, prefix, states, after, gq, gk, gv)
+        for copy in copies:
+            copy.wait()
+
+    by_pair(body, mixed, oth_mixed)
 
 
 def third_grads_kernel(q, k, v, gm, prefix, states, after, *refs):
@@ -406,17 +447,24 @@
         )
 
     prefixes, (intra, states, queries_t) = scan(pieces, sizes, False, forward)
-    mixed, prefix, *stats = call(
-        mixed_kernel,
-        [wide, shape(cols, HEAD_DIM, BF16)] + [shape(2 * blocks, HEAD_DIM)] * head_size,
-        [intra, queries, grad_out, *prefixes],
-        QUAD * head_flops,
-        "mixed",
-    )
+    stats_shape = shape(2 * blocks, HEAD_DIM)
+
+    def mix(is_own, pieces, count, *before):
+        return call(
+            functools.partial(mixed_kernel, is_own),
+            [shape(rows, PAIR), shape(cols, HEAD_DIM, BF16)] + [stats_shape] * count,
+            [intra, queries, grad_out, *pieces, *before],
+            2 * head_flops,
+            "mixed",
+            scratch=[pltpu.VMEM((cols, HEAD_DIM), BF16)],
+        )
+
+    mixed, prefix, stats = mix(True, prefixes[:2], 1)
+    oth_mixed, prefix, *stats = mix(False, prefixes[2:], head_size, stats, prefix)
     gm, inverse, after, *pieces = call(
         functools.partial(norm_kernel, cols * head_size),
         [narrow, shape(blocks, HEAD_DIM), states_shape] + pieces_shape,
-        [mixed, queries_t, grad_out, *all_parts(stats, "head")],
+        [mixed, oth_mixed, queries_t, grad_out, *all_parts(stats, "head")],
         QUAD * head_flops,
         "norm",
         scratch=[pieces_scratch],
@@ -437,10 +485,10 @@
             parts = call(
                 second_grads_kernel,
                 [head_narrow] + [head_wide] * 2 + [narrow],
-                args + [mixed, inverse, token],
+                args + [mixed, oth_mixed, inverse, token],
                 grads_flops,
                 "second_grads",
-                spaces={len(args) + 2: pl.ANY},
+                spaces={len(args) + 3: pl.ANY},
                 outs={3: pl.ANY},
                 scratch=[pltpu.VMEM((rows, cols), BF16), pltpu.SemaphoreType.DMA((chunks,))],
             )

time: 50.1 us -> 49.8 us (level)
  waiting for transfers between devices: 11.9 us -> 11.3 us
    ppermute x14, waiting for transfers between devices: 9.99 us -> 9.42 us  [exchange(): return lax.ppermute(value, ('seq', 'head'), pairs)]
    pallas_call x12 -> x13, Pallas kernels: 14.1 us -> 14.4 us  [call(): return list(kernel(*args))]
  transfers between devices with their start and end apart: 17 -> 17, of which waited for: 12 -> 12; matrix products, arithmetic and copies ran while one was open for 0% -> 0% of each run, Pallas kernels for 17% -> 18%
where the time goes in v10:
time: 49.8 us; the launch traced here: 49.7 us
  starting transfers between devices  23.2 us (47%)
  Pallas kernels  14.4 us (29%)
  waiting for transfers between devices  11.3 us (23%)
  between operations  0.77 us (2%)
    ppermute x14, starting transfers between devices, exchange(): return lax.ppermute(value, ('seq', 'head'), pairs)  21.3 us
    pallas_call x13, Pallas kernels, call(): return list(kernel(*args))  14.4 us
    ppermute x14, waiting for transfers between devices, exchange(): return lax.ppermute(value, ('seq', 'head'), pairs)  9.42 us
    ppermute x3, starting transfers between devices, all_parts(): parts.append(lax.ppermute(values[by], axis, pairs))  1.92 us
    ppermute x3, waiting for transfers between devices, all_parts(): parts.append(lax.ppermute(values[by], axis, pairs))  1.87 us
  transfers between devices with their start and end apart: 17, of which 12 were waited for; matrix products, arithmetic and copies ran while one was open for 0% of the time, Pallas kernels for 18%

profile of v10, /device:TPU:0, one launch (start us, length us, event | category | flops | bytes accessed | tf_op | source)
XLA Modules:
  0.0 49.7 jit_solution(1353877785207117885)
XLA Ops:
  0.6 0.0 copy-start
  0.6 1.9 %local_state.1 = (f32[128,128]{1,0:T(8,128)S(1)}, f32[128,128]{1,0:T(8,128)S(1)}, f32[128,128]{1,0:T(8,128)S(1)}, f32[128,128]{1,0:T(8,128)S(1)}, bf16[1024,512]...) custom-call(bf16[1024,512]{1,0:T(8,128)(2,1)} %k_hbm.1, bf16[1024,512]{1,0:T(8,128)(2,1)} %v_hbm.1), custom_call_target="tpu_custom_call" | custom-call | flops 134217728 | bytes 4456448 | tf_op jit(solution)/shard_map/local_state/pallas_call | solution.py:60
  2.6 4.0 %collective-permute-start = (f32[128,128]{1,0:T(8,128)S(1)}, f32[128,128]{1,0:T(8,128)S(1)}, u32[]{:S(2)}, u32[]{:S(2)}) collective-permute-start(f32[128,128]{1,0:T(8,128)S(1)} %get-tuple-element.56), channel_id=1, source_target_pairs={{0,12},{1,13},{2,14},{3,15},{4,8},{5,9},{6,10},{7,11},{8,4},{9,5},... | collective-permute-start | bytes 196616 | tf_op jit(solution)/shard_map/ppermute | solution.py:100
  6.6 0.4 collective-permute-start.1
  7.1 0.2 collective-permute-start.2
  7.3 0.0 copy-done
  7.3 0.0 copy-start.1
  7.3 2.0 %intra.1 = (f32[1024,512]{1,0:T(8,128)S(1)}, f32[1536,128]{1,0:T(8,128)S(1)}, bf16[512,1024]{1,0:T(8,128)(2,1)S(1)}) custom-call(bf16[1024,512]{1,0:T(8,128)(2,1)S(1)} %copy-done, bf16[1024,512]{1,0:T(8,128)(2,1)S(1)} %get-tuple-element.52.k, bf16[1024,512]{1,0:T(8,128)(2,1)S(1)} %get-tuple-element.53.v), custom_call_target="tpu_custom_call" | custom-call | flops 805306368 | bytes 7077888 | tf_op jit(solution)/shard_map/intra/pallas_call | solution.py:60
  9.2 0.0 collective-permute-done.refs_1_
  9.2 1.7 %collective-permute-done.1.refs_2_ = f32[128,128]{1,0:T(8,128)S(1)} collective-permute-done((f32[128,128]{1,0:T(8,128)S(1)}, f32[128,128]{1,0:T(8,128)S(1)}, u32[]{:S(2)}, u32[]{:S(2)}) %collective-permute-start.1) | collective-permute-done | bytes 65568 | tf_op jit(solution)/shard_map/ppermute | solution.py:100
  10.9 0.4 collective-permute-done.2.refs_3_
  11.3 2.7 %collective-permute-start.3 = (f32[128,128]{1,0:T(8,128)S(1)}, f32[128,128]{1,0:T(8,128)S(1)}, u32[]{:S(2)}, u32[]{:S(2)}) collective-permute-start(f32[128,128]{1,0:T(8,128)S(1)} %quad_sum.2), channel_id=1, source_target_pairs={{0,16},{1,17},{2,18},{3,19},{4,20},{5,21},{6,22},{7,23},{8,24},{9,... | collective-permute-start | bytes 196616 | tf_op jit(solution)/shard_map/ppermute | solution.py:100
  14.0 2.6 %collective-permute-done.3.refs_4_ = f32[128,128]{1,0:T(8,128)S(1)} collective-permute-done((f32[128,128]{1,0:T(8,128)S(1)}, f32[128,128]{1,0:T(8,128)S(1)}, u32[]{:S(2)}, u32[]{:S(2)}) %collective-permute-start.3) | collective-permute-done | bytes 65568 | tf_op jit(solution)/shard_map/ppermute | solution.py:100
  16.6 0.1 finish.2
  16.6 1.6 %collective-permute-start.4 = (f32[128,128]{1,0:T(8,128)S(1)}, f32[128,128]{1,0:T(8,128)S(1)}, u32[]{:S(2)}, u32[]{:S(2)}) collective-permute-start(f32[128,128]{1,0:T(8,128)S(1)} %get-tuple-element.61), channel_id=1, source_target_pairs={{0,12},{1,13},{2,14},{3,15},{4,8},{5,9},{6,10},{7,11},{8,4},{9,5},... | collective-permute-start | bytes 196616 | tf_op jit(solution)/shard_map/ppermute | solution.py:100
  18.3 0.3 collective-permute-start.5
  18.6 1.6 %collective-permute-start.6 = (f32[128,128]{1,0:T(8,128)S(1)}, f32[128,128]{1,0:T(8,128)S(1)}, u32[]{:S(2)}, u32[]{:S(2)}) collective-permute-start(f32[128,128]{1,0:T(8,128)S(1)} %get-tuple-element.64), channel_id=1, source_target_pairs={{0,4},{1,5},{2,6},{3,7},{4,0},{5,1},{6,2},{7,3},{8,12},{9,13},{10,... | collective-permute-start | bytes 196616 | tf_op jit(solution)/shard_map/ppermute | solution.py:100
  20.2 1.7 %collective-permute-done.4.refs_1_ = f32[128,128]{1,0:T(8,128)S(1)} collective-permute-done((f32[128,128]{1,0:T(8,128)S(1)}, f32[128,128]{1,0:T(8,128)S(1)}, u32[]{:S(2)}, u32[]{:S(2)}) %collective-permute-start.4) | collective-permute-done | bytes 65568 | tf_op jit(solution)/shard_map/ppermute | solution.py:100
  21.9 0.0 copy-done.1
  21.9 0.5 %mixed.2 = (f32[1024,256]{1,0:T(8,128)S(1)}, bf16[512,128]{1,0:T(8,128)(2,1)S(1)}, f32[16,128]{1,0:T(8,128)S(1)}) custom-call(f32[1024,512]{1,0:T(8,128)S(1)} %get-tuple-element.54.intra, bf16[1024,512]{1,0:T(8,128)(2,1)S(1)} %copy-done, bf16[1024,512]{1,0:T(8,128)(2,1)S(1)} %copy-done.1, f32[128,128]{1,0:T(8,128)S(1)} %get-tuple-element.60.refs_0_, ...), custom_call_target="tpu_custom_call" | custom-call | flops 67108864 | bytes 5513216 | tf_op jit(solution)/shard_map/mixed/pallas_call | solution.py:60
  22.4 0.1 collective-permute-done.5.refs_0_
  22.5 0.3 collective-permute-done.6.refs_1_
  22.9 0.5 %mixed.3 = (f32[1024,256]{1,0:T(8,128)S(1)}, bf16[512,128]{1,0:T(8,128)(2,1)S(1)}, f32[16,128]{1,0:T(8,128)S(1)}, f32[16,128]{1,0:T(8,128)S(1)}, f32[16,128]{1,0:T(8,128)S(1)}, /*index=5*/f32[16,128]{1,0:T(8,128)S(1)}) custom-call(f32[1024,512]{1,0:T(8,128)S(1)} %get-tuple-element.54.intra, bf16[1024,512]{1,0:T(8,128)(2,1)S(1)} %copy-done, ...), custom_call_target="tpu_custom_call" | custom-call | flops 67108864 | bytes 5677056 | tf_op jit(solution)/shard_map/mixed/pallas_call | solution.py:60
  23.4 0.1 collective-permute-start.7
  23.5 1.8 %collective-permute-start.8 = (f32[16,128]{1,0:T(8,128)S(1)}, f32[16,128]{1,0:T(8,128)S(1)}, u32[]{:S(2)}, u32[]{:S(2)}) collective-permute-start(f32[16,128]{1,0:T(8,128)S(1)} %get-tuple-element.70), channel_id=1, source_target_pairs={{0,2},{1,3},{2,0},{3,1},{4,6},{5,7},{6,4},{7,5},{8,10},{9,11},{10,... | collective-permute-start | bytes 24584 | tf_op jit(solution)/shard_map/ppermute | solution.py:406
  25.3 0.1 collective-permute-start.9
  25.4 1.2 %collective-permute-done.7.refs_1_ = f32[16,128]{1,0:T(8,128)S(1)} collective-permute-done((f32[16,128]{1,0:T(8,128)S(1)}, f32[16,128]{1,0:T(8,128)S(1)}, u32[]{:S(2)}, u32[]{:S(2)}) %collective-permute-start.7) | collective-permute-done | bytes 8224 | tf_op jit(solution)/shard_map/ppermute | solution.py:406
  26.6 0.7 %collective-permute-done.8.refs_2_ = f32[16,128]{1,0:T(8,128)S(1)} collective-permute-done((f32[16,128]{1,0:T(8,128)S(1)}, f32[16,128]{1,0:T(8,128)S(1)}, u32[]{:S(2)}, u32[]{:S(2)}) %collective-permute-start.8) | collective-permute-done | bytes 8224 | tf_op jit(solution)/shard_map/ppermute | solution.py:406
  27.2 0.0 collective-permute-done.9.refs_3_
  27.2 0.8 %norm.1 = (bf16[1024,512]{1,0:T(8,128)(2,1)S(1)}, f32[8,128]{1,0:T(8,128)S(1)}, f32[1536,128]{1,0:T(8,128)S(1)}, f32[128,128]{1,0:T(8,128)S(1)}, f32[128,128]{1,...) custom-call(f32[1024,256]{1,0:T(8,128)S(1)} %get-tuple-element.62.mixed, ...), custom_call_target="tpu_custom_call" | custom-call | flops 134217728 | bytes 6328320 | tf_op jit(solution)/shard_map/norm/pallas_call | solution.py:60
  28.1 2.7 %collective-permute-start.10 = (f32[128,128]{1,0:T(8,128)S(1)}, f32[128,128]{1,0:T(8,128)S(1)}, u32[]{:S(2)}, u32[]{:S(2)}) collective-permute-start(f32[128,128]{1,0:T(8,128)S(1)} %get-tuple-element.78), channel_id=1, source_target_pairs={{0,12},{1,13},{2,14},{3,15},{4,8},{5,9},{6,10},{7,11},{8,4},{9,5},... | collective-permute-start | bytes 196616 | tf_op jit(solution)/shard_map/ppermute | solution.py:100
  30.7 0.5 %collective-permute-start.11 = (f32[128,128]{1,0:T(8,128)S(1)}, f32[128,128]{1,0:T(8,128)S(1)}, u32[]{:S(2)}, u32[]{:S(2)}) collective-permute-start(f32[128,128]{1,0:T(8,128)S(1)} %get-tuple-element.79), channel_id=1, source_target_pairs={{0,4},{1,5},{2,6},{3,7},{4,0},{5,1},{6,2},{7,3},{8,12},{9,13},{10,... | collective-permute-start | bytes 196616 | tf_op jit(solution)/shard_map/ppermute | solution.py:100
  31.3 0.4 collective-permute-start.12
  31.6 2.5 %first_grads.1 = (bf16[1024,128]{1,0:T(8,128)(2,1)S(1)}, bf16[1024,128]{1,0:T(8,128)(2,1)S(1)}, f32[1024,128]{1,0:T(8,128)S(1)}, f32[1024,128]{1,0:T(8,128)S(1)}...) custom-call(bf16[1024,512]{1,0:T(8,128)(2,1)S(1)} %copy-done, bf16[1024,512]{1,0:T(8,128)(2,1)S(1)} %get-tuple-element.52.k, ...), custom_call_target="tpu_custom_call" | custom-call | flops 1006632960 | bytes 8519680 | tf_op jit(solution)/shard_map/first_grads/pallas_call | solution.py:60
  34.1 0.0 collective-permute-done.10.refs_1_
  34.1 0.9 %collective-permute-done.11.refs_2_ = f32[128,128]{1,0:T(8,128)S(1)} collective-permute-done((f32[128,128]{1,0:T(8,128)S(1)}, f32[128,128]{1,0:T(8,128)S(1)}, u32[]{:S(2)}, u32[]{:S(2)}) %collective-permute-start.11) | collective-permute-done | bytes 65568 | tf_op jit(solution)/shard_map/ppermute | solution.py:100
  35.0 0.5 %collective-permute-done.12.refs_3_ = f32[128,128]{1,0:T(8,128)S(1)} collective-permute-done((f32[128,128]{1,0:T(8,128)S(1)}, f32[128,128]{1,0:T(8,128)S(1)}, u32[]{:S(2)}, u32[]{:S(2)}) %collective-permute-start.12) | collective-permute-done | bytes 65568 | tf_op jit(solution)/shard_map/ppermute | solution.py:100
  35.5 3.3 %collective-permute-start.13 = (f32[128,128]{1,0:T(8,128)S(1)}, f32[128,128]{1,0:T(8,128)S(1)}, u32[]{:S(2)}, u32[]{:S(2)}) collective-permute-start(f32[128,128]{1,0:T(8,128)S(1)} %quad_sum.3.refs_0_), channel_id=1, source_target_pairs={{0,16},{1,17},{2,18},{3,19},{4,20},{5,21},{6,22},{7,23},{8,24},{9,... | collective-permute-start | bytes 196616 | tf_op jit(solution)/shard_map/ppermute | solution.py:100
  38.9 2.2 %second_grads.1 = (bf16[1024,128]{1,0:T(8,128)(2,1)S(1)}, f32[1024,128]{1,0:T(8,128)S(1)}, f32[1024,128]{1,0:T(8,128)S(1)}, bf16[1024,512]{1,0:T(8,128)(2,1)}) custom-call(bf16[1024,512]{1,0:T(8,128)(2,1)S(1)} %copy-done, bf16[1024,512]{1,0:T(8,128)(2,1)S(1)} %get-tuple-element.52.k, bf16[1024,512]{1,0:T(8,128)(2,1)S(1)} %get-tuple-element.53.v, ...), custom_call_target="tpu_custom_call" | custom-call | flops 503316480 | bytes 10424320 | tf_op jit(solution)/shard_map/second_grads/pallas_call | solution.py:60
  41.1 0.8 %collective-permute-done.13.refs_4_ = f32[128,128]{1,0:T(8,128)S(1)} collective-permute-done((f32[128,128]{1,0:T(8,128)S(1)}, f32[128,128]{1,0:T(8,128)S(1)}, u32[]{:S(2)}, u32[]{:S(2)}) %collective-permute-start.13) | collective-permute-done | bytes 65568 | tf_op jit(solution)/shard_map/ppermute | solution.py:100
  41.9 0.1 finish.3
  41.9 0.5 collective-permute-start.14
  42.4 1.3 %collective-permute-start.15 = (f32[128,128]{1,0:T(8,128)S(1)}, f32[128,128]{1,0:T(8,128)S(1)}, u32[]{:S(2)}, u32[]{:S(2)}) collective-permute-start(f32[128,128]{1,0:T(8,128)S(1)} %get-tuple-element.96), channel_id=1, source_target_pairs={{0,4},{1,5},{2,6},{3,7},{4,0},{5,1},{6,2},{7,3},{8,12},{9,13},{10,... | collective-permute-start | bytes 196616 | tf_op jit(solution)/shard_map/ppermute | solution.py:100
  43.7 1.8 %collective-permute-start.16 = (f32[128,128]{1,0:T(8,128)S(1)}, f32[128,128]{1,0:T(8,128)S(1)}, u32[]{:S(2)}, u32[]{:S(2)}) collective-permute-start(f32[128,128]{1,0:T(8,128)S(1)} %get-tuple-element.97), channel_id=1, source_target_pairs={{0,8},{1,9},{2,10},{3,11},{4,12},{5,13},{6,14},{7,15},{8,0},{9,1},... | collective-permute-start | bytes 196616 | tf_op jit(solution)/shard_map/ppermute | solution.py:100
  45.5 2.0 %third_grads.1 = (f32[1024,128]{1,0:T(8,128)S(1)}, f32[1024,128]{1,0:T(8,128)S(1)}, bf16[1024,512]{1,0:T(8,128)(2,1)}) custom-call(bf16[1024,512]{1,0:T(8,128)(2,1)S(1)} %copy-done, bf16[1024,512]{1,0:T(8,128)(2,1)S(1)} %get-tuple-element.52.k, bf16[1024,512]{1,0:T(8,128)(2,1)S(1)} %get-tuple-element.53.v, bf16[1024,512]{1,0:T(8,128)(2,1)S(1)} %get-tuple-element.72.gm, ...), custom_call_target="tpu_custom_call" | custom-call | flops 503316480 | bytes 8847360 | tf_op jit(solution)/shard_map/third_grads/pallas_call | solution.py:60
  47.5 0.0 collective-permute-done.14.refs_9_
  47.5 0.0 collective-permute-done.15.refs_10_
  47.5 0.4 collective-permute-done.16.refs_11_
  47.9 1.7 %last.1 = (bf16[1024,512]{1,0:T(8,128)(2,1)}, bf16[1024,512]{1,0:T(8,128)(2,1)}) custom-call(bf16[1024,512]{1,0:T(8,128)(2,1)S(1)} %get-tuple-element.52.k, bf16[1024,512]{1,0:T(8,128)(2,1)S(1)} %get-tuple-element.53.v, f32[1024,128]{1,0:T(8,128)S(1)} %get-tuple-element.89.refs_0_, f32[1024,128]{1,0:T(8,128)S(1)} %get-tuple-element.81.refs_4_.refs_1_, ...), custom_call_target="tpu_custom_call" | custom-call | flops 268435456 | bytes 8650752 | tf_op jit(solution)/shard_map/last/pallas_call | solution.py:60
  (2 shorter events, 0.0 us)
Async XLA Ops:
  0.6 6.6 %copy-start = (bf16[1024,512]{1,0:T(8,128)(2,1)S(1)}, bf16[1024,512]{1,0:T(8,128)(2,1)}, u32[]{:S(2)}) copy-start(bf16[1024,512]{1,0:T(8,128)(2,1)} %q.11) | copy-start | bytes 3145732
  2.6 6.6 %collective-permute-start = (f32[128,128]{1,0:T(8,128)S(1)}, f32[128,128]{1,0:T(8,128)S(1)}, u32[]{:S(2)}, u32[]{:S(2)}) collective-permute-start(f32[128,128]{1,0:T(8,128)S(1)} %get-tuple-element.56), channel_id=1, source_target_pairs={{0,12},{1,13},{2,14},{3,15},{4,8},{5,9},{6,10},{7,11},{8,4},{9,5},... | collective-permute-start | bytes 196616 | tf_op jit(solution)/shard_map/ppermute | solution.py:100
  6.6 4.3 %collective-permute-start.1 = (f32[128,128]{1,0:T(8,128)S(1)}, f32[128,128]{1,0:T(8,128)S(1)}, u32[]{:S(2)}, u32[]{:S(2)}) collective-permute-start(f32[128,128]{1,0:T(8,128)S(1)} %get-tuple-element.57), channel_id=1, source_target_pairs={{0,8},{1,9},{2,10},{3,11},{4,12},{5,13},{6,14},{7,15},{8,0},{9,1},... | collective-permute-start | bytes 196616 | tf_op jit(solution)/shard_map/ppermute | solution.py:100
  7.1 4.3 %collective-permute-start.2 = (f32[128,128]{1,0:T(8,128)S(1)}, f32[128,128]{1,0:T(8,128)S(1)}, u32[]{:S(2)}, u32[]{:S(2)}) collective-permute-start(f32[128,128]{1,0:T(8,128)S(1)} %get-tuple-element.58), channel_id=1, source_target_pairs={{0,4},{1,5},{2,6},{3,7},{4,0},{5,1},{6,2},{7,3},{8,12},{9,13},{10,... | collective-permute-start | bytes 196616 | tf_op jit(solution)/shard_map/ppermute | solution.py:100
  7.3 14.6 %copy-start.1 = (bf16[1024,512]{1,0:T(8,128)(2,1)S(1)}, bf16[1024,512]{1,0:T(8,128)(2,1)}, u32[]{:S(2)}) copy-start(bf16[1024,512]{1,0:T(8,128)(2,1)} %g.5) | copy-start | bytes 3145732
  11.3 5.2 %collective-permute-start.3 = (f32[128,128]{1,0:T(8,128)S(1)}, f32[128,128]{1,0:T(8,128)S(1)}, u32[]{:S(2)}, u32[]{:S(2)}) collective-permute-start(f32[128,128]{1,0:T(8,128)S(1)} %quad_sum.2), channel_id=1, source_target_pairs={{0,16},{1,17},{2,18},{3,19},{4,20},{5,21},{6,22},{7,23},{8,24},{9,... | collective-permute-start | bytes 196616 | tf_op jit(solution)/shard_map/ppermute | solution.py:100
  16.6 5.2 %collective-permute-start.4 = (f32[128,128]{1,0:T(8,128)S(1)}, f32[128,128]{1,0:T(8,128)S(1)}, u32[]{:S(2)}, u32[]{:S(2)}) collective-permute-start(f32[128,128]{1,0:T(8,128)S(1)} %get-tuple-element.61), channel_id=1, source_target_pairs={{0,12},{1,13},{2,14},{3,15},{4,8},{5,9},{6,10},{7,11},{8,4},{9,5},... | collective-permute-start | bytes 196616 | tf_op jit(solution)/shard_map/ppermute | solution.py:100
  18.3 4.3 %collective-permute-start.5 = (f32[128,128]{1,0:T(8,128)S(1)}, f32[128,128]{1,0:T(8,128)S(1)}, u32[]{:S(2)}, u32[]{:S(2)}) collective-permute-start(f32[128,128]{1,0:T(8,128)S(1)} %get-tuple-element.63), channel_id=1, source_target_pairs={{0,8},{1,9},{2,10},{3,11},{4,12},{5,13},{6,14},{7,15},{8,0},{9,1},... | collective-permute-start | bytes 196616 | tf_op jit(solution)/shard_map/ppermute | solution.py:100
  18.6 4.3 %collective-permute-start.6 = (f32[128,128]{1,0:T(8,128)S(1)}, f32[128,128]{1,0:T(8,128)S(1)}, u32[]{:S(2)}, u32[]{:S(2)}) collective-permute-start(f32[128,128]{1,0:T(8,128)S(1)} %get-tuple-element.64), channel_id=1, source_target_pairs={{0,4},{1,5},{2,6},{3,7},{4,0},{5,1},{6,2},{7,3},{8,12},{9,13},{10,... | collective-permute-start | bytes 196616 | tf_op jit(solution)/shard_map/ppermute | solution.py:100
  23.4 3.1 %collective-permute-start.7 = (f32[16,128]{1,0:T(8,128)S(1)}, f32[16,128]{1,0:T(8,128)S(1)}, u32[]{:S(2)}, u32[]{:S(2)}) collective-permute-start(f32[16,128]{1,0:T(8,128)S(1)} %get-tuple-element.69), channel_id=1, source_target_pairs={{0,3},{1,2},{2,1},{3,0},{4,7},{5,6},{6,5},{7,4},{8,11},{9,10},{10,... | collective-permute-start | bytes 24584 | tf_op jit(solution)/shard_map/ppermute | solution.py:406
  23.5 3.7 %collective-permute-start.8 = (f32[16,128]{1,0:T(8,128)S(1)}, f32[16,128]{1,0:T(8,128)S(1)}, u32[]{:S(2)}, u32[]{:S(2)}) collective-permute-start(f32[16,128]{1,0:T(8,128)S(1)} %get-tuple-element.70), channel_id=1, source_target_pairs={{0,2},{1,3},{2,0},{3,1},{4,6},{5,7},{6,4},{7,5},{8,10},{9,11},{10,... | collective-permute-start | bytes 24584 | tf_op jit(solution)/shard_map/ppermute | solution.py:406
  25.3 1.9 %collective-permute-start.9 = (f32[16,128]{1,0:T(8,128)S(1)}, f32[16,128]{1,0:T(8,128)S(1)}, u32[]{:S(2)}, u32[]{:S(2)}) collective-permute-start(f32[16,128]{1,0:T(8,128)S(1)} %get-tuple-element.71), channel_id=1, source_target_pairs={{0,1},{1,0},{2,3},{3,2},{4,5},{5,4},{6,7},{7,6},{8,9},{9,8},{10,11... | collective-permute-start | bytes 24584 | tf_op jit(solution)/shard_map/ppermute | solution.py:406
  28.1 6.1 %collective-permute-start.10 = (f32[128,128]{1,0:T(8,128)S(1)}, f32[128,128]{1,0:T(8,128)S(1)}, u32[]{:S(2)}, u32[]{:S(2)}) collective-permute-start(f32[128,128]{1,0:T(8,128)S(1)} %get-tuple-element.78), channel_id=1, source_target_pairs={{0,12},{1,13},{2,14},{3,15},{4,8},{5,9},{6,10},{7,11},{8,4},{9,5},... | collective-permute-start | bytes 196616 | tf_op jit(solution)/shard_map/ppermute | solution.py:100
  30.7 4.3 %collective-permute-start.11 = (f32[128,128]{1,0:T(8,128)S(1)}, f32[128,128]{1,0:T(8,128)S(1)}, u32[]{:S(2)}, u32[]{:S(2)}) collective-permute-start(f32[128,128]{1,0:T(8,128)S(1)} %get-tuple-element.79), channel_id=1, source_target_pairs={{0,4},{1,5},{2,6},{3,7},{4,0},{5,1},{6,2},{7,3},{8,12},{9,13},{10,... | collective-permute-start | bytes 196616 | tf_op jit(solution)/shard_map/ppermute | solution.py:100
  31.3 4.3 %collective-permute-start.12 = (f32[128,128]{1,0:T(8,128)S(1)}, f32[128,128]{1,0:T(8,128)S(1)}, u32[]{:S(2)}, u32[]{:S(2)}) collective-permute-start(f32[128,128]{1,0:T(8,128)S(1)} %get-tuple-element.80), channel_id=1, source_target_pairs={{0,8},{1,9},{2,10},{3,11},{4,12},{5,13},{6,14},{7,15},{8,0},{9,1},... | collective-permute-start | bytes 196616 | tf_op jit(solution)/shard_map/ppermute | solution.py:100
  35.5 6.3 %collective-permute-start.13 = (f32[128,128]{1,0:T(8,128)S(1)}, f32[128,128]{1,0:T(8,128)S(1)}, u32[]{:S(2)}, u32[]{:S(2)}) collective-permute-start(f32[128,128]{1,0:T(8,128)S(1)} %quad_sum.3.refs_0_), channel_id=1, source_target_pairs={{0,16},{1,17},{2,18},{3,19},{4,20},{5,21},{6,22},{7,23},{8,24},{9,... | collective-permute-start | bytes 196616 | tf_op jit(solution)/shard_map/ppermute | solution.py:100
  41.9 5.5 %collective-permute-start.14 = (f32[128,128]{1,0:T(8,128)S(1)}, f32[128,128]{1,0:T(8,128)S(1)}, u32[]{:S(2)}, u32[]{:S(2)}) collective-permute-start(f32[128,128]{1,0:T(8,128)S(1)} %get-tuple-element.95), channel_id=1, source_target_pairs={{0,12},{1,13},{2,14},{3,15},{4,8},{5,9},{6,10},{7,11},{8,4},{9,5},... | collective-permute-start | bytes 196616 | tf_op jit(solution)/shard_map/ppermute | solution.py:100
  42.4 5.1 %collective-permute-start.15 = (f32[128,128]{1,0:T(8,128)S(1)}, f32[128,128]{1,0:T(8,128)S(1)}, u32[]{:S(2)}, u32[]{:S(2)}) collective-permute-start(f32[128,128]{1,0:T(8,128)S(1)} %get-tuple-element.96), channel_id=1, source_target_pairs={{0,4},{1,5},{2,6},{3,7},{4,0},{5,1},{6,2},{7,3},{8,12},{9,13},{10,... | collective-permute-start | bytes 196616 | tf_op jit(solution)/shard_map/ppermute | solution.py:100
  43.7 4.3 %collective-permute-start.16 = (f32[128,128]{1,0:T(8,128)S(1)}, f32[128,128]{1,0:T(8,128)S(1)}, u32[]{:S(2)}, u32[]{:S(2)}) collective-permute-start(f32[128,128]{1,0:T(8,128)S(1)} %get-tuple-element.97), channel_id=1, source_target_pairs={{0,8},{1,9},{2,10},{3,11},{4,12},{5,13},{6,14},{7,15},{8,0},{9,1},... | collective-permute-start | bytes 196616 | tf_op jit(solution)/shard_map/ppermute | solution.py:100

commit v11 on v10

--- a/solution.py
+++ b/solution.py
@@ -29,8 +29,8 @@
     return slice(h * HEAD_DIM, (h + 1) * HEAD_DIM)
 
 
-def chunk_slices(rows):
-    return [slice(start, start + CHUNK) for start in range(0, rows, CHUNK)]
+def chunk_slices(rows, size=CHUNK):
+    return [slice(start, start + size) for start in range(0, rows, size)]
 
 
 def causal(transposed=False):
@@ -384,14 +384,15 @@
     gk_hbm, gv_hbm, gk, gv, suffix, sems = refs[-6:]
     load_pieces(pieces, ORDERS[True][1], suffix)
     copies = []
-    for n, at in enumerate(chunk_slices(k.shape[0])):
-        for h in range(QUAD):
-            part = head_slice(h)
-            state = suffix[part, :]
-            gk[at, part] = (gks[h][at, :] + dot(v[at, part], state, 1, 1)).astype(BF16)
-            gv[at, part] = (gvs[h][at, :] + dot(k[at, part], state, 1, 0)).astype(BF16)
-        for j, (src, dst) in enumerate(((gk, gk_hbm), (gv, gv_hbm))):
-            copies.append(pltpu.make_async_copy(src.at[at], dst.at[at], sems.at[j, n]))
+    for j, (parts, left, contract, out, hbm) in enumerate(
+        ((gvs, k, 0, gv, gv_hbm), (gks, v, 1, gk, gk_hbm))
+    ):
+        for n, at in enumerate(chunk_slices(k.shape[0])):
+            for h in range(QUAD):
+                part = head_slice(h)
+                new = dot(left[at, part], suffix[part, :], 1, contract)
+                out[at, part] = (parts[h][at, :] + new).astype(BF16)
+            copies.append(pltpu.make_async_copy(out.at[at], hbm.at[at], sems.at[j, n]))
             copies[-1].start()
     for copy in copies:
         copy.wait()

time: 49.8 us -> 49.7 us (level)
  transfers between devices with their start and end apart: 17 -> 17, of which waited for: 12 -> 12; matrix products, arithmetic and copies ran while one was open for 0% -> 0% of each run, Pallas kernels for 18% -> 19%
where the time goes in v11:
time: 49.7 us; the launch traced here: 49.6 us
  starting transfers between devices  23.2 us (47%)
  Pallas kernels  14.3 us (29%)
  waiting for transfers between devices  11.3 us (23%)
  between operations  0.77 us (2%)
    ppermute x14, starting transfers between devices, exchange(): return lax.ppermute(value, ('seq', 'head'), pairs)  21.3 us
    pallas_call x13, Pallas kernels, call(): return list(kernel(*args))  14.3 us
    ppermute x14, waiting for transfers between devices, exchange(): return lax.ppermute(value, ('seq', 'head'), pairs)  9.42 us
    ppermute x3, starting transfers between devices, all_parts(): parts.append(lax.ppermute(values[by], axis, pairs))  1.92 us
    ppermute x3, waiting for transfers between devices, all_parts(): parts.append(lax.ppermute(values[by], axis, pairs))  1.87 us
  transfers between devices with their start and end apart: 17, of which 12 were waited for; matrix products, arithmetic and copies ran while one was open for 0% of the time, Pallas kernels for 19%

profile of v11, /device:TPU:0, one launch (start us, length us, event | category | flops | bytes accessed | tf_op | source)
XLA Modules:
  0.0 49.6 jit_solution(15505910581043862407)
XLA Ops:
  0.6 0.0 copy-start
  0.6 1.9 %local_state.1 = (f32[128,128]{1,0:T(8,128)S(1)}, f32[128,128]{1,0:T(8,128)S(1)}, f32[128,128]{1,0:T(8,128)S(1)}, f32[128,128]{1,0:T(8,128)S(1)}, bf16[1024,512]...) custom-call(bf16[1024,512]{1,0:T(8,128)(2,1)} %k_hbm.1, bf16[1024,512]{1,0:T(8,128)(2,1)} %v_hbm.1), custom_call_target="tpu_custom_call" | custom-call | flops 134217728 | bytes 4456448 | tf_op jit(solution)/shard_map/local_state/pallas_call | solution.py:60
  2.6 4.0 %collective-permute-start = (f32[128,128]{1,0:T(8,128)S(1)}, f32[128,128]{1,0:T(8,128)S(1)}, u32[]{:S(2)}, u32[]{:S(2)}) collective-permute-start(f32[128,128]{1,0:T(8,128)S(1)} %get-tuple-element.56), channel_id=1, source_target_pairs={{0,12},{1,13},{2,14},{3,15},{4,8},{5,9},{6,10},{7,11},{8,4},{9,5},... | collective-permute-start | bytes 196616 | tf_op jit(solution)/shard_map/ppermute | solution.py:100
  6.6 0.4 collective-permute-start.1
  7.1 0.2 collective-permute-start.2
  7.3 0.0 copy-done
  7.3 0.0 copy-start.1
  7.3 2.0 %intra.1 = (f32[1024,512]{1,0:T(8,128)S(1)}, f32[1536,128]{1,0:T(8,128)S(1)}, bf16[512,1024]{1,0:T(8,128)(2,1)S(1)}) custom-call(bf16[1024,512]{1,0:T(8,128)(2,1)S(1)} %copy-done, bf16[1024,512]{1,0:T(8,128)(2,1)S(1)} %get-tuple-element.52.k, bf16[1024,512]{1,0:T(8,128)(2,1)S(1)} %get-tuple-element.53.v), custom_call_target="tpu_custom_call" | custom-call | flops 805306368 | bytes 7077888 | tf_op jit(solution)/shard_map/intra/pallas_call | solution.py:60
  9.2 0.0 collective-permute-done.refs_1_
  9.2 1.7 %collective-permute-done.1.refs_2_ = f32[128,128]{1,0:T(8,128)S(1)} collective-permute-done((f32[128,128]{1,0:T(8,128)S(1)}, f32[128,128]{1,0:T(8,128)S(1)}, u32[]{:S(2)}, u32[]{:S(2)}) %collective-permute-start.1) | collective-permute-done | bytes 65568 | tf_op jit(solution)/shard_map/ppermute | solution.py:100
  10.9 0.4 collective-permute-done.2.refs_3_
  11.3 2.7 %collective-permute-start.3 = (f32[128,128]{1,0:T(8,128)S(1)}, f32[128,128]{1,0:T(8,128)S(1)}, u32[]{:S(2)}, u32[]{:S(2)}) collective-permute-start(f32[128,128]{1,0:T(8,128)S(1)} %quad_sum.2), channel_id=1, source_target_pairs={{0,16},{1,17},{2,18},{3,19},{4,20},{5,21},{6,22},{7,23},{8,24},{9,... | collective-permute-start | bytes 196616 | tf_op jit(solution)/shard_map/ppermute | solution.py:100
  14.0 2.6 %collective-permute-done.3.refs_4_ = f32[128,128]{1,0:T(8,128)S(1)} collective-permute-done((f32[128,128]{1,0:T(8,128)S(1)}, f32[128,128]{1,0:T(8,128)S(1)}, u32[]{:S(2)}, u32[]{:S(2)}) %collective-permute-start.3) | collective-permute-done | bytes 65568 | tf_op jit(solution)/shard_map/ppermute | solution.py:100
  16.6 0.1 finish.2
  16.6 1.6 %collective-permute-start.4 = (f32[128,128]{1,0:T(8,128)S(1)}, f32[128,128]{1,0:T(8,128)S(1)}, u32[]{:S(2)}, u32[]{:S(2)}) collective-permute-start(f32[128,128]{1,0:T(8,128)S(1)} %get-tuple-element.61), channel_id=1, source_target_pairs={{0,12},{1,13},{2,14},{3,15},{4,8},{5,9},{6,10},{7,11},{8,4},{9,5},... | collective-permute-start | bytes 196616 | tf_op jit(solution)/shard_map/ppermute | solution.py:100
  18.3 0.3 collective-permute-start.5
  18.6 1.6 %collective-permute-start.6 = (f32[128,128]{1,0:T(8,128)S(1)}, f32[128,128]{1,0:T(8,128)S(1)}, u32[]{:S(2)}, u32[]{:S(2)}) collective-permute-start(f32[128,128]{1,0:T(8,128)S(1)} %get-tuple-element.64), channel_id=1, source_target_pairs={{0,4},{1,5},{2,6},{3,7},{4,0},{5,1},{6,2},{7,3},{8,12},{9,13},{10,... | collective-permute-start | bytes 196616 | tf_op jit(solution)/shard_map/ppermute | solution.py:100
  20.2 1.7 %collective-permute-done.4.refs_1_ = f32[128,128]{1,0:T(8,128)S(1)} collective-permute-done((f32[128,128]{1,0:T(8,128)S(1)}, f32[128,128]{1,0:T(8,128)S(1)}, u32[]{:S(2)}, u32[]{:S(2)}) %collective-permute-start.4) | collective-permute-done | bytes 65568 | tf_op jit(solution)/shard_map/ppermute | solution.py:100
  21.9 0.0 copy-done.1
  21.9 0.5 %mixed.2 = (f32[1024,256]{1,0:T(8,128)S(1)}, bf16[512,128]{1,0:T(8,128)(2,1)S(1)}, f32[16,128]{1,0:T(8,128)S(1)}) custom-call(f32[1024,512]{1,0:T(8,128)S(1)} %get-tuple-element.54.intra, bf16[1024,512]{1,0:T(8,128)(2,1)S(1)} %copy-done, bf16[1024,512]{1,0:T(8,128)(2,1)S(1)} %copy-done.1, f32[128,128]{1,0:T(8,128)S(1)} %get-tuple-element.60.refs_0_, ...), custom_call_target="tpu_custom_call" | custom-call | flops 67108864 | bytes 5513216 | tf_op jit(solution)/shard_map/mixed/pallas_call | solution.py:60
  22.4 0.1 collective-permute-done.5.refs_0_
  22.5 0.3 collective-permute-done.6.refs_1_
  22.9 0.5 %mixed.3 = (f32[1024,256]{1,0:T(8,128)S(1)}, bf16[512,128]{1,0:T(8,128)(2,1)S(1)}, f32[16,128]{1,0:T(8,128)S(1)}, f32[16,128]{1,0:T(8,128)S(1)}, f32[16,128]{1,0:T(8,128)S(1)}, /*index=5*/f32[16,128]{1,0:T(8,128)S(1)}) custom-call(f32[1024,512]{1,0:T(8,128)S(1)} %get-tuple-element.54.intra, bf16[1024,512]{1,0:T(8,128)(2,1)S(1)} %copy-done, ...), custom_call_target="tpu_custom_call" | custom-call | flops 67108864 | bytes 5677056 | tf_op jit(solution)/shard_map/mixed/pallas_call | solution.py:60
  23.4 0.1 collective-permute-start.7
  23.5 1.8 %collective-permute-start.8 = (f32[16,128]{1,0:T(8,128)S(1)}, f32[16,128]{1,0:T(8,128)S(1)}, u32[]{:S(2)}, u32[]{:S(2)}) collective-permute-start(f32[16,128]{1,0:T(8,128)S(1)} %get-tuple-element.70), channel_id=1, source_target_pairs={{0,2},{1,3},{2,0},{3,1},{4,6},{5,7},{6,4},{7,5},{8,10},{9,11},{10,... | collective-permute-start | bytes 24584 | tf_op jit(solution)/shard_map/ppermute | solution.py:407
  25.3 0.1 collective-permute-start.9
  25.4 1.2 %collective-permute-done.7.refs_1_ = f32[16,128]{1,0:T(8,128)S(1)} collective-permute-done((f32[16,128]{1,0:T(8,128)S(1)}, f32[16,128]{1,0:T(8,128)S(1)}, u32[]{:S(2)}, u32[]{:S(2)}) %collective-permute-start.7) | collective-permute-done | bytes 8224 | tf_op jit(solution)/shard_map/ppermute | solution.py:407
  26.6 0.7 %collective-permute-done.8.refs_2_ = f32[16,128]{1,0:T(8,128)S(1)} collective-permute-done((f32[16,128]{1,0:T(8,128)S(1)}, f32[16,128]{1,0:T(8,128)S(1)}, u32[]{:S(2)}, u32[]{:S(2)}) %collective-permute-start.8) | collective-permute-done | bytes 8224 | tf_op jit(solution)/shard_map/ppermute | solution.py:407
  27.2 0.0 collective-permute-done.9.refs_3_
  27.2 0.8 %norm.1 = (bf16[1024,512]{1,0:T(8,128)(2,1)S(1)}, f32[8,128]{1,0:T(8,128)S(1)}, f32[1536,128]{1,0:T(8,128)S(1)}, f32[128,128]{1,0:T(8,128)S(1)}, f32[128,128]{1,...) custom-call(f32[1024,256]{1,0:T(8,128)S(1)} %get-tuple-element.62.mixed, ...), custom_call_target="tpu_custom_call" | custom-call | flops 134217728 | bytes 6328320 | tf_op jit(solution)/shard_map/norm/pallas_call | solution.py:60
  28.1 2.7 %collective-permute-start.10 = (f32[128,128]{1,0:T(8,128)S(1)}, f32[128,128]{1,0:T(8,128)S(1)}, u32[]{:S(2)}, u32[]{:S(2)}) collective-permute-start(f32[128,128]{1,0:T(8,128)S(1)} %get-tuple-element.78), channel_id=1, source_target_pairs={{0,12},{1,13},{2,14},{3,15},{4,8},{5,9},{6,10},{7,11},{8,4},{9,5},... | collective-permute-start | bytes 196616 | tf_op jit(solution)/shard_map/ppermute | solution.py:100
  30.7 0.5 %collective-permute-start.11 = (f32[128,128]{1,0:T(8,128)S(1)}, f32[128,128]{1,0:T(8,128)S(1)}, u32[]{:S(2)}, u32[]{:S(2)}) collective-permute-start(f32[128,128]{1,0:T(8,128)S(1)} %get-tuple-element.79), channel_id=1, source_target_pairs={{0,4},{1,5},{2,6},{3,7},{4,0},{5,1},{6,2},{7,3},{8,12},{9,13},{10,... | collective-permute-start | bytes 196616 | tf_op jit(solution)/shard_map/ppermute | solution.py:100
  31.3 0.4 collective-permute-start.12
  31.6 2.5 %first_grads.1 = (bf16[1024,128]{1,0:T(8,128)(2,1)S(1)}, bf16[1024,128]{1,0:T(8,128)(2,1)S(1)}, f32[1024,128]{1,0:T(8,128)S(1)}, f32[1024,128]{1,0:T(8,128)S(1)}...) custom-call(bf16[1024,512]{1,0:T(8,128)(2,1)S(1)} %copy-done, bf16[1024,512]{1,0:T(8,128)(2,1)S(1)} %get-tuple-element.52.k, ...), custom_call_target="tpu_custom_call" | custom-call | flops 1006632960 | bytes 8519680 | tf_op jit(solution)/shard_map/first_grads/pallas_call | solution.py:60
  34.1 0.0 collective-permute-done.10.refs_1_
  34.1 0.9 %collective-permute-done.11.refs_2_ = f32[128,128]{1,0:T(8,128)S(1)} collective-permute-done((f32[128,128]{1,0:T(8,128)S(1)}, f32[128,128]{1,0:T(8,128)S(1)}, u32[]{:S(2)}, u32[]{:S(2)}) %collective-permute-start.11) | collective-permute-done | bytes 65568 | tf_op jit(solution)/shard_map/ppermute | solution.py:100
  35.0 0.5 %collective-permute-done.12.refs_3_ = f32[128,128]{1,0:T(8,128)S(1)} collective-permute-done((f32[128,128]{1,0:T(8,128)S(1)}, f32[128,128]{1,0:T(8,128)S(1)}, u32[]{:S(2)}, u32[]{:S(2)}) %collective-permute-start.12) | collective-permute-done | bytes 65568 | tf_op jit(solution)/shard_map/ppermute | solution.py:100
  35.5 3.3 %collective-permute-start.13 = (f32[128,128]{1,0:T(8,128)S(1)}, f32[128,128]{1,0:T(8,128)S(1)}, u32[]{:S(2)}, u32[]{:S(2)}) collective-permute-start(f32[128,128]{1,0:T(8,128)S(1)} %quad_sum.3.refs_0_), channel_id=1, source_target_pairs={{0,16},{1,17},{2,18},{3,19},{4,20},{5,21},{6,22},{7,23},{8,24},{9,... | collective-permute-start | bytes 196616 | tf_op jit(solution)/shard_map/ppermute | solution.py:100
  38.9 2.2 %second_grads.1 = (bf16[1024,128]{1,0:T(8,128)(2,1)S(1)}, f32[1024,128]{1,0:T(8,128)S(1)}, f32[1024,128]{1,0:T(8,128)S(1)}, bf16[1024,512]{1,0:T(8,128)(2,1)}) custom-call(bf16[1024,512]{1,0:T(8,128)(2,1)S(1)} %copy-done, bf16[1024,512]{1,0:T(8,128)(2,1)S(1)} %get-tuple-element.52.k, bf16[1024,512]{1,0:T(8,128)(2,1)S(1)} %get-tuple-element.53.v, ...), custom_call_target="tpu_custom_call" | custom-call | flops 503316480 | bytes 10424320 | tf_op jit(solution)/shard_map/second_grads/pallas_call | solution.py:60
  41.1 0.8 %collective-permute-done.13.refs_4_ = f32[128,128]{1,0:T(8,128)S(1)} collective-permute-done((f32[128,128]{1,0:T(8,128)S(1)}, f32[128,128]{1,0:T(8,128)S(1)}, u32[]{:S(2)}, u32[]{:S(2)}) %collective-permute-start.13) | collective-permute-done | bytes 65568 | tf_op jit(solution)/shard_map/ppermute | solution.py:100
  41.9 0.1 finish.3
  41.9 0.5 collective-permute-start.14
  42.4 1.3 %collective-permute-start.15 = (f32[128,128]{1,0:T(8,128)S(1)}, f32[128,128]{1,0:T(8,128)S(1)}, u32[]{:S(2)}, u32[]{:S(2)}) collective-permute-start(f32[128,128]{1,0:T(8,128)S(1)} %get-tuple-element.96), channel_id=1, source_target_pairs={{0,4},{1,5},{2,6},{3,7},{4,0},{5,1},{6,2},{7,3},{8,12},{9,13},{10,... | collective-permute-start | bytes 196616 | tf_op jit(solution)/shard_map/ppermute | solution.py:100
  43.7 1.8 %collective-permute-start.16 = (f32[128,128]{1,0:T(8,128)S(1)}, f32[128,128]{1,0:T(8,128)S(1)}, u32[]{:S(2)}, u32[]{:S(2)}) collective-permute-start(f32[128,128]{1,0:T(8,128)S(1)} %get-tuple-element.97), channel_id=1, source_target_pairs={{0,8},{1,9},{2,10},{3,11},{4,12},{5,13},{6,14},{7,15},{8,0},{9,1},... | collective-permute-start | bytes 196616 | tf_op jit(solution)/shard_map/ppermute | solution.py:100
  45.5 2.0 %third_grads.1 = (f32[1024,128]{1,0:T(8,128)S(1)}, f32[1024,128]{1,0:T(8,128)S(1)}, bf16[1024,512]{1,0:T(8,128)(2,1)}) custom-call(bf16[1024,512]{1,0:T(8,128)(2,1)S(1)} %copy-done, bf16[1024,512]{1,0:T(8,128)(2,1)S(1)} %get-tuple-element.52.k, bf16[1024,512]{1,0:T(8,128)(2,1)S(1)} %get-tuple-element.53.v, bf16[1024,512]{1,0:T(8,128)(2,1)S(1)} %get-tuple-element.72.gm, ...), custom_call_target="tpu_custom_call" | custom-call | flops 503316480 | bytes 8847360 | tf_op jit(solution)/shard_map/third_grads/pallas_call | solution.py:60
  47.5 0.0 collective-permute-done.14.refs_9_
  47.5 0.0 collective-permute-done.15.refs_10_
  47.5 0.4 collective-permute-done.16.refs_11_
  47.9 1.6 %last.1 = (bf16[1024,512]{1,0:T(8,128)(2,1)}, bf16[1024,512]{1,0:T(8,128)(2,1)}) custom-call(bf16[1024,512]{1,0:T(8,128)(2,1)S(1)} %get-tuple-element.52.k, bf16[1024,512]{1,0:T(8,128)(2,1)S(1)} %get-tuple-element.53.v, f32[1024,128]{1,0:T(8,128)S(1)} %get-tuple-element.89.refs_0_, f32[1024,128]{1,0:T(8,128)S(1)} %get-tuple-element.81.refs_4_.refs_1_, ...), custom_call_target="tpu_custom_call" | custom-call | flops 268435456 | bytes 8650752 | tf_op jit(solution)/shard_map/last/pallas_call | solution.py:60
  (2 shorter events, 0.0 us)
Async XLA Ops:
  0.6 6.6 %copy-start = (bf16[1024,512]{1,0:T(8,128)(2,1)S(1)}, bf16[1024,512]{1,0:T(8,128)(2,1)}, u32[]{:S(2)}) copy-start(bf16[1024,512]{1,0:T(8,128)(2,1)} %q.11) | copy-start | bytes 3145732
  2.6 6.6 %collective-permute-start = (f32[128,128]{1,0:T(8,128)S(1)}, f32[128,128]{1,0:T(8,128)S(1)}, u32[]{:S(2)}, u32[]{:S(2)}) collective-permute-start(f32[128,128]{1,0:T(8,128)S(1)} %get-tuple-element.56), channel_id=1, source_target_pairs={{0,12},{1,13},{2,14},{3,15},{4,8},{5,9},{6,10},{7,11},{8,4},{9,5},... | collective-permute-start | bytes 196616 | tf_op jit(solution)/shard_map/ppermute | solution.py:100
  6.6 4.3 %collective-permute-start.1 = (f32[128,128]{1,0:T(8,128)S(1)}, f32[128,128]{1,0:T(8,128)S(1)}, u32[]{:S(2)}, u32[]{:S(2)}) collective-permute-start(f32[128,128]{1,0:T(8,128)S(1)} %get-tuple-element.57), channel_id=1, source_target_pairs={{0,8},{1,9},{2,10},{3,11},{4,12},{5,13},{6,14},{7,15},{8,0},{9,1},... | collective-permute-start | bytes 196616 | tf_op jit(solution)/shard_map/ppermute | solution.py:100
  7.1 4.3 %collective-permute-start.2 = (f32[128,128]{1,0:T(8,128)S(1)}, f32[128,128]{1,0:T(8,128)S(1)}, u32[]{:S(2)}, u32[]{:S(2)}) collective-permute-start(f32[128,128]{1,0:T(8,128)S(1)} %get-tuple-element.58), channel_id=1, source_target_pairs={{0,4},{1,5},{2,6},{3,7},{4,0},{5,1},{6,2},{7,3},{8,12},{9,13},{10,... | collective-permute-start | bytes 196616 | tf_op jit(solution)/shard_map/ppermute | solution.py:100
  7.3 14.6 %copy-start.1 = (bf16[1024,512]{1,0:T(8,128)(2,1)S(1)}, bf16[1024,512]{1,0:T(8,128)(2,1)}, u32[]{:S(2)}) copy-start(bf16[1024,512]{1,0:T(8,128)(2,1)} %g.5) | copy-start | bytes 3145732
  11.3 5.2 %collective-permute-start.3 = (f32[128,128]{1,0:T(8,128)S(1)}, f32[128,128]{1,0:T(8,128)S(1)}, u32[]{:S(2)}, u32[]{:S(2)}) collective-permute-start(f32[128,128]{1,0:T(8,128)S(1)} %quad_sum.2), channel_id=1, source_target_pairs={{0,16},{1,17},{2,18},{3,19},{4,20},{5,21},{6,22},{7,23},{8,24},{9,... | collective-permute-start | bytes 196616 | tf_op jit(solution)/shard_map/ppermute | solution.py:100
  16.6 5.2 %collective-permute-start.4 = (f32[128,128]{1,0:T(8,128)S(1)}, f32[128,128]{1,0:T(8,128)S(1)}, u32[]{:S(2)}, u32[]{:S(2)}) collective-permute-start(f32[128,128]{1,0:T(8,128)S(1)} %get-tuple-element.61), channel_id=1, source_target_pairs={{0,12},{1,13},{2,14},{3,15},{4,8},{5,9},{6,10},{7,11},{8,4},{9,5},... | collective-permute-start | bytes 196616 | tf_op jit(solution)/shard_map/ppermute | solution.py:100
  18.3 4.3 %collective-permute-start.5 = (f32[128,128]{1,0:T(8,128)S(1)}, f32[128,128]{1,0:T(8,128)S(1)}, u32[]{:S(2)}, u32[]{:S(2)}) collective-permute-start(f32[128,128]{1,0:T(8,128)S(1)} %get-tuple-element.63), channel_id=1, source_target_pairs={{0,8},{1,9},{2,10},{3,11},{4,12},{5,13},{6,14},{7,15},{8,0},{9,1},... | collective-permute-start | bytes 196616 | tf_op jit(solution)/shard_map/ppermute | solution.py:100
  18.6 4.3 %collective-permute-start.6 = (f32[128,128]{1,0:T(8,128)S(1)}, f32[128,128]{1,0:T(8,128)S(1)}, u32[]{:S(2)}, u32[]{:S(2)}) collective-permute-start(f32[128,128]{1,0:T(8,128)S(1)} %get-tuple-element.64), channel_id=1, source_target_pairs={{0,4},{1,5},{2,6},{3,7},{4,0},{5,1},{6,2},{7,3},{8,12},{9,13},{10,... | collective-permute-start | bytes 196616 | tf_op jit(solution)/shard_map/ppermute | solution.py:100
  23.4 3.1 %collective-permute-start.7 = (f32[16,128]{1,0:T(8,128)S(1)}, f32[16,128]{1,0:T(8,128)S(1)}, u32[]{:S(2)}, u32[]{:S(2)}) collective-permute-start(f32[16,128]{1,0:T(8,128)S(1)} %get-tuple-element.69), channel_id=1, source_target_pairs={{0,3},{1,2},{2,1},{3,0},{4,7},{5,6},{6,5},{7,4},{8,11},{9,10},{10,... | collective-permute-start | bytes 24584 | tf_op jit(solution)/shard_map/ppermute | solution.py:407
  23.5 3.7 %collective-permute-start.8 = (f32[16,128]{1,0:T(8,128)S(1)}, f32[16,128]{1,0:T(8,128)S(1)}, u32[]{:S(2)}, u32[]{:S(2)}) collective-permute-start(f32[16,128]{1,0:T(8,128)S(1)} %get-tuple-element.70), channel_id=1, source_target_pairs={{0,2},{1,3},{2,0},{3,1},{4,6},{5,7},{6,4},{7,5},{8,10},{9,11},{10,... | collective-permute-start | bytes 24584 | tf_op jit(solution)/shard_map/ppermute | solution.py:407
  25.3 1.9 %collective-permute-start.9 = (f32[16,128]{1,0:T(8,128)S(1)}, f32[16,128]{1,0:T(8,128)S(1)}, u32[]{:S(2)}, u32[]{:S(2)}) collective-permute-start(f32[16,128]{1,0:T(8,128)S(1)} %get-tuple-element.71), channel_id=1, source_target_pairs={{0,1},{1,0},{2,3},{3,2},{4,5},{5,4},{6,7},{7,6},{8,9},{9,8},{10,11... | collective-permute-start | bytes 24584 | tf_op jit(solution)/shard_map/ppermute | solution.py:407
  28.1 6.1 %collective-permute-start.10 = (f32[128,128]{1,0:T(8,128)S(1)}, f32[128,128]{1,0:T(8,128)S(1)}, u32[]{:S(2)}, u32[]{:S(2)}) collective-permute-start(f32[128,128]{1,0:T(8,128)S(1)} %get-tuple-element.78), channel_id=1, source_target_pairs={{0,12},{1,13},{2,14},{3,15},{4,8},{5,9},{6,10},{7,11},{8,4},{9,5},... | collective-permute-start | bytes 196616 | tf_op jit(solution)/shard_map/ppermute | solution.py:100
  30.7 4.3 %collective-permute-start.11 = (f32[128,128]{1,0:T(8,128)S(1)}, f32[128,128]{1,0:T(8,128)S(1)}, u32[]{:S(2)}, u32[]{:S(2)}) collective-permute-start(f32[128,128]{1,0:T(8,128)S(1)} %get-tuple-element.79), channel_id=1, source_target_pairs={{0,4},{1,5},{2,6},{3,7},{4,0},{5,1},{6,2},{7,3},{8,12},{9,13},{10,... | collective-permute-start | bytes 196616 | tf_op jit(solution)/shard_map/ppermute | solution.py:100
  31.3 4.3 %collective-permute-start.12 = (f32[128,128]{1,0:T(8,128)S(1)}, f32[128,128]{1,0:T(8,128)S(1)}, u32[]{:S(2)}, u32[]{:S(2)}) collective-permute-start(f32[128,128]{1,0:T(8,128)S(1)} %get-tuple-element.80), channel_id=1, source_target_pairs={{0,8},{1,9},{2,10},{3,11},{4,12},{5,13},{6,14},{7,15},{8,0},{9,1},... | collective-permute-start | bytes 196616 | tf_op jit(solution)/shard_map/ppermute | solution.py:100
  35.5 6.3 %collective-permute-start.13 = (f32[128,128]{1,0:T(8,128)S(1)}, f32[128,128]{1,0:T(8,128)S(1)}, u32[]{:S(2)}, u32[]{:S(2)}) collective-permute-start(f32[128,128]{1,0:T(8,128)S(1)} %quad_sum.3.refs_0_), channel_id=1, source_target_pairs={{0,16},{1,17},{2,18},{3,19},{4,20},{5,21},{6,22},{7,23},{8,24},{9,... | collective-permute-start | bytes 196616 | tf_op jit(solution)/shard_map/ppermute | solution.py:100
  41.9 5.5 %collective-permute-start.14 = (f32[128,128]{1,0:T(8,128)S(1)}, f32[128,128]{1,0:T(8,128)S(1)}, u32[]{:S(2)}, u32[]{:S(2)}) collective-permute-start(f32[128,128]{1,0:T(8,128)S(1)} %get-tuple-element.95), channel_id=1, source_target_pairs={{0,12},{1,13},{2,14},{3,15},{4,8},{5,9},{6,10},{7,11},{8,4},{9,5},... | collective-permute-start | bytes 196616 | tf_op jit(solution)/shard_map/ppermute | solution.py:100
  42.4 5.1 %collective-permute-start.15 = (f32[128,128]{1,0:T(8,128)S(1)}, f32[128,128]{1,0:T(8,128)S(1)}, u32[]{:S(2)}, u32[]{:S(2)}) collective-permute-start(f32[128,128]{1,0:T(8,128)S(1)} %get-tuple-element.96), channel_id=1, source_target_pairs={{0,4},{1,5},{2,6},{3,7},{4,0},{5,1},{6,2},{7,3},{8,12},{9,13},{10,... | collective-permute-start | bytes 196616 | tf_op jit(solution)/shard_map/ppermute | solution.py:100
  43.7 4.3 %collective-permute-start.16 = (f32[128,128]{1,0:T(8,128)S(1)}, f32[128,128]{1,0:T(8,128)S(1)}, u32[]{:S(2)}, u32[]{:S(2)}) collective-permute-start(f32[128,128]{1,0:T(8,128)S(1)} %get-tuple-element.97), channel_id=1, source_target_pairs={{0,8},{1,9},{2,10},{3,11},{4,12},{5,13},{6,14},{7,15},{8,0},{9,1},... | collective-permute-start | bytes 196616 | tf_op jit(solution)/shard_map/ppermute | solution.py:100

commit v12 on v11

--- a/solution.py
+++ b/solution.py
@@ -229,6 +229,17 @@
             intra[at, part] = out
             new = dot(ki, vi, 0, 0)
             state = state + new if n else new
+
+
+def scores_kernel(q, k, token, scores_t):
+    keep = causal(True)
+    rows = q.shape[0]
+    for h in range(q.shape[1] // HEAD_DIM):
+        part = head_slice(h)
+        for at in chunk_slices(rows):
+            raw = dot(k[at, part], q[at, part], 1, 1)
+            to = slice(h * rows + at.start, h * rows + at.stop)
+            scores_t[to, :] = jnp.where(keep, raw, 0.0).astype(BF16)
 
 
 def row_sums(tile):
@@ -308,14 +319,14 @@
         piece[...] = scratch[rows_at(ORDERS[True][0], slot), :]
 
 
-def head_grads(h, q, k, v, gm, prefix, states, after, gq, gk, gv, finished=None):
-    cols, part = q.shape[1], head_slice(h)
+def head_grads(h, q, k, v, gm, prefix, states, after, scores, gq, gk, gv, finished=None):
+    (rows, cols), part = q.shape, head_slice(h)
     keep, keep_t = causal(), causal(True)
     chunks = chunk_slices(q.shape[0])
     first = prefix[part, :].astype(F32)
     for n, at in enumerate(chunks):
         qi, ki, vi, gi = q[at, part], k[at, part], v[at, part], gm[at, part]
-        scores_t = jnp.where(keep_t, dot(ki, qi, 1, 1), 0.0).astype(BF16)
+        scores_t = scores[h * rows + at.start : h * rows + at.stop, :]
         grad_scores = jnp.where(keep, dot(gi, vi, 1, 1), 0.0).astype(BF16)
         grad_scores_t = jnp.where(keep_t, dot(vi, gi, 1, 1), 0.0).astype(BF16)
         entering = first
@@ -335,13 +346,14 @@
             finished(n, at)
 
 
-def first_grads_kernel(q, k, v, gm, prefix, states, after, *refs):
+def first_grads_kernel(q, k, v, gm, prefix, states, after, scores, *refs):
     gqs, gks, gvs = refs[:2], refs[2:4], refs[4:]
     for h in range(2):
-        head_grads(h, q, k, v, gm, prefix, states, after, gqs[h], gks[h], gvs[h])
-
-
-def second_grads_kernel(q, k, v, gm, prefix, states, after, mixed, oth_mixed, inverse, *refs):
+        head_grads(h, q, k, v, gm, prefix, states, after, scores, gqs[h], gks[h], gvs[h])
+
+
+def second_grads_kernel(q, k, v, gm, prefix, states, after, scores, *refs):
+    mixed, oth_mixed, inverse = refs[:3]
     gq, gk, gv, out_hbm, out, sems = refs[-6:]
     shape = (HEAD_DIM, HEAD_DIM)
 
@@ -355,14 +367,14 @@
                     out[head_slice(i), head_slice(h)] = (value * a).astype(BF16)
             copies.append(pltpu.make_async_copy(out.at[at], out_hbm.at[at], sems.at[n]))
             copies[-1].start()
-        head_grads(2, q, k, v, gm, prefix, states, after, gq, gk, gv)
+        head_grads(2, q, k, v, gm, prefix, states, after, scores, gq, gk, gv)
         for copy in copies:
             copy.wait()
 
     by_pair(body, mixed, oth_mixed)
 
 
-def third_grads_kernel(q, k, v, gm, prefix, states, after, *refs):
+def third_grads_kernel(q, k, v, gm, prefix, states, after, scores, *refs):
     gqs, (gk, gv, gq_hbm, gq, sems) = refs[:3], refs[-5:]
     copies = []
 
@@ -373,7 +385,7 @@
     for h in range(3):
         send(gqs[h], h, slice(0, q.shape[0]), sems.at[h])
     head_grads(
-        3, q, k, v, gm, prefix, states, after, gq, gk, gv, lambda n, at: send(gq, 3, at, sems.at[3 + n])
+        3, q, k, v, gm, prefix, states, after, scores, gq, gk, gv, lambda n, at: send(gq, 3, at, sems.at[3 + n])
     )
     for copy in copies:
         copy.wait()
@@ -437,8 +449,17 @@
     )
 
     def forward(phase, token):
-        if phase:
+        if phase == 2:
             return []
+        if phase == 1:
+            return call(
+                scores_kernel,
+                [shape(QUAD * rows, CHUNK, BF16)],
+                [queries, keys, token],
+                QUAD * chunk_flops,
+                "scores",
+                spaces={2: pl.ANY},
+            )
         return call(
             intra_kernel,
             [wide, states_shape, shape(cols, rows, BF16)],
@@ -447,7 +468,7 @@
             "intra",
         )
 
-    prefixes, (intra, states, queries_t) = scan(pieces, sizes, False, forward)
+    prefixes, (intra, states, queries_t, scores) = scan(pieces, sizes, False, forward)
     stats_shape = shape(2 * blocks, HEAD_DIM)
 
     def mix(is_own, pieces, count, *before):
@@ -470,8 +491,8 @@
         "norm",
         scratch=[pieces_scratch],
     )
-    args = [queries, keys, values, gm, prefix, states, after]
-    grads_flops = 6 * chunk_flops + 3 * head_flops
+    args = [queries, keys, values, gm, prefix, states, after, scores]
+    grads_flops = 5 * chunk_flops + 3 * head_flops
 
     def backward(phase, token):
         if phase == 0:

time: 49.7 us -> 49.7 us (level)
    pallas_call x13 -> x14, Pallas kernels: 14.3 us -> 14.2 us  [call(): return list(kernel(*args))]
  transfers between devices with their start and end apart: 17 -> 17, of which waited for: 12 -> 12; matrix products, arithmetic and copies ran while one was open for 0% -> 0% of each run, Pallas kernels for 19% -> 18%
where the time goes in v12:
time: 49.7 us; the launch traced here: 49.6 us
  starting transfers between devices  23.2 us (47%)
  Pallas kernels  14.2 us (29%)
  waiting for transfers between devices  11.4 us (23%)
  between operations  0.78 us (2%)
    ppermute x14, starting transfers between devices, exchange(): return lax.ppermute(value, ('seq', 'head'), pairs)  21.3 us
    pallas_call x14, Pallas kernels, call(): return list(kernel(*args))  14.2 us
    ppermute x14, waiting for transfers between devices, exchange(): return lax.ppermute(value, ('seq', 'head'), pairs)  9.55 us
    ppermute x3, starting transfers between devices, all_parts(): parts.append(lax.ppermute(values[by], axis, pairs))  1.92 us
    ppermute x3, waiting for transfers between devices, all_parts(): parts.append(lax.ppermute(values[by], axis, pairs))  1.87 us
  transfers between devices with their start and end apart: 17, of which 12 were waited for; matrix products, arithmetic and copies ran while one was open for 0% of the time, Pallas kernels for 18%

profile of v12, /device:TPU:0, one launch (start us, length us, event | category | flops | bytes accessed | tf_op | source)
XLA Modules:
  0.0 49.6 jit_solution(13366313986100123895)
XLA Ops:
  0.6 0.0 copy-start
  0.6 1.9 %local_state.1 = (f32[128,128]{1,0:T(8,128)S(1)}, f32[128,128]{1,0:T(8,128)S(1)}, f32[128,128]{1,0:T(8,128)S(1)}, f32[128,128]{1,0:T(8,128)S(1)}, bf16[1024,512]...) custom-call(bf16[1024,512]{1,0:T(8,128)(2,1)} %k_hbm.1, bf16[1024,512]{1,0:T(8,128)(2,1)} %v_hbm.1), custom_call_target="tpu_custom_call" | custom-call | flops 134217728 | bytes 4456448 | tf_op jit(solution)/shard_map/local_state/pallas_call | solution.py:60
  2.6 4.0 %collective-permute-start = (f32[128,128]{1,0:T(8,128)S(1)}, f32[128,128]{1,0:T(8,128)S(1)}, u32[]{:S(2)}, u32[]{:S(2)}) collective-permute-start(f32[128,128]{1,0:T(8,128)S(1)} %get-tuple-element.56), channel_id=1, source_target_pairs={{0,12},{1,13},{2,14},{3,15},{4,8},{5,9},{6,10},{7,11},{8,4},{9,5},... | collective-permute-start | bytes 196616 | tf_op jit(solution)/shard_map/ppermute | solution.py:100
  6.6 0.4 collective-permute-start.1
  7.1 0.2 collective-permute-start.2
  7.3 0.0 copy-done
  7.3 1.9 %intra.1 = (f32[1024,512]{1,0:T(8,128)S(1)}, f32[1536,128]{1,0:T(8,128)S(1)}, bf16[512,1024]{1,0:T(8,128)(2,1)S(1)}) custom-call(bf16[1024,512]{1,0:T(8,128)(2,1)S(1)} %copy-done, bf16[1024,512]{1,0:T(8,128)(2,1)S(1)} %get-tuple-element.52.k, bf16[1024,512]{1,0:T(8,128)(2,1)S(1)} %get-tuple-element.53.v), custom_call_target="tpu_custom_call" | custom-call | flops 805306368 | bytes 7077888 | tf_op jit(solution)/shard_map/intra/pallas_call | solution.py:60
  9.2 0.0 collective-permute-done.refs_1_
  9.2 1.7 %collective-permute-done.1.refs_2_ = f32[128,128]{1,0:T(8,128)S(1)} collective-permute-done((f32[128,128]{1,0:T(8,128)S(1)}, f32[128,128]{1,0:T(8,128)S(1)}, u32[]{:S(2)}, u32[]{:S(2)}) %collective-permute-start.1) | collective-permute-done | bytes 65568 | tf_op jit(solution)/shard_map/ppermute | solution.py:100
  10.9 0.4 collective-permute-done.2.refs_3_
  11.3 2.7 %collective-permute-start.3 = (f32[128,128]{1,0:T(8,128)S(1)}, f32[128,128]{1,0:T(8,128)S(1)}, u32[]{:S(2)}, u32[]{:S(2)}) collective-permute-start(f32[128,128]{1,0:T(8,128)S(1)} %quad_sum.2.token), channel_id=1, source_target_pairs={{0,16},{1,17},{2,18},{3,19},{4,20},{5,21},{6,22},{7,23},{8,24},{9,... | collective-permute-start | bytes 196616 | tf_op jit(solution)/shard_map/ppermute | solution.py:100
  14.0 0.7 %scores.1.refs_5_ = bf16[4096,256]{1,0:T(8,128)(2,1)S(1)} custom-call(bf16[1024,512]{1,0:T(8,128)(2,1)S(1)} %copy-done, bf16[1024,512]{1,0:T(8,128)(2,1)S(1)} %get-tuple-element.52.k, f32[128,128]{1,0:T(8,128)S(1)} %quad_sum.2.token), custom_call_target="tpu_custom_call" | custom-call | flops 268435456 | bytes 4259840 | tf_op jit(solution)/shard_map/scores/pallas_call | solution.py:60
  14.7 0.0 copy-start.1
  14.7 1.8 %collective-permute-done.3.refs_4_ = f32[128,128]{1,0:T(8,128)S(1)} collective-permute-done((f32[128,128]{1,0:T(8,128)S(1)}, f32[128,128]{1,0:T(8,128)S(1)}, u32[]{:S(2)}, u32[]{:S(2)}) %collective-permute-start.3) | collective-permute-done | bytes 65568 | tf_op jit(solution)/shard_map/ppermute | solution.py:100
  16.6 0.1 finish.2
  16.6 1.6 %collective-permute-start.4 = (f32[128,128]{1,0:T(8,128)S(1)}, f32[128,128]{1,0:T(8,128)S(1)}, u32[]{:S(2)}, u32[]{:S(2)}) collective-permute-start(f32[128,128]{1,0:T(8,128)S(1)} %get-tuple-element.61), channel_id=1, source_target_pairs={{0,12},{1,13},{2,14},{3,15},{4,8},{5,9},{6,10},{7,11},{8,4},{9,5},... | collective-permute-start | bytes 196616 | tf_op jit(solution)/shard_map/ppermute | solution.py:100
  18.3 0.3 collective-permute-start.5
  18.6 1.6 %collective-permute-start.6 = (f32[128,128]{1,0:T(8,128)S(1)}, f32[128,128]{1,0:T(8,128)S(1)}, u32[]{:S(2)}, u32[]{:S(2)}) collective-permute-start(f32[128,128]{1,0:T(8,128)S(1)} %get-tuple-element.64), channel_id=1, source_target_pairs={{0,4},{1,5},{2,6},{3,7},{4,0},{5,1},{6,2},{7,3},{8,12},{9,13},{10,... | collective-permute-start | bytes 196616 | tf_op jit(solution)/shard_map/ppermute | solution.py:100
  20.2 1.7 %collective-permute-done.4.refs_1_ = f32[128,128]{1,0:T(8,128)S(1)} collective-permute-done((f32[128,128]{1,0:T(8,128)S(1)}, f32[128,128]{1,0:T(8,128)S(1)}, u32[]{:S(2)}, u32[]{:S(2)}) %collective-permute-start.4) | collective-permute-done | bytes 65568 | tf_op jit(solution)/shard_map/ppermute | solution.py:100
  21.9 0.0 copy-done.1
  21.9 0.5 %mixed.2 = (f32[1024,256]{1,0:T(8,128)S(1)}, bf16[512,128]{1,0:T(8,128)(2,1)S(1)}, f32[16,128]{1,0:T(8,128)S(1)}) custom-call(f32[1024,512]{1,0:T(8,128)S(1)} %get-tuple-element.54.intra, bf16[1024,512]{1,0:T(8,128)(2,1)S(1)} %copy-done, bf16[1024,512]{1,0:T(8,128)(2,1)S(1)} %copy-done.1, f32[128,128]{1,0:T(8,128)S(1)} %get-tuple-element.60.refs_0_, ...), custom_call_target="tpu_custom_call" | custom-call | flops 67108864 | bytes 5513216 | tf_op jit(solution)/shard_map/mixed/pallas_call | solution.py:60
  22.4 0.1 collective-permute-done.5.refs_0_
  22.5 0.3 collective-permute-done.6.refs_1_
  22.9 0.5 %mixed.3 = (f32[1024,256]{1,0:T(8,128)S(1)}, bf16[512,128]{1,0:T(8,128)(2,1)S(1)}, f32[16,128]{1,0:T(8,128)S(1)}, f32[16,128]{1,0:T(8,128)S(1)}, f32[16,128]{1,0:T(8,128)S(1)}, /*index=5*/f32[16,128]{1,0:T(8,128)S(1)}) custom-call(f32[1024,512]{1,0:T(8,128)S(1)} %get-tuple-element.54.intra, bf16[1024,512]{1,0:T(8,128)(2,1)S(1)} %copy-done, ...), custom_call_target="tpu_custom_call" | custom-call | flops 67108864 | bytes 5677056 | tf_op jit(solution)/shard_map/mixed/pallas_call | solution.py:60
  23.4 0.1 collective-permute-start.7
  23.5 1.8 %collective-permute-start.8 = (f32[16,128]{1,0:T(8,128)S(1)}, f32[16,128]{1,0:T(8,128)S(1)}, u32[]{:S(2)}, u32[]{:S(2)}) collective-permute-start(f32[16,128]{1,0:T(8,128)S(1)} %get-tuple-element.70), channel_id=1, source_target_pairs={{0,2},{1,3},{2,0},{3,1},{4,6},{5,7},{6,4},{7,5},{8,10},{9,11},{10,... | collective-permute-start | bytes 24584 | tf_op jit(solution)/shard_map/ppermute | solution.py:419
  25.3 0.1 collective-permute-start.9
  25.3 1.2 %collective-permute-done.7.refs_1_ = f32[16,128]{1,0:T(8,128)S(1)} collective-permute-done((f32[16,128]{1,0:T(8,128)S(1)}, f32[16,128]{1,0:T(8,128)S(1)}, u32[]{:S(2)}, u32[]{:S(2)}) %collective-permute-start.7) | collective-permute-done | bytes 8224 | tf_op jit(solution)/shard_map/ppermute | solution.py:419
  26.6 0.7 %collective-permute-done.8.refs_2_ = f32[16,128]{1,0:T(8,128)S(1)} collective-permute-done((f32[16,128]{1,0:T(8,128)S(1)}, f32[16,128]{1,0:T(8,128)S(1)}, u32[]{:S(2)}, u32[]{:S(2)}) %collective-permute-start.8) | collective-permute-done | bytes 8224 | tf_op jit(solution)/shard_map/ppermute | solution.py:419
  27.2 0.0 collective-permute-done.9.refs_3_
  27.2 0.8 %norm.1 = (bf16[1024,512]{1,0:T(8,128)(2,1)S(1)}, f32[8,128]{1,0:T(8,128)S(1)}, f32[1536,128]{1,0:T(8,128)S(1)}, f32[128,128]{1,0:T(8,128)S(1)}, f32[128,128]{1,...) custom-call(f32[1024,256]{1,0:T(8,128)S(1)} %get-tuple-element.62.mixed.refs_0_, ...), custom_call_target="tpu_custom_call" | custom-call | flops 134217728 | bytes 6328320 | tf_op jit(solution)/shard_map/norm/pallas_call | solution.py:60
  28.1 2.7 %collective-permute-start.10 = (f32[128,128]{1,0:T(8,128)S(1)}, f32[128,128]{1,0:T(8,128)S(1)}, u32[]{:S(2)}, u32[]{:S(2)}) collective-permute-start(f32[128,128]{1,0:T(8,128)S(1)} %get-tuple-element.78), channel_id=1, source_target_pairs={{0,12},{1,13},{2,14},{3,15},{4,8},{5,9},{6,10},{7,11},{8,4},{9,5},... | collective-permute-start | bytes 196616 | tf_op jit(solution)/shard_map/ppermute | solution.py:100
  30.7 0.5 %collective-permute-start.11 = (f32[128,128]{1,0:T(8,128)S(1)}, f32[128,128]{1,0:T(8,128)S(1)}, u32[]{:S(2)}, u32[]{:S(2)}) collective-permute-start(f32[128,128]{1,0:T(8,128)S(1)} %get-tuple-element.79), channel_id=1, source_target_pairs={{0,4},{1,5},{2,6},{3,7},{4,0},{5,1},{6,2},{7,3},{8,12},{9,13},{10,... | collective-permute-start | bytes 196616 | tf_op jit(solution)/shard_map/ppermute | solution.py:100
  31.2 0.4 collective-permute-start.12
  31.6 2.1 %first_grads.1 = (bf16[1024,128]{1,0:T(8,128)(2,1)S(1)}, bf16[1024,128]{1,0:T(8,128)(2,1)S(1)}, f32[1024,128]{1,0:T(8,128)S(1)}, f32[1024,128]{1,0:T(8,128)S(1)}...) custom-call(bf16[1024,512]{1,0:T(8,128)(2,1)S(1)} %copy-done, bf16[1024,512]{1,0:T(8,128)(2,1)S(1)} %get-tuple-element.52.k, ...), custom_call_target="tpu_custom_call" | custom-call | flops 872415232 | bytes 10616832 | tf_op jit(solution)/shard_map/first_grads/pallas_call | solution.py:60
  33.7 0.0 collective-permute-done.10.refs_1_
  33.8 1.3 %collective-permute-done.11.refs_2_ = f32[128,128]{1,0:T(8,128)S(1)} collective-permute-done((f32[128,128]{1,0:T(8,128)S(1)}, f32[128,128]{1,0:T(8,128)S(1)}, u32[]{:S(2)}, u32[]{:S(2)}) %collective-permute-start.11) | collective-permute-done | bytes 65568 | tf_op jit(solution)/shard_map/ppermute | solution.py:100
  35.0 0.5 %collective-permute-done.12.refs_3_ = f32[128,128]{1,0:T(8,128)S(1)} collective-permute-done((f32[128,128]{1,0:T(8,128)S(1)}, f32[128,128]{1,0:T(8,128)S(1)}, u32[]{:S(2)}, u32[]{:S(2)}) %collective-permute-start.12) | collective-permute-done | bytes 65568 | tf_op jit(solution)/shard_map/ppermute | solution.py:100
  35.5 3.3 %collective-permute-start.13 = (f32[128,128]{1,0:T(8,128)S(1)}, f32[128,128]{1,0:T(8,128)S(1)}, u32[]{:S(2)}, u32[]{:S(2)}) collective-permute-start(f32[128,128]{1,0:T(8,128)S(1)} %quad_sum.3.refs_3_), channel_id=1, source_target_pairs={{0,16},{1,17},{2,18},{3,19},{4,20},{5,21},{6,22},{7,23},{8,24},{9,... | collective-permute-start | bytes 196616 | tf_op jit(solution)/shard_map/ppermute | solution.py:100
  38.8 2.0 %second_grads.1 = (bf16[1024,128]{1,0:T(8,128)(2,1)S(1)}, f32[1024,128]{1,0:T(8,128)S(1)}, f32[1024,128]{1,0:T(8,128)S(1)}, bf16[1024,512]{1,0:T(8,128)(2,1)}) custom-call(bf16[1024,512]{1,0:T(8,128)(2,1)S(1)} %copy-done, bf16[1024,512]{1,0:T(8,128)(2,1)S(1)} %get-tuple-element.52.k, bf16[1024,512]{1,0:T(8,128)(2,1)S(1)} %get-tuple-element.53.v, ...), custom_call_target="tpu_custom_call" | custom-call | flops 436207616 | bytes 12521472 | tf_op jit(solution)/shard_map/second_grads/pallas_call | solution.py:60
  40.8 1.0 %collective-permute-done.13.refs_4_ = f32[128,128]{1,0:T(8,128)S(1)} collective-permute-done((f32[128,128]{1,0:T(8,128)S(1)}, f32[128,128]{1,0:T(8,128)S(1)}, u32[]{:S(2)}, u32[]{:S(2)}) %collective-permute-start.13) | collective-permute-done | bytes 65568 | tf_op jit(solution)/shard_map/ppermute | solution.py:100
  41.9 0.1 finish.3
  41.9 0.4 collective-permute-start.14
  42.3 1.4 %collective-permute-start.15 = (f32[128,128]{1,0:T(8,128)S(1)}, f32[128,128]{1,0:T(8,128)S(1)}, u32[]{:S(2)}, u32[]{:S(2)}) collective-permute-start(f32[128,128]{1,0:T(8,128)S(1)} %get-tuple-element.96), channel_id=1, source_target_pairs={{0,4},{1,5},{2,6},{3,7},{4,0},{5,1},{6,2},{7,3},{8,12},{9,13},{10,... | collective-permute-start | bytes 196616 | tf_op jit(solution)/shard_map/ppermute | solution.py:100
  43.7 1.8 %collective-permute-start.16 = (f32[128,128]{1,0:T(8,128)S(1)}, f32[128,128]{1,0:T(8,128)S(1)}, u32[]{:S(2)}, u32[]{:S(2)}) collective-permute-start(f32[128,128]{1,0:T(8,128)S(1)} %get-tuple-element.97), channel_id=1, source_target_pairs={{0,8},{1,9},{2,10},{3,11},{4,12},{5,13},{6,14},{7,15},{8,0},{9,1},... | collective-permute-start | bytes 196616 | tf_op jit(solution)/shard_map/ppermute | solution.py:100
  45.5 1.8 %third_grads.1 = (f32[1024,128]{1,0:T(8,128)S(1)}, f32[1024,128]{1,0:T(8,128)S(1)}, bf16[1024,512]{1,0:T(8,128)(2,1)}) custom-call(bf16[1024,512]{1,0:T(8,128)(2,1)S(1)} %copy-done, bf16[1024,512]{1,0:T(8,128)(2,1)S(1)} %get-tuple-element.52.k, bf16[1024,512]{1,0:T(8,128)(2,1)S(1)} %get-tuple-element.53.v, bf16[1024,512]{1,0:T(8,128)(2,1)S(1)} %get-tuple-element.72.gm, ...), custom_call_target="tpu_custom_call" | custom-call | flops 436207616 | bytes 10944512 | tf_op jit(solution)/shard_map/third_grads/pallas_call | solution.py:60
  47.2 0.0 collective-permute-done.14.refs_9_
  47.3 0.0 collective-permute-done.15.refs_10_
  47.3 0.7 %collective-permute-done.16.refs_11_ = f32[128,128]{1,0:T(8,128)S(1)} collective-permute-done((f32[128,128]{1,0:T(8,128)S(1)}, f32[128,128]{1,0:T(8,128)S(1)}, u32[]{:S(2)}, u32[]{:S(2)}) %collective-permute-start.16) | collective-permute-done | bytes 65568 | tf_op jit(solution)/shard_map/ppermute | solution.py:100
  47.9 1.6 %last.1 = (bf16[1024,512]{1,0:T(8,128)(2,1)}, bf16[1024,512]{1,0:T(8,128)(2,1)}) custom-call(bf16[1024,512]{1,0:T(8,128)(2,1)S(1)} %get-tuple-element.52.k, bf16[1024,512]{1,0:T(8,128)(2,1)S(1)} %get-tuple-element.53.v, f32[1024,128]{1,0:T(8,128)S(1)} %get-tuple-element.89.refs_0_, f32[1024,128]{1,0:T(8,128)S(1)} %get-tuple-element.81.refs_4_.refs_1_, ...), custom_call_target="tpu_custom_call" | custom-call | flops 268435456 | bytes 8650752 | tf_op jit(solution)/shard_map/last/pallas_call | solution.py:60
  (2 shorter events, 0.0 us)
Async XLA Ops:
  0.6 6.6 %copy-start = (bf16[1024,512]{1,0:T(8,128)(2,1)S(1)}, bf16[1024,512]{1,0:T(8,128)(2,1)}, u32[]{:S(2)}) copy-start(bf16[1024,512]{1,0:T(8,128)(2,1)} %q.13) | copy-start | bytes 3145732
  2.6 6.6 %collective-permute-start = (f32[128,128]{1,0:T(8,128)S(1)}, f32[128,128]{1,0:T(8,128)S(1)}, u32[]{:S(2)}, u32[]{:S(2)}) collective-permute-start(f32[128,128]{1,0:T(8,128)S(1)} %get-tuple-element.56), channel_id=1, source_target_pairs={{0,12},{1,13},{2,14},{3,15},{4,8},{5,9},{6,10},{7,11},{8,4},{9,5},... | collective-permute-start | bytes 196616 | tf_op jit(solution)/shard_map/ppermute | solution.py:100
  6.6 4.3 %collective-permute-start.1 = (f32[128,128]{1,0:T(8,128)S(1)}, f32[128,128]{1,0:T(8,128)S(1)}, u32[]{:S(2)}, u32[]{:S(2)}) collective-permute-start(f32[128,128]{1,0:T(8,128)S(1)} %get-tuple-element.57), channel_id=1, source_target_pairs={{0,8},{1,9},{2,10},{3,11},{4,12},{5,13},{6,14},{7,15},{8,0},{9,1},... | collective-permute-start | bytes 196616 | tf_op jit(solution)/shard_map/ppermute | solution.py:100
  7.1 4.3 %collective-permute-start.2 = (f32[128,128]{1,0:T(8,128)S(1)}, f32[128,128]{1,0:T(8,128)S(1)}, u32[]{:S(2)}, u32[]{:S(2)}) collective-permute-start(f32[128,128]{1,0:T(8,128)S(1)} %get-tuple-element.58), channel_id=1, source_target_pairs={{0,4},{1,5},{2,6},{3,7},{4,0},{5,1},{6,2},{7,3},{8,12},{9,13},{10,... | collective-permute-start | bytes 196616 | tf_op jit(solution)/shard_map/ppermute | solution.py:100
  11.3 5.2 %collective-permute-start.3 = (f32[128,128]{1,0:T(8,128)S(1)}, f32[128,128]{1,0:T(8,128)S(1)}, u32[]{:S(2)}, u32[]{:S(2)}) collective-permute-start(f32[128,128]{1,0:T(8,128)S(1)} %quad_sum.2.token), channel_id=1, source_target_pairs={{0,16},{1,17},{2,18},{3,19},{4,20},{5,21},{6,22},{7,23},{8,24},{9,... | collective-permute-start | bytes 196616 | tf_op jit(solution)/shard_map/ppermute | solution.py:100
  14.7 7.2 %copy-start.1 = (bf16[1024,512]{1,0:T(8,128)(2,1)S(1)}, bf16[1024,512]{1,0:T(8,128)(2,1)}, u32[]{:S(2)}) copy-start(bf16[1024,512]{1,0:T(8,128)(2,1)} %g.5) | copy-start | bytes 3145732
  16.6 5.2 %collective-permute-start.4 = (f32[128,128]{1,0:T(8,128)S(1)}, f32[128,128]{1,0:T(8,128)S(1)}, u32[]{:S(2)}, u32[]{:S(2)}) collective-permute-start(f32[128,128]{1,0:T(8,128)S(1)} %get-tuple-element.61), channel_id=1, source_target_pairs={{0,12},{1,13},{2,14},{3,15},{4,8},{5,9},{6,10},{7,11},{8,4},{9,5},... | collective-permute-start | bytes 196616 | tf_op jit(solution)/shard_map/ppermute | solution.py:100
  18.3 4.3 %collective-permute-start.5 = (f32[128,128]{1,0:T(8,128)S(1)}, f32[128,128]{1,0:T(8,128)S(1)}, u32[]{:S(2)}, u32[]{:S(2)}) collective-permute-start(f32[128,128]{1,0:T(8,128)S(1)} %get-tuple-element.63), channel_id=1, source_target_pairs={{0,8},{1,9},{2,10},{3,11},{4,12},{5,13},{6,14},{7,15},{8,0},{9,1},... | collective-permute-start | bytes 196616 | tf_op jit(solution)/shard_map/ppermute | solution.py:100
  18.6 4.3 %collective-permute-start.6 = (f32[128,128]{1,0:T(8,128)S(1)}, f32[128,128]{1,0:T(8,128)S(1)}, u32[]{:S(2)}, u32[]{:S(2)}) collective-permute-start(f32[128,128]{1,0:T(8,128)S(1)} %get-tuple-element.64), channel_id=1, source_target_pairs={{0,4},{1,5},{2,6},{3,7},{4,0},{5,1},{6,2},{7,3},{8,12},{9,13},{10,... | collective-permute-start | bytes 196616 | tf_op jit(solution)/shard_map/ppermute | solution.py:100
  23.4 3.1 %collective-permute-start.7 = (f32[16,128]{1,0:T(8,128)S(1)}, f32[16,128]{1,0:T(8,128)S(1)}, u32[]{:S(2)}, u32[]{:S(2)}) collective-permute-start(f32[16,128]{1,0:T(8,128)S(1)} %get-tuple-element.69), channel_id=1, source_target_pairs={{0,3},{1,2},{2,1},{3,0},{4,7},{5,6},{6,5},{7,4},{8,11},{9,10},{10,... | collective-permute-start | bytes 24584 | tf_op jit(solution)/shard_map/ppermute | solution.py:419
  23.5 3.7 %collective-permute-start.8 = (f32[16,128]{1,0:T(8,128)S(1)}, f32[16,128]{1,0:T(8,128)S(1)}, u32[]{:S(2)}, u32[]{:S(2)}) collective-permute-start(f32[16,128]{1,0:T(8,128)S(1)} %get-tuple-element.70), channel_id=1, source_target_pairs={{0,2},{1,3},{2,0},{3,1},{4,6},{5,7},{6,4},{7,5},{8,10},{9,11},{10,... | collective-permute-start | bytes 24584 | tf_op jit(solution)/shard_map/ppermute | solution.py:419
  25.3 1.9 %collective-permute-start.9 = (f32[16,128]{1,0:T(8,128)S(1)}, f32[16,128]{1,0:T(8,128)S(1)}, u32[]{:S(2)}, u32[]{:S(2)}) collective-permute-start(f32[16,128]{1,0:T(8,128)S(1)} %get-tuple-element.71), channel_id=1, source_target_pairs={{0,1},{1,0},{2,3},{3,2},{4,5},{5,4},{6,7},{7,6},{8,9},{9,8},{10,11... | collective-permute-start | bytes 24584 | tf_op jit(solution)/shard_map/ppermute | solution.py:419
  28.1 5.7 %collective-permute-start.10 = (f32[128,128]{1,0:T(8,128)S(1)}, f32[128,128]{1,0:T(8,128)S(1)}, u32[]{:S(2)}, u32[]{:S(2)}) collective-permute-start(f32[128,128]{1,0:T(8,128)S(1)} %get-tuple-element.78), channel_id=1, source_target_pairs={{0,12},{1,13},{2,14},{3,15},{4,8},{5,9},{6,10},{7,11},{8,4},{9,5},... | collective-permute-start | bytes 196616 | tf_op jit(solution)/shard_map/ppermute | solution.py:100
  30.7 4.3 %collective-permute-start.11 = (f32[128,128]{1,0:T(8,128)S(1)}, f32[128,128]{1,0:T(8,128)S(1)}, u32[]{:S(2)}, u32[]{:S(2)}) collective-permute-start(f32[128,128]{1,0:T(8,128)S(1)} %get-tuple-element.79), channel_id=1, source_target_pairs={{0,4},{1,5},{2,6},{3,7},{4,0},{5,1},{6,2},{7,3},{8,12},{9,13},{10,... | collective-permute-start | bytes 196616 | tf_op jit(solution)/shard_map/ppermute | solution.py:100
  31.2 4.3 %collective-permute-start.12 = (f32[128,128]{1,0:T(8,128)S(1)}, f32[128,128]{1,0:T(8,128)S(1)}, u32[]{:S(2)}, u32[]{:S(2)}) collective-permute-start(f32[128,128]{1,0:T(8,128)S(1)} %get-tuple-element.80), channel_id=1, source_target_pairs={{0,8},{1,9},{2,10},{3,11},{4,12},{5,13},{6,14},{7,15},{8,0},{9,1},... | collective-permute-start | bytes 196616 | tf_op jit(solution)/shard_map/ppermute | solution.py:100
  35.5 6.3 %collective-permute-start.13 = (f32[128,128]{1,0:T(8,128)S(1)}, f32[128,128]{1,0:T(8,128)S(1)}, u32[]{:S(2)}, u32[]{:S(2)}) collective-permute-start(f32[128,128]{1,0:T(8,128)S(1)} %quad_sum.3.refs_3_), channel_id=1, source_target_pairs={{0,16},{1,17},{2,18},{3,19},{4,20},{5,21},{6,22},{7,23},{8,24},{9,... | collective-permute-start | bytes 196616 | tf_op jit(solution)/shard_map/ppermute | solution.py:100
  41.9 5.3 %collective-permute-start.14 = (f32[128,128]{1,0:T(8,128)S(1)}, f32[128,128]{1,0:T(8,128)S(1)}, u32[]{:S(2)}, u32[]{:S(2)}) collective-permute-start(f32[128,128]{1,0:T(8,128)S(1)} %get-tuple-element.95), channel_id=1, source_target_pairs={{0,12},{1,13},{2,14},{3,15},{4,8},{5,9},{6,10},{7,11},{8,4},{9,5},... | collective-permute-start | bytes 196616 | tf_op jit(solution)/shard_map/ppermute | solution.py:100
  42.3 5.0 %collective-permute-start.15 = (f32[128,128]{1,0:T(8,128)S(1)}, f32[128,128]{1,0:T(8,128)S(1)}, u32[]{:S(2)}, u32[]{:S(2)}) collective-permute-start(f32[128,128]{1,0:T(8,128)S(1)} %get-tuple-element.96), channel_id=1, source_target_pairs={{0,4},{1,5},{2,6},{3,7},{4,0},{5,1},{6,2},{7,3},{8,12},{9,13},{10,... | collective-permute-start | bytes 196616 | tf_op jit(solution)/shard_map/ppermute | solution.py:100
  43.7 4.3 %collective-permute-start.16 = (f32[128,128]{1,0:T(8,128)S(1)}, f32[128,128]{1,0:T(8,128)S(1)}, u32[]{:S(2)}, u32[]{:S(2)}) collective-permute-start(f32[128,128]{1,0:T(8,128)S(1)} %get-tuple-element.97), channel_id=1, source_target_pairs={{0,8},{1,9},{2,10},{3,11},{4,12},{5,13},{6,14},{7,15},{8,0},{9,1},... | collective-permute-start | bytes 196616 | tf_op jit(solution)/shard_map/ppermute | solution.py:100

commit v13 on v11

--- a/solution.py
+++ b/solution.py
@@ -238,8 +238,10 @@
 def mixed_kernel(is_own, intra, q, g, *refs):
     pieces, refs = refs[:2], refs[2:]
     before, refs = ([], refs) if is_own else (refs[:2], refs[2:])
-    mixed, prefix, *stats, scratch = refs
-    load_pieces(pieces, ORDERS[False][1], scratch, 0 if is_own else 2)
+    mixed, prefix, *stats = refs
+    in_order = number_at(ORDERS[False][1], 0 if is_own else 2) // 2 == 0
+    one, two = (piece[...].astype(BF16) for piece in pieces)
+    states = [jnp.where(in_order, one, two), jnp.where(in_order, two, one)]
     blocks = q.shape[0] // HEAD_DIM
 
     def pair(p):
@@ -247,7 +249,7 @@
             square = cross = None
             for j in range(2):
                 part, whole = head_slice(j), head_slice(2 * p + j)
-                m = intra[at, whole] + dot(q[at, whole], scratch[whole, :], 1, 0)
+                m = intra[at, whole] + dot(q[at, whole], states[j], 1, 0)
                 mixed[at, part] = m
                 s, c = m * m, m * g[at, whole].astype(F32)
                 square = s if square is None else square + s
@@ -259,8 +261,8 @@
                     if before:
                         sums = sums + before[0][i : i + 1, :]
                     stats[0][i : i + 1, :] = sums
-        part = slice(p * PAIR, (p + 1) * PAIR)
-        prefix[part, :] = scratch[part, :]
+        for j in range(2):
+            prefix[head_slice(2 * p + j), :] = states[j]
         if before:
             part = slice((1 - p) * PAIR, (2 - p) * PAIR)
             prefix[part, :] = before[1][part, :]
@@ -457,7 +459,6 @@
             [intra, queries, grad_out, *pieces, *before],
             2 * head_flops,
             "mixed",
-            scratch=[pltpu.VMEM((cols, HEAD_DIM), BF16)],
         )
 
     mixed, prefix, stats = mix(True, prefixes[:2], 1)

time: 49.7 us -> 49.7 us (level)
  no operation moved by 1% of the time
where the time goes in v13:
time: 49.7 us; the launch traced here: 49.6 us
  starting transfers between devices  23.2 us (47%)
  Pallas kernels  14.3 us (29%)
  waiting for transfers between devices  11.3 us (23%)
  between operations  0.76 us (2%)
    ppermute x14, starting transfers between devices, exchange(): return lax.ppermute(value, ('seq', 'head'), pairs)  21.3 us
    pallas_call x13, Pallas kernels, call(): return list(kernel(*args))  14.3 us
    ppermute x14, waiting for transfers between devices, exchange(): return lax.ppermute(value, ('seq', 'head'), pairs)  9.42 us
    ppermute x3, starting transfers between devices, all_parts(): parts.append(lax.ppermute(values[by], axis, pairs))  1.92 us
    ppermute x3, waiting for transfers between devices, all_parts(): parts.append(lax.ppermute(values[by], axis, pairs))  1.87 us
  transfers between devices with their start and end apart: 17, of which 12 were waited for; matrix products, arithmetic and copies ran while one was open for 0% of the time, Pallas kernels for 19%

profile of v13, /device:TPU:0, one launch (start us, length us, event | category | flops | bytes accessed | tf_op | source)
XLA Modules:
  0.0 49.6 jit_solution(385910413644468381)
XLA Ops:
  0.6 0.0 copy-start
  0.6 1.9 %local_state.1 = (f32[128,128]{1,0:T(8,128)S(1)}, f32[128,128]{1,0:T(8,128)S(1)}, f32[128,128]{1,0:T(8,128)S(1)}, f32[128,128]{1,0:T(8,128)S(1)}, bf16[1024,512]...) custom-call(bf16[1024,512]{1,0:T(8,128)(2,1)} %k_hbm.1, bf16[1024,512]{1,0:T(8,128)(2,1)} %v_hbm.1), custom_call_target="tpu_custom_call" | custom-call | flops 134217728 | bytes 4456448 | tf_op jit(solution)/shard_map/local_state/pallas_call | solution.py:60
  2.6 4.0 %collective-permute-start = (f32[128,128]{1,0:T(8,128)S(1)}, f32[128,128]{1,0:T(8,128)S(1)}, u32[]{:S(2)}, u32[]{:S(2)}) collective-permute-start(f32[128,128]{1,0:T(8,128)S(1)} %get-tuple-element.56), channel_id=1, source_target_pairs={{0,12},{1,13},{2,14},{3,15},{4,8},{5,9},{6,10},{7,11},{8,4},{9,5},... | collective-permute-start | bytes 196616 | tf_op jit(solution)/shard_map/ppermute | solution.py:100
  6.6 0.4 collective-permute-start.1
  7.1 0.2 collective-permute-start.2
  7.3 0.0 copy-done
  7.3 0.0 copy-start.1
  7.3 2.0 %intra.1 = (f32[1024,512]{1,0:T(8,128)S(1)}, f32[1536,128]{1,0:T(8,128)S(1)}, bf16[512,1024]{1,0:T(8,128)(2,1)S(1)}) custom-call(bf16[1024,512]{1,0:T(8,128)(2,1)S(1)} %copy-done, bf16[1024,512]{1,0:T(8,128)(2,1)S(1)} %get-tuple-element.52.k, bf16[1024,512]{1,0:T(8,128)(2,1)S(1)} %get-tuple-element.53.v), custom_call_target="tpu_custom_call" | custom-call | flops 805306368 | bytes 7077888 | tf_op jit(solution)/shard_map/intra/pallas_call | solution.py:60
  9.2 0.0 collective-permute-done.refs_1_
  9.2 1.7 %collective-permute-done.1.refs_2_ = f32[128,128]{1,0:T(8,128)S(1)} collective-permute-done((f32[128,128]{1,0:T(8,128)S(1)}, f32[128,128]{1,0:T(8,128)S(1)}, u32[]{:S(2)}, u32[]{:S(2)}) %collective-permute-start.1) | collective-permute-done | bytes 65568 | tf_op jit(solution)/shard_map/ppermute | solution.py:100
  10.9 0.4 collective-permute-done.2.refs_3_
  11.3 2.7 %collective-permute-start.3 = (f32[128,128]{1,0:T(8,128)S(1)}, f32[128,128]{1,0:T(8,128)S(1)}, u32[]{:S(2)}, u32[]{:S(2)}) collective-permute-start(f32[128,128]{1,0:T(8,128)S(1)} %quad_sum.2), channel_id=1, source_target_pairs={{0,16},{1,17},{2,18},{3,19},{4,20},{5,21},{6,22},{7,23},{8,24},{9,... | collective-permute-start | bytes 196616 | tf_op jit(solution)/shard_map/ppermute | solution.py:100
  14.0 2.6 %collective-permute-done.3.refs_4_ = f32[128,128]{1,0:T(8,128)S(1)} collective-permute-done((f32[128,128]{1,0:T(8,128)S(1)}, f32[128,128]{1,0:T(8,128)S(1)}, u32[]{:S(2)}, u32[]{:S(2)}) %collective-permute-start.3) | collective-permute-done | bytes 65568 | tf_op jit(solution)/shard_map/ppermute | solution.py:100
  16.6 0.1 finish.2
  16.6 1.6 %collective-permute-start.4 = (f32[128,128]{1,0:T(8,128)S(1)}, f32[128,128]{1,0:T(8,128)S(1)}, u32[]{:S(2)}, u32[]{:S(2)}) collective-permute-start(f32[128,128]{1,0:T(8,128)S(1)} %get-tuple-element.61), channel_id=1, source_target_pairs={{0,12},{1,13},{2,14},{3,15},{4,8},{5,9},{6,10},{7,11},{8,4},{9,5},... | collective-permute-start | bytes 196616 | tf_op jit(solution)/shard_map/ppermute | solution.py:100
  18.3 0.3 collective-permute-start.5
  18.6 1.6 %collective-permute-start.6 = (f32[128,128]{1,0:T(8,128)S(1)}, f32[128,128]{1,0:T(8,128)S(1)}, u32[]{:S(2)}, u32[]{:S(2)}) collective-permute-start(f32[128,128]{1,0:T(8,128)S(1)} %get-tuple-element.64), channel_id=1, source_target_pairs={{0,4},{1,5},{2,6},{3,7},{4,0},{5,1},{6,2},{7,3},{8,12},{9,13},{10,... | collective-permute-start | bytes 196616 | tf_op jit(solution)/shard_map/ppermute | solution.py:100
  20.2 1.7 %collective-permute-done.4.refs_1_ = f32[128,128]{1,0:T(8,128)S(1)} collective-permute-done((f32[128,128]{1,0:T(8,128)S(1)}, f32[128,128]{1,0:T(8,128)S(1)}, u32[]{:S(2)}, u32[]{:S(2)}) %collective-permute-start.4) | collective-permute-done | bytes 65568 | tf_op jit(solution)/shard_map/ppermute | solution.py:100
  21.9 0.0 copy-done.1
  21.9 0.5 %mixed.2 = (f32[1024,256]{1,0:T(8,128)S(1)}, bf16[512,128]{1,0:T(8,128)(2,1)S(1)}, f32[16,128]{1,0:T(8,128)S(1)}) custom-call(f32[1024,512]{1,0:T(8,128)S(1)} %get-tuple-element.54.intra, bf16[1024,512]{1,0:T(8,128)(2,1)S(1)} %copy-done, bf16[1024,512]{1,0:T(8,128)(2,1)S(1)} %copy-done.1, f32[128,128]{1,0:T(8,128)S(1)} %get-tuple-element.60.refs_0_, ...), custom_call_target="tpu_custom_call" | custom-call | flops 67108864 | bytes 5513216 | tf_op jit(solution)/shard_map/mixed/pallas_call | solution.py:60
  22.4 0.1 collective-permute-done.5.refs_0_
  22.5 0.3 collective-permute-done.6.refs_1_
  22.9 0.5 %mixed.3 = (f32[1024,256]{1,0:T(8,128)S(1)}, bf16[512,128]{1,0:T(8,128)(2,1)S(1)}, f32[16,128]{1,0:T(8,128)S(1)}, f32[16,128]{1,0:T(8,128)S(1)}, f32[16,128]{1,0:T(8,128)S(1)}, /*index=5*/f32[16,128]{1,0:T(8,128)S(1)}) custom-call(f32[1024,512]{1,0:T(8,128)S(1)} %get-tuple-element.54.intra, bf16[1024,512]{1,0:T(8,128)(2,1)S(1)} %copy-done, ...), custom_call_target="tpu_custom_call" | custom-call | flops 67108864 | bytes 5677056 | tf_op jit(solution)/shard_map/mixed/pallas_call | solution.py:60
  23.4 0.1 collective-permute-start.7
  23.5 1.8 %collective-permute-start.8 = (f32[16,128]{1,0:T(8,128)S(1)}, f32[16,128]{1,0:T(8,128)S(1)}, u32[]{:S(2)}, u32[]{:S(2)}) collective-permute-start(f32[16,128]{1,0:T(8,128)S(1)} %get-tuple-element.70), channel_id=1, source_target_pairs={{0,2},{1,3},{2,0},{3,1},{4,6},{5,7},{6,4},{7,5},{8,10},{9,11},{10,... | collective-permute-start | bytes 24584 | tf_op jit(solution)/shard_map/ppermute | solution.py:409
  25.3 0.1 collective-permute-start.9
  25.3 1.2 %collective-permute-done.7.refs_1_ = f32[16,128]{1,0:T(8,128)S(1)} collective-permute-done((f32[16,128]{1,0:T(8,128)S(1)}, f32[16,128]{1,0:T(8,128)S(1)}, u32[]{:S(2)}, u32[]{:S(2)}) %collective-permute-start.7) | collective-permute-done | bytes 8224 | tf_op jit(solution)/shard_map/ppermute | solution.py:409
  26.6 0.7 %collective-permute-done.8.refs_2_ = f32[16,128]{1,0:T(8,128)S(1)} collective-permute-done((f32[16,128]{1,0:T(8,128)S(1)}, f32[16,128]{1,0:T(8,128)S(1)}, u32[]{:S(2)}, u32[]{:S(2)}) %collective-permute-start.8) | collective-permute-done | bytes 8224 | tf_op jit(solution)/shard_map/ppermute | solution.py:409
  27.2 0.0 collective-permute-done.9.refs_3_
  27.2 0.8 %norm.1 = (bf16[1024,512]{1,0:T(8,128)(2,1)S(1)}, f32[8,128]{1,0:T(8,128)S(1)}, f32[1536,128]{1,0:T(8,128)S(1)}, f32[128,128]{1,0:T(8,128)S(1)}, f32[128,128]{1,...) custom-call(f32[1024,256]{1,0:T(8,128)S(1)} %get-tuple-element.62.mixed, ...), custom_call_target="tpu_custom_call" | custom-call | flops 134217728 | bytes 6328320 | tf_op jit(solution)/shard_map/norm/pallas_call | solution.py:60
  28.1 2.7 %collective-permute-start.10 = (f32[128,128]{1,0:T(8,128)S(1)}, f32[128,128]{1,0:T(8,128)S(1)}, u32[]{:S(2)}, u32[]{:S(2)}) collective-permute-start(f32[128,128]{1,0:T(8,128)S(1)} %get-tuple-element.78), channel_id=1, source_target_pairs={{0,12},{1,13},{2,14},{3,15},{4,8},{5,9},{6,10},{7,11},{8,4},{9,5},... | collective-permute-start | bytes 196616 | tf_op jit(solution)/shard_map/ppermute | solution.py:100
  30.7 0.5 %collective-permute-start.11 = (f32[128,128]{1,0:T(8,128)S(1)}, f32[128,128]{1,0:T(8,128)S(1)}, u32[]{:S(2)}, u32[]{:S(2)}) collective-permute-start(f32[128,128]{1,0:T(8,128)S(1)} %get-tuple-element.79), channel_id=1, source_target_pairs={{0,4},{1,5},{2,6},{3,7},{4,0},{5,1},{6,2},{7,3},{8,12},{9,13},{10,... | collective-permute-start | bytes 196616 | tf_op jit(solution)/shard_map/ppermute | solution.py:100
  31.3 0.4 collective-permute-start.12
  31.6 2.5 %first_grads.1 = (bf16[1024,128]{1,0:T(8,128)(2,1)S(1)}, bf16[1024,128]{1,0:T(8,128)(2,1)S(1)}, f32[1024,128]{1,0:T(8,128)S(1)}, f32[1024,128]{1,0:T(8,128)S(1)}...) custom-call(bf16[1024,512]{1,0:T(8,128)(2,1)S(1)} %copy-done, bf16[1024,512]{1,0:T(8,128)(2,1)S(1)} %get-tuple-element.52.k, ...), custom_call_target="tpu_custom_call" | custom-call | flops 1006632960 | bytes 8519680 | tf_op jit(solution)/shard_map/first_grads/pallas_call | solution.py:60
  34.1 0.0 collective-permute-done.10.refs_1_
  34.1 0.9 %collective-permute-done.11.refs_2_ = f32[128,128]{1,0:T(8,128)S(1)} collective-permute-done((f32[128,128]{1,0:T(8,128)S(1)}, f32[128,128]{1,0:T(8,128)S(1)}, u32[]{:S(2)}, u32[]{:S(2)}) %collective-permute-start.11) | collective-permute-done | bytes 65568 | tf_op jit(solution)/shard_map/ppermute | solution.py:100
  35.0 0.5 %collective-permute-done.12.refs_3_ = f32[128,128]{1,0:T(8,128)S(1)} collective-permute-done((f32[128,128]{1,0:T(8,128)S(1)}, f32[128,128]{1,0:T(8,128)S(1)}, u32[]{:S(2)}, u32[]{:S(2)}) %collective-permute-start.12) | collective-permute-done | bytes 65568 | tf_op jit(solution)/shard_map/ppermute | solution.py:100
  35.6 3.3 %collective-permute-start.13 = (f32[128,128]{1,0:T(8,128)S(1)}, f32[128,128]{1,0:T(8,128)S(1)}, u32[]{:S(2)}, u32[]{:S(2)}) collective-permute-start(f32[128,128]{1,0:T(8,128)S(1)} %quad_sum.3.refs_0_), channel_id=1, source_target_pairs={{0,16},{1,17},{2,18},{3,19},{4,20},{5,21},{6,22},{7,23},{8,24},{9,... | collective-permute-start | bytes 196616 | tf_op jit(solution)/shard_map/ppermute | solution.py:100
  38.9 2.2 %second_grads.1 = (bf16[1024,128]{1,0:T(8,128)(2,1)S(1)}, f32[1024,128]{1,0:T(8,128)S(1)}, f32[1024,128]{1,0:T(8,128)S(1)}, bf16[1024,512]{1,0:T(8,128)(2,1)}) custom-call(bf16[1024,512]{1,0:T(8,128)(2,1)S(1)} %copy-done, bf16[1024,512]{1,0:T(8,128)(2,1)S(1)} %get-tuple-element.52.k, bf16[1024,512]{1,0:T(8,128)(2,1)S(1)} %get-tuple-element.53.v, ...), custom_call_target="tpu_custom_call" | custom-call | flops 503316480 | bytes 10424320 | tf_op jit(solution)/shard_map/second_grads/pallas_call | solution.py:60
  41.1 0.8 %collective-permute-done.13.refs_4_ = f32[128,128]{1,0:T(8,128)S(1)} collective-permute-done((f32[128,128]{1,0:T(8,128)S(1)}, f32[128,128]{1,0:T(8,128)S(1)}, u32[]{:S(2)}, u32[]{:S(2)}) %collective-permute-start.13) | collective-permute-done | bytes 65568 | tf_op jit(solution)/shard_map/ppermute | solution.py:100
  41.9 0.1 finish.3
  41.9 0.5 collective-permute-start.14
  42.4 1.3 %collective-permute-start.15 = (f32[128,128]{1,0:T(8,128)S(1)}, f32[128,128]{1,0:T(8,128)S(1)}, u32[]{:S(2)}, u32[]{:S(2)}) collective-permute-start(f32[128,128]{1,0:T(8,128)S(1)} %get-tuple-element.96), channel_id=1, source_target_pairs={{0,4},{1,5},{2,6},{3,7},{4,0},{5,1},{6,2},{7,3},{8,12},{9,13},{10,... | collective-permute-start | bytes 196616 | tf_op jit(solution)/shard_map/ppermute | solution.py:100
  43.7 1.8 %collective-permute-start.16 = (f32[128,128]{1,0:T(8,128)S(1)}, f32[128,128]{1,0:T(8,128)S(1)}, u32[]{:S(2)}, u32[]{:S(2)}) collective-permute-start(f32[128,128]{1,0:T(8,128)S(1)} %get-tuple-element.97), channel_id=1, source_target_pairs={{0,8},{1,9},{2,10},{3,11},{4,12},{5,13},{6,14},{7,15},{8,0},{9,1},... | collective-permute-start | bytes 196616 | tf_op jit(solution)/shard_map/ppermute | solution.py:100
  45.5 2.0 %third_grads.1 = (f32[1024,128]{1,0:T(8,128)S(1)}, f32[1024,128]{1,0:T(8,128)S(1)}, bf16[1024,512]{1,0:T(8,128)(2,1)}) custom-call(bf16[1024,512]{1,0:T(8,128)(2,1)S(1)} %copy-done, bf16[1024,512]{1,0:T(8,128)(2,1)S(1)} %get-tuple-element.52.k, bf16[1024,512]{1,0:T(8,128)(2,1)S(1)} %get-tuple-element.53.v, bf16[1024,512]{1,0:T(8,128)(2,1)S(1)} %get-tuple-element.72.gm, ...), custom_call_target="tpu_custom_call" | custom-call | flops 503316480 | bytes 8847360 | tf_op jit(solution)/shard_map/third_grads/pallas_call | solution.py:60
  47.5 0.0 collective-permute-done.14.refs_9_
  47.5 0.0 collective-permute-done.15.refs_10_
  47.5 0.4 collective-permute-done.16.refs_11_
  47.9 1.6 %last.1 = (bf16[1024,512]{1,0:T(8,128)(2,1)}, bf16[1024,512]{1,0:T(8,128)(2,1)}) custom-call(bf16[1024,512]{1,0:T(8,128)(2,1)S(1)} %get-tuple-element.52.k, bf16[1024,512]{1,0:T(8,128)(2,1)S(1)} %get-tuple-element.53.v, f32[1024,128]{1,0:T(8,128)S(1)} %get-tuple-element.89.refs_0_, f32[1024,128]{1,0:T(8,128)S(1)} %get-tuple-element.81.refs_4_.refs_1_, ...), custom_call_target="tpu_custom_call" | custom-call | flops 268435456 | bytes 8650752 | tf_op jit(solution)/shard_map/last/pallas_call | solution.py:60
  (2 shorter events, 0.0 us)
Async XLA Ops:
  0.6 6.6 %copy-start = (bf16[1024,512]{1,0:T(8,128)(2,1)S(1)}, bf16[1024,512]{1,0:T(8,128)(2,1)}, u32[]{:S(2)}) copy-start(bf16[1024,512]{1,0:T(8,128)(2,1)} %q.11) | copy-start | bytes 3145732
  2.6 6.6 %collective-permute-start = (f32[128,128]{1,0:T(8,128)S(1)}, f32[128,128]{1,0:T(8,128)S(1)}, u32[]{:S(2)}, u32[]{:S(2)}) collective-permute-start(f32[128,128]{1,0:T(8,128)S(1)} %get-tuple-element.56), channel_id=1, source_target_pairs={{0,12},{1,13},{2,14},{3,15},{4,8},{5,9},{6,10},{7,11},{8,4},{9,5},... | collective-permute-start | bytes 196616 | tf_op jit(solution)/shard_map/ppermute | solution.py:100
  6.6 4.3 %collective-permute-start.1 = (f32[128,128]{1,0:T(8,128)S(1)}, f32[128,128]{1,0:T(8,128)S(1)}, u32[]{:S(2)}, u32[]{:S(2)}) collective-permute-start(f32[128,128]{1,0:T(8,128)S(1)} %get-tuple-element.57), channel_id=1, source_target_pairs={{0,8},{1,9},{2,10},{3,11},{4,12},{5,13},{6,14},{7,15},{8,0},{9,1},... | collective-permute-start | bytes 196616 | tf_op jit(solution)/shard_map/ppermute | solution.py:100
  7.1 4.3 %collective-permute-start.2 = (f32[128,128]{1,0:T(8,128)S(1)}, f32[128,128]{1,0:T(8,128)S(1)}, u32[]{:S(2)}, u32[]{:S(2)}) collective-permute-start(f32[128,128]{1,0:T(8,128)S(1)} %get-tuple-element.58), channel_id=1, source_target_pairs={{0,4},{1,5},{2,6},{3,7},{4,0},{5,1},{6,2},{7,3},{8,12},{9,13},{10,... | collective-permute-start | bytes 196616 | tf_op jit(solution)/shard_map/ppermute | solution.py:100
  7.3 14.6 %copy-start.1 = (bf16[1024,512]{1,0:T(8,128)(2,1)S(1)}, bf16[1024,512]{1,0:T(8,128)(2,1)}, u32[]{:S(2)}) copy-start(bf16[1024,512]{1,0:T(8,128)(2,1)} %g.5) | copy-start | bytes 3145732
  11.3 5.2 %collective-permute-start.3 = (f32[128,128]{1,0:T(8,128)S(1)}, f32[128,128]{1,0:T(8,128)S(1)}, u32[]{:S(2)}, u32[]{:S(2)}) collective-permute-start(f32[128,128]{1,0:T(8,128)S(1)} %quad_sum.2), channel_id=1, source_target_pairs={{0,16},{1,17},{2,18},{3,19},{4,20},{5,21},{6,22},{7,23},{8,24},{9,... | collective-permute-start | bytes 196616 | tf_op jit(solution)/shard_map/ppermute | solution.py:100
  16.6 5.2 %collective-permute-start.4 = (f32[128,128]{1,0:T(8,128)S(1)}, f32[128,128]{1,0:T(8,128)S(1)}, u32[]{:S(2)}, u32[]{:S(2)}) collective-permute-start(f32[128,128]{1,0:T(8,128)S(1)} %get-tuple-element.61), channel_id=1, source_target_pairs={{0,12},{1,13},{2,14},{3,15},{4,8},{5,9},{6,10},{7,11},{8,4},{9,5},... | collective-permute-start | bytes 196616 | tf_op jit(solution)/shard_map/ppermute | solution.py:100
  18.3 4.3 %collective-permute-start.5 = (f32[128,128]{1,0:T(8,128)S(1)}, f32[128,128]{1,0:T(8,128)S(1)}, u32[]{:S(2)}, u32[]{:S(2)}) collective-permute-start(f32[128,128]{1,0:T(8,128)S(1)} %get-tuple-element.63), channel_id=1, source_target_pairs={{0,8},{1,9},{2,10},{3,11},{4,12},{5,13},{6,14},{7,15},{8,0},{9,1},... | collective-permute-start | bytes 196616 | tf_op jit(solution)/shard_map/ppermute | solution.py:100
  18.6 4.3 %collective-permute-start.6 = (f32[128,128]{1,0:T(8,128)S(1)}, f32[128,128]{1,0:T(8,128)S(1)}, u32[]{:S(2)}, u32[]{:S(2)}) collective-permute-start(f32[128,128]{1,0:T(8,128)S(1)} %get-tuple-element.64), channel_id=1, source_target_pairs={{0,4},{1,5},{2,6},{3,7},{4,0},{5,1},{6,2},{7,3},{8,12},{9,13},{10,... | collective-permute-start | bytes 196616 | tf_op jit(solution)/shard_map/ppermute | solution.py:100
  23.4 3.1 %collective-permute-start.7 = (f32[16,128]{1,0:T(8,128)S(1)}, f32[16,128]{1,0:T(8,128)S(1)}, u32[]{:S(2)}, u32[]{:S(2)}) collective-permute-start(f32[16,128]{1,0:T(8,128)S(1)} %get-tuple-element.69), channel_id=1, source_target_pairs={{0,3},{1,2},{2,1},{3,0},{4,7},{5,6},{6,5},{7,4},{8,11},{9,10},{10,... | collective-permute-start | bytes 24584 | tf_op jit(solution)/shard_map/ppermute | solution.py:409
  23.5 3.7 %collective-permute-start.8 = (f32[16,128]{1,0:T(8,128)S(1)}, f32[16,128]{1,0:T(8,128)S(1)}, u32[]{:S(2)}, u32[]{:S(2)}) collective-permute-start(f32[16,128]{1,0:T(8,128)S(1)} %get-tuple-element.70), channel_id=1, source_target_pairs={{0,2},{1,3},{2,0},{3,1},{4,6},{5,7},{6,4},{7,5},{8,10},{9,11},{10,... | collective-permute-start | bytes 24584 | tf_op jit(solution)/shard_map/ppermute | solution.py:409
  25.3 1.9 %collective-permute-start.9 = (f32[16,128]{1,0:T(8,128)S(1)}, f32[16,128]{1,0:T(8,128)S(1)}, u32[]{:S(2)}, u32[]{:S(2)}) collective-permute-start(f32[16,128]{1,0:T(8,128)S(1)} %get-tuple-element.71), channel_id=1, source_target_pairs={{0,1},{1,0},{2,3},{3,2},{4,5},{5,4},{6,7},{7,6},{8,9},{9,8},{10,11... | collective-permute-start | bytes 24584 | tf_op jit(solution)/shard_map/ppermute | solution.py:409
  28.1 6.1 %collective-permute-start.10 = (f32[128,128]{1,0:T(8,128)S(1)}, f32[128,128]{1,0:T(8,128)S(1)}, u32[]{:S(2)}, u32[]{:S(2)}) collective-permute-start(f32[128,128]{1,0:T(8,128)S(1)} %get-tuple-element.78), channel_id=1, source_target_pairs={{0,12},{1,13},{2,14},{3,15},{4,8},{5,9},{6,10},{7,11},{8,4},{9,5},... | collective-permute-start | bytes 196616 | tf_op jit(solution)/shard_map/ppermute | solution.py:100
  30.7 4.3 %collective-permute-start.11 = (f32[128,128]{1,0:T(8,128)S(1)}, f32[128,128]{1,0:T(8,128)S(1)}, u32[]{:S(2)}, u32[]{:S(2)}) collective-permute-start(f32[128,128]{1,0:T(8,128)S(1)} %get-tuple-element.79), channel_id=1, source_target_pairs={{0,4},{1,5},{2,6},{3,7},{4,0},{5,1},{6,2},{7,3},{8,12},{9,13},{10,... | collective-permute-start | bytes 196616 | tf_op jit(solution)/shard_map/ppermute | solution.py:100
  31.3 4.3 %collective-permute-start.12 = (f32[128,128]{1,0:T(8,128)S(1)}, f32[128,128]{1,0:T(8,128)S(1)}, u32[]{:S(2)}, u32[]{:S(2)}) collective-permute-start(f32[128,128]{1,0:T(8,128)S(1)} %get-tuple-element.80), channel_id=1, source_target_pairs={{0,8},{1,9},{2,10},{3,11},{4,12},{5,13},{6,14},{7,15},{8,0},{9,1},... | collective-permute-start | bytes 196616 | tf_op jit(solution)/shard_map/ppermute | solution.py:100
  35.6 6.3 %collective-permute-start.13 = (f32[128,128]{1,0:T(8,128)S(1)}, f32[128,128]{1,0:T(8,128)S(1)}, u32[]{:S(2)}, u32[]{:S(2)}) collective-permute-start(f32[128,128]{1,0:T(8,128)S(1)} %quad_sum.3.refs_0_), channel_id=1, source_target_pairs={{0,16},{1,17},{2,18},{3,19},{4,20},{5,21},{6,22},{7,23},{8,24},{9,... | collective-permute-start | bytes 196616 | tf_op jit(solution)/shard_map/ppermute | solution.py:100
  41.9 5.6 %collective-permute-start.14 = (f32[128,128]{1,0:T(8,128)S(1)}, f32[128,128]{1,0:T(8,128)S(1)}, u32[]{:S(2)}, u32[]{:S(2)}) collective-permute-start(f32[128,128]{1,0:T(8,128)S(1)} %get-tuple-element.95), channel_id=1, source_target_pairs={{0,12},{1,13},{2,14},{3,15},{4,8},{5,9},{6,10},{7,11},{8,4},{9,5},... | collective-permute-start | bytes 196616 | tf_op jit(solution)/shard_map/ppermute | solution.py:100
  42.4 5.1 %collective-permute-start.15 = (f32[128,128]{1,0:T(8,128)S(1)}, f32[128,128]{1,0:T(8,128)S(1)}, u32[]{:S(2)}, u32[]{:S(2)}) collective-permute-start(f32[128,128]{1,0:T(8,128)S(1)} %get-tuple-element.96), channel_id=1, source_target_pairs={{0,4},{1,5},{2,6},{3,7},{4,0},{5,1},{6,2},{7,3},{8,12},{9,13},{10,... | collective-permute-start | bytes 196616 | tf_op jit(solution)/shard_map/ppermute | solution.py:100
  43.7 4.3 %collective-permute-start.16 = (f32[128,128]{1,0:T(8,128)S(1)}, f32[128,128]{1,0:T(8,128)S(1)}, u32[]{:S(2)}, u32[]{:S(2)}) collective-permute-start(f32[128,128]{1,0:T(8,128)S(1)} %get-tuple-element.97), channel_id=1, source_target_pairs={{0,8},{1,9},{2,10},{3,11},{4,12},{5,13},{6,14},{7,15},{8,0},{9,1},... | collective-permute-start | bytes 196616 | tf_op jit(solution)/shard_map/ppermute | solution.py:100

commit v14 on v12

--- a/solution.py
+++ b/solution.py
@@ -249,8 +249,10 @@
 def mixed_kernel(is_own, intra, q, g, *refs):
     pieces, refs = refs[:2], refs[2:]
     before, refs = ([], refs) if is_own else (refs[:2], refs[2:])
-    mixed, prefix, *stats, scratch = refs
-    load_pieces(pieces, ORDERS[False][1], scratch, 0 if is_own else 2)
+    mixed, prefix, *stats = refs
+    in_order = number_at(ORDERS[False][1], 0 if is_own else 2) // 2 == 0
+    one, two = (piece[...].astype(BF16) for piece in pieces)
+    states = [jnp.where(in_order, one, two), jnp.where(in_order, two, one)]
     blocks = q.shape[0] // HEAD_DIM
 
     def pair(p):
@@ -258,7 +260,7 @@
             square = cross = None
             for j in range(2):
                 part, whole = head_slice(j), head_slice(2 * p + j)
-                m = intra[at, whole] + dot(q[at, whole], scratch[whole, :], 1, 0)
+                m = intra[at, whole] + dot(q[at, whole], states[j], 1, 0)
                 mixed[at, part] = m
                 s, c = m * m, m * g[at, whole].astype(F32)
                 square = s if square is None else square + s
@@ -270,8 +272,8 @@
                     if before:
                         sums = sums + before[0][i : i + 1, :]
                     stats[0][i : i + 1, :] = sums
-        part = slice(p * PAIR, (p + 1) * PAIR)
-        prefix[part, :] = scratch[part, :]
+        for j in range(2):
+            prefix[head_slice(2 * p + j), :] = states[j]
         if before:
             part = slice((1 - p) * PAIR, (2 - p) * PAIR)
             prefix[part, :] = before[1][part, :]
@@ -478,7 +480,6 @@
             [intra, queries, grad_out, *pieces, *before],
             2 * head_flops,
             "mixed",
-            scratch=[pltpu.VMEM((cols, HEAD_DIM), BF16)],
         )
 
     mixed, prefix, stats = mix(True, prefixes[:2], 1)

time: 49.7 us -> 49.7 us (level)
  no operation moved by 1% of the time
where the time goes in v14:
time: 49.7 us; the launch traced here: 49.6 us
  starting transfers between devices  23.2 us (47%)
  Pallas kernels  14.1 us (28%)
  waiting for transfers between devices  11.4 us (23%)
  between operations  0.77 us (2%)
    ppermute x14, starting transfers between devices, exchange(): return lax.ppermute(value, ('seq', 'head'), pairs)  21.3 us
    pallas_call x14, Pallas kernels, call(): return list(kernel(*args))  14.1 us
    ppermute x14, waiting for transfers between devices, exchange(): return lax.ppermute(value, ('seq', 'head'), pairs)  9.57 us
    ppermute x3, starting transfers between devices, all_parts(): parts.append(lax.ppermute(values[by], axis, pairs))  1.92 us
    ppermute x3, waiting for transfers between devices, all_parts(): parts.append(lax.ppermute(values[by], axis, pairs))  1.87 us
  transfers between devices with their start and end apart: 17, of which 12 were waited for; matrix products, arithmetic and copies ran while one was open for 0% of the time, Pallas kernels for 18%

profile of v14, /device:TPU:0, one launch (start us, length us, event | category | flops | bytes accessed | tf_op | source)
XLA Modules:
  0.0 49.6 jit_solution(2382160374274184333)
XLA Ops:
  0.6 0.0 copy-start
  0.6 1.9 %local_state.1 = (f32[128,128]{1,0:T(8,128)S(1)}, f32[128,128]{1,0:T(8,128)S(1)}, f32[128,128]{1,0:T(8,128)S(1)}, f32[128,128]{1,0:T(8,128)S(1)}, bf16[1024,512]...) custom-call(bf16[1024,512]{1,0:T(8,128)(2,1)} %k_hbm.1, bf16[1024,512]{1,0:T(8,128)(2,1)} %v_hbm.1), custom_call_target="tpu_custom_call" | custom-call | flops 134217728 | bytes 4456448 | tf_op jit(solution)/shard_map/local_state/pallas_call | solution.py:60
  2.6 4.0 %collective-permute-start = (f32[128,128]{1,0:T(8,128)S(1)}, f32[128,128]{1,0:T(8,128)S(1)}, u32[]{:S(2)}, u32[]{:S(2)}) collective-permute-start(f32[128,128]{1,0:T(8,128)S(1)} %get-tuple-element.56), channel_id=1, source_target_pairs={{0,12},{1,13},{2,14},{3,15},{4,8},{5,9},{6,10},{7,11},{8,4},{9,5},... | collective-permute-start | bytes 196616 | tf_op jit(solution)/shard_map/ppermute | solution.py:100
  6.6 0.4 collective-permute-start.1
  7.1 0.2 collective-permute-start.2
  7.3 0.0 copy-done
  7.3 1.9 %intra.1 = (f32[1024,512]{1,0:T(8,128)S(1)}, f32[1536,128]{1,0:T(8,128)S(1)}, bf16[512,1024]{1,0:T(8,128)(2,1)S(1)}) custom-call(bf16[1024,512]{1,0:T(8,128)(2,1)S(1)} %copy-done, bf16[1024,512]{1,0:T(8,128)(2,1)S(1)} %get-tuple-element.52.k, bf16[1024,512]{1,0:T(8,128)(2,1)S(1)} %get-tuple-element.53.v), custom_call_target="tpu_custom_call" | custom-call | flops 805306368 | bytes 7077888 | tf_op jit(solution)/shard_map/intra/pallas_call | solution.py:60
  9.2 0.0 collective-permute-done.refs_1_
  9.2 1.7 %collective-permute-done.1.refs_2_ = f32[128,128]{1,0:T(8,128)S(1)} collective-permute-done((f32[128,128]{1,0:T(8,128)S(1)}, f32[128,128]{1,0:T(8,128)S(1)}, u32[]{:S(2)}, u32[]{:S(2)}) %collective-permute-start.1) | collective-permute-done | bytes 65568 | tf_op jit(solution)/shard_map/ppermute | solution.py:100
  10.9 0.4 collective-permute-done.2.refs_3_
  11.3 2.7 %collective-permute-start.3 = (f32[128,128]{1,0:T(8,128)S(1)}, f32[128,128]{1,0:T(8,128)S(1)}, u32[]{:S(2)}, u32[]{:S(2)}) collective-permute-start(f32[128,128]{1,0:T(8,128)S(1)} %quad_sum.2.token), channel_id=1, source_target_pairs={{0,16},{1,17},{2,18},{3,19},{4,20},{5,21},{6,22},{7,23},{8,24},{9,... | collective-permute-start | bytes 196616 | tf_op jit(solution)/shard_map/ppermute | solution.py:100
  14.0 0.7 %scores.1.refs_5_ = bf16[4096,256]{1,0:T(8,128)(2,1)S(1)} custom-call(bf16[1024,512]{1,0:T(8,128)(2,1)S(1)} %copy-done, bf16[1024,512]{1,0:T(8,128)(2,1)S(1)} %get-tuple-element.52.k, f32[128,128]{1,0:T(8,128)S(1)} %quad_sum.2.token), custom_call_target="tpu_custom_call" | custom-call | flops 268435456 | bytes 4259840 | tf_op jit(solution)/shard_map/scores/pallas_call | solution.py:60
  14.7 0.0 copy-start.1
  14.7 1.8 %collective-permute-done.3.refs_4_ = f32[128,128]{1,0:T(8,128)S(1)} collective-permute-done((f32[128,128]{1,0:T(8,128)S(1)}, f32[128,128]{1,0:T(8,128)S(1)}, u32[]{:S(2)}, u32[]{:S(2)}) %collective-permute-start.3) | collective-permute-done | bytes 65568 | tf_op jit(solution)/shard_map/ppermute | solution.py:100
  16.6 0.1 finish.2
  16.6 1.6 %collective-permute-start.4 = (f32[128,128]{1,0:T(8,128)S(1)}, f32[128,128]{1,0:T(8,128)S(1)}, u32[]{:S(2)}, u32[]{:S(2)}) collective-permute-start(f32[128,128]{1,0:T(8,128)S(1)} %get-tuple-element.61), channel_id=1, source_target_pairs={{0,12},{1,13},{2,14},{3,15},{4,8},{5,9},{6,10},{7,11},{8,4},{9,5},... | collective-permute-start | bytes 196616 | tf_op jit(solution)/shard_map/ppermute | solution.py:100
  18.3 0.3 collective-permute-start.5
  18.6 1.6 %collective-permute-start.6 = (f32[128,128]{1,0:T(8,128)S(1)}, f32[128,128]{1,0:T(8,128)S(1)}, u32[]{:S(2)}, u32[]{:S(2)}) collective-permute-start(f32[128,128]{1,0:T(8,128)S(1)} %get-tuple-element.64), channel_id=1, source_target_pairs={{0,4},{1,5},{2,6},{3,7},{4,0},{5,1},{6,2},{7,3},{8,12},{9,13},{10,... | collective-permute-start | bytes 196616 | tf_op jit(solution)/shard_map/ppermute | solution.py:100
  20.2 1.7 %collective-permute-done.4.refs_1_ = f32[128,128]{1,0:T(8,128)S(1)} collective-permute-done((f32[128,128]{1,0:T(8,128)S(1)}, f32[128,128]{1,0:T(8,128)S(1)}, u32[]{:S(2)}, u32[]{:S(2)}) %collective-permute-start.4) | collective-permute-done | bytes 65568 | tf_op jit(solution)/shard_map/ppermute | solution.py:100
  21.9 0.0 copy-done.1
  21.9 0.5 %mixed.2 = (f32[1024,256]{1,0:T(8,128)S(1)}, bf16[512,128]{1,0:T(8,128)(2,1)S(1)}, f32[16,128]{1,0:T(8,128)S(1)}) custom-call(f32[1024,512]{1,0:T(8,128)S(1)} %get-tuple-element.54.intra, bf16[1024,512]{1,0:T(8,128)(2,1)S(1)} %copy-done, bf16[1024,512]{1,0:T(8,128)(2,1)S(1)} %copy-done.1, f32[128,128]{1,0:T(8,128)S(1)} %get-tuple-element.60.refs_0_, ...), custom_call_target="tpu_custom_call" | custom-call | flops 67108864 | bytes 5513216 | tf_op jit(solution)/shard_map/mixed/pallas_call | solution.py:60
  22.4 0.1 collective-permute-done.5.refs_0_
  22.5 0.3 collective-permute-done.6.refs_1_
  22.9 0.5 %mixed.3 = (f32[1024,256]{1,0:T(8,128)S(1)}, bf16[512,128]{1,0:T(8,128)(2,1)S(1)}, f32[16,128]{1,0:T(8,128)S(1)}, f32[16,128]{1,0:T(8,128)S(1)}, f32[16,128]{1,0:T(8,128)S(1)}, /*index=5*/f32[16,128]{1,0:T(8,128)S(1)}) custom-call(f32[1024,512]{1,0:T(8,128)S(1)} %get-tuple-element.54.intra, bf16[1024,512]{1,0:T(8,128)(2,1)S(1)} %copy-done, ...), custom_call_target="tpu_custom_call" | custom-call | flops 67108864 | bytes 5677056 | tf_op jit(solution)/shard_map/mixed/pallas_call | solution.py:60
  23.4 0.1 collective-permute-start.7
  23.5 1.8 %collective-permute-start.8 = (f32[16,128]{1,0:T(8,128)S(1)}, f32[16,128]{1,0:T(8,128)S(1)}, u32[]{:S(2)}, u32[]{:S(2)}) collective-permute-start(f32[16,128]{1,0:T(8,128)S(1)} %get-tuple-element.70), channel_id=1, source_target_pairs={{0,2},{1,3},{2,0},{3,1},{4,6},{5,7},{6,4},{7,5},{8,10},{9,11},{10,... | collective-permute-start | bytes 24584 | tf_op jit(solution)/shard_map/ppermute | solution.py:421
  25.3 0.1 collective-permute-start.9
  25.3 1.2 %collective-permute-done.7.refs_1_ = f32[16,128]{1,0:T(8,128)S(1)} collective-permute-done((f32[16,128]{1,0:T(8,128)S(1)}, f32[16,128]{1,0:T(8,128)S(1)}, u32[]{:S(2)}, u32[]{:S(2)}) %collective-permute-start.7) | collective-permute-done | bytes 8224 | tf_op jit(solution)/shard_map/ppermute | solution.py:421
  26.5 0.7 %collective-permute-done.8.refs_2_ = f32[16,128]{1,0:T(8,128)S(1)} collective-permute-done((f32[16,128]{1,0:T(8,128)S(1)}, f32[16,128]{1,0:T(8,128)S(1)}, u32[]{:S(2)}, u32[]{:S(2)}) %collective-permute-start.8) | collective-permute-done | bytes 8224 | tf_op jit(solution)/shard_map/ppermute | solution.py:421
  27.2 0.0 collective-permute-done.9.refs_3_
  27.2 0.8 %norm.1 = (bf16[1024,512]{1,0:T(8,128)(2,1)S(1)}, f32[8,128]{1,0:T(8,128)S(1)}, f32[1536,128]{1,0:T(8,128)S(1)}, f32[128,128]{1,0:T(8,128)S(1)}, f32[128,128]{1,...) custom-call(f32[1024,256]{1,0:T(8,128)S(1)} %get-tuple-element.62.mixed.refs_0_, ...), custom_call_target="tpu_custom_call" | custom-call | flops 134217728 | bytes 6328320 | tf_op jit(solution)/shard_map/norm/pallas_call | solution.py:60
  28.0 2.7 %collective-permute-start.10 = (f32[128,128]{1,0:T(8,128)S(1)}, f32[128,128]{1,0:T(8,128)S(1)}, u32[]{:S(2)}, u32[]{:S(2)}) collective-permute-start(f32[128,128]{1,0:T(8,128)S(1)} %get-tuple-element.78), channel_id=1, source_target_pairs={{0,12},{1,13},{2,14},{3,15},{4,8},{5,9},{6,10},{7,11},{8,4},{9,5},... | collective-permute-start | bytes 196616 | tf_op jit(solution)/shard_map/ppermute | solution.py:100
  30.7 0.5 %collective-permute-start.11 = (f32[128,128]{1,0:T(8,128)S(1)}, f32[128,128]{1,0:T(8,128)S(1)}, u32[]{:S(2)}, u32[]{:S(2)}) collective-permute-start(f32[128,128]{1,0:T(8,128)S(1)} %get-tuple-element.79), channel_id=1, source_target_pairs={{0,4},{1,5},{2,6},{3,7},{4,0},{5,1},{6,2},{7,3},{8,12},{9,13},{10,... | collective-permute-start | bytes 196616 | tf_op jit(solution)/shard_map/ppermute | solution.py:100
  31.2 0.3 collective-permute-start.12
  31.6 2.1 %first_grads.1 = (bf16[1024,128]{1,0:T(8,128)(2,1)S(1)}, bf16[1024,128]{1,0:T(8,128)(2,1)S(1)}, f32[1024,128]{1,0:T(8,128)S(1)}, f32[1024,128]{1,0:T(8,128)S(1)}...) custom-call(bf16[1024,512]{1,0:T(8,128)(2,1)S(1)} %copy-done, bf16[1024,512]{1,0:T(8,128)(2,1)S(1)} %get-tuple-element.52.k, ...), custom_call_target="tpu_custom_call" | custom-call | flops 872415232 | bytes 10616832 | tf_op jit(solution)/shard_map/first_grads/pallas_call | solution.py:60
  33.7 0.0 collective-permute-done.10.refs_1_
  33.7 1.3 %collective-permute-done.11.refs_2_ = f32[128,128]{1,0:T(8,128)S(1)} collective-permute-done((f32[128,128]{1,0:T(8,128)S(1)}, f32[128,128]{1,0:T(8,128)S(1)}, u32[]{:S(2)}, u32[]{:S(2)}) %collective-permute-start.11) | collective-permute-done | bytes 65568 | tf_op jit(solution)/shard_map/ppermute | solution.py:100
  35.0 0.5 %collective-permute-done.12.refs_3_ = f32[128,128]{1,0:T(8,128)S(1)} collective-permute-done((f32[128,128]{1,0:T(8,128)S(1)}, f32[128,128]{1,0:T(8,128)S(1)}, u32[]{:S(2)}, u32[]{:S(2)}) %collective-permute-start.12) | collective-permute-done | bytes 65568 | tf_op jit(solution)/shard_map/ppermute | solution.py:100
  35.5 3.3 %collective-permute-start.13 = (f32[128,128]{1,0:T(8,128)S(1)}, f32[128,128]{1,0:T(8,128)S(1)}, u32[]{:S(2)}, u32[]{:S(2)}) collective-permute-start(f32[128,128]{1,0:T(8,128)S(1)} %quad_sum.3.refs_3_), channel_id=1, source_target_pairs={{0,16},{1,17},{2,18},{3,19},{4,20},{5,21},{6,22},{7,23},{8,24},{9,... | collective-permute-start | bytes 196616 | tf_op jit(solution)/shard_map/ppermute | solution.py:100
  38.8 2.0 %second_grads.1 = (bf16[1024,128]{1,0:T(8,128)(2,1)S(1)}, f32[1024,128]{1,0:T(8,128)S(1)}, f32[1024,128]{1,0:T(8,128)S(1)}, bf16[1024,512]{1,0:T(8,128)(2,1)}) custom-call(bf16[1024,512]{1,0:T(8,128)(2,1)S(1)} %copy-done, bf16[1024,512]{1,0:T(8,128)(2,1)S(1)} %get-tuple-element.52.k, bf16[1024,512]{1,0:T(8,128)(2,1)S(1)} %get-tuple-element.53.v, ...), custom_call_target="tpu_custom_call" | custom-call | flops 436207616 | bytes 12521472 | tf_op jit(solution)/shard_map/second_grads/pallas_call | solution.py:60
  40.8 1.0 %collective-permute-done.13.refs_4_ = f32[128,128]{1,0:T(8,128)S(1)} collective-permute-done((f32[128,128]{1,0:T(8,128)S(1)}, f32[128,128]{1,0:T(8,128)S(1)}, u32[]{:S(2)}, u32[]{:S(2)}) %collective-permute-start.13) | collective-permute-done | bytes 65568 | tf_op jit(solution)/shard_map/ppermute | solution.py:100
  41.8 0.1 finish.3
  41.9 0.4 collective-permute-start.14
  42.3 1.4 %collective-permute-start.15 = (f32[128,128]{1,0:T(8,128)S(1)}, f32[128,128]{1,0:T(8,128)S(1)}, u32[]{:S(2)}, u32[]{:S(2)}) collective-permute-start(f32[128,128]{1,0:T(8,128)S(1)} %get-tuple-element.96), channel_id=1, source_target_pairs={{0,4},{1,5},{2,6},{3,7},{4,0},{5,1},{6,2},{7,3},{8,12},{9,13},{10,... | collective-permute-start | bytes 196616 | tf_op jit(solution)/shard_map/ppermute | solution.py:100
  43.7 1.8 %collective-permute-start.16 = (f32[128,128]{1,0:T(8,128)S(1)}, f32[128,128]{1,0:T(8,128)S(1)}, u32[]{:S(2)}, u32[]{:S(2)}) collective-permute-start(f32[128,128]{1,0:T(8,128)S(1)} %get-tuple-element.97), channel_id=1, source_target_pairs={{0,8},{1,9},{2,10},{3,11},{4,12},{5,13},{6,14},{7,15},{8,0},{9,1},... | collective-permute-start | bytes 196616 | tf_op jit(solution)/shard_map/ppermute | solution.py:100
  45.5 1.8 %third_grads.1 = (f32[1024,128]{1,0:T(8,128)S(1)}, f32[1024,128]{1,0:T(8,128)S(1)}, bf16[1024,512]{1,0:T(8,128)(2,1)}) custom-call(bf16[1024,512]{1,0:T(8,128)(2,1)S(1)} %copy-done, bf16[1024,512]{1,0:T(8,128)(2,1)S(1)} %get-tuple-element.52.k, bf16[1024,512]{1,0:T(8,128)(2,1)S(1)} %get-tuple-element.53.v, bf16[1024,512]{1,0:T(8,128)(2,1)S(1)} %get-tuple-element.72.gm, ...), custom_call_target="tpu_custom_call" | custom-call | flops 436207616 | bytes 10944512 | tf_op jit(solution)/shard_map/third_grads/pallas_call | solution.py:60
  47.2 0.0 collective-permute-done.14.refs_9_
  47.2 0.0 collective-permute-done.15.refs_10_
  47.2 0.7 %collective-permute-done.16.refs_11_ = f32[128,128]{1,0:T(8,128)S(1)} collective-permute-done((f32[128,128]{1,0:T(8,128)S(1)}, f32[128,128]{1,0:T(8,128)S(1)}, u32[]{:S(2)}, u32[]{:S(2)}) %collective-permute-start.16) | collective-permute-done | bytes 65568 | tf_op jit(solution)/shard_map/ppermute | solution.py:100
  47.9 1.6 %last.1 = (bf16[1024,512]{1,0:T(8,128)(2,1)}, bf16[1024,512]{1,0:T(8,128)(2,1)}) custom-call(bf16[1024,512]{1,0:T(8,128)(2,1)S(1)} %get-tuple-element.52.k, bf16[1024,512]{1,0:T(8,128)(2,1)S(1)} %get-tuple-element.53.v, f32[1024,128]{1,0:T(8,128)S(1)} %get-tuple-element.89.refs_0_, f32[1024,128]{1,0:T(8,128)S(1)} %get-tuple-element.81.refs_4_.refs_1_, ...), custom_call_target="tpu_custom_call" | custom-call | flops 268435456 | bytes 8650752 | tf_op jit(solution)/shard_map/last/pallas_call | solution.py:60
  (2 shorter events, 0.0 us)
Async XLA Ops:
  0.6 6.6 %copy-start = (bf16[1024,512]{1,0:T(8,128)(2,1)S(1)}, bf16[1024,512]{1,0:T(8,128)(2,1)}, u32[]{:S(2)}) copy-start(bf16[1024,512]{1,0:T(8,128)(2,1)} %q.13) | copy-start | bytes 3145732
  2.6 6.6 %collective-permute-start = (f32[128,128]{1,0:T(8,128)S(1)}, f32[128,128]{1,0:T(8,128)S(1)}, u32[]{:S(2)}, u32[]{:S(2)}) collective-permute-start(f32[128,128]{1,0:T(8,128)S(1)} %get-tuple-element.56), channel_id=1, source_target_pairs={{0,12},{1,13},{2,14},{3,15},{4,8},{5,9},{6,10},{7,11},{8,4},{9,5},... | collective-permute-start | bytes 196616 | tf_op jit(solution)/shard_map/ppermute | solution.py:100
  6.6 4.3 %collective-permute-start.1 = (f32[128,128]{1,0:T(8,128)S(1)}, f32[128,128]{1,0:T(8,128)S(1)}, u32[]{:S(2)}, u32[]{:S(2)}) collective-permute-start(f32[128,128]{1,0:T(8,128)S(1)} %get-tuple-element.57), channel_id=1, source_target_pairs={{0,8},{1,9},{2,10},{3,11},{4,12},{5,13},{6,14},{7,15},{8,0},{9,1},... | collective-permute-start | bytes 196616 | tf_op jit(solution)/shard_map/ppermute | solution.py:100
  7.1 4.3 %collective-permute-start.2 = (f32[128,128]{1,0:T(8,128)S(1)}, f32[128,128]{1,0:T(8,128)S(1)}, u32[]{:S(2)}, u32[]{:S(2)}) collective-permute-start(f32[128,128]{1,0:T(8,128)S(1)} %get-tuple-element.58), channel_id=1, source_target_pairs={{0,4},{1,5},{2,6},{3,7},{4,0},{5,1},{6,2},{7,3},{8,12},{9,13},{10,... | collective-permute-start | bytes 196616 | tf_op jit(solution)/shard_map/ppermute | solution.py:100
  11.3 5.2 %collective-permute-start.3 = (f32[128,128]{1,0:T(8,128)S(1)}, f32[128,128]{1,0:T(8,128)S(1)}, u32[]{:S(2)}, u32[]{:S(2)}) collective-permute-start(f32[128,128]{1,0:T(8,128)S(1)} %quad_sum.2.token), channel_id=1, source_target_pairs={{0,16},{1,17},{2,18},{3,19},{4,20},{5,21},{6,22},{7,23},{8,24},{9,... | collective-permute-start | bytes 196616 | tf_op jit(solution)/shard_map/ppermute | solution.py:100
  14.7 7.2 %copy-start.1 = (bf16[1024,512]{1,0:T(8,128)(2,1)S(1)}, bf16[1024,512]{1,0:T(8,128)(2,1)}, u32[]{:S(2)}) copy-start(bf16[1024,512]{1,0:T(8,128)(2,1)} %g.5) | copy-start | bytes 3145732
  16.6 5.2 %collective-permute-start.4 = (f32[128,128]{1,0:T(8,128)S(1)}, f32[128,128]{1,0:T(8,128)S(1)}, u32[]{:S(2)}, u32[]{:S(2)}) collective-permute-start(f32[128,128]{1,0:T(8,128)S(1)} %get-tuple-element.61), channel_id=1, source_target_pairs={{0,12},{1,13},{2,14},{3,15},{4,8},{5,9},{6,10},{7,11},{8,4},{9,5},... | collective-permute-start | bytes 196616 | tf_op jit(solution)/shard_map/ppermute | solution.py:100
  18.3 4.3 %collective-permute-start.5 = (f32[128,128]{1,0:T(8,128)S(1)}, f32[128,128]{1,0:T(8,128)S(1)}, u32[]{:S(2)}, u32[]{:S(2)}) collective-permute-start(f32[128,128]{1,0:T(8,128)S(1)} %get-tuple-element.63), channel_id=1, source_target_pairs={{0,8},{1,9},{2,10},{3,11},{4,12},{5,13},{6,14},{7,15},{8,0},{9,1},... | collective-permute-start | bytes 196616 | tf_op jit(solution)/shard_map/ppermute | solution.py:100
  18.6 4.3 %collective-permute-start.6 = (f32[128,128]{1,0:T(8,128)S(1)}, f32[128,128]{1,0:T(8,128)S(1)}, u32[]{:S(2)}, u32[]{:S(2)}) collective-permute-start(f32[128,128]{1,0:T(8,128)S(1)} %get-tuple-element.64), channel_id=1, source_target_pairs={{0,4},{1,5},{2,6},{3,7},{4,0},{5,1},{6,2},{7,3},{8,12},{9,13},{10,... | collective-permute-start | bytes 196616 | tf_op jit(solution)/shard_map/ppermute | solution.py:100
  23.4 3.1 %collective-permute-start.7 = (f32[16,128]{1,0:T(8,128)S(1)}, f32[16,128]{1,0:T(8,128)S(1)}, u32[]{:S(2)}, u32[]{:S(2)}) collective-permute-start(f32[16,128]{1,0:T(8,128)S(1)} %get-tuple-element.69), channel_id=1, source_target_pairs={{0,3},{1,2},{2,1},{3,0},{4,7},{5,6},{6,5},{7,4},{8,11},{9,10},{10,... | collective-permute-start | bytes 24584 | tf_op jit(solution)/shard_map/ppermute | solution.py:421
  23.5 3.7 %collective-permute-start.8 = (f32[16,128]{1,0:T(8,128)S(1)}, f32[16,128]{1,0:T(8,128)S(1)}, u32[]{:S(2)}, u32[]{:S(2)}) collective-permute-start(f32[16,128]{1,0:T(8,128)S(1)} %get-tuple-element.70), channel_id=1, source_target_pairs={{0,2},{1,3},{2,0},{3,1},{4,6},{5,7},{6,4},{7,5},{8,10},{9,11},{10,... | collective-permute-start | bytes 24584 | tf_op jit(solution)/shard_map/ppermute | solution.py:421
  25.3 1.9 %collective-permute-start.9 = (f32[16,128]{1,0:T(8,128)S(1)}, f32[16,128]{1,0:T(8,128)S(1)}, u32[]{:S(2)}, u32[]{:S(2)}) collective-permute-start(f32[16,128]{1,0:T(8,128)S(1)} %get-tuple-element.71), channel_id=1, source_target_pairs={{0,1},{1,0},{2,3},{3,2},{4,5},{5,4},{6,7},{7,6},{8,9},{9,8},{10,11... | collective-permute-start | bytes 24584 | tf_op jit(solution)/shard_map/ppermute | solution.py:421
  28.0 5.7 %collective-permute-start.10 = (f32[128,128]{1,0:T(8,128)S(1)}, f32[128,128]{1,0:T(8,128)S(1)}, u32[]{:S(2)}, u32[]{:S(2)}) collective-permute-start(f32[128,128]{1,0:T(8,128)S(1)} %get-tuple-element.78), channel_id=1, source_target_pairs={{0,12},{1,13},{2,14},{3,15},{4,8},{5,9},{6,10},{7,11},{8,4},{9,5},... | collective-permute-start | bytes 196616 | tf_op jit(solution)/shard_map/ppermute | solution.py:100
  30.7 4.3 %collective-permute-start.11 = (f32[128,128]{1,0:T(8,128)S(1)}, f32[128,128]{1,0:T(8,128)S(1)}, u32[]{:S(2)}, u32[]{:S(2)}) collective-permute-start(f32[128,128]{1,0:T(8,128)S(1)} %get-tuple-element.79), channel_id=1, source_target_pairs={{0,4},{1,5},{2,6},{3,7},{4,0},{5,1},{6,2},{7,3},{8,12},{9,13},{10,... | collective-permute-start | bytes 196616 | tf_op jit(solution)/shard_map/ppermute | solution.py:100
  31.2 4.3 %collective-permute-start.12 = (f32[128,128]{1,0:T(8,128)S(1)}, f32[128,128]{1,0:T(8,128)S(1)}, u32[]{:S(2)}, u32[]{:S(2)}) collective-permute-start(f32[128,128]{1,0:T(8,128)S(1)} %get-tuple-element.80), channel_id=1, source_target_pairs={{0,8},{1,9},{2,10},{3,11},{4,12},{5,13},{6,14},{7,15},{8,0},{9,1},... | collective-permute-start | bytes 196616 | tf_op jit(solution)/shard_map/ppermute | solution.py:100
  35.5 6.3 %collective-permute-start.13 = (f32[128,128]{1,0:T(8,128)S(1)}, f32[128,128]{1,0:T(8,128)S(1)}, u32[]{:S(2)}, u32[]{:S(2)}) collective-permute-start(f32[128,128]{1,0:T(8,128)S(1)} %quad_sum.3.refs_3_), channel_id=1, source_target_pairs={{0,16},{1,17},{2,18},{3,19},{4,20},{5,21},{6,22},{7,23},{8,24},{9,... | collective-permute-start | bytes 196616 | tf_op jit(solution)/shard_map/ppermute | solution.py:100
  41.9 5.3 %collective-permute-start.14 = (f32[128,128]{1,0:T(8,128)S(1)}, f32[128,128]{1,0:T(8,128)S(1)}, u32[]{:S(2)}, u32[]{:S(2)}) collective-permute-start(f32[128,128]{1,0:T(8,128)S(1)} %get-tuple-element.95), channel_id=1, source_target_pairs={{0,12},{1,13},{2,14},{3,15},{4,8},{5,9},{6,10},{7,11},{8,4},{9,5},... | collective-permute-start | bytes 196616 | tf_op jit(solution)/shard_map/ppermute | solution.py:100
  42.3 5.0 %collective-permute-start.15 = (f32[128,128]{1,0:T(8,128)S(1)}, f32[128,128]{1,0:T(8,128)S(1)}, u32[]{:S(2)}, u32[]{:S(2)}) collective-permute-start(f32[128,128]{1,0:T(8,128)S(1)} %get-tuple-element.96), channel_id=1, source_target_pairs={{0,4},{1,5},{2,6},{3,7},{4,0},{5,1},{6,2},{7,3},{8,12},{9,13},{10,... | collective-permute-start | bytes 196616 | tf_op jit(solution)/shard_map/ppermute | solution.py:100
  43.7 4.3 %collective-permute-start.16 = (f32[128,128]{1,0:T(8,128)S(1)}, f32[128,128]{1,0:T(8,128)S(1)}, u32[]{:S(2)}, u32[]{:S(2)}) collective-permute-start(f32[128,128]{1,0:T(8,128)S(1)} %get-tuple-element.97), channel_id=1, source_target_pairs={{0,8},{1,9},{2,10},{3,11},{4,12},{5,13},{6,14},{7,15},{8,0},{9,1},... | collective-permute-start | bytes 196616 | tf_op jit(solution)/shard_map/ppermute | solution.py:100
